TPU v7x, 32 devices: a whole 2x2x4 slice. The times are simulated.
32 devices in a mesh: gx: 8 (over z, x), gy: 4 (over y, core).
Axes of the slice: x: 2, y: 2, z: 4, core: 2. Of those that a mesh axis runs over, the one named last changes fastest.
Arguments:
- leaf_maps: float32 [1, 4096, 8192], P(None, 'gy', 'gx'), may hold values from -5 to 14, as said below
Outputs:
- quad_maps: float32 [1, 4096, 8192], P(None, 'gy', 'gx')
Inputs may be any that keep to these rules, and one draw needn't show every extreme that they name: `leaf_maps`: every patch's block is symmetric and positive definite.
All inputs are finite; a program needn't handle non-finite values.
Results may differ from a plain program's by a relative error of at most 0.000067.
Values sent between devices are 32-bit elements; how exact they have to be, the bound alone decides.
No kernel may reach another device: no remote copies, remote signals or barrier semaphores. Data moves between devices by JAX's collectives and lax.ppermute only.
A program may use at most 128 MiB of HBM per device.

v0:
```python
import jax
import jax.numpy as jnp
from jax import lax
from jax.sharding import PartitionSpec as P


def partner_2(value, axis, apart):
    mask = 2**apart
    pairs = [(source, source ^ mask) for source in range(lax.axis_size(axis))]
    return lax.ppermute(value, axis, pairs)


def pick_rows(matrix, labels, row_labels, edge_width):
    return jnp.concatenate(
        [
            matrix[
                :,
                labels.index(label_id) * edge_width : (labels.index(label_id) + 1) * edge_width,
                :,
            ]
            for label_id in row_labels
        ],
        axis=1,
    )


def pick_cols(matrix, labels, col_labels, edge_width):
    return jnp.concatenate(
        [
            matrix[
                :,
                :,
                labels.index(label_id) * edge_width : (labels.index(label_id) + 1) * edge_width,
            ]
            for label_id in col_labels
        ],
        axis=2,
    )


def cholesky_apply(coupling, target):
    factor = jnp.linalg.cholesky(coupling)
    half_way = jax.scipy.linalg.solve_triangular(factor, target, lower=True)
    return jax.scipy.linalg.solve_triangular(factor, half_way, lower=True, trans=1)


def merge(first_map, first_labels, second_map, second_labels, shared, out_order, edge_width):
    coupling = pick_cols(
        pick_rows(first_map, first_labels, shared, edge_width), first_labels, shared, edge_width
    )
    coupling = coupling + pick_cols(
        pick_rows(second_map, second_labels, shared, edge_width), second_labels, shared, edge_width
    )
    pieces = []
    direct_rows = []
    for label_id in out_order:
        if label_id in first_labels:
            source, source_labels = (first_map, first_labels)
        else:
            source, source_labels = (second_map, second_labels)
        row_band = pick_rows(source, source_labels, [label_id], edge_width)
        pieces.append(pick_cols(row_band, source_labels, shared, edge_width))
        blocks = []
        for other_id in out_order:
            if other_id in source_labels:
                blocks.append(pick_cols(row_band, source_labels, [other_id], edge_width))
            else:
                blocks.append(jnp.zeros((row_band.shape[0], edge_width, edge_width), jnp.float32))
        direct_rows.append(jnp.concatenate(blocks, axis=2))
    edge_rows = jnp.concatenate(pieces, axis=1)
    direct = jnp.concatenate(direct_rows, axis=1)
    solved = cholesky_apply(coupling, jnp.swapaxes(edge_rows, 1, 2))
    return direct - jnp.einsum("fik,fkj->fij", edge_rows, solved, precision=lax.Precision.HIGHEST)


def body(leaf_maps):
    edge_width = leaf_maps.shape[1] // 4
    block_span = 4 * edge_width
    column_bit = lax.axis_index("gx") // (lax.axis_size("gx") // 2)
    row_bit = lax.axis_index("gy") // (lax.axis_size("gy") // 2)
    far_x = lax.axis_size("gx").bit_length() - 2
    far_y = lax.axis_size("gy").bit_length() - 2
    partner = partner_2(leaf_maps, "gy", far_y)
    lower_leaf = jnp.where(row_bit == 0, leaf_maps, partner)
    upper_leaf = jnp.where(row_bit == 0, partner, leaf_maps)
    column_map = merge(
        lower_leaf, [0, 1, 2, 9], upper_leaf, [3, 4, 9, 5], [9], [0, 3, 1, 4, 2, 5], edge_width
    )
    beside = partner_2(column_map, "gx", far_x)
    left_map = jnp.where(column_bit == 0, column_map, beside)
    right_map = jnp.where(column_bit == 0, beside, column_map)
    whole_quad = merge(
        left_map,
        [0, 1, 8, 9, 4, 6],
        right_map,
        [8, 9, 2, 3, 5, 7],
        [8, 9],
        [0, 2, 4, 5, 1, 3, 6, 7],
        edge_width,
    )
    row_band = lax.dynamic_slice_in_dim(whole_quad, row_bit * block_span, block_span, 1)
    return lax.dynamic_slice_in_dim(row_band, column_bit * block_span, block_span, 2)


def solution(mesh):
    return jax.shard_map(
        body,
        mesh=mesh,
        in_specs=(P(None, "gy", "gx"),),
        out_specs=P(None, "gy", "gx"),
        check_vma=False,
    )
```

profile of v0, /device:TPU:24, one launch (start us, length us, event | category | flops | bytes accessed | tf_op | source)
XLA Modules:
  0.0 876.7 jit_solution(4730268715105711759)
XLA Ops:
  0.0 5.3 copy.16
  6.9 91.0 %collective-permute-done = f32[1,1024,1024]{1,2,0:T(8,128)} collective-permute-done((f32[1,1024,1024]{1,2,0:T(8,128)}, f32[1,1024,1024]{1,2,0:T(8,128)}, u32[]{:S(2)}, u32[]{:S(2)}) %collective-permute-start) | collective-permute-done | bytes 4194336 | tf_op jit(solution)/shard_map/ppermute | solution.py:10
  98.0 4.4 broadcast_select_fusion.2
  113.1 11.7 %custom-call.51 = f32[1,128,128]{2,1,0:T(8,128)S(1)} custom-call(f32[1,128,128]{2,1,0:T(8,128)S(1)} %copy.19), custom_call_target="Cholesky" | custom-call | tf_op jit(solution)/shard_map/jit(cholesky)/cholesky | solution.py:42
  125.0 9.8 %custom-call.62 = f32[1,1,128,128]{2,3,1,0:T(8,128)S(1)} custom-call(f32[1,1,128,128]{3,2,1,0:T(8,128)S(1)} %get-tuple-element.121), custom_call_target="InvertDiagBlocksLowerTriangular" | custom-call | tf_op jit(solution)/shard_map/jit(cholesky)/cholesky/custom-call.10 | solution.py:42
  137.8 12.9 %custom-call.52 = f32[1,128,128]{2,1,0:T(8,128)S(1)} custom-call(f32[1,128,128]{2,1,0:T(8,128)} %copy.21), custom_call_target="Cholesky" | custom-call | tf_op jit(solution)/shard_map/jit(cholesky)/cholesky | solution.py:42
  155.3 7.4 while.2
  156.0 2.3 dynamic-slice.22
  159.7 2.2 dynamic-slice.22
  162.7 20.5 %custom-call.53 = f32[2,128,128]{1,2,0:T(8,128)S(1)} custom-call(f32[2,128,128]{2,1,0:T(8,128)} %get-tuple-element.13), custom_call_target="InvertDiagBlocksLowerTriangular" | custom-call | tf_op jit(solution)/shard_map/jit(_solve_triangular)/triangular_solve | solution.py:44
  184.0 1.7 convolution_subtract_fusion.2
  187.4 1.8 convolution_subtract_fusion.1
  193.8 10.5 %fusion = f32[1,1536,1536]{1,2,0:T(8,128)} fusion(f32[1536,1536]{0,1:T(8,128)S(1)} %bitcast_dynamic-update-slice_fusion.10, f32[128,1536]{1,0:T(8,128)S(1)} %fusion.66, f32[128,1536]{1,0:T(8,128)S(1)} %fusion.65, f32[1,1536,256]{1,2,0:T(8,128)S(1)} %constant_dynamic-update-slice_fusion.36), kind=kOutput, calls=%fused_computation.5 | convolution fusion | flops 7250509824 | bytes 22020096 | tf_op jit(solution)/shard_map/fik,fkj->fij/dot_general | solution.py:73
  206.3 405.1 %collective-permute-done.1 = f32[1,1536,1536]{1,2,0:T(8,128)} collective-permute-done((f32[1,1536,1536]{1,2,0:T(8,128)}, f32[1,1536,1536]{1,2,0:T(8,128)}, u32[]{:S(2)}, u32[]{:S(2)}) %collective-permute-start.1) | collective-permute-done | bytes 9437216 | tf_op jit(solution)/shard_map/ppermute | solution.py:10
  611.4 7.7 broadcast_select_fusion
  619.1 3.6 copy-done
  622.7 2.8 copy-done.1
  626.7 1.6 copy.25
  628.6 11.7 %custom-call.54 = f32[1,128,128]{2,1,0:T(8,128)S(1)} custom-call(f32[1,128,128]{2,1,0:T(8,128)S(1)} %cholesky.339), custom_call_target="Cholesky" | custom-call | tf_op jit(solution)/shard_map/jit(cholesky)/cholesky | solution.py:42
  640.5 1.9 slice_dynamic-update-slice_fusion.7
  642.3 2.3 constant_dynamic-update-slice_fusion.97
  644.6 2.2 constant_dynamic-update-slice_fusion.104
  648.2 9.8 %custom-call.55 = f32[1,1,128,128]{2,3,1,0:T(8,128)S(1)} custom-call(f32[1,1,128,128]{3,2,1,0:T(8,128)S(1)} %get-tuple-element.119), custom_call_target="InvertDiagBlocksLowerTriangular" | custom-call | tf_op jit(solution)/shard_map/jit(cholesky)/cholesky | solution.py:42
  658.7 11.7 %custom-call.56 = f32[1,128,128]{2,1,0:T(8,128)S(1)} custom-call(f32[1,128,128]{2,1,0:T(8,128)S(1)} %cholesky.343), custom_call_target="Cholesky" | custom-call | tf_op jit(solution)/shard_map/jit(cholesky)/cholesky | solution.py:42
  671.1 10.2 %custom-call.57 = f32[1,1,128,128]{2,3,1,0:T(8,128)S(1)} custom-call(f32[1,1,128,128]{3,2,1,0:T(8,128)S(1)} %get-tuple-element.116), custom_call_target="InvertDiagBlocksLowerTriangular" | custom-call | tf_op jit(solution)/shard_map/jit(cholesky)/cholesky | solution.py:42
  682.0 11.7 %custom-call.58 = f32[1,128,128]{2,1,0:T(8,128)S(1)} custom-call(f32[1,128,128]{2,1,0:T(8,128)S(1)} %cholesky.348), custom_call_target="Cholesky" | custom-call | tf_op jit(solution)/shard_map/jit(cholesky)/cholesky | solution.py:42
  694.4 9.8 %custom-call.63 = f32[1,1,128,128]{2,3,1,0:T(8,128)S(1)} custom-call(f32[1,1,128,128]{3,2,1,0:T(8,128)S(1)} %get-tuple-element.113), custom_call_target="InvertDiagBlocksLowerTriangular" | custom-call | tf_op jit(solution)/shard_map/jit(cholesky)/cholesky/custom-call.10 | solution.py:42
  704.8 11.8 %custom-call.59 = f32[1,128,128]{2,1,0:T(8,128)S(1)} custom-call(f32[1,128,128]{2,1,0:T(8,128)S(1)} %fusion.43), custom_call_target="Cholesky" | custom-call | tf_op jit(solution)/shard_map/jit(cholesky)/cholesky | solution.py:42
  720.1 7.8 while.3
  727.9 39.3 %custom-call.60 = f32[4,128,128]{1,2,0:T(8,128)S(1)} custom-call(f32[4,128,128]{2,1,0:T(8,128)S(1)} %get-tuple-element.21), custom_call_target="InvertDiagBlocksLowerTriangular" | custom-call | tf_op jit(solution)/shard_map/jit(_solve_triangular)/triangular_solve | solution.py:44
  769.4 2.2 constant_dynamic-update-slice_fusion.102
  774.5 2.2 constant_dynamic-update-slice_fusion.100
  792.9 2.0 fusion.25
  801.7 2.1 fusion.22
  804.8 29.1 %fusion.1 = f32[2048,2048]{0,1:T(8,128)S(1)} fusion(f32[128,2048]{1,0:T(8,128)S(1)} %fusion.73, f32[128,2048]{1,0:T(8,128)S(1)} %fusion.71, f32[128,2048]{1,0:T(8,128)S(1)} %fusion.69, f32[128,2048]{1,0:T(8,128)S(1)} %fusion.68, f32[1,2048,512]{1,2,0:T(8,128)S(1)} %slice_dynamic-update-slice_fusion), kind=kOutput, calls=%fused_computation.9 | convolution fusion | flops 25772949504 | bytes 25165824 | tf_op jit(solution)/shard_map/fik,fkj->fij/dot_general | solution.py:73
  834.7 2.0 constant_dynamic-update-slice_fusion.95
  837.5 2.0 constant_dynamic-update-slice_fusion.93
  840.3 2.0 constant_dynamic-update-slice_fusion.91
  843.1 1.6 bitcast_dynamic-update-slice_fusion.9
  844.7 2.2 constant_dynamic-update-slice_fusion.98
  846.9 3.2 bitcast_dynamic-update-slice_fusion.8
  850.1 1.6 bitcast_dynamic-update-slice_fusion.7
  851.7 3.2 bitcast_dynamic-update-slice_fusion.6
  856.4 3.2 bitcast_dynamic-update-slice_fusion.4
  859.6 1.5 bitcast_dynamic-update-slice_fusion.3
  861.1 3.2 bitcast_dynamic-update-slice_fusion.2
  864.3 6.6 dynamic-slice_subtract_fusion
  871.0 5.3 copy.28
  (185 shorter events, 78.8 us)
Async XLA Ops:
  5.3 92.6 %collective-permute-start = (f32[1,1024,1024]{1,2,0:T(8,128)}, f32[1,1024,1024]{1,2,0:T(8,128)}, u32[]{:S(2)}, u32[]{:S(2)}) collective-permute-start(f32[1,1024,1024]{1,2,0:T(8,128)} %copy.16), channel_id=1, source_target_pairs={{0,2},{1,3},{2,0},{3,1},{4,6},{5,7},{6,4},{7,5},{8,10},{9,11},{10,... | collective-permute-start | bytes 12582920 | tf_op jit(solution)/shard_map/ppermute | solution.py:10
  102.4 2.0 copy-start.3
  104.6 1.2 copy-start.9
  105.8 1.1 copy-start.11
  106.9 1.2 copy-start.13
  108.1 1.2 copy-start.15
  109.2 1.1 copy-start.17
  112.3 0.8 copy-start.19
  186.6 3.4 copy-start.18
  187.4 2.6 copy-start.14
  187.4 2.7 copy-start.16
  190.0 1.4 copy-start.12
  191.6 1.4 copy-start.10
  204.2 407.1 %collective-permute-start.1 = (f32[1,1536,1536]{1,2,0:T(8,128)}, f32[1,1536,1536]{1,2,0:T(8,128)}, u32[]{:S(2)}, u32[]{:S(2)}) collective-permute-start(f32[1,1536,1536]{1,2,0:T(8,128)} %fusion), channel_id=1, source_target_pairs={{0,16},{4,20},{8,24},{12,28},{16,0},{20,4},{24,8},{28,12},{1,17},{... | collective-permute-start | bytes 28311560 | tf_op jit(solution)/shard_map/ppermute | solution.py:10
  619.1 3.6 copy-start
  619.1 6.4 copy-start.1
  626.7 1.7 copy-start.4
  771.6 8.0 copy-start.2
  804.8 29.9 %copy-start.7 = (f32[1,256,2048]{1,2,0:T(8,128)S(1)}, f32[1,256,2048]{1,2,0:T(8,128)}, u32[]{:S(2)}) copy-start(f32[1,256,2048]{1,2,0:T(8,128)} %get-tuple-element.81) | copy-start | bytes 6291460
  804.8 29.9 %copy-start.6 = (f32[1,256,2048]{1,2,0:T(8,128)S(1)}, f32[1,256,2048]{1,2,0:T(8,128)}, u32[]{:S(2)}) copy-start(f32[1,256,2048]{1,2,0:T(8,128)} %get-tuple-element.82) | copy-start | bytes 6291460
  804.8 29.9 %copy-start.5 = (f32[1,256,2048]{1,2,0:T(8,128)S(1)}, f32[1,256,2048]{1,2,0:T(8,128)}, u32[]{:S(2)}) copy-start(f32[1,256,2048]{1,2,0:T(8,128)} %get-tuple-element.83) | copy-start | bytes 6291460
  856.4 3.2 copy-start.8
where the time goes:
time: 889 us; the launch traced here: 877 us
  waiting for transfers between devices  496 us (56%)
  other arithmetic  197 us (22%)
  local copies, waits for them, and re-layouts  108 us (12%)
  matrix products  67.6 us (8%)
    ppermute x2, waiting for transfers between devices, partner_2(): return lax.ppermute(value, axis, pairs)  496 us
    another operation x22, other arithmetic, cholesky_apply(): factor = jnp.linalg.cholesky(coupling)  115 us
    unnamed x110, local copies, waits for them, and re-layouts  75.6 us
    another operation x6, other arithmetic, cholesky_apply(): jax.scipy.linalg.solve_triangular(factor, half_way, lower=True, trans=1)  60.7 us
    dot_general x2, matrix products, merge(): jnp.einsum('fik,fkj->fij', edge_rows, solved, precision=lax.Precision.HIG...  39.5 us
    another operation x23, local copies, waits for them, and re-layouts  20.4 us
  transfers between devices with their start and end apart: 2, of which 2 were waited for; matrix products, arithmetic and copies ran while one was open for 0% of the time, Pallas kernels for 0%

commit v1 on v0

v1 whole, which is shorter than its diff:
```python
import jax
import jax.numpy as jnp
from jax import lax
from jax.experimental import pallas as pl
from jax.experimental.pallas import tpu as pltpu
from jax.sharding import PartitionSpec as P

F32 = jnp.float32
BF16 = jnp.bfloat16
T = 128
HBM = pl.BlockSpec(memory_space=pl.ANY)
VMEM = pl.BlockSpec(memory_space=pltpu.VMEM)
SMEM = pl.BlockSpec(memory_space=pltpu.SMEM)
PARAMS = pltpu.CompilerParams(vmem_limit_bytes=56 * 2**20)


def dot(a, b, dims=((1,), (0,))):
    return lax.dot_general(
        a, b, (dims, ((), ())), precision=lax.Precision.HIGHEST, preferred_element_type=F32
    )


def dot16(a, b, dims=((1,), (0,))):
    return lax.dot_general(a, b, (dims, ((), ())), preferred_element_type=F32)


def split(a):
    high = a.astype(BF16)
    return high, (a - high.astype(F32)).astype(BF16)


def dot3(a, b, dims=((1,), (0,))):
    return dot16(a[0], b[0], dims) + (dot16(a[0], b[1], dims) + dot16(a[1], b[0], dims))


NT = ((1,), (1,))
TN = ((0,), (0,))


def upper(n):
    return [(i, j) for i in range(n) for j in range(i, n)]


def panel(rows, c0):
    n = rows.shape[1]
    sub = lax.broadcasted_iota(jnp.int32, (8, n), 0)
    lane = lax.broadcasted_iota(jnp.int32, (8, n), 1)
    cols = [jnp.broadcast_to(rows[:, c0 + k : c0 + k + 1], (8, n)) for k in range(8)]
    out = jnp.where((lane >= c0) & (lane < c0 + 8), (lane - c0 == sub).astype(F32), rows)
    for k in range(8):
        inv = 1.0 / cols[k][k : k + 1, :]
        here = sub == k
        mult = cols[k]
        pivot_row = out[k : k + 1, :] * inv
        out = jnp.where(here, pivot_row, out - mult * pivot_row)
        for j in range(k + 1, 8):
            pivot = cols[j][k : k + 1, :] * inv
            cols[j] = jnp.where(here, pivot, cols[j] - mult * pivot)
    return out


def put_rows(matrix, rows, r0):
    parts = [matrix[:r0]] if r0 else []
    parts.append(rows)
    if r0 + rows.shape[0] < matrix.shape[0]:
        parts.append(matrix[r0 + rows.shape[0] :])
    return jnp.concatenate(parts, axis=0)


def invert_tiles(mats):
    n = mats[0].shape[0]
    lane = lax.broadcasted_iota(jnp.int32, (n, n), 1)
    for c0 in range(0, n, 8):
        done = []
        for m in mats:
            rows = panel(m[c0 : c0 + 8, :], c0)
            wide = put_rows(jnp.zeros((n, n), F32), rows, c0)
            rest = jnp.where((lane >= c0) & (lane < c0 + 8), 0.0, m) - dot(m, wide)
            done.append(put_rows(rest, rows, c0))
        mats = done
    return mats


def invert_in_place(refs):
    n = refs[0].shape[0]
    for p in range(0, n, T):
        pivots = invert_tiles([ref[p : p + T, p : p + T] for ref in refs])
        for ref, pivot in zip(refs, pivots):
            rows = dot(pivot, ref[p : p + T, :])
            parts = ([rows[:, :p]] if p else []) + [pivot]
            if p + T < n:
                parts.append(rows[:, p + T :])
            rows = jnp.concatenate(parts, axis=1)
            for q in range(0, n, T):
                if q != p:
                    change = dot(ref[q : q + T, p : p + T], rows)
                    ref[q : q + T, p : p + T] = jnp.zeros((T, T), F32)
                    ref[q : q + T, :] = ref[q : q + T, :] - change
            ref[p : p + T, :] = rows


def cut_kernel(place, leaf, inner, cross, outer, sem):
    e = leaf.shape[1] // 4
    v, u = place[0], place[1]
    ext = [v, 2 + u]
    inn = [1 - v, 3 - u]

    def src(side_r, side_c, r, c, size):
        return leaf.at[
            0,
            pl.ds(pl.multiple_of(side_r * e + r * size, T), size),
            pl.ds(pl.multiple_of(side_c * e + c * size, T), size),
        ]

    copies = []

    def add(source, target):
        copies.append(pltpu.make_async_copy(source, target, sem.at[len(copies)]))
        copies[-1].start()

    tiles = e // T
    at = 0
    for side in (1, 0):
        for r, c in upper(tiles):
            add(src(inn[side], inn[side], r, c, T), inner.at[pl.ds(at, T)])
            at += T
    for r in range(tiles):
        for c in range(tiles):
            add(src(inn[0], inn[1], r, c, T), inner.at[pl.ds(at, T)])
            at += T
    for r in range(2):
        for c in range(2):
            add(src(ext[r], inn[c], 0, 0, e), cross.at[pl.ds(r * e, e), pl.ds(c * e, e)])
    at = 0
    for r, c in upper(2 * tiles):
        add(
            src(ext[r // tiles], ext[c // tiles], r % tiles, c % tiles, T),
            outer.at[pl.ds(at, T)],
        )
        at += T
    for copy in copies:
        copy.wait()


def cut(place, leaf):
    e = leaf.shape[1] // 4
    tiles = e // T
    n_inner = 2 * len(upper(tiles)) + tiles * tiles
    n_outer = len(upper(2 * tiles))
    n_copies = n_inner + 4 + n_outer
    return pl.pallas_call(
        cut_kernel,
        out_shape=[
            jax.ShapeDtypeStruct((n_inner * T, T), F32),
            jax.ShapeDtypeStruct((2 * e, 2 * e), F32),
            jax.ShapeDtypeStruct((n_outer * T, T), F32),
        ],
        in_specs=[SMEM, HBM],
        out_specs=[HBM, HBM, HBM],
        scratch_shapes=[pltpu.SemaphoreType.DMA((n_copies,))],
        compiler_params=PARAMS,
        name="cut_leaf",
    )(place, leaf)


def unpack(ref, at, tiles):
    held = {}
    for r, c in upper(tiles):
        held[r, c] = ref[pl.ds(at, T), :]
        if c > r:
            held[c, r] = held[r, c].T
        at += T
    return jnp.concatenate(
        [jnp.concatenate([held[r, c] for c in range(tiles)], axis=1) for r in range(tiles)], axis=0
    )


def unpack_full(ref, at, tiles):
    rows = []
    for r in range(tiles):
        rows.append(
            jnp.concatenate([ref[pl.ds(at + (r * tiles + c) * T, T), :] for c in range(tiles)], axis=1)
        )
    return jnp.concatenate(rows, axis=0)


def factor_kernel(place, mine, across, along, corner, high, low, h0, h1, side, coup, full, cols):
    e = h0.shape[0]
    tiles = e // T
    sym = len(upper(tiles)) * T
    h0[...] = unpack(mine, 0, tiles) + unpack(along, 0, tiles)
    h1[...] = unpack(across, 0, tiles) + unpack(corner, 0, tiles)
    invert_in_place([h0, h1])
    coup[:e, :e] = unpack_full(mine, 2 * sym, tiles)
    coup[:e, e:] = unpack_full(across, 2 * sym, tiles)
    coup[e:, :e] = unpack_full(along, 2 * sym, tiles)
    coup[e:, e:] = unpack_full(corner, 2 * sym, tiles)
    cols[:, :e] = dot(coup[:, :e], h0[...])
    cols[:, e:] = dot(coup[:, e:], h1[...])
    side[...] = -dot(cols[...], coup[...], NT)
    side[:e, :e] = side[:e, :e] + (unpack(mine, sym, tiles) + unpack(across, sym, tiles))
    side[e:, e:] = side[e:, e:] + (unpack(along, sym, tiles) + unpack(corner, sym, tiles))
    invert_in_place([side])
    flow = cols[...]
    flow16 = split(flow)
    away = dot3(split(side[...]), flow16)
    full[...] = dot3(flow16, split(away), TN)
    full[:e, :e] = full[:e, :e] + h0[...]
    full[e:, e:] = full[e:, e:] + h1[...]

    def emit(value, rows, columns):
        high[rows, columns], low[rows, columns] = split(value)

    first, rest = slice(0, e), slice(e, 3 * e)
    emit(full[...], rest, rest)
    emit(-away[:e, :], first, rest)
    same = place[0] == place[1]

    @pl.when(same)
    def _():
        emit(side[:e, :e], first, first)
        emit(-away[:e, :].T, rest, first)

    @pl.when(jnp.logical_not(same))
    def _():
        emit(side[:e, e:], first, first)
        emit(-away[e:, :].T, rest, first)


def factor(place, mine, across, along, corner, e):
    return pl.pallas_call(
        factor_kernel,
        out_shape=[jax.ShapeDtypeStruct((3 * e, 3 * e), BF16)] * 2,
        in_specs=[SMEM, VMEM, VMEM, VMEM, VMEM],
        out_specs=[VMEM, VMEM],
        scratch_shapes=[
            pltpu.VMEM((e, e), F32),
            pltpu.VMEM((e, e), F32),
            pltpu.VMEM((2 * e, 2 * e), F32),
            pltpu.VMEM((2 * e, 2 * e), F32),
            pltpu.VMEM((2 * e, 2 * e), F32),
            pltpu.VMEM((2 * e, 2 * e), F32),
        ],
        compiler_params=PARAMS,
        cost_estimate=pl.CostEstimate(flops=30 * 10**9, bytes_accessed=5 * 10**6, transcendentals=0),
        name="invert_coupling",
    )(place, mine, across, along, corner)


def rows_kernel(mine, across, high, low, top, bottom):
    e = mine.shape[1] // 2
    whole = (high[...], low[...])
    for at, leaf in enumerate((mine, across)):
        first = split(leaf[:, :e])
        second = split(leaf[:, e:])
        inner = slice((1 + at) * e, (2 + at) * e)
        value = dot3(first, (whole[0][:e], whole[1][:e])) + dot3(
            second, (whole[0][inner], whole[1][inner])
        )
        rows = slice(2 * e * at, 2 * e * (at + 1))
        top[rows, :], bottom[rows, :] = split(value)


def row_products(mine, across, high, low):
    e = mine.shape[1] // 2
    return pl.pallas_call(
        rows_kernel,
        out_shape=[jax.ShapeDtypeStruct((4 * e, 3 * e), BF16)] * 2,
        in_specs=[VMEM] * 4,
        out_specs=[VMEM] * 2,
        compiler_params=PARAMS,
        cost_estimate=pl.CostEstimate(flops=3 * 10**9, bytes_accessed=7 * 10**6, transcendentals=0),
        name="row_products",
    )(mine, across, high, low)


def result_kernel(
    place, leaf, mine, across, along, corner, top, bottom, outer0, outer1, out, own, col, sem
):
    e = mine.shape[1] // 2
    tiles = e // T
    v, u = place[0], place[1]
    same = u == v
    ext = [v, 2 + u]
    copies = []
    for r in range(2):
        for c in range(2):
            copies.append(
                pltpu.make_async_copy(
                    leaf.at[
                        0,
                        pl.ds(pl.multiple_of(ext[r] * e, T), e),
                        pl.ds(pl.multiple_of(ext[c] * e, T), e),
                    ],
                    own.at[pl.ds(r * e, e), pl.ds(c * e, e)],
                    sem.at[2 * r + c],
                )
            )
            copies[-1].start()

    @pl.when(same)
    def _():
        col[0] = mine[...]
        col[1] = across[...]

    @pl.when(jnp.logical_not(same))
    def _():
        col[0] = along[...]
        col[1] = corner[...]

    def spot(side, which):
        return pl.ds(pl.multiple_of((2 * side + (v if which == 0 else 1 - v)) * e, T), e)

    for b in range(2):
        right = split(col[b])
        for a in range(2):
            rows = slice(2 * e * a, 2 * e * (a + 1))
            inner = slice((1 + b) * e, (2 + b) * e)
            left = [
                jnp.concatenate([ref[rows, :e], ref[rows, inner]], axis=1) for ref in (top, bottom)
            ]
            value = -dot3(left, right, NT)
            for r in range(2):
                for c in range(2):
                    out[0, spot(r, a), spot(c, b)] = value[r * e : (r + 1) * e, c * e : (c + 1) * e]
    for copy in copies:
        copy.wait()

    @pl.when(same)
    def _():
        held = {}
        for at, (i, j) in enumerate(upper(2 * tiles)):
            ref = outer0 if at < outer0.shape[0] // T else outer1
            at -= 0 if ref is outer0 else outer0.shape[0] // T
            held[i, j] = ref[at * T : (at + 1) * T, :]
            held[j, i] = held[i, j] if i == j else held[i, j].T
        for r in range(2):
            for c in range(2):
                out[0, spot(r, 0), spot(c, 0)] = (
                    out[0, spot(r, 0), spot(c, 0)] + own[r * e : (r + 1) * e, c * e : (c + 1) * e]
                )
                block = jnp.concatenate(
                    [
                        jnp.concatenate(
                            [held[r * tiles + i, c * tiles + j] for j in range(tiles)], axis=1
                        )
                        for i in range(tiles)
                    ],
                    axis=0,
                )
                out[0, spot(r, 1), spot(c, 1)] = out[0, spot(r, 1), spot(c, 1)] + block


def result(place, leaf, mine, across, along, corner, top, bottom, outer0, outer1):
    e = mine.shape[1] // 2
    return pl.pallas_call(
        result_kernel,
        out_shape=jax.ShapeDtypeStruct((1, 4 * e, 4 * e), F32),
        in_specs=[SMEM, HBM] + [VMEM] * 8,
        out_specs=VMEM,
        scratch_shapes=[
            pltpu.VMEM((2 * e, 2 * e), F32),
            pltpu.VMEM((2, 2 * e, 2 * e), F32),
            pltpu.SemaphoreType.DMA((4,)),
        ],
        compiler_params=PARAMS,
        cost_estimate=pl.CostEstimate(flops=4 * 10**9, bytes_accessed=12 * 10**6, transcendentals=0),
        name="result",
    )(place, leaf, mine, across, along, corner, top, bottom, outer0, outer1)


def solution(mesh):
    nx, ny = mesh.shape["gx"], mesh.shape["gy"]
    devices = [(x, y) for x in range(nx) for y in range(ny)]

    def is_same(x, y):
        return x // (nx // 2) == y // (ny // 2)

    def send(value, along_y, only=None):
        pairs = []
        for x, y in devices:
            if only is None or is_same(x, y) == only:
                to = (x, (y + ny // 2) % ny) if along_y else ((x + nx // 2) % nx, y)
                pairs.append((x * ny + y, to[0] * ny + to[1]))
        return lax.ppermute(value, ("gx", "gy"), pairs)

    def body(leaf):
        e = leaf.shape[1] // 4
        v = lax.axis_index("gx") // (nx // 2)
        u = lax.axis_index("gy") // (ny // 2)
        place = jnp.stack([v, u]).astype(jnp.int32)
        inner, cross, outer = cut(place, leaf)
        half = outer.shape[0] // 2
        inner_x = send(inner, False)
        inner_y = send(inner, True)
        passed = send(outer[half:], True, only=False)
        inner_d = send(inner_x, True)
        cross_x = send(cross, False)
        cross_y = send(cross, True, only=True)
        cross_d = send(cross_x, True, only=True)
        outer0 = send(jnp.where(u == v, passed, outer[:half]), False)
        outer1 = send(outer0, True, only=False)
        high, low = factor(place, inner, inner_x, inner_y, inner_d, e)
        top, bottom = row_products(cross, cross_x, high, low)
        return result(place, leaf, cross, cross_x, cross_y, cross_d, top, bottom, outer0, outer1)

    return jax.shard_map(
        body,
        mesh=mesh,
        in_specs=(P(None, "gy", "gx"),),
        out_specs=P(None, "gy", "gx"),
        check_vma=False,
    )
```

time: 889 us -> 238 us (0.27); the launches traced: 877 us -> 235 us
  waiting for transfers between devices: 496 us -> 79.1 us
  other arithmetic: 197 us -> 1.67 us
  Pallas kernels: 0 us -> 137 us
  local copies, waits for them, and re-layouts: 108 us -> 2.39 us
  matrix products: 67.6 us -> 0 us
  starting transfers between devices: 1.85 us -> 14.1 us
    ppermute x2 -> x9, waiting for transfers between devices: 496 us -> 79.1 us  [send(): return lax.ppermute(value, ('gx', 'gy'), pairs)]
    another operation x28 -> x1, other arithmetic: 176 us -> 0.66 us  [body(): place = jnp.stack([v, u]).astype(jnp.int32)]
    pallas_call x0 -> x4, Pallas kernels: none -> 137 us  [the longest x1 73.5 us: cut(): pl.pallas_call(cut_kernel, out_shape=[jax.ShapeDtypeStruct((n_inner * T,...]
    unnamed x110 -> x14, local copies, waits for them, and re-layouts: 75.6 us -> 1.39 us
    dot_general x2 -> x0, matrix products: 39.5 us -> none  [merge(): jnp.einsum('fik,fkj->fij', edge_rows, solved, precision=lax.Precision.HIG...]
    another operation x28 -> x0, matrix products: 28.1 us -> none  [the longest x10 12.1 us: cholesky_apply(): jax.scipy.linalg.solve_triangular(factor, half_way, lower=True, trans=1)]
    another operation x36 -> x0, local copies, waits for them, and re-layouts: 21.7 us -> none
    ppermute x2 -> x9, starting transfers between devices: 1.85 us -> 14.1 us  [send(): return lax.ppermute(value, ('gx', 'gy'), pairs)]
  transfers between devices with their start and end apart: 2 -> 9, of which waited for: 2 -> 2; matrix products, arithmetic and copies ran while one was open for 0% -> 1% of each run, Pallas kernels for 0% -> 23%
where the time goes in v1:
time: 238 us; the launch traced here: 235 us
  Pallas kernels  137 us (58%)
  waiting for transfers between devices  79.1 us (33%)
  starting transfers between devices  14.1 us (6%)
  local copies, waits for them, and re-layouts  2.39 us (1%)
    ppermute x9, waiting for transfers between devices, send(): return lax.ppermute(value, ('gx', 'gy'), pairs)  79.1 us
    pallas_call x1, Pallas kernels, cut(): pl.pallas_call(cut_kernel, out_shape=[jax.ShapeDtypeStruct((n_inner * T,...  73.5 us
    pallas_call x1, Pallas kernels, factor(): pl.pallas_call(factor_kernel, out_shape=[jax.ShapeDtypeStruct((3 * e, 3 *...  48.1 us
    ppermute x9, starting transfers between devices, send(): return lax.ppermute(value, ('gx', 'gy'), pairs)  14.1 us
    pallas_call x1, Pallas kernels, result(): pl.pallas_call(result_kernel, out_shape=jax.ShapeDtypeStruct((1, 4 * e, 4...  9.03 us
    pallas_call x1, Pallas kernels, row_products(): pl.pallas_call(rows_kernel, out_shape=[jax.ShapeDtypeStruct((4 * e, 3 * e...  6.68 us
  transfers between devices with their start and end apart: 9, of which 2 were waited for; matrix products, arithmetic and copies ran while one was open for 1% of the time, Pallas kernels for 23%

profile of v1, /device:TPU:24, one launch (start us, length us, event | category | flops | bytes accessed | tf_op | source)
XLA Modules:
  0.0 234.9 jit_solution(8788592659895894551)
XLA Ops:
  0.0 0.7 pad_add_fusion.place
  0.7 73.5 %cut_leaf.1 = (f32[1280,128]{1,0:T(8,128)}, f32[512,512]{1,0:T(8,128)}, f32[1280,128]{1,0:T(8,128)}) custom-call(s32[2]{0:T(128)} %pad_add_fusion.place, f32[1,1024,1024]{2,1,0:T(8,128)} %leaf.3), custom_call_target="tpu_custom_call" | custom-call | tf_op jit(solution)/shard_map/cut_leaf/pallas_call | solution.py:151
  74.1 0.0 copy-start
  74.1 0.4 collective-permute-start.3
  74.5 2.6 %collective-permute-start = (f32[512,512]{1,0:T(8,128)}, f32[512,512]{1,0:T(8,128)S(1)}, u32[]{:S(2)}, u32[]{:S(2)}) collective-permute-start(f32[512,512]{1,0:T(8,128)} %get-tuple-element.12.mine), channel_id=1, source_target_pairs={{0,16},{1,17},{2,18},{3,19},{4,20},{5,21},{6,22},{7,23},{8,24},{9,... | collective-permute-start | bytes 3145736 | tf_op jit(solution)/shard_map/ppermute | solution.py:385
  77.1 1.0 slice.6
  78.1 3.4 %collective-permute-start.6 = (f32[640,128]{1,0:T(8,128)S(1)}, f32[640,128]{1,0:T(8,128)S(1)}, u32[]{:S(2)}, u32[]{:S(2)}) collective-permute-start(f32[640,128]{1,0:T(8,128)S(1)} %slice.6), channel_id=1, source_target_pairs={{2,0},{3,1},{6,4},{7,5},{10,8},{11,9},{14,12},{15,13},{16,18},{17,... | collective-permute-start | bytes 983048 | tf_op jit(solution)/shard_map/ppermute | solution.py:385
  81.6 0.1 collective-permute-start.4
  81.7 46.6 %collective-permute-done.3.across = f32[1280,128]{1,0:T(8,128)S(1)} collective-permute-done((f32[1280,128]{1,0:T(8,128)}, f32[1280,128]{1,0:T(8,128)S(1)}, u32[]{:S(2)}, u32[]{:S(2)}) %collective-permute-start.3) | collective-permute-done | bytes 655392 | tf_op jit(solution)/shard_map/ppermute | solution.py:385
  128.3 0.0 copy-start.6
  128.3 1.5 collective-permute-start.5
  129.8 0.0 collective-permute-done.6
  129.8 1.0 slice_select_fusion
  130.8 0.1 collective-permute-start.7
  130.9 0.0 copy-done
  130.9 1.3 collective-permute-start.1
  132.2 32.5 %collective-permute-done.7.outer0 = f32[640,128]{1,0:T(8,128)S(1)} collective-permute-done((f32[640,128]{1,0:T(8,128)S(1)}, f32[640,128]{1,0:T(8,128)S(1)}, u32[]{:S(2)}, u32[]{:S(2)}) %collective-permute-start.7) | collective-permute-done | bytes 327712 | tf_op jit(solution)/shard_map/ppermute | solution.py:385
  164.7 0.0 copy-start.4
  164.7 3.4 %collective-permute-start.8 = (f32[640,128]{1,0:T(8,128)S(1)}, f32[640,128]{1,0:T(8,128)S(1)}, u32[]{:S(2)}, u32[]{:S(2)}) collective-permute-start(f32[640,128]{1,0:T(8,128)S(1)} %collective-permute-done.7.outer0), channel_id=1, source_target_pairs={{2,0},{3,1},{6,4},{7,5},{10,8},{11,9},{14,12},{15,13},{16,18},{17,... | collective-permute-start | bytes 983048 | tf_op jit(solution)/shard_map/ppermute | solution.py:385
  168.1 0.0 collective-permute-done.across
  168.1 0.0 copy-start.1
  168.2 1.3 collective-permute-start.2
  169.5 0.0 collective-permute-done.4.along
  169.5 0.0 collective-permute-done.5.corner
  169.5 0.0 copy-done.6
  169.5 48.1 %invert_coupling.1 = (bf16[768,768]{1,0:T(8,128)(2,1)}, bf16[768,768]{1,0:T(8,128)(2,1)}) custom-call(s32[2]{0:T(128)} %pad_add_fusion.place, f32[1280,128]{1,0:T(8,128)} %get-tuple-element.13.mine, f32[1280,128]{1,0:T(8,128)} %copy-done.6, f32[1280,128]{1,0:T(8,128)} %collective-permute-done.4.along, f32[1280,128]{1,0:T(8,128)} %collective-permute-done.5.corner), custom_call_target="tpu_custom_call" | custom-call | flops 30000001024 | bytes 5000000 | tf_op jit(solution)/shard_map/invert_coupling/pallas_call | solution.py:231
  217.6 0.0 copy-done.4
  217.6 0.0 copy-done.1
  217.6 6.7 %row_products.1 = (bf16[1024,768]{1,0:T(8,128)(2,1)}, bf16[1024,768]{1,0:T(8,128)(2,1)}) custom-call(f32[512,512]{1,0:T(8,128)} %get-tuple-element.12.mine, f32[512,512]{1,0:T(8,128)} %copy-done.1, bf16[768,768]{1,0:T(8,128)(2,1)} %get-tuple-element.14.high, bf16[768,768]{1,0:T(8,128)(2,1)} %get-tuple-element.15.low), custom_call_target="tpu_custom_call" | custom-call | flops 3000000000 | bytes 7000000 | tf_op jit(solution)/shard_map/row_products/pallas_call | solution.py:266
  224.2 0.0 collective-permute-done.8.outer1
  224.2 0.0 copy-start.5
  224.2 0.0 collective-permute-done.1.along
  224.3 0.0 copy-start.2
  224.3 0.0 collective-permute-done.2.corner
  224.3 0.0 copy-start.3
  224.3 0.7 copy-done.5
  225.0 0.4 copy-done.2
  225.4 0.3 copy-done.3
  225.7 9.0 %result.1 = f32[1,1024,1024]{2,1,0:T(8,128)} custom-call(s32[2]{0:T(128)} %pad_add_fusion.place, f32[1,1024,1024]{2,1,0:T(8,128)} %leaf.3, f32[512,512]{1,0:T(8,128)} %get-tuple-element.12.mine, f32[512,512]{1,0:T(8,128)} %copy-done.1, f32[512,512]{1,0:T(8,128)} %copy-done.2, f32[512,512]{1,0:T(8,128)} %copy-done.3, ...), custom_call_target="tpu_custom_call" | custom-call | flops 4000000000 | bytes 12000000 | tf_op jit(solution)/shard_map/result/pallas_call | solution.py:356
Async XLA Ops:
  74.1 56.8 %copy-start = (f32[512,512]{1,0:T(8,128)S(1)}, f32[512,512]{1,0:T(8,128)}, u32[]{:S(2)}) copy-start(f32[512,512]{1,0:T(8,128)} %get-tuple-element.12.mine) | copy-start | bytes 3145732
  74.1 54.1 %collective-permute-start.3 = (f32[1280,128]{1,0:T(8,128)}, f32[1280,128]{1,0:T(8,128)S(1)}, u32[]{:S(2)}, u32[]{:S(2)}) collective-permute-start(f32[1280,128]{1,0:T(8,128)} %get-tuple-element.13.mine), channel_id=1, source_target_pairs={{0,16},{1,17},{2,18},{3,19},{4,20},{5,21},{6,22},{7,23},{8,24},{9,... | collective-permute-start | bytes 1966088 | tf_op jit(solution)/shard_map/ppermute | solution.py:385
  74.5 93.6 %collective-permute-start = (f32[512,512]{1,0:T(8,128)}, f32[512,512]{1,0:T(8,128)S(1)}, u32[]{:S(2)}, u32[]{:S(2)}) collective-permute-start(f32[512,512]{1,0:T(8,128)} %get-tuple-element.12.mine), channel_id=1, source_target_pairs={{0,16},{1,17},{2,18},{3,19},{4,20},{5,21},{6,22},{7,23},{8,24},{9,... | collective-permute-start | bytes 3145736 | tf_op jit(solution)/shard_map/ppermute | solution.py:385
  78.1 51.7 %collective-permute-start.6 = (f32[640,128]{1,0:T(8,128)S(1)}, f32[640,128]{1,0:T(8,128)S(1)}, u32[]{:S(2)}, u32[]{:S(2)}) collective-permute-start(f32[640,128]{1,0:T(8,128)S(1)} %slice.6), channel_id=1, source_target_pairs={{2,0},{3,1},{6,4},{7,5},{10,8},{11,9},{14,12},{15,13},{16,18},{17,... | collective-permute-start | bytes 983048 | tf_op jit(solution)/shard_map/ppermute | solution.py:385
  81.6 87.9 %collective-permute-start.4 = (f32[1280,128]{1,0:T(8,128)}, f32[1280,128]{1,0:T(8,128)}, u32[]{:S(2)}, u32[]{:S(2)}) collective-permute-start(f32[1280,128]{1,0:T(8,128)} %get-tuple-element.13.mine), channel_id=1, source_target_pairs={{0,2},{1,3},{2,0},{3,1},{4,6},{5,7},{6,4},{7,5},{8,10},{9,11},{10,... | collective-permute-start | bytes 1966088 | tf_op jit(solution)/shard_map/ppermute | solution.py:385
  128.3 41.2 %copy-start.6 = (f32[1280,128]{1,0:T(8,128)}, f32[1280,128]{1,0:T(8,128)S(1)}, u32[]{:S(2)}) copy-start(f32[1280,128]{1,0:T(8,128)S(1)} %collective-permute-done.3.across) | copy-start | bytes 1966084
  128.3 41.2 %collective-permute-start.5 = (f32[1280,128]{1,0:T(8,128)S(1)}, f32[1280,128]{1,0:T(8,128)}, u32[]{:S(2)}, u32[]{:S(2)}) collective-permute-start(f32[1280,128]{1,0:T(8,128)S(1)} %collective-permute-done.3.across), channel_id=1, source_target_pairs={{0,2},{1,3},{2,0},{3,1},{4,6},{5,7},{6,4},{7,5},{8,10},{9,11},{10,... | collective-permute-start | bytes 1966088 | tf_op jit(solution)/shard_map/ppermute | solution.py:385
  130.8 33.9 %collective-permute-start.7 = (f32[640,128]{1,0:T(8,128)S(1)}, f32[640,128]{1,0:T(8,128)S(1)}, u32[]{:S(2)}, u32[]{:S(2)}) collective-permute-start(f32[640,128]{1,0:T(8,128)S(1)} %slice_select_fusion), channel_id=1, source_target_pairs={{0,16},{1,17},{2,18},{3,19},{4,20},{5,21},{6,22},{7,23},{8,24},{9,... | collective-permute-start | bytes 983048 | tf_op jit(solution)/shard_map/ppermute | solution.py:385
  130.9 93.4 %collective-permute-start.1 = (f32[512,512]{1,0:T(8,128)S(1)}, f32[512,512]{1,0:T(8,128)S(1)}, u32[]{:S(2)}, u32[]{:S(2)}) collective-permute-start(f32[512,512]{1,0:T(8,128)S(1)} %copy-done), channel_id=1, source_target_pairs={{0,2},{1,3},{4,6},{5,7},{8,10},{9,11},{12,14},{13,15},{18,16},{19,... | collective-permute-start | bytes 3145736 | tf_op jit(solution)/shard_map/ppermute | solution.py:385
  164.7 52.9 %copy-start.4 = (f32[640,128]{1,0:T(8,128)}, f32[640,128]{1,0:T(8,128)S(1)}, u32[]{:S(2)}) copy-start(f32[640,128]{1,0:T(8,128)S(1)} %collective-permute-done.7.outer0) | copy-start | bytes 983044
  164.7 59.5 %collective-permute-start.8 = (f32[640,128]{1,0:T(8,128)S(1)}, f32[640,128]{1,0:T(8,128)S(1)}, u32[]{:S(2)}, u32[]{:S(2)}) collective-permute-start(f32[640,128]{1,0:T(8,128)S(1)} %collective-permute-done.7.outer0), channel_id=1, source_target_pairs={{2,0},{3,1},{6,4},{7,5},{10,8},{11,9},{14,12},{15,13},{16,18},{17,... | collective-permute-start | bytes 983048 | tf_op jit(solution)/shard_map/ppermute | solution.py:385
  168.1 49.4 %copy-start.1 = (f32[512,512]{1,0:T(8,128)}, f32[512,512]{1,0:T(8,128)S(1)}, u32[]{:S(2)}) copy-start(f32[512,512]{1,0:T(8,128)S(1)} %collective-permute-done.across) | copy-start | bytes 3145732
  168.2 56.1 %collective-permute-start.2 = (f32[512,512]{1,0:T(8,128)S(1)}, f32[512,512]{1,0:T(8,128)S(1)}, u32[]{:S(2)}, u32[]{:S(2)}) collective-permute-start(f32[512,512]{1,0:T(8,128)S(1)} %collective-permute-done.across), channel_id=1, source_target_pairs={{0,2},{1,3},{4,6},{5,7},{8,10},{9,11},{12,14},{13,15},{18,16},{19,... | collective-permute-start | bytes 3145736 | tf_op jit(solution)/shard_map/ppermute | solution.py:385
  224.2 0.7 copy-start.5
  224.3 1.1 copy-start.2
  224.3 1.4 copy-start.3

commit v2 on v1

--- a/solution.py
+++ b/solution.py
@@ -1,3 +1,5 @@
+import functools
+
 import jax
 import jax.numpy as jnp
 from jax import lax
@@ -81,9 +83,9 @@
     return mats
 
 
-def invert_in_place(refs):
+def invert_in_place(refs, start=0, stop=None):
     n = refs[0].shape[0]
-    for p in range(0, n, T):
+    for p in range(start, n if stop is None else stop, T):
         pivots = invert_tiles([ref[p : p + T, p : p + T] for ref in refs])
         for ref, pivot in zip(refs, pivots):
             rows = dot(pivot, ref[p : p + T, :])
@@ -99,67 +101,94 @@
             ref[p : p + T, :] = rows
 
 
-def cut_kernel(place, leaf, inner, cross, outer, sem):
+def leaf_block(leaf, side_r, side_c, r, c, size):
     e = leaf.shape[1] // 4
+    return leaf.at[
+        0,
+        pl.ds(pl.multiple_of(side_r * e + r * size, T), size),
+        pl.ds(pl.multiple_of(side_c * e + c * size, T), size),
+    ]
+
+
+def run_copies(pairs, sem):
+    copies = [pltpu.make_async_copy(a, b, sem.at[i]) for i, (a, b) in enumerate(pairs)]
+    for copy in copies:
+        copy.start()
+    for copy in copies:
+        copy.wait()
+
+
+def cut_inner_kernel(place, leaf, hh, sr, sem):
+    tiles = leaf.shape[1] // 4 // T
+    x_in, y_in = 1 - place[0], 3 - place[1]
+    pairs = []
+    for at, (r, c) in enumerate(upper(tiles)):
+        pairs.append((leaf_block(leaf, y_in, y_in, r, c, T), hh.at[pl.ds(at * T, T)]))
+    for at, (r, c) in enumerate(upper(tiles)):
+        pairs.append((leaf_block(leaf, x_in, x_in, r, c, T), sr.at[pl.ds(at * T, T)]))
+    for at in range(tiles * tiles):
+        r, c = at // tiles, at % tiles
+        spot = (len(upper(tiles)) + at) * T
+        pairs.append((leaf_block(leaf, x_in, y_in, r, c, T), sr.at[pl.ds(spot, T)]))
+    run_copies(pairs, sem)
+
+
+def cut_inner(place, leaf):
+    tiles = leaf.shape[1] // 4 // T
+    n_sym, n_full = len(upper(tiles)), tiles * tiles
+    return pl.pallas_call(
+        cut_inner_kernel,
+        out_shape=[
+            jax.ShapeDtypeStruct((n_sym * T, T), F32),
+            jax.ShapeDtypeStruct(((n_sym + n_full) * T, T), F32),
+        ],
+        in_specs=[SMEM, HBM],
+        out_specs=[VMEM, VMEM],
+        scratch_shapes=[pltpu.SemaphoreType.DMA((2 * n_sym + n_full,))],
+        compiler_params=PARAMS,
+        name="cut_inner",
+    )(place, leaf)
+
+
+def cut_outer_kernel(place, leaf, *refs):
+    *cross, outer0, outer1, sem = refs
+    e = leaf.shape[1] // 4
+    tiles = e // T
     v, u = place[0], place[1]
     ext = [v, 2 + u]
     inn = [1 - v, 3 - u]
-
-    def src(side_r, side_c, r, c, size):
-        return leaf.at[
-            0,
-            pl.ds(pl.multiple_of(side_r * e + r * size, T), size),
-            pl.ds(pl.multiple_of(side_c * e + c * size, T), size),
-        ]
-
-    copies = []
-
-    def add(source, target):
-        copies.append(pltpu.make_async_copy(source, target, sem.at[len(copies)]))
-        copies[-1].start()
-
-    tiles = e // T
-    at = 0
-    for side in (1, 0):
-        for r, c in upper(tiles):
-            add(src(inn[side], inn[side], r, c, T), inner.at[pl.ds(at, T)])
-            at += T
-    for r in range(tiles):
-        for c in range(tiles):
-            add(src(inn[0], inn[1], r, c, T), inner.at[pl.ds(at, T)])
-            at += T
-    for r in range(2):
-        for c in range(2):
-            add(src(ext[r], inn[c], 0, 0, e), cross.at[pl.ds(r * e, e), pl.ds(c * e, e)])
-    at = 0
-    for r, c in upper(2 * tiles):
-        add(
-            src(ext[r // tiles], ext[c // tiles], r % tiles, c % tiles, T),
-            outer.at[pl.ds(at, T)],
-        )
-        at += T
-    for copy in copies:
-        copy.wait()
-
-
-def cut(place, leaf):
+    pairs = []
+    row = 0
+    for ref in cross:
+        for at in range(0, ref.shape[0], T):
+            for c in range(2):
+                source = leaf.at[
+                    0,
+                    pl.ds(pl.multiple_of(ext[row // e] * e + row % e, T), T),
+                    pl.ds(pl.multiple_of(inn[c] * e, T), e),
+                ]
+                pairs.append((source, ref.at[pl.ds(at, T), pl.ds(c * e, e)]))
+            row += T
+    for at, (r, c) in enumerate(upper(2 * tiles)):
+        half = outer0.shape[0]
+        ref, spot = (outer0, at * T) if at * T < half else (outer1, at * T - half)
+        source = leaf_block(leaf, ext[r // tiles], ext[c // tiles], r % tiles, c % tiles, T)
+        pairs.append((source, ref.at[pl.ds(spot, T)]))
+    run_copies(pairs, sem)
+
+
+def cut_outer(place, leaf, chunks):
     e = leaf.shape[1] // 4
-    tiles = e // T
-    n_inner = 2 * len(upper(tiles)) + tiles * tiles
-    n_outer = len(upper(2 * tiles))
-    n_copies = n_inner + 4 + n_outer
-    return pl.pallas_call(
-        cut_kernel,
-        out_shape=[
-            jax.ShapeDtypeStruct((n_inner * T, T), F32),
-            jax.ShapeDtypeStruct((2 * e, 2 * e), F32),
-            jax.ShapeDtypeStruct((n_outer * T, T), F32),
-        ],
+    n_outer = len(upper(2 * (e // T)))
+    return pl.pallas_call(
+        cut_outer_kernel,
+        out_shape=[jax.ShapeDtypeStruct((rows, 2 * e), F32) for rows in chunks]
+        + [jax.ShapeDtypeStruct((n_outer // 2 * T, T), F32)] * 2,
         in_specs=[SMEM, HBM],
-        out_specs=[HBM, HBM, HBM],
-        scratch_shapes=[pltpu.SemaphoreType.DMA((n_copies,))],
-        compiler_params=PARAMS,
-        name="cut_leaf",
+        out_specs=[VMEM] * (len(chunks) + 2),
+        scratch_shapes=[pltpu.SemaphoreType.DMA((n_outer + 4 * e // T,))],
+        compiler_params=PARAMS,
+        name="cut_outer",
     )(place, leaf)
 
 
@@ -184,25 +213,72 @@
     return jnp.concatenate(rows, axis=0)
 
 
-def factor_kernel(place, mine, across, along, corner, high, low, h0, h1, side, coup, full, cols):
+def pack(ref, value, tiles):
+    for at, (r, c) in enumerate(upper(tiles)):
+        ref[at * T : (at + 1) * T, :] = value[r * T : (r + 1) * T, c * T : (c + 1) * T]
+
+
+def invert_side_kernel(mine, along, whole, packed, held):
+    tiles = whole.shape[0] // T
+    held[...] = unpack(mine, 0, tiles) + unpack(along, 0, tiles)
+    invert_in_place([held])
+    whole[...] = held[...]
+    pack(packed, held[...], tiles)
+
+
+def invert_side(mine, along, e):
+    return pl.pallas_call(
+        invert_side_kernel,
+        out_shape=[jax.ShapeDtypeStruct((e, e), F32), jax.ShapeDtypeStruct(mine.shape, F32)],
+        in_specs=[VMEM, VMEM],
+        out_specs=[VMEM, VMEM],
+        scratch_shapes=[pltpu.VMEM((e, e), F32)],
+        compiler_params=PARAMS,
+        cost_estimate=pl.CostEstimate(flops=10**10, bytes_accessed=10**6, transcendentals=0),
+        name="invert_side",
+    )(mine, along)
+
+
+def factor_start_kernel(h0, h1_tiles, mine, across, along, corner, side, cols, h1, coup):
     e = h0.shape[0]
     tiles = e // T
     sym = len(upper(tiles)) * T
-    h0[...] = unpack(mine, 0, tiles) + unpack(along, 0, tiles)
-    h1[...] = unpack(across, 0, tiles) + unpack(corner, 0, tiles)
-    invert_in_place([h0, h1])
-    coup[:e, :e] = unpack_full(mine, 2 * sym, tiles)
-    coup[:e, e:] = unpack_full(across, 2 * sym, tiles)
-    coup[e:, :e] = unpack_full(along, 2 * sym, tiles)
-    coup[e:, e:] = unpack_full(corner, 2 * sym, tiles)
+    h1[...] = unpack(h1_tiles, 0, tiles)
+    coup[:e, :e] = unpack_full(mine, sym, tiles)
+    coup[:e, e:] = unpack_full(across, sym, tiles)
+    coup[e:, :e] = unpack_full(along, sym, tiles)
+    coup[e:, e:] = unpack_full(corner, sym, tiles)
     cols[:, :e] = dot(coup[:, :e], h0[...])
     cols[:, e:] = dot(coup[:, e:], h1[...])
     side[...] = -dot(cols[...], coup[...], NT)
-    side[:e, :e] = side[:e, :e] + (unpack(mine, sym, tiles) + unpack(across, sym, tiles))
-    side[e:, e:] = side[e:, e:] + (unpack(along, sym, tiles) + unpack(corner, sym, tiles))
-    invert_in_place([side])
-    flow = cols[...]
-    flow16 = split(flow)
+    side[:e, :e] = side[:e, :e] + (unpack(mine, 0, tiles) + unpack(across, 0, tiles))
+    side[e:, e:] = side[e:, e:] + (unpack(along, 0, tiles) + unpack(corner, 0, tiles))
+    invert_in_place([side], 0, e)
+
+
+def factor_start(h0, h1_tiles, mine, across, along, corner):
+    e = h0.shape[0]
+    return pl.pallas_call(
+        factor_start_kernel,
+        out_shape=[
+            jax.ShapeDtypeStruct((2 * e, 2 * e), F32),
+            jax.ShapeDtypeStruct((2 * e, 2 * e), F32),
+            jax.ShapeDtypeStruct((e, e), F32),
+        ],
+        in_specs=[VMEM] * 6,
+        out_specs=[VMEM] * 3,
+        scratch_shapes=[pltpu.VMEM((2 * e, 2 * e), F32)],
+        compiler_params=PARAMS,
+        cost_estimate=pl.CostEstimate(flops=12 * 10**9, bytes_accessed=5 * 10**6, transcendentals=0),
+        name="factor_start",
+    )(h0, h1_tiles, mine, across, along, corner)
+
+
+def factor_end_kernel(place, side_in, cols, h0, h1, high, low, side, full):
+    e = h0.shape[0]
+    side[...] = side_in[...]
+    invert_in_place([side], e, 2 * e)
+    flow16 = split(cols[...])
     away = dot3(split(side[...]), flow16)
     full[...] = dot3(flow16, split(away), TN)
     full[:e, :e] = full[:e, :e] + h0[...]
@@ -227,30 +303,30 @@
         emit(-away[e:, :].T, rest, first)
 
 
-def factor(place, mine, across, along, corner, e):
-    return pl.pallas_call(
-        factor_kernel,
+def factor_end(place, side, cols, h0, h1):
+    e = h0.shape[0]
+    return pl.pallas_call(
+        factor_end_kernel,
         out_shape=[jax.ShapeDtypeStruct((3 * e, 3 * e), BF16)] * 2,
-        in_specs=[SMEM, VMEM, VMEM, VMEM, VMEM],
+        in_specs=[SMEM] + [VMEM] * 4,
         out_specs=[VMEM, VMEM],
-        scratch_shapes=[
-            pltpu.VMEM((e, e), F32),
-            pltpu.VMEM((e, e), F32),
-            pltpu.VMEM((2 * e, 2 * e), F32),
-            pltpu.VMEM((2 * e, 2 * e), F32),
-            pltpu.VMEM((2 * e, 2 * e), F32),
-            pltpu.VMEM((2 * e, 2 * e), F32),
-        ],
-        compiler_params=PARAMS,
-        cost_estimate=pl.CostEstimate(flops=30 * 10**9, bytes_accessed=5 * 10**6, transcendentals=0),
-        name="invert_coupling",
-    )(place, mine, across, along, corner)
-
-
-def rows_kernel(mine, across, high, low, top, bottom):
-    e = mine.shape[1] // 2
+        scratch_shapes=[pltpu.VMEM((2 * e, 2 * e), F32), pltpu.VMEM((2 * e, 2 * e), F32)],
+        compiler_params=PARAMS,
+        cost_estimate=pl.CostEstimate(flops=12 * 10**9, bytes_accessed=5 * 10**6, transcendentals=0),
+        name="factor_end",
+    )(place, side, cols, h0, h1)
+
+
+def join(refs):
+    return jnp.concatenate([ref[...] for ref in refs], axis=0)
+
+
+def rows_kernel(high, low, *refs):
+    *leaves, top, bottom = refs
+    n = len(leaves) // 2
+    e = leaves[0].shape[1] // 2
     whole = (high[...], low[...])
-    for at, leaf in enumerate((mine, across)):
+    for at, leaf in enumerate((join(leaves[:n]), join(leaves[n:]))):
         first = split(leaf[:, :e])
         second = split(leaf[:, e:])
         inner = slice((1 + at) * e, (2 + at) * e)
@@ -261,23 +337,23 @@
         top[rows, :], bottom[rows, :] = split(value)
 
 
-def row_products(mine, across, high, low):
-    e = mine.shape[1] // 2
+def row_products(high, low, mine, across):
+    e = mine[0].shape[1] // 2
     return pl.pallas_call(
         rows_kernel,
         out_shape=[jax.ShapeDtypeStruct((4 * e, 3 * e), BF16)] * 2,
-        in_specs=[VMEM] * 4,
+        in_specs=[VMEM] * (2 + 2 * len(mine)),
         out_specs=[VMEM] * 2,
         compiler_params=PARAMS,
         cost_estimate=pl.CostEstimate(flops=3 * 10**9, bytes_accessed=7 * 10**6, transcendentals=0),
         name="row_products",
-    )(mine, across, high, low)
-
-
-def result_kernel(
-    place, leaf, mine, across, along, corner, top, bottom, outer0, outer1, out, own, col, sem
-):
-    e = mine.shape[1] // 2
+    )(high, low, *mine, *across)
+
+
+def result_kernel(n, place, leaf, top, bottom, outer0, outer1, *refs):
+    mine, across, along, corner = (refs[i * n : (i + 1) * n] for i in range(4))
+    out, own, col, sem = refs[4 * n :]
+    e = mine[0].shape[1] // 2
     tiles = e // T
     v, u = place[0], place[1]
     same = u == v
@@ -287,11 +363,7 @@
         for c in range(2):
             copies.append(
                 pltpu.make_async_copy(
-                    leaf.at[
-                        0,
-                        pl.ds(pl.multiple_of(ext[r] * e, T), e),
-                        pl.ds(pl.multiple_of(ext[c] * e, T), e),
-                    ],
+                    leaf_block(leaf, ext[r], ext[c], 0, 0, e),
                     own.at[pl.ds(r * e, e), pl.ds(c * e, e)],
                     sem.at[2 * r + c],
                 )
@@ -300,13 +372,13 @@
 
     @pl.when(same)
     def _():
-        col[0] = mine[...]
-        col[1] = across[...]
+        col[0] = join(mine)
+        col[1] = join(across)
 
     @pl.when(jnp.logical_not(same))
     def _():
-        col[0] = along[...]
-        col[1] = corner[...]
+        col[0] = join(along)
+        col[1] = join(corner)
 
     def spot(side, which):
         return pl.ds(pl.multiple_of((2 * side + (v if which == 0 else 1 - v)) * e, T), e)
@@ -351,12 +423,13 @@
                 out[0, spot(r, 1), spot(c, 1)] = out[0, spot(r, 1), spot(c, 1)] + block
 
 
-def result(place, leaf, mine, across, along, corner, top, bottom, outer0, outer1):
-    e = mine.shape[1] // 2
-    return pl.pallas_call(
-        result_kernel,
+def result(place, leaf, top, bottom, outer0, outer1, mine, across, along, corner):
+    e = leaf.shape[1] // 4
+    n = len(mine)
+    return pl.pallas_call(
+        functools.partial(result_kernel, n),
         out_shape=jax.ShapeDtypeStruct((1, 4 * e, 4 * e), F32),
-        in_specs=[SMEM, HBM] + [VMEM] * 8,
+        in_specs=[SMEM, HBM] + [VMEM] * (4 + 4 * n),
         out_specs=VMEM,
         scratch_shapes=[
             pltpu.VMEM((2 * e, 2 * e), F32),
@@ -366,7 +439,11 @@
         compiler_params=PARAMS,
         cost_estimate=pl.CostEstimate(flops=4 * 10**9, bytes_accessed=12 * 10**6, transcendentals=0),
         name="result",
-    )(place, leaf, mine, across, along, corner, top, bottom, outer0, outer1)
+    )(place, leaf, top, bottom, outer0, outer1, *mine, *across, *along, *corner)
+
+
+def tie(*values):
+    return lax.optimization_barrier(values)
 
 
 def solution(mesh):
@@ -389,20 +466,35 @@
         v = lax.axis_index("gx") // (nx // 2)
         u = lax.axis_index("gy") // (ny // 2)
         place = jnp.stack([v, u]).astype(jnp.int32)
-        inner, cross, outer = cut(place, leaf)
-        half = outer.shape[0] // 2
-        inner_x = send(inner, False)
-        inner_y = send(inner, True)
-        passed = send(outer[half:], True, only=False)
-        inner_d = send(inner_x, True)
-        cross_x = send(cross, False)
-        cross_y = send(cross, True, only=True)
-        cross_d = send(cross_x, True, only=True)
-        outer0 = send(jnp.where(u == v, passed, outer[:half]), False)
+        hh, sr = cut_inner(place, leaf)
+        hh_y = send(hh, True)
+        sr_x = send(sr, False)
+        sr_y = send(sr, True)
+        ca, cb, cc, outer0, outer1 = cut_outer(place, leaf, (e // 2, e // 2, e))
+        passed = send(outer1, True, only=False)
+        ca_x = send(ca, False)
+        ca_y = send(ca, True, only=True)
+        h0, h0_tiles = invert_side(hh, hh_y, e)
+        h1_tiles = send(h0_tiles, False)
+        sr_d = send(sr_x, True)
+        cb, cc, sr_d, h1_tiles, ca_x = tie(cb, cc, sr_d, h1_tiles, ca_x)
+        cb_x = send(cb, False)
+        ca_d = send(ca_x, True, only=True)
+        cb_y = send(cb, True, only=True)
+        side, cols, h1 = factor_start(h0, h1_tiles, sr, sr_x, sr_y, sr_d)
+        cc, cb_x, side, passed = tie(cc, cb_x, side, passed)
+        cb_d = send(cb_x, True, only=True)
+        outer0 = send(jnp.where(u == v, passed, outer0), False)
+        cc_x = send(cc, False)
+        cc_y = send(cc, True, only=True)
+        high, low = factor_end(place, side, cols, h0, h1)
+        cc_x, outer0, high = tie(cc_x, outer0, high)
+        cc_d = send(cc_x, True, only=True)
         outer1 = send(outer0, True, only=False)
-        high, low = factor(place, inner, inner_x, inner_y, inner_d, e)
-        top, bottom = row_products(cross, cross_x, high, low)
-        return result(place, leaf, cross, cross_x, cross_y, cross_d, top, bottom, outer0, outer1)
+        mine, across = (ca, cb, cc), (ca_x, cb_x, cc_x)
+        along, corner = (ca_y, cb_y, cc_y), (ca_d, cb_d, cc_d)
+        top, bottom = row_products(high, low, mine, across)
+        return result(place, leaf, top, bottom, outer0, outer1, mine, across, along, corner)
 
     return jax.shard_map(
         body,

time: 238 us -> 160 us (0.67); the launches traced: 235 us -> 160 us
  Pallas kernels: 137 us -> 74.5 us
  waiting for transfers between devices: 79.1 us -> 51 us
  starting transfers between devices: 14.1 us -> 30.4 us
    pallas_call x3 -> x6, Pallas kernels: 131 us -> 67.9 us  [the longest x1 18.9 us: factor_end(): pl.pallas_call(factor_end_kernel, out_shape=[jax.ShapeDtypeStruct((3 * e,...]
    ppermute x9 -> x17, waiting for transfers between devices: 79.1 us -> 51 us  [send(): return lax.ppermute(value, ('gx', 'gy'), pairs)]
    ppermute x9 -> x17, starting transfers between devices: 14.1 us -> 30.4 us  [send(): return lax.ppermute(value, ('gx', 'gy'), pairs)]
  transfers between devices with their start and end apart: 9 -> 17, of which waited for: 2 -> 5; matrix products, arithmetic and copies ran while one was open for 1% -> 0% of each run, Pallas kernels for 23% -> 39%
where the time goes in v2:
time: 160 us
  Pallas kernels  74.5 us (47%)
  waiting for transfers between devices  51 us (32%)
  starting transfers between devices  30.4 us (19%)
  local copies, waits for them, and re-layouts  2.63 us (2%)
    ppermute x17, waiting for transfers between devices, send(): return lax.ppermute(value, ('gx', 'gy'), pairs)  51 us
    ppermute x17, starting transfers between devices, send(): return lax.ppermute(value, ('gx', 'gy'), pairs)  30.4 us
    pallas_call x1, Pallas kernels, factor_end(): pl.pallas_call(factor_end_kernel, out_shape=[jax.ShapeDtypeStruct((3 * e,...  18.9 us
    pallas_call x1, Pallas kernels, factor_start(): pl.pallas_call(factor_start_kernel, out_shape=[jax.ShapeDtypeStruct((2 *...  18.8 us
    pallas_call x1, Pallas kernels, invert_side(): pl.pallas_call(invert_side_kernel, out_shape=[jax.ShapeDtypeStruct((e, e)...  14.6 us
    pallas_call x1, Pallas kernels, result(): pl.pallas_call(functools.partial(result_kernel, n), out_shape=jax.ShapeDt...  9.3 us
    pallas_call x1, Pallas kernels, row_products(): pl.pallas_call(rows_kernel, out_shape=[jax.ShapeDtypeStruct((4 * e, 3 * e...  6.66 us
    pallas_call x1, Pallas kernels, cut_outer(): pl.pallas_call(cut_outer_kernel, out_shape=[jax.ShapeDtypeStruct((rows, 2...  3.51 us
  transfers between devices with their start and end apart: 17, of which 5 were waited for; matrix products, arithmetic and copies ran while one was open for 0% of the time, Pallas kernels for 39%

profile of v2, /device:TPU:24, one launch (start us, length us, event | category | flops | bytes accessed | tf_op | source)
XLA Modules:
  0.0 159.7 jit_solution(13552180457749023094)
XLA Ops:
  0.0 0.6 pad_add_fusion.place
  0.6 2.7 %cut_inner.1 = (f32[384,128]{1,0:T(8,128)}, f32[896,128]{1,0:T(8,128)}) custom-call(s32[2]{0:T(128)} %pad_add_fusion.place, f32[1,1024,1024]{2,1,0:T(8,128)} %leaf.5), custom_call_target="tpu_custom_call" | custom-call | tf_op jit(solution)/shard_map/cut_inner/pallas_call | solution.py:139
  3.3 0.4 collective-permute-start
  3.7 1.5 collective-permute-start.2
  5.3 0.5 collective-permute-start.6
  5.8 3.5 %cut_outer.1 = (f32[128,512]{1,0:T(8,128)}, f32[128,512]{1,0:T(8,128)}, f32[256,512]{1,0:T(8,128)}, f32[640,128]{1,0:T(8,128)}, f32[640,128]{1,0:T(8,128)}) custom-call(s32[2]{0:T(128)} %pad_add_fusion.place, f32[1,1024,1024]{2,1,0:T(8,128)} %leaf.5), custom_call_target="tpu_custom_call" | custom-call | tf_op jit(solution)/shard_map/cut_outer/pallas_call | solution.py:183
  9.3 2.7 %collective-permute-start.4 = (f32[128,512]{1,0:T(8,128)}, f32[128,512]{1,0:T(8,128)S(1)}, u32[]{:S(2)}, u32[]{:S(2)}) collective-permute-start(f32[128,512]{1,0:T(8,128)} %get-tuple-element.38.refs_0_), channel_id=1, source_target_pairs={{0,16},{1,17},{2,18},{3,19},{4,20},{5,21},{6,22},{7,23},{8,24},{9,... | collective-permute-start | bytes 786440 | tf_op jit(solution)/shard_map/ppermute | solution.py:462
  12.0 20.2 %collective-permute-done.across = f32[896,128]{1,0:T(8,128)S(1)} collective-permute-done((f32[896,128]{1,0:T(8,128)}, f32[896,128]{1,0:T(8,128)S(1)}, u32[]{:S(2)}, u32[]{:S(2)}) %collective-permute-start) | collective-permute-done | bytes 458784 | tf_op jit(solution)/shard_map/ppermute | solution.py:462
  32.2 1.5 collective-permute-start.1
  33.7 0.0 collective-permute-done.2.along
  33.7 0.7 copy-done.20
  34.4 14.6 %invert_side.1 = (f32[256,256]{1,0:T(8,128)}, f32[384,128]{1,0:T(8,128)}) custom-call(f32[384,128]{1,0:T(8,128)} %get-tuple-element.36.mine, f32[384,128]{1,0:T(8,128)} %copy-done.20), custom_call_target="tpu_custom_call" | custom-call | flops 10000000000 | bytes 1000000 | tf_op jit(solution)/shard_map/invert_side/pallas_call | solution.py:230
  49.0 0.0 collective-permute-start.3
  49.0 1.3 collective-permute-start.11
  50.3 0.0 collective-permute-done.4.refs_3_
  50.4 4.6 %collective-permute-start.7 = (f32[640,128]{1,0:T(8,128)S(1)}, f32[640,128]{1,0:T(8,128)S(1)}, u32[]{:S(2)}, u32[]{:S(2)}) collective-permute-start(f32[640,128]{1,0:T(8,128)S(1)} %copy-done.18), channel_id=1, source_target_pairs={{2,0},{3,1},{6,4},{7,5},{10,8},{11,9},{14,12},{15,13},{16,18},{17,... | collective-permute-start | bytes 983048 | tf_op jit(solution)/shard_map/ppermute | solution.py:462
  55.0 3.5 %collective-permute-done.3.h1_tiles = f32[384,128]{1,0:T(8,128)S(1)} collective-permute-done((f32[384,128]{1,0:T(8,128)}, f32[384,128]{1,0:T(8,128)S(1)}, u32[]{:S(2)}, u32[]{:S(2)}) %collective-permute-start.3) | collective-permute-done | bytes 196640 | tf_op jit(solution)/shard_map/ppermute | solution.py:462
  58.5 0.0 collective-permute-done.1.corner
  58.5 1.5 collective-permute-start.14
  60.0 0.6 collective-permute-start.5
  60.6 0.0 collective-permute-done.6.along
  60.6 0.8 copy-done.16
  61.4 18.8 %factor_start.1 = (f32[512,512]{1,0:T(8,128)}, f32[512,512]{1,0:T(8,128)}, f32[256,256]{1,0:T(8,128)}) custom-call(f32[256,256]{1,0:T(8,128)} %get-tuple-element.41.h0, f32[384,128]{1,0:T(8,128)} %copy-done.19, f32[896,128]{1,0:T(8,128)} %get-tuple-element.35.mine, f32[896,128]{1,0:T(8,128)} %copy-done.15, f32[896,128]{1,0:T(8,128)} %copy-done.16, ...), custom_call_target="tpu_custom_call" | custom-call | flops 12000000000 | bytes 5000000 | tf_op jit(solution)/shard_map/factor_start/pallas_call | solution.py:261
  80.2 0.0 collective-permute-done.7
  80.2 0.0 collective-permute-done.5.refs_4_
  80.2 1.5 collective-permute-start.13
  81.8 5.7 %collective-permute-start.8 = (f32[256,512]{1,0:T(8,128)S(1)}, f32[256,512]{1,0:T(8,128)S(1)}, u32[]{:S(2)}, u32[]{:S(2)}) collective-permute-start(f32[256,512]{1,0:T(8,128)S(1)} %copy-done), channel_id=1, source_target_pairs={{0,16},{1,17},{2,18},{3,19},{4,20},{5,21},{6,22},{7,23},{8,24},{9,... | collective-permute-start | bytes 1572872 | tf_op jit(solution)/shard_map/ppermute | solution.py:462
  87.5 0.1 collective-permute-start.9
  87.6 18.9 %factor_end.1 = (bf16[768,768]{1,0:T(8,128)(2,1)}, bf16[768,768]{1,0:T(8,128)(2,1)}) custom-call(s32[2]{0:T(128)} %pad_add_fusion.place, f32[512,512]{1,0:T(8,128)} %get-tuple-element.49.side_in, f32[512,512]{1,0:T(8,128)} %get-tuple-element.50.cols, f32[256,256]{1,0:T(8,128)} %get-tuple-element.41.h0, f32[256,256]{1,0:T(8,128)} %get-tuple-element.51.h1), custom_call_target="tpu_custom_call" | custom-call | flops 12000000000 | bytes 5000000 | tf_op jit(solution)/shard_map/factor_end/pallas_call | solution.py:308
  106.5 15.5 %collective-permute-done.9.outer0 = f32[640,128]{1,0:T(8,128)S(1)} collective-permute-done((f32[640,128]{1,0:T(8,128)S(1)}, f32[640,128]{1,0:T(8,128)S(1)}, u32[]{:S(2)}, u32[]{:S(2)}) %collective-permute-start.9) | collective-permute-done | bytes 327712 | tf_op jit(solution)/shard_map/ppermute | solution.py:462
  122.0 0.0 collective-permute-done.8.refs_5_
  122.0 1.3 collective-permute-start.16
  123.3 4.6 %collective-permute-start.10 = (f32[640,128]{1,0:T(8,128)S(1)}, f32[640,128]{1,0:T(8,128)S(1)}, u32[]{:S(2)}, u32[]{:S(2)}) collective-permute-start(f32[640,128]{1,0:T(8,128)S(1)} %collective-permute-done.9.outer0), channel_id=1, source_target_pairs={{2,0},{3,1},{6,4},{7,5},{10,8},{11,9},{14,12},{15,13},{16,18},{17,... | collective-permute-start | bytes 983048 | tf_op jit(solution)/shard_map/ppermute | solution.py:462
  127.9 0.0 collective-permute-done.11.refs_6_
  128.0 1.3 collective-permute-start.12
  129.3 0.0 collective-permute-done.14.refs_9_
  129.3 1.3 collective-permute-start.15
  130.6 6.7 %row_products.1 = (bf16[1024,768]{1,0:T(8,128)(2,1)}, bf16[1024,768]{1,0:T(8,128)(2,1)}) custom-call(bf16[768,768]{1,0:T(8,128)(2,1)} %get-tuple-element.53.high, bf16[768,768]{1,0:T(8,128)(2,1)} %get-tuple-element.54.low, f32[128,512]{1,0:T(8,128)} %get-tuple-element.38.refs_0_, f32[128,512]{1,0:T(8,128)} %get-tuple-element.40.refs_1_, ...), custom_call_target="tpu_custom_call" | custom-call | flops 3000000000 | bytes 7000000 | tf_op jit(solution)/shard_map/row_products/pallas_call | solution.py:342
  137.3 7.1 %collective-permute-done.12.refs_7_ = f32[128,512]{1,0:T(8,128)S(1)} collective-permute-done((f32[128,512]{1,0:T(8,128)S(1)}, f32[128,512]{1,0:T(8,128)S(1)}, u32[]{:S(2)}, u32[]{:S(2)}) %collective-permute-start.12) | collective-permute-done | bytes 262176 | tf_op jit(solution)/shard_map/ppermute | solution.py:462
  144.3 4.7 %collective-permute-done.15.refs_10_ = f32[128,512]{1,0:T(8,128)S(1)} collective-permute-done((f32[128,512]{1,0:T(8,128)S(1)}, f32[128,512]{1,0:T(8,128)S(1)}, u32[]{:S(2)}, u32[]{:S(2)}) %collective-permute-start.15) | collective-permute-done | bytes 262176 | tf_op jit(solution)/shard_map/ppermute | solution.py:462
  149.0 0.0 collective-permute-done.13.refs_8_
  149.0 0.0 collective-permute-done.10.outer1
  149.0 0.0 collective-permute-done.16.refs_11_
  149.1 0.7 copy-done.14
  149.7 0.2 copy-done.1
  149.9 0.1 copy-done.6
  150.0 0.2 copy-done.3
  150.2 9.3 %result.1 = f32[1,1024,1024]{2,1,0:T(8,128)} custom-call(s32[2]{0:T(128)} %pad_add_fusion.place, f32[1,1024,1024]{2,1,0:T(8,128)} %leaf.5, bf16[1024,768]{1,0:T(8,128)(2,1)} %get-tuple-element.58.top, bf16[1024,768]{1,0:T(8,128)(2,1)} %get-tuple-element.59.bottom, f32[640,128]{1,0:T(8,128)} %copy-done.5, f32[640,128]{1,0:T(8,128)} %copy-done.6, ...), custom_call_target="tpu_custom_call" | custom-call | flops 4000000000 | bytes 12000000 | tf_op jit(solution)/shard_map/result/pallas_call | solution.py:429
  (37 shorter events, 0.1 us)
Async XLA Ops:
  3.3 28.9 %collective-permute-start = (f32[896,128]{1,0:T(8,128)}, f32[896,128]{1,0:T(8,128)S(1)}, u32[]{:S(2)}, u32[]{:S(2)}) collective-permute-start(f32[896,128]{1,0:T(8,128)} %get-tuple-element.35.mine), channel_id=1, source_target_pairs={{0,16},{1,17},{2,18},{3,19},{4,20},{5,21},{6,22},{7,23},{8,24},{9,... | collective-permute-start | bytes 1376264 | tf_op jit(solution)/shard_map/ppermute | solution.py:462
  3.7 30.0 %collective-permute-start.2 = (f32[384,128]{1,0:T(8,128)}, f32[384,128]{1,0:T(8,128)S(1)}, u32[]{:S(2)}, u32[]{:S(2)}) collective-permute-start(f32[384,128]{1,0:T(8,128)} %get-tuple-element.36.mine), channel_id=1, source_target_pairs={{0,2},{1,3},{2,0},{3,1},{4,6},{5,7},{6,4},{7,5},{8,10},{9,11},{10,... | collective-permute-start | bytes 589832 | tf_op jit(solution)/shard_map/ppermute | solution.py:462
  5.3 55.3 %collective-permute-start.6 = (f32[896,128]{1,0:T(8,128)}, f32[896,128]{1,0:T(8,128)S(1)}, u32[]{:S(2)}, u32[]{:S(2)}) collective-permute-start(f32[896,128]{1,0:T(8,128)} %get-tuple-element.35.mine), channel_id=1, source_target_pairs={{0,2},{1,3},{2,0},{3,1},{4,6},{5,7},{6,4},{7,5},{8,10},{9,11},{10,... | collective-permute-start | bytes 1376264 | tf_op jit(solution)/shard_map/ppermute | solution.py:462
  9.3 39.7 %copy-start.7 = (f32[128,512]{1,0:T(8,128)S(1)}, f32[128,512]{1,0:T(8,128)}, u32[]{:S(2)}) copy-start(f32[128,512]{1,0:T(8,128)} %get-tuple-element.38.refs_0_) | copy-start | bytes 786436
  9.3 41.1 %copy-start.18 = (f32[640,128]{1,0:T(8,128)S(1)}, f32[640,128]{1,0:T(8,128)}, u32[]{:S(2)}) copy-start(f32[640,128]{1,0:T(8,128)} %get-tuple-element.45) | copy-start | bytes 983044
  9.3 50.7 %copy-start.8 = (f32[128,512]{1,0:T(8,128)S(1)}, f32[128,512]{1,0:T(8,128)}, u32[]{:S(2)}) copy-start(f32[128,512]{1,0:T(8,128)} %get-tuple-element.40.refs_1_) | copy-start | bytes 786436
  9.3 41.0 %collective-permute-start.4 = (f32[128,512]{1,0:T(8,128)}, f32[128,512]{1,0:T(8,128)S(1)}, u32[]{:S(2)}, u32[]{:S(2)}) collective-permute-start(f32[128,512]{1,0:T(8,128)} %get-tuple-element.38.refs_0_), channel_id=1, source_target_pairs={{0,16},{1,17},{2,18},{3,19},{4,20},{5,21},{6,22},{7,23},{8,24},{9,... | collective-permute-start | bytes 786440 | tf_op jit(solution)/shard_map/ppermute | solution.py:462
  32.2 16.8 %copy-start.15 = (f32[896,128]{1,0:T(8,128)}, f32[896,128]{1,0:T(8,128)S(1)}, u32[]{:S(2)}) copy-start(f32[896,128]{1,0:T(8,128)S(1)} %collective-permute-done.across) | copy-start | bytes 1376260
  32.2 26.3 %collective-permute-start.1 = (f32[896,128]{1,0:T(8,128)S(1)}, f32[896,128]{1,0:T(8,128)S(1)}, u32[]{:S(2)}, u32[]{:S(2)}) collective-permute-start(f32[896,128]{1,0:T(8,128)S(1)} %collective-permute-done.across), channel_id=1, source_target_pairs={{0,2},{1,3},{2,0},{3,1},{4,6},{5,7},{6,4},{7,5},{8,10},{9,11},{10,... | collective-permute-start | bytes 1376264 | tf_op jit(solution)/shard_map/ppermute | solution.py:462
  33.7 0.7 copy-start.20
  49.0 9.4 %collective-permute-start.3 = (f32[384,128]{1,0:T(8,128)}, f32[384,128]{1,0:T(8,128)S(1)}, u32[]{:S(2)}, u32[]{:S(2)}) collective-permute-start(f32[384,128]{1,0:T(8,128)} %get-tuple-element.37), channel_id=1, source_target_pairs={{0,16},{1,17},{2,18},{3,19},{4,20},{5,21},{6,22},{7,23},{8,24},{9,... | collective-permute-start | bytes 589832 | tf_op jit(solution)/shard_map/ppermute | solution.py:462
  49.0 78.9 %collective-permute-start.11 = (f32[128,512]{1,0:T(8,128)S(1)}, f32[128,512]{1,0:T(8,128)S(1)}, u32[]{:S(2)}, u32[]{:S(2)}) collective-permute-start(f32[128,512]{1,0:T(8,128)S(1)} %copy-done.7), channel_id=1, source_target_pairs={{0,2},{1,3},{4,6},{5,7},{8,10},{9,11},{12,14},{13,15},{18,16},{19,... | collective-permute-start | bytes 786440 | tf_op jit(solution)/shard_map/ppermute | solution.py:462
  50.4 29.8 %copy-start.9 = (f32[128,512]{1,0:T(8,128)}, f32[128,512]{1,0:T(8,128)S(1)}, u32[]{:S(2)}) copy-start(f32[128,512]{1,0:T(8,128)S(1)} %collective-permute-done.4.refs_3_) | copy-start | bytes 786436
  50.4 29.8 %collective-permute-start.7 = (f32[640,128]{1,0:T(8,128)S(1)}, f32[640,128]{1,0:T(8,128)S(1)}, u32[]{:S(2)}, u32[]{:S(2)}) collective-permute-start(f32[640,128]{1,0:T(8,128)S(1)} %copy-done.18), channel_id=1, source_target_pairs={{2,0},{3,1},{6,4},{7,5},{10,8},{11,9},{14,12},{15,13},{16,18},{17,... | collective-permute-start | bytes 983048 | tf_op jit(solution)/shard_map/ppermute | solution.py:462
  58.5 2.1 %copy-start.19 = (f32[384,128]{1,0:T(8,128)}, f32[384,128]{1,0:T(8,128)S(1)}, u32[]{:S(2)}) copy-start(f32[384,128]{1,0:T(8,128)S(1)} %collective-permute-done.3.h1_tiles) | copy-start | bytes 589828
  58.5 2.1 %copy-start.17 = (f32[896,128]{1,0:T(8,128)}, f32[896,128]{1,0:T(8,128)S(1)}, u32[]{:S(2)}) copy-start(f32[896,128]{1,0:T(8,128)S(1)} %collective-permute-done.1.corner) | copy-start | bytes 1376260
  58.5 70.8 %collective-permute-start.14 = (f32[128,512]{1,0:T(8,128)S(1)}, f32[128,512]{1,0:T(8,128)S(1)}, u32[]{:S(2)}, u32[]{:S(2)}) collective-permute-start(f32[128,512]{1,0:T(8,128)S(1)} %collective-permute-done.4.refs_3_), channel_id=1, source_target_pairs={{0,2},{1,3},{4,6},{5,7},{8,10},{9,11},{12,14},{13,15},{18,16},{19,... | collective-permute-start | bytes 786440 | tf_op jit(solution)/shard_map/ppermute | solution.py:462
  60.0 20.2 %collective-permute-start.5 = (f32[128,512]{1,0:T(8,128)S(1)}, f32[128,512]{1,0:T(8,128)S(1)}, u32[]{:S(2)}, u32[]{:S(2)}) collective-permute-start(f32[128,512]{1,0:T(8,128)S(1)} %copy-done.8), channel_id=1, source_target_pairs={{0,16},{1,17},{2,18},{3,19},{4,20},{5,21},{6,22},{7,23},{8,24},{9,... | collective-permute-start | bytes 786440 | tf_op jit(solution)/shard_map/ppermute | solution.py:462
  60.6 0.8 copy-start.16
  61.4 18.8 %copy-start = (f32[256,512]{1,0:T(8,128)S(1)}, f32[256,512]{1,0:T(8,128)}, u32[]{:S(2)}) copy-start(f32[256,512]{1,0:T(8,128)} %get-tuple-element.46.refs_2_) | copy-start | bytes 1572868
  61.4 26.1 %copy-start.4 = (f32[640,128]{1,0:T(8,128)S(1)}, f32[640,128]{1,0:T(8,128)}, u32[]{:S(2)}) copy-start(f32[640,128]{1,0:T(8,128)} %get-tuple-element.48) | copy-start | bytes 983044
  80.2 49.1 %copy-start.12 = (f32[128,512]{1,0:T(8,128)}, f32[128,512]{1,0:T(8,128)S(1)}, u32[]{:S(2)}) copy-start(f32[128,512]{1,0:T(8,128)S(1)} %collective-permute-done.5.refs_4_) | copy-start | bytes 786436
  80.2 68.8 %collective-permute-start.13 = (f32[256,512]{1,0:T(8,128)S(1)}, f32[256,512]{1,0:T(8,128)S(1)}, u32[]{:S(2)}, u32[]{:S(2)}) collective-permute-start(f32[256,512]{1,0:T(8,128)S(1)} %copy-done), channel_id=1, source_target_pairs={{0,2},{1,3},{4,6},{5,7},{8,10},{9,11},{12,14},{13,15},{18,16},{19,... | collective-permute-start | bytes 1572872 | tf_op jit(solution)/shard_map/ppermute | solution.py:462
  81.8 40.3 %collective-permute-start.8 = (f32[256,512]{1,0:T(8,128)S(1)}, f32[256,512]{1,0:T(8,128)S(1)}, u32[]{:S(2)}, u32[]{:S(2)}) collective-permute-start(f32[256,512]{1,0:T(8,128)S(1)} %copy-done), channel_id=1, source_target_pairs={{0,16},{1,17},{2,18},{3,19},{4,20},{5,21},{6,22},{7,23},{8,24},{9,... | collective-permute-start | bytes 1572872 | tf_op jit(solution)/shard_map/ppermute | solution.py:462
  87.5 34.5 %collective-permute-start.9 = (f32[640,128]{1,0:T(8,128)S(1)}, f32[640,128]{1,0:T(8,128)S(1)}, u32[]{:S(2)}, u32[]{:S(2)}) collective-permute-start(f32[640,128]{1,0:T(8,128)S(1)} %broadcast_select_fusion), channel_id=1, source_target_pairs={{0,16},{1,17},{2,18},{3,19},{4,20},{5,21},{6,22},{7,23},{8,24},{9,... | collective-permute-start | bytes 983048 | tf_op jit(solution)/shard_map/ppermute | solution.py:462
  122.0 15.2 %copy-start.5 = (f32[640,128]{1,0:T(8,128)}, f32[640,128]{1,0:T(8,128)S(1)}, u32[]{:S(2)}) copy-start(f32[640,128]{1,0:T(8,128)S(1)} %collective-permute-done.9.outer0) | copy-start | bytes 983044
  122.0 8.6 %copy-start.2 = (f32[256,512]{1,0:T(8,128)}, f32[256,512]{1,0:T(8,128)S(1)}, u32[]{:S(2)}) copy-start(f32[256,512]{1,0:T(8,128)S(1)} %collective-permute-done.8.refs_5_) | copy-start | bytes 1572868
  122.0 27.0 %collective-permute-start.16 = (f32[256,512]{1,0:T(8,128)S(1)}, f32[256,512]{1,0:T(8,128)S(1)}, u32[]{:S(2)}, u32[]{:S(2)}) collective-permute-start(f32[256,512]{1,0:T(8,128)S(1)} %collective-permute-done.8.refs_5_), channel_id=1, source_target_pairs={{0,2},{1,3},{4,6},{5,7},{8,10},{9,11},{12,14},{13,15},{18,16},{19,... | collective-permute-start | bytes 1572872 | tf_op jit(solution)/shard_map/ppermute | solution.py:462
  123.3 25.7 %collective-permute-start.10 = (f32[640,128]{1,0:T(8,128)S(1)}, f32[640,128]{1,0:T(8,128)S(1)}, u32[]{:S(2)}, u32[]{:S(2)}) collective-permute-start(f32[640,128]{1,0:T(8,128)S(1)} %collective-permute-done.9.outer0), channel_id=1, source_target_pairs={{2,0},{3,1},{6,4},{7,5},{10,8},{11,9},{14,12},{15,13},{16,18},{17,... | collective-permute-start | bytes 983048 | tf_op jit(solution)/shard_map/ppermute | solution.py:462
  128.0 9.3 %copy-start.10 = (f32[128,512]{1,0:T(8,128)}, f32[128,512]{1,0:T(8,128)S(1)}, u32[]{:S(2)}) copy-start(f32[128,512]{1,0:T(8,128)S(1)} %collective-permute-done.11.refs_6_) | copy-start | bytes 786436
  128.0 16.4 %collective-permute-start.12 = (f32[128,512]{1,0:T(8,128)S(1)}, f32[128,512]{1,0:T(8,128)S(1)}, u32[]{:S(2)}, u32[]{:S(2)}) collective-permute-start(f32[128,512]{1,0:T(8,128)S(1)} %copy-done.8), channel_id=1, source_target_pairs={{0,2},{1,3},{4,6},{5,7},{8,10},{9,11},{12,14},{13,15},{18,16},{19,... | collective-permute-start | bytes 786440 | tf_op jit(solution)/shard_map/ppermute | solution.py:462
  129.3 8.0 %copy-start.11 = (f32[128,512]{1,0:T(8,128)}, f32[128,512]{1,0:T(8,128)S(1)}, u32[]{:S(2)}) copy-start(f32[128,512]{1,0:T(8,128)S(1)} %collective-permute-done.14.refs_9_) | copy-start | bytes 786436
  129.3 19.7 %collective-permute-start.15 = (f32[128,512]{1,0:T(8,128)S(1)}, f32[128,512]{1,0:T(8,128)S(1)}, u32[]{:S(2)}, u32[]{:S(2)}) collective-permute-start(f32[128,512]{1,0:T(8,128)S(1)} %collective-permute-done.5.refs_4_), channel_id=1, source_target_pairs={{0,2},{1,3},{4,6},{5,7},{8,10},{9,11},{12,14},{13,15},{18,16},{19,... | collective-permute-start | bytes 786440 | tf_op jit(solution)/shard_map/ppermute | solution.py:462
  144.3 4.7 %copy-start.13 = (f32[128,512]{1,0:T(8,128)}, f32[128,512]{1,0:T(8,128)S(1)}, u32[]{:S(2)}) copy-start(f32[128,512]{1,0:T(8,128)S(1)} %collective-permute-done.12.refs_7_) | copy-start | bytes 786436
  149.0 0.7 copy-start.14
  149.0 0.9 copy-start.1
  149.0 1.0 copy-start.6
  149.0 1.1 copy-start.3

commit v3 on v0

v3 whole, which is shorter than its diff:
```python
import functools

import jax
import jax.numpy as jnp
from jax import lax
from jax.experimental import pallas as pl
from jax.experimental.pallas import tpu as pltpu
from jax.sharding import PartitionSpec as P

F32 = jnp.float32
BF16 = jnp.bfloat16
T = 128
R = 16
HBM = pl.BlockSpec(memory_space=pl.ANY)
VMEM = pl.BlockSpec(memory_space=pltpu.VMEM)
SMEM = pl.BlockSpec(memory_space=pltpu.SMEM)
PARAMS = pltpu.CompilerParams(vmem_limit_bytes=32 * 2**20)


def dot(a, b, dims=((1,), (0,))):
    return lax.dot_general(
        a, b, (dims, ((), ())), precision=lax.Precision.HIGHEST, preferred_element_type=F32
    )


def dot16(a, b, dims=((1,), (0,))):
    return lax.dot_general(a, b, (dims, ((), ())), preferred_element_type=F32)


def split(a):
    high = a.astype(BF16)
    return high, (a - high.astype(F32)).astype(BF16)


def dot3(a, b, dims=((1,), (0,))):
    return dot16(a[0], b[0], dims) + (dot16(a[0], b[1], dims) + dot16(a[1], b[0], dims))


NT = ((1,), (1,))
TN = ((0,), (0,))


def upper(n):
    return [(i, j) for i in range(n) for j in range(i, n)]


def across_lanes(x, k):
    return jnp.broadcast_to(x[:, k : k + 1], x.shape)


def across_rows(x, k):
    return jnp.broadcast_to(x[k : k + 1, :], x.shape)


def panel(rows, c0, lower):
    sub = lax.broadcasted_iota(jnp.int32, rows.shape, 0)
    lane = lax.broadcasted_iota(jnp.int32, rows.shape, 1)
    cols = [across_lanes(rows, c0 + k) for k in range(R)]
    out = jnp.where((lane >= c0) & (lane < c0 + R), (lane - c0 == sub).astype(F32), rows)
    half = out
    scale = jnp.ones_like(rows)
    for k in range(R):
        pivot = across_rows(cols[k], k)
        inv = 1.0 / pivot
        here = sub == k
        mult = cols[k]

        def step(x):
            row = across_rows(x, k) * inv
            return jnp.where(here, row, x - mult * row)

        if lower:
            scale = jnp.where(here, pivot, scale)
            half = half - jnp.where(sub > k, mult, 0.0) * (across_rows(half, k) * inv)
        out = step(out)
        for j in range(k + 1, R):
            cols[j] = step(cols[j])
    return out, half * lax.rsqrt(scale) if lower else None


def put_rows(matrix, rows, r0):
    parts = [matrix[:r0]] if r0 else []
    parts.append(rows)
    if r0 + rows.shape[0] < matrix.shape[0]:
        parts.append(matrix[r0 + rows.shape[0] :])
    return jnp.concatenate(parts, axis=0)


def invert_tile(m, lower=False):
    lane = lax.broadcasted_iota(jnp.int32, (T, T), 1)
    sub = lax.broadcasted_iota(jnp.int32, (T, T), 0)
    rows = m[:R]
    for c0 in range(0, T, R):
        swept, half = panel(rows, c0, lower)
        if c0 + R < T:
            old = m[c0 + R : c0 + 2 * R]
            inside = (lane[:R] >= c0) & (lane[:R] < c0 + R)
            rows = jnp.where(inside, 0.0, old)
            for k in range(R):
                rows = rows - across_lanes(old, c0 + k) * across_rows(swept, k)
        wide = put_rows(jnp.zeros((T, T), F32), swept, c0)
        rest = jnp.where((lane >= c0) & (lane < c0 + R), 0.0, m) - dot(m, wide)
        if lower:
            rest = jnp.where(sub < c0, m, rest)
        m = put_rows(rest, half if lower else swept, c0)
    return jnp.where(lane > sub, 0.0, m) if lower else m


def sweep(ref, start, stop):
    n = ref.shape[0]
    for p in range(start, stop, T):
        pivot = invert_tile(ref[p : p + T, p : p + T])
        rows = dot(pivot, ref[p : p + T, :])
        parts = ([rows[:, :p]] if p else []) + [pivot]
        if p + T < n:
            parts.append(rows[:, p + T :])
        rows = jnp.concatenate(parts, axis=1)
        for q in range(0, n, T):
            if q != p:
                change = dot(ref[q : q + T, p : p + T], rows)
                ref[q : q + T, p : p + T] = jnp.zeros((T, T), F32)
                ref[q : q + T, :] = ref[q : q + T, :] - change
        ref[p : p + T, :] = rows


def inverse_factor(ref):
    n = ref.shape[0]
    for p in range(0, n, T):
        pivot = invert_tile(ref[p : p + T, p : p + T], lower=True)
        scaled = dot(pivot, ref[p : p + T, :])
        for q in range(p + T, n, T):
            weight = scaled[:, q : q + T]
            ref[q : q + T, :] = ref[q : q + T, :] - dot(weight, scaled, TN)
            ref[q : q + T, p : p + T] = -dot(weight, pivot, TN)
        for q in range(0, n, T):
            if q < p:
                ref[p : p + T, q : q + T] = scaled[:, q : q + T]
            else:
                ref[p : p + T, q : q + T] = pivot if q == p else jnp.zeros((T, T), F32)


def leaf_block(leaf, side_r, side_c, r, c, size):
    e = leaf.shape[1] // 4
    return leaf.at[
        0,
        pl.ds(pl.multiple_of(side_r * e + r * size, T), size),
        pl.ds(pl.multiple_of(side_c * e + c * size, T), size),
    ]


def run_copies(pairs, sem):
    copies = [pltpu.make_async_copy(a, b, sem.at[i]) for i, (a, b) in enumerate(pairs)]
    for copy in copies:
        copy.start()
    for copy in copies:
        copy.wait()


def sides(place):
    v, u = place[0], place[1]
    return [v, 2 + u], [1 - v, 3 - u]


def unpack(ref, at, tiles):
    held = {}
    for r, c in upper(tiles):
        held[r, c] = ref[at : at + T, :]
        if c > r:
            held[c, r] = held[r, c].T
        at += T
    return jnp.concatenate(
        [jnp.concatenate([held[r, c] for c in range(tiles)], axis=1) for r in range(tiles)], axis=0
    )


def unpack_full(ref, at, tiles):
    rows = []
    for r in range(tiles):
        spots = [at + (r * tiles + c) * T for c in range(tiles)]
        rows.append(jnp.concatenate([ref[x : x + T, :] for x in spots], axis=1))
    return jnp.concatenate(rows, axis=0)


def call(kernel, name, outs, ins, scratch, flops, **more):
    return pl.pallas_call(
        kernel,
        out_shape=[jax.ShapeDtypeStruct(shape, dtype) for shape, dtype in outs],
        in_specs=[spec for spec, _ in ins],
        out_specs=more.pop("out_specs", [VMEM] * len(outs)),
        scratch_shapes=scratch,
        compiler_params=PARAMS,
        cost_estimate=pl.CostEstimate(flops=flops, bytes_accessed=10**6, transcendentals=0),
        name=name,
        **more,
    )(*[value for _, value in ins])


def cut_first_kernel(place, leaf, hh, a, sem):
    tiles = leaf.shape[1] // 4 // T
    ext, inn = sides(place)
    n_sym = len(upper(tiles))
    pairs = []
    for at, (r, c) in enumerate(upper(tiles)):
        pairs.append((leaf_block(leaf, inn[1], inn[1], r, c, T), hh.at[pl.ds(at * T, T)]))
        pairs.append((leaf_block(leaf, inn[0], inn[0], r, c, T), a.at[pl.ds(at * T, T)]))
    for at in range(tiles * tiles):
        source = leaf_block(leaf, ext[0], inn[0], at // tiles, at % tiles, T)
        pairs.append((source, a.at[pl.ds((n_sym + at) * T, T)]))
    run_copies(pairs, sem)


def cut_first(place, leaf):
    tiles = leaf.shape[1] // 4 // T
    n_sym, n_full = len(upper(tiles)), tiles * tiles
    return call(
        cut_first_kernel,
        "cut_first",
        [((n_sym * T, T), F32), (((n_sym + n_full) * T, T), F32)],
        [(SMEM, place), (HBM, leaf)],
        [pltpu.SemaphoreType.DMA((2 * n_sym + n_full,))],
        10**8,
    )


def cut_second_kernel(place, leaf, b, c1, c2, outer0, outer1, sem):
    e = leaf.shape[1] // 4
    tiles = e // T
    ext, inn = sides(place)
    pairs = [
        (leaf_block(leaf, inn[0], inn[1], 0, 0, e), b),
        (leaf_block(leaf, ext[1], inn[0], 0, 0, e), c1.at[pl.ds(0, e)]),
        (leaf_block(leaf, ext[0], inn[1], 0, 0, e), c1.at[pl.ds(e, e)]),
        (leaf_block(leaf, ext[1], inn[1], 0, 0, e), c2),
    ]
    half = outer0.shape[0]
    for at, (r, c) in enumerate(upper(2 * tiles)):
        ref, spot = (outer0, at * T) if at * T < half else (outer1, at * T - half)
        source = leaf_block(leaf, ext[r // tiles], ext[c // tiles], r % tiles, c % tiles, T)
        pairs.append((source, ref.at[pl.ds(spot, T)]))
    run_copies(pairs, sem)


def cut_second(place, leaf):
    e = leaf.shape[1] // 4
    n_outer = len(upper(2 * (e // T)))
    return call(
        cut_second_kernel,
        "cut_second",
        [((e, e), F32), ((2 * e, e), F32), ((e, e), F32)] + [((n_outer // 2 * T, T), F32)] * 2,
        [(SMEM, place), (HBM, leaf)],
        [pltpu.SemaphoreType.DMA((n_outer + 4,))],
        10**8,
    )


def gauge_kernel(place, mine, along, b, c1, c2, outer1, b_out, c1_out, c2_out, swap, held):
    e = held.shape[0]
    held[...] = unpack(mine, 0, e // T) + unpack(along, 0, e // T)
    inverse_factor(held)
    b_out[...] = dot(b[...], held[...], NT)
    factor = split(held[...])
    c1_out[:e, :] = c1[:e, :]
    c1_out[e:, :] = dot3(split(c1[e:, :]), factor, NT)
    c2_out[...] = dot3(split(c2[...]), factor, NT)
    same = place[0] == place[1]

    @pl.when(same)
    def _():
        swap[: 2 * e, :] = c1_out[...]
        swap[2 * e :, :] = c2_out[...]

    @pl.when(jnp.logical_not(same))
    def _():
        swap[: outer1.shape[0], :T] = outer1[...]


def gauge(place, mine, along, b, c1, c2, outer1):
    e = b.shape[0]
    return call(
        gauge_kernel,
        "gauge_side",
        [((e, e), F32), ((2 * e, e), F32), ((e, e), F32), ((3 * e, e), F32)],
        [(SMEM, place)] + [(VMEM, x) for x in (mine, along, b, c1, c2, outer1)],
        [pltpu.VMEM((e, e), F32)],
        5 * 10**9,
    )


def couple(b):
    mine, across, along, corner = (ref[...] for ref in b)
    return jnp.concatenate(
        [jnp.concatenate([mine, across], axis=1), jnp.concatenate([along, corner], axis=1)], axis=0
    )


def factor_start_kernel(a0, a1, a2, a3, b0, b1, b2, b3, side):
    e = b0.shape[0]
    tiles = e // T
    coup = couple((b0, b1, b2, b3))
    side[...] = -dot(coup, coup, NT)
    side[:e, :e] = side[:e, :e] + (unpack(a0, 0, tiles) + unpack(a1, 0, tiles))
    side[e:, e:] = side[e:, e:] + (unpack(a2, 0, tiles) + unpack(a3, 0, tiles))
    sweep(side, 0, e)


def factor_start(a, b):
    e = b[0].shape[0]
    return call(
        factor_start_kernel,
        "factor_start",
        [((2 * e, 2 * e), F32)],
        [(VMEM, x) for x in (*a, *b)],
        [],
        8 * 10**9,
    )[0]


def factor_end_kernel(place, side_in, b0, b1, b2, b3, high, low, side, full):
    e = b0.shape[0]
    side[...] = side_in[...]
    sweep(side, e, 2 * e)
    coup = split(couple((b0, b1, b2, b3)))
    away = dot3(split(side[...]), coup)
    shape = full.shape
    unit = lax.broadcasted_iota(jnp.int32, shape, 0) == lax.broadcasted_iota(jnp.int32, shape, 1)
    full[...] = dot3(coup, split(away), TN) + unit.astype(F32)

    def emit(value, rows, columns):
        high[rows, columns], low[rows, columns] = split(value)

    first, rest = slice(0, e), slice(e, 3 * e)
    emit(full[...], rest, rest)
    emit(-away[:e, :], first, rest)
    same = place[0] == place[1]

    @pl.when(same)
    def _():
        emit(side[:e, :e], first, first)
        emit(-away[:e, :].T, rest, first)

    @pl.when(jnp.logical_not(same))
    def _():
        emit(side[:e, e:], first, first)
        emit(-away[e:, :].T, rest, first)


def factor_end(place, side, b):
    e = b[0].shape[0]
    return call(
        factor_end_kernel,
        "factor_end",
        [((3 * e, 3 * e), BF16)] * 2,
        [(SMEM, place), (VMEM, side)] + [(VMEM, x) for x in b],
        [pltpu.VMEM((2 * e, 2 * e), F32), pltpu.VMEM((2 * e, 2 * e), F32)],
        8 * 10**9,
    )


def cross_block(a, c):
    e = c[0].shape[1]
    n_sym = len(upper(e // T)) * T
    c = jnp.concatenate([ref[...] for ref in c], axis=0)
    return jnp.concatenate(
        [
            jnp.concatenate([unpack_full(a, n_sym, e // T), c[e : 2 * e]], axis=1),
            jnp.concatenate([c[:e], c[2 * e :]], axis=1),
        ],
        axis=0,
    )


def times_inverse(cross, high, low, inner):
    e = cross.shape[1] // 2
    return dot3(split(cross[:, :e]), (high[:e], low[:e])) + dot3(
        split(cross[:, e:]), (high[inner], low[inner])
    )


def rows_kernel(place, leaf, high, low, a0, c01, c02, a2, swapped, top, bottom, block, col, own, sem):
    e = c02.shape[0]
    ext, _ = sides(place)
    copies = []
    for r in range(2):
        for c in range(2):
            target = own.at[pl.ds(r * e, e), pl.ds(c * e, e)]
            source = leaf_block(leaf, ext[r], ext[c], 0, 0, e)
            copies.append(pltpu.make_async_copy(source, target, sem.at[2 * r + c]))
            copies[-1].start()
    same = place[0] == place[1]
    mine = cross_block(a0, (c01, c02))

    @pl.when(same)
    def _():
        col[...] = mine

    @pl.when(jnp.logical_not(same))
    def _():
        col[...] = cross_block(a2, (swapped,))

    left = split(times_inverse(mine, high[...], low[...], slice(e, 2 * e)))
    top[...], bottom[...] = left
    left = [x[:, : 2 * e] for x in left]
    block[...] = -dot3(left, split(col[...]), NT)
    for copy in copies:
        copy.wait()

    @pl.when(same)
    def _():
        block[...] = block[...] + own[...]


def own_rows(place, leaf, high, low, a0, c0, a2, swapped):
    e = leaf.shape[1] // 4
    return call(
        rows_kernel,
        "own_rows",
        [((2 * e, 3 * e), BF16)] * 2 + [((2 * e, 2 * e), F32)],
        [(SMEM, place), (HBM, leaf)] + [(VMEM, x) for x in (high, low, a0, *c0, a2, swapped)],
        [
            pltpu.VMEM((2 * e, 2 * e), F32),
            pltpu.VMEM((2 * e, 2 * e), F32),
            pltpu.SemaphoreType.DMA((4,)),
        ],
        3 * 10**9,
    )


def spot(place, e, side, which):
    x = place[0] if which == 0 else 1 - place[0]
    return pl.ds(pl.multiple_of((2 * side + x) * e, T), e)


def products_kernel(
    place, high, low, top, bottom, block, a0, c01, c02, a1, c11, c12, a2, swapped, a3, c31, c32, out, col
):
    e = c02.shape[0]
    same = place[0] == place[1]
    across = cross_block(a1, (c11, c12))

    @pl.when(same)
    def _():
        col[0] = cross_block(a0, (c01, c02))
        col[1] = across

    @pl.when(jnp.logical_not(same))
    def _():
        col[0] = cross_block(a2, (swapped,))
        col[1] = cross_block(a3, (c31, c32))

    def write(value, a, b):
        for r in range(2):
            for c in range(2):
                out[0, spot(place, e, r, a), spot(place, e, c, b)] = value[
                    r * e : (r + 1) * e, c * e : (c + 1) * e
                ]

    write(block[...], 0, 0)
    rows = [
        (top[...], bottom[...]),
        split(times_inverse(across, high[...], low[...], slice(2 * e, 3 * e))),
    ]
    for a, b in ((1, 0), (0, 1), (1, 1)):
        inner = slice((1 + b) * e, (2 + b) * e)
        left = [jnp.concatenate([x[:, :e], x[:, inner]], axis=1) for x in rows[a]]
        write(-dot3(left, split(col[b]), NT), a, b)


def products(place, high, low, top, bottom, block, a, c0, c1, swapped, c3):
    e = swapped.shape[1]
    return call(
        products_kernel,
        "products",
        [((1, 4 * e, 4 * e), F32)],
        [(SMEM, place)]
        + [(VMEM, x) for x in (high, low, top, bottom, block)]
        + [(VMEM, x) for x in (a[0], *c0, a[1], *c1, a[2], swapped, a[3], *c3)],
        [pltpu.VMEM((2, 2 * e, 2 * e), F32)],
        4 * 10**9,
    )[0]


def add_outer_kernel(place, before, outer0, outer1, out, held, sem):
    e = out.shape[1] // 4
    tiles = e // T
    spots = [
        (
            out.at[0, spot(place, e, r, 1), spot(place, e, c, 1)],
            held.at[pl.ds(r * e, e), pl.ds(c * e, e)],
        )
        for r in range(2)
        for c in range(2)
    ]

    @pl.when(place[0] == place[1])
    def _():
        run_copies(spots, sem)
        half = outer0.shape[0]
        for at, (i, j) in enumerate(upper(2 * tiles)):
            ref, at = (outer0, at * T) if at * T < half else (outer1, at * T - half)
            piece = ref[at : at + T, :]
            r, c = slice(i * T, (i + 1) * T), slice(j * T, (j + 1) * T)
            held[r, c] = held[r, c] + piece
            if i != j:
                held[c, r] = held[c, r] + piece.T
        run_copies([(b, a) for a, b in spots], sem)


def add_outer(place, before, outer0, outer1):
    e = before.shape[1] // 4
    return call(
        add_outer_kernel,
        "add_outer",
        [(before.shape, F32)],
        [(SMEM, place), (HBM, before), (VMEM, outer0), (VMEM, outer1)],
        [pltpu.VMEM((2 * e, 2 * e), F32), pltpu.SemaphoreType.DMA((4,))],
        10**8,
        out_specs=[HBM],
        input_output_aliases={1: 0},
    )[0]


def tie(*values):
    return lax.optimization_barrier(values)


def solution(mesh):
    nx, ny = mesh.shape["gx"], mesh.shape["gy"]
    devices = [(x, y) for x in range(nx) for y in range(ny)]

    def is_same(x, y):
        return x // (nx // 2) == y // (ny // 2)

    def send(value, along_y, only=None):
        pairs = []
        for x, y in devices:
            if only is None or is_same(x, y) == only:
                to = (x, (y + ny // 2) % ny) if along_y else ((x + nx // 2) % nx, y)
                pairs.append((x * ny + y, to[0] * ny + to[1]))
        return lax.ppermute(value, ("gx", "gy"), pairs)

    def body(leaf):
        e = leaf.shape[1] // 4
        v = lax.axis_index("gx") // (nx // 2)
        u = lax.axis_index("gy") // (ny // 2)
        place = jnp.stack([v, u]).astype(jnp.int32)
        hh, a = cut_first(place, leaf)
        hh_y = send(hh, True)
        a_x = send(a, False)
        a_y = send(a, True)
        b, c1, c2, outer0, outer1 = cut_second(place, leaf)
        b, c1, c2, swap = gauge(place, hh, hh_y, b, c1, c2, outer1)
        b_x = send(b, False)
        b_y = send(b, True)
        a_x, b = tie(a_x, b)
        a_d = send(a_x, True)
        b_d = send(b_x, True)
        c1, swap, b_x = tie(c1, swap, b_x)
        c1_x = send(c1, False)
        swapped = send(swap, True)
        side = factor_start((a, a_x, a_y, a_d), (b, b_x, b_y, b_d))
        c2, c1_x, side = tie(c2, c1_x, side)
        c2_x = send(c2, False)
        c1_d = send(c1_x, True, only=True)
        high, low = factor_end(place, side, (b, b_x, b_y, b_d))
        passed = swapped[: outer0.shape[0], :T]
        outer0, high = tie(jnp.where(u == v, passed, outer0), high)
        outer0 = send(outer0, False)
        c2_d = send(c2_x, True, only=True)
        top, bottom, block = own_rows(place, leaf, high, low, a, (c1, c2), a_y, swapped)
        outer1 = send(outer0, True, only=False)
        out = products(
            place, high, low, top, bottom, block, (a, a_x, a_y, a_d), (c1, c2), (c1_x, c2_x), swapped, (c1_d, c2_d)
        )
        return add_outer(place, out, outer0, outer1)

    return jax.shard_map(
        body,
        mesh=mesh,
        in_specs=(P(None, "gy", "gx"),),
        out_specs=P(None, "gy", "gx"),
        check_vma=False,
    )
```

time: 889 us -> 112 us (0.13)
  the two profiles are of different devices: /device:TPU:24 before, /device:TPU:0 now
where the time goes in v3:
time: 112 us
  Pallas kernels  48.3 us (43%)
  waiting for transfers between devices  37 us (33%)
  starting transfers between devices  23.3 us (21%)
  local copies, waits for them, and re-layouts  2.9 us (3%)
    pallas_call x8, Pallas kernels, call(): pl.pallas_call(kernel, out_shape=[jax.ShapeDtypeStruct(shape, dtype) for...  48.3 us
    ppermute x14, waiting for transfers between devices, send(): return lax.ppermute(value, ('gx', 'gy'), pairs)  37 us
    ppermute x14, starting transfers between devices, send(): return lax.ppermute(value, ('gx', 'gy'), pairs)  23.3 us
    unnamed x8, local copies, waits for them, and re-layouts  2.9 us
  transfers between devices with their start and end apart: 14, of which 6 were waited for; matrix products, arithmetic and copies ran while one was open for 0% of the time, Pallas kernels for 40%

profile of v3, /device:TPU:0, one launch (start us, length us, event | category | flops | bytes accessed | tf_op | source)
XLA Modules:
  0.0 112.0 jit_solution(11908364389748854338)
XLA Ops:
  0.0 0.1 pad_add_fusion.place
  0.1 0.0 copy-start
  0.1 2.2 %copy-done = f32[1,1024,1024]{2,1,0:T(8,128)S(1)} copy-done((f32[1,1024,1024]{2,1,0:T(8,128)S(1)}, f32[1,1024,1024]{2,1,0:T(8,128)}, u32[]{:S(2)}) %copy-start) | copy-done | bytes 4194328
  2.3 0.8 cut_first.1
  3.0 3.0 %collective-permute-start = (f32[384,128]{1,0:T(8,128)S(1)}, f32[384,128]{1,0:T(8,128)S(1)}, u32[]{:S(2)}, u32[]{:S(2)}) collective-permute-start(f32[384,128]{1,0:T(8,128)S(1)} %get-tuple-element.31.mine), channel_id=1, source_target_pairs={{0,2},{1,3},{2,0},{3,1},{4,6},{5,7},{6,4},{7,5},{8,10},{9,11},{10,... | collective-permute-start | bytes 589832 | tf_op jit(solution)/shard_map/ppermute | solution.py:539
  6.1 2.6 %collective-permute-start.4 = (f32[896,128]{1,0:T(8,128)S(1)}, f32[896,128]{1,0:T(8,128)S(1)}, u32[]{:S(2)}, u32[]{:S(2)}) collective-permute-start(f32[896,128]{1,0:T(8,128)S(1)} %get-tuple-element.43.a0), channel_id=1, source_target_pairs={{0,16},{1,17},{2,18},{3,19},{4,20},{5,21},{6,22},{7,23},{8,24},{9,... | collective-permute-start | bytes 1376264 | tf_op jit(solution)/shard_map/ppermute | solution.py:539
  8.7 0.9 cut_second.1
  9.6 1.4 %collective-permute-done.along = f32[384,128]{1,0:T(8,128)S(1)} collective-permute-done((f32[384,128]{1,0:T(8,128)S(1)}, f32[384,128]{1,0:T(8,128)S(1)}, u32[]{:S(2)}, u32[]{:S(2)}) %collective-permute-start) | collective-permute-done | bytes 196640 | tf_op jit(solution)/shard_map/ppermute | solution.py:539
  11.0 8.7 %gauge_side.1 = (f32[256,256]{1,0:T(8,128)}, f32[512,256]{1,0:T(8,128)S(1)}, f32[256,256]{1,0:T(8,128)S(1)}, f32[768,256]{1,0:T(8,128)S(1)}) custom-call(s32[2]{0:T(128)S(1)} %pad_add_fusion.place, f32[384,128]{1,0:T(8,128)S(1)} %get-tuple-element.31.mine, f32[384,128]{1,0:T(8,128)S(1)} %collective-permute-done.along, f32[256,256]{1,0:T(8,128)S(1)} %get-tuple-element.32.b, ...), custom_call_target="tpu_custom_call" | custom-call | flops 5000000000 | bytes 1000000 | tf_op jit(solution)/shard_map/gauge_side/pallas_call | solution.py:185
  19.7 0.0 copy-start.2
  19.7 0.7 copy-done.2
  20.4 2.8 %collective-permute-start.1 = (f32[256,256]{1,0:T(8,128)}, f32[256,256]{1,0:T(8,128)}, u32[]{:S(2)}, u32[]{:S(2)}) collective-permute-start(f32[256,256]{1,0:T(8,128)} %get-tuple-element.45.b0), channel_id=1, source_target_pairs={{0,16},{1,17},{2,18},{3,19},{4,20},{5,21},{6,22},{7,23},{8,24},{9,... | collective-permute-start | bytes 786440 | tf_op jit(solution)/shard_map/ppermute | solution.py:539
  23.2 1.5 %collective-permute-start.5 = (f32[896,128]{1,0:T(8,128)S(1)}, f32[896,128]{1,0:T(8,128)S(1)}, u32[]{:S(2)}, u32[]{:S(2)}) collective-permute-start(f32[896,128]{1,0:T(8,128)S(1)} %get-tuple-element.43.a0), channel_id=1, source_target_pairs={{0,2},{1,3},{2,0},{3,1},{4,6},{5,7},{6,4},{7,5},{8,10},{9,11},{10,... | collective-permute-start | bytes 1376264 | tf_op jit(solution)/shard_map/ppermute | solution.py:539
  24.7 10.9 %collective-permute-done.4.a1 = f32[896,128]{1,0:T(8,128)S(1)} collective-permute-done((f32[896,128]{1,0:T(8,128)S(1)}, f32[896,128]{1,0:T(8,128)S(1)}, u32[]{:S(2)}, u32[]{:S(2)}) %collective-permute-start.4) | collective-permute-done | bytes 458784 | tf_op jit(solution)/shard_map/ppermute | solution.py:539
  35.6 0.4 collective-permute-start.6
  36.0 1.6 %collective-permute-start.7 = (f32[256,256]{1,0:T(8,128)}, f32[256,256]{1,0:T(8,128)}, u32[]{:S(2)}, u32[]{:S(2)}) collective-permute-start(f32[256,256]{1,0:T(8,128)} %get-tuple-element.45.b0), channel_id=1, source_target_pairs={{0,2},{1,3},{2,0},{3,1},{4,6},{5,7},{6,4},{7,5},{8,10},{9,11},{10,... | collective-permute-start | bytes 786440 | tf_op jit(solution)/shard_map/ppermute | solution.py:539
  37.6 2.5 %collective-permute-done.1.b1 = f32[256,256]{1,0:T(8,128)} collective-permute-done((f32[256,256]{1,0:T(8,128)}, f32[256,256]{1,0:T(8,128)}, u32[]{:S(2)}, u32[]{:S(2)}) %collective-permute-start.1) | collective-permute-done | bytes 262176 | tf_op jit(solution)/shard_map/ppermute | solution.py:539
  40.1 0.5 collective-permute-start.8
  40.6 0.0 copy-start.3
  40.6 0.0 collective-permute-start.3
  40.6 14.2 %collective-permute-done.7.b2 = f32[256,256]{1,0:T(8,128)} collective-permute-done((f32[256,256]{1,0:T(8,128)}, f32[256,256]{1,0:T(8,128)}, u32[]{:S(2)}, u32[]{:S(2)}) %collective-permute-start.7) | collective-permute-done | bytes 262176 | tf_op jit(solution)/shard_map/ppermute | solution.py:539
  54.7 0.4 collective-permute-start.2
  55.2 0.0 collective-permute-done.5.a2
  55.2 5.2 %collective-permute-done.8.b3 = f32[256,256]{1,0:T(8,128)} collective-permute-done((f32[256,256]{1,0:T(8,128)}, f32[256,256]{1,0:T(8,128)}, u32[]{:S(2)}, u32[]{:S(2)}) %collective-permute-start.8) | collective-permute-done | bytes 262176 | tf_op jit(solution)/shard_map/ppermute | solution.py:539
  60.4 0.0 collective-permute-done.6.a3
  60.4 10.6 %factor_start.1.side_in = f32[512,512]{1,0:T(8,128)S(1)} custom-call(f32[896,128]{1,0:T(8,128)S(1)} %get-tuple-element.43.a0, f32[896,128]{1,0:T(8,128)S(1)} %collective-permute-done.4.a1, f32[896,128]{1,0:T(8,128)S(1)} %collective-permute-done.5.a2, f32[896,128]{1,0:T(8,128)S(1)} %collective-permute-done.6.a3, f32[256,256]{1,0:T(8,128)} %get-tuple-element.45.b0, ...), custom_call_target="tpu_custom_call" | custom-call | flops 8000000000 | bytes 1000000 | tf_op jit(solution)/shard_map/factor_start/pallas_call | solution.py:185
  71.0 0.0 collective-permute-done.3.c11
  71.0 0.0 copy-done.3
  71.0 0.0 copy-start.1
  71.0 0.1 collective-permute-start.9
  71.1 2.9 %collective-permute-start.10 = (f32[512,256]{1,0:T(8,128)S(1)}, f32[512,256]{1,0:T(8,128)S(1)}, u32[]{:S(2)}, u32[]{:S(2)}) collective-permute-start(f32[512,256]{1,0:T(8,128)S(1)} %collective-permute-done.3.c11), channel_id=1, source_target_pairs={{0,2},{1,3},{4,6},{5,7},{8,10},{9,11},{12,14},{13,15},{18,16},{19,... | collective-permute-start | bytes 1572872 | tf_op jit(solution)/shard_map/ppermute | solution.py:539
  74.0 11.3 %factor_end.1 = (bf16[768,768]{1,0:T(8,128)(2,1)S(1)}, bf16[768,768]{1,0:T(8,128)(2,1)S(1)}) custom-call(s32[2]{0:T(128)S(1)} %pad_add_fusion.place, f32[512,512]{1,0:T(8,128)S(1)} %factor_start.1.side_in, f32[256,256]{1,0:T(8,128)} %get-tuple-element.45.b0, f32[256,256]{1,0:T(8,128)} %collective-permute-done.1.b1, f32[256,256]{1,0:T(8,128)} %collective-permute-done.7.b2, ...), custom_call_target="tpu_custom_call" | custom-call | flops 8000000000 | bytes 1000000 | tf_op jit(solution)/shard_map/factor_end/pallas_call | solution.py:185
  85.3 0.0 collective-permute-done.2.swapped
  85.4 1.6 %collective-permute-start.12 = (f32[640,128]{1,0:T(8,128)S(1)}, f32[640,128]{1,0:T(8,128)S(1)}, u32[]{:S(2)}, u32[]{:S(2)}) collective-permute-start(f32[640,128]{1,0:T(8,128)S(1)} %slice_select_fusion), channel_id=1, source_target_pairs={{0,16},{1,17},{2,18},{3,19},{4,20},{5,21},{6,22},{7,23},{8,24},{9,... | collective-permute-start | bytes 983048 | tf_op jit(solution)/shard_map/ppermute | solution.py:539
  87.0 0.0 collective-permute-done.9.c12
  87.0 4.6 %collective-permute-start.11 = (f32[256,256]{1,0:T(8,128)S(1)}, f32[256,256]{1,0:T(8,128)S(1)}, u32[]{:S(2)}, u32[]{:S(2)}) collective-permute-start(f32[256,256]{1,0:T(8,128)S(1)} %collective-permute-done.9.c12), channel_id=1, source_target_pairs={{0,2},{1,3},{4,6},{5,7},{8,10},{9,11},{12,14},{13,15},{18,16},{19,... | collective-permute-start | bytes 786440 | tf_op jit(solution)/shard_map/ppermute | solution.py:539
  91.6 0.0 copy-done.1
  91.6 4.6 %own_rows.1 = (bf16[512,768]{1,0:T(8,128)(2,1)S(1)}, bf16[512,768]{1,0:T(8,128)(2,1)S(1)}, f32[512,512]{1,0:T(8,128)S(1)}) custom-call(s32[2]{0:T(128)S(1)} %pad_add_fusion.place, f32[1,1024,1024]{2,1,0:T(8,128)S(1)} %copy-done.1, bf16[768,768]{1,0:T(8,128)(2,1)S(1)} %get-tuple-element.49.high, bf16[768,768]{1,0:T(8,128)(2,1)S(1)} %get-tuple-element.50.low, ...), custom_call_target="tpu_custom_call" | custom-call | flops 3000000000 | bytes 1000000 | tf_op jit(solution)/shard_map/own_rows/pallas_call | solution.py:185
  96.2 2.8 %collective-permute-done.12.outer0 = f32[640,128]{1,0:T(8,128)S(1)} collective-permute-done((f32[640,128]{1,0:T(8,128)S(1)}, f32[640,128]{1,0:T(8,128)S(1)}, u32[]{:S(2)}, u32[]{:S(2)}) %collective-permute-start.12) | collective-permute-done | bytes 327712 | tf_op jit(solution)/shard_map/ppermute | solution.py:539
  99.1 1.3 %collective-permute-start.13 = (f32[640,128]{1,0:T(8,128)S(1)}, f32[640,128]{1,0:T(8,128)S(1)}, u32[]{:S(2)}, u32[]{:S(2)}) collective-permute-start(f32[640,128]{1,0:T(8,128)S(1)} %collective-permute-done.12.outer0), channel_id=1, source_target_pairs={{2,0},{3,1},{6,4},{7,5},{10,8},{11,9},{14,12},{15,13},{16,18},{17,... | collective-permute-start | bytes 983048 | tf_op jit(solution)/shard_map/ppermute | solution.py:539
  100.4 0.0 collective-permute-done.11.c32
  100.4 0.0 collective-permute-done.10.c31
  100.4 8.5 %products.1.before = f32[1,1024,1024]{2,1,0:T(8,128)} custom-call(s32[2]{0:T(128)S(1)} %pad_add_fusion.place, bf16[768,768]{1,0:T(8,128)(2,1)S(1)} %get-tuple-element.49.high, bf16[768,768]{1,0:T(8,128)(2,1)S(1)} %get-tuple-element.50.low, bf16[512,768]{1,0:T(8,128)(2,1)S(1)} %get-tuple-element.52.top, bf16[512,768]{1,0:T(8,128)(2,1)S(1)} %get-tuple-element.53.bottom, ...), custom_call_target="tpu_custom_call" | custom-call | flops 4000000000 | bytes 1000000 | tf_op jit(solution)/shard_map/products/pallas_call | solution.py:185
  108.9 0.0 collective-permute-done.13.outer1
  108.9 2.9 %add_outer.1 = f32[1,1024,1024]{2,1,0:T(8,128)} custom-call(s32[2]{0:T(128)S(1)} %pad_add_fusion.place, f32[1,1024,1024]{2,1,0:T(8,128)} %products.1.before, f32[640,128]{1,0:T(8,128)S(1)} %collective-permute-done.12.outer0, f32[640,128]{1,0:T(8,128)S(1)} %collective-permute-done.13.outer1), custom_call_target="tpu_custom_call", output_to_operand_aliasing={{}: (1, {})} | custom-call | flops 100000000 | bytes 1000000 | tf_op jit(solution)/shard_map/add_outer/pallas_call | solution.py:185
  (1 shorter events, 0.0 us)
Async XLA Ops:
  0.1 2.2 %copy-start = (f32[1,1024,1024]{2,1,0:T(8,128)S(1)}, f32[1,1024,1024]{2,1,0:T(8,128)}, u32[]{:S(2)}) copy-start(f32[1,1024,1024]{2,1,0:T(8,128)} %leaf.5) | copy-start | bytes 12582916
  3.0 7.9 %collective-permute-start = (f32[384,128]{1,0:T(8,128)S(1)}, f32[384,128]{1,0:T(8,128)S(1)}, u32[]{:S(2)}, u32[]{:S(2)}) collective-permute-start(f32[384,128]{1,0:T(8,128)S(1)} %get-tuple-element.31.mine), channel_id=1, source_target_pairs={{0,2},{1,3},{2,0},{3,1},{4,6},{5,7},{6,4},{7,5},{8,10},{9,11},{10,... | collective-permute-start | bytes 589832 | tf_op jit(solution)/shard_map/ppermute | solution.py:539
  6.1 29.5 %collective-permute-start.4 = (f32[896,128]{1,0:T(8,128)S(1)}, f32[896,128]{1,0:T(8,128)S(1)}, u32[]{:S(2)}, u32[]{:S(2)}) collective-permute-start(f32[896,128]{1,0:T(8,128)S(1)} %get-tuple-element.43.a0), channel_id=1, source_target_pairs={{0,16},{1,17},{2,18},{3,19},{4,20},{5,21},{6,22},{7,23},{8,24},{9,... | collective-permute-start | bytes 1376264 | tf_op jit(solution)/shard_map/ppermute | solution.py:539
  19.7 0.7 copy-start.2
  20.4 19.7 %collective-permute-start.1 = (f32[256,256]{1,0:T(8,128)}, f32[256,256]{1,0:T(8,128)}, u32[]{:S(2)}, u32[]{:S(2)}) collective-permute-start(f32[256,256]{1,0:T(8,128)} %get-tuple-element.45.b0), channel_id=1, source_target_pairs={{0,16},{1,17},{2,18},{3,19},{4,20},{5,21},{6,22},{7,23},{8,24},{9,... | collective-permute-start | bytes 786440 | tf_op jit(solution)/shard_map/ppermute | solution.py:539
  23.2 32.0 %collective-permute-start.5 = (f32[896,128]{1,0:T(8,128)S(1)}, f32[896,128]{1,0:T(8,128)S(1)}, u32[]{:S(2)}, u32[]{:S(2)}) collective-permute-start(f32[896,128]{1,0:T(8,128)S(1)} %get-tuple-element.43.a0), channel_id=1, source_target_pairs={{0,2},{1,3},{2,0},{3,1},{4,6},{5,7},{6,4},{7,5},{8,10},{9,11},{10,... | collective-permute-start | bytes 1376264 | tf_op jit(solution)/shard_map/ppermute | solution.py:539
  35.6 24.8 %collective-permute-start.6 = (f32[896,128]{1,0:T(8,128)S(1)}, f32[896,128]{1,0:T(8,128)S(1)}, u32[]{:S(2)}, u32[]{:S(2)}) collective-permute-start(f32[896,128]{1,0:T(8,128)S(1)} %collective-permute-done.4.a1), channel_id=1, source_target_pairs={{0,2},{1,3},{2,0},{3,1},{4,6},{5,7},{6,4},{7,5},{8,10},{9,11},{10,... | collective-permute-start | bytes 1376264 | tf_op jit(solution)/shard_map/ppermute | solution.py:539
  36.0 18.8 %collective-permute-start.7 = (f32[256,256]{1,0:T(8,128)}, f32[256,256]{1,0:T(8,128)}, u32[]{:S(2)}, u32[]{:S(2)}) collective-permute-start(f32[256,256]{1,0:T(8,128)} %get-tuple-element.45.b0), channel_id=1, source_target_pairs={{0,2},{1,3},{2,0},{3,1},{4,6},{5,7},{6,4},{7,5},{8,10},{9,11},{10,... | collective-permute-start | bytes 786440 | tf_op jit(solution)/shard_map/ppermute | solution.py:539
  40.1 20.2 %collective-permute-start.8 = (f32[256,256]{1,0:T(8,128)}, f32[256,256]{1,0:T(8,128)}, u32[]{:S(2)}, u32[]{:S(2)}) collective-permute-start(f32[256,256]{1,0:T(8,128)} %collective-permute-done.1.b1), channel_id=1, source_target_pairs={{0,2},{1,3},{2,0},{3,1},{4,6},{5,7},{6,4},{7,5},{8,10},{9,11},{10,... | collective-permute-start | bytes 786440 | tf_op jit(solution)/shard_map/ppermute | solution.py:539
  40.6 30.4 %copy-start.3 = (f32[256,256]{1,0:T(8,128)S(1)}, f32[256,256]{1,0:T(8,128)}, u32[]{:S(2)}) copy-start(f32[256,256]{1,0:T(8,128)} %copy-done.2) | copy-start | bytes 786436
  40.6 30.4 %collective-permute-start.3 = (f32[512,256]{1,0:T(8,128)S(1)}, f32[512,256]{1,0:T(8,128)S(1)}, u32[]{:S(2)}, u32[]{:S(2)}) collective-permute-start(f32[512,256]{1,0:T(8,128)S(1)} %get-tuple-element.42.c01), channel_id=1, source_target_pairs={{0,16},{1,17},{2,18},{3,19},{4,20},{5,21},{6,22},{7,23},{8,24},{9,... | collective-permute-start | bytes 1572872 | tf_op jit(solution)/shard_map/ppermute | solution.py:539
  54.7 30.6 %collective-permute-start.2 = (f32[768,256]{1,0:T(8,128)S(1)}, f32[768,256]{1,0:T(8,128)S(1)}, u32[]{:S(2)}, u32[]{:S(2)}) collective-permute-start(f32[768,256]{1,0:T(8,128)S(1)} %get-tuple-element.39), channel_id=1, source_target_pairs={{0,2},{1,3},{2,0},{3,1},{4,6},{5,7},{6,4},{7,5},{8,10},{9,11},{10,... | collective-permute-start | bytes 2359304 | tf_op jit(solution)/shard_map/ppermute | solution.py:539
  71.0 20.6 %copy-start.1 = (f32[1,1024,1024]{2,1,0:T(8,128)S(1)}, f32[1,1024,1024]{2,1,0:T(8,128)}, u32[]{:S(2)}) copy-start(f32[1,1024,1024]{2,1,0:T(8,128)} %leaf.5) | copy-start | bytes 12582916
  71.0 15.9 %collective-permute-start.9 = (f32[256,256]{1,0:T(8,128)S(1)}, f32[256,256]{1,0:T(8,128)S(1)}, u32[]{:S(2)}, u32[]{:S(2)}) collective-permute-start(f32[256,256]{1,0:T(8,128)S(1)} %copy-done.3), channel_id=1, source_target_pairs={{0,16},{1,17},{2,18},{3,19},{4,20},{5,21},{6,22},{7,23},{8,24},{9,... | collective-permute-start | bytes 786440 | tf_op jit(solution)/shard_map/ppermute | solution.py:539
  71.1 29.2 %collective-permute-start.10 = (f32[512,256]{1,0:T(8,128)S(1)}, f32[512,256]{1,0:T(8,128)S(1)}, u32[]{:S(2)}, u32[]{:S(2)}) collective-permute-start(f32[512,256]{1,0:T(8,128)S(1)} %collective-permute-done.3.c11), channel_id=1, source_target_pairs={{0,2},{1,3},{4,6},{5,7},{8,10},{9,11},{12,14},{13,15},{18,16},{19,... | collective-permute-start | bytes 1572872 | tf_op jit(solution)/shard_map/ppermute | solution.py:539
  85.4 13.7 %collective-permute-start.12 = (f32[640,128]{1,0:T(8,128)S(1)}, f32[640,128]{1,0:T(8,128)S(1)}, u32[]{:S(2)}, u32[]{:S(2)}) collective-permute-start(f32[640,128]{1,0:T(8,128)S(1)} %slice_select_fusion), channel_id=1, source_target_pairs={{0,16},{1,17},{2,18},{3,19},{4,20},{5,21},{6,22},{7,23},{8,24},{9,... | collective-permute-start | bytes 983048 | tf_op jit(solution)/shard_map/ppermute | solution.py:539
  87.0 13.4 %collective-permute-start.11 = (f32[256,256]{1,0:T(8,128)S(1)}, f32[256,256]{1,0:T(8,128)S(1)}, u32[]{:S(2)}, u32[]{:S(2)}) collective-permute-start(f32[256,256]{1,0:T(8,128)S(1)} %collective-permute-done.9.c12), channel_id=1, source_target_pairs={{0,2},{1,3},{4,6},{5,7},{8,10},{9,11},{12,14},{13,15},{18,16},{19,... | collective-permute-start | bytes 786440 | tf_op jit(solution)/shard_map/ppermute | solution.py:539
  99.1 9.8 %collective-permute-start.13 = (f32[640,128]{1,0:T(8,128)S(1)}, f32[640,128]{1,0:T(8,128)S(1)}, u32[]{:S(2)}, u32[]{:S(2)}) collective-permute-start(f32[640,128]{1,0:T(8,128)S(1)} %collective-permute-done.12.outer0), channel_id=1, source_target_pairs={{2,0},{3,1},{6,4},{7,5},{10,8},{11,9},{14,12},{15,13},{16,18},{17,... | collective-permute-start | bytes 983048 | tf_op jit(solution)/shard_map/ppermute | solution.py:539

commit v4 on v3

--- a/solution.py
+++ b/solution.py
@@ -1,4 +1,4 @@
-import functools
+import math
 
 import jax
 import jax.numpy as jnp
@@ -11,6 +11,7 @@
 BF16 = jnp.bfloat16
 T = 128
 R = 16
+COST = 1000
 HBM = pl.BlockSpec(memory_space=pl.ANY)
 VMEM = pl.BlockSpec(memory_space=pltpu.VMEM)
 SMEM = pl.BlockSpec(memory_space=pltpu.SMEM)
@@ -181,7 +182,7 @@
     return jnp.concatenate(rows, axis=0)
 
 
-def call(kernel, name, outs, ins, scratch, flops, **more):
+def call(kernel, name, outs, ins, scratch, **more):
     return pl.pallas_call(
         kernel,
         out_shape=[jax.ShapeDtypeStruct(shape, dtype) for shape, dtype in outs],
@@ -189,23 +190,31 @@
         out_specs=more.pop("out_specs", [VMEM] * len(outs)),
         scratch_shapes=scratch,
         compiler_params=PARAMS,
-        cost_estimate=pl.CostEstimate(flops=flops, bytes_accessed=10**6, transcendentals=0),
+        cost_estimate=pl.CostEstimate(flops=COST, bytes_accessed=COST, transcendentals=0),
         name=name,
         **more,
     )(*[value for _, value in ins])
 
 
-def cut_first_kernel(place, leaf, hh, a, sem):
+def block_tiles(leaf, side_r, side_c, at):
+    tiles = leaf.shape[1] // 4 // T
+    return leaf_block(leaf, side_r, side_c, at // tiles, at % tiles, T)
+
+
+def cut_first_kernel(place, leaf, a, hs, sem):
     tiles = leaf.shape[1] // 4 // T
     ext, inn = sides(place)
     n_sym = len(upper(tiles))
     pairs = []
     for at, (r, c) in enumerate(upper(tiles)):
-        pairs.append((leaf_block(leaf, inn[1], inn[1], r, c, T), hh.at[pl.ds(at * T, T)]))
-        pairs.append((leaf_block(leaf, inn[0], inn[0], r, c, T), a.at[pl.ds(at * T, T)]))
+        source = leaf_block(leaf, inn[0], inn[0], r, c, T)
+        pairs.append((source, a.at[pl.ds(at * T, T)]))
+        pairs.append((source, hs.at[pl.ds((n_sym + at) * T, T)]))
+        pairs.append((leaf_block(leaf, inn[1], inn[1], r, c, T), hs.at[pl.ds(at * T, T)]))
     for at in range(tiles * tiles):
-        source = leaf_block(leaf, ext[0], inn[0], at // tiles, at % tiles, T)
-        pairs.append((source, a.at[pl.ds((n_sym + at) * T, T)]))
+        pairs.append(
+            (block_tiles(leaf, ext[0], inn[0], at), a.at[pl.ds((n_sym + at) * T, T)])
+        )
     run_copies(pairs, sem)
 
 
@@ -215,29 +224,44 @@
     return call(
         cut_first_kernel,
         "cut_first",
-        [((n_sym * T, T), F32), (((n_sym + n_full) * T, T), F32)],
+        [(((n_sym + n_full) * T, T), F32), ((2 * n_sym * T, T), F32)],
         [(SMEM, place), (HBM, leaf)],
-        [pltpu.SemaphoreType.DMA((2 * n_sym + n_full,))],
-        10**8,
-    )
-
-
-def cut_second_kernel(place, leaf, b, c1, c2, outer0, outer1, sem):
+        [pltpu.SemaphoreType.DMA((3 * n_sym + n_full,))],
+    )
+
+
+def cut_second_kernel(place, leaf, outer0, swap, b, c, sem):
     e = leaf.shape[1] // 4
     tiles = e // T
     ext, inn = sides(place)
     pairs = [
         (leaf_block(leaf, inn[0], inn[1], 0, 0, e), b),
-        (leaf_block(leaf, ext[1], inn[0], 0, 0, e), c1.at[pl.ds(0, e)]),
-        (leaf_block(leaf, ext[0], inn[1], 0, 0, e), c1.at[pl.ds(e, e)]),
-        (leaf_block(leaf, ext[1], inn[1], 0, 0, e), c2),
+        (leaf_block(leaf, ext[1], inn[0], 0, 0, e), c.at[pl.ds(0, e)]),
+        (leaf_block(leaf, ext[0], inn[1], 0, 0, e), c.at[pl.ds(e, e)]),
+        (leaf_block(leaf, ext[1], inn[1], 0, 0, e), c.at[pl.ds(2 * e, e)]),
     ]
-    half = outer0.shape[0]
+    half = outer0.shape[0] // T
+    second = []
     for at, (r, c) in enumerate(upper(2 * tiles)):
-        ref, spot = (outer0, at * T) if at * T < half else (outer1, at * T - half)
         source = leaf_block(leaf, ext[r // tiles], ext[c // tiles], r % tiles, c % tiles, T)
-        pairs.append((source, ref.at[pl.ds(spot, T)]))
+        if at < half:
+            pairs.append((source, outer0.at[pl.ds(at * T, T)]))
+        else:
+            second.append((source, swap.at[pl.ds((at - half) * T, T)]))
     run_copies(pairs, sem)
+    same = place[0] == place[1]
+
+    @pl.when(same)
+    def _():
+        cross = [
+            (block_tiles(leaf, ext[0], inn[0], at), swap.at[pl.ds(at * T, T)])
+            for at in range(tiles * tiles)
+        ]
+        run_copies(cross, sem)
+
+    @pl.when(jnp.logical_not(same))
+    def _():
+        run_copies(second, sem)
 
 
 def cut_second(place, leaf):
@@ -246,43 +270,34 @@
     return call(
         cut_second_kernel,
         "cut_second",
-        [((e, e), F32), ((2 * e, e), F32), ((e, e), F32)] + [((n_outer // 2 * T, T), F32)] * 2,
+        [((n_outer // 2 * T, T), F32)] * 2 + [((e, e), F32), ((3 * e, e), F32)],
         [(SMEM, place), (HBM, leaf)],
-        [pltpu.SemaphoreType.DMA((n_outer + 4,))],
-        10**8,
-    )
-
-
-def gauge_kernel(place, mine, along, b, c1, c2, outer1, b_out, c1_out, c2_out, swap, held):
+        [pltpu.SemaphoreType.DMA((n_outer // 2 + 4,))],
+    )
+
+
+def gauge_kernel(mine, along, b, c, b_out, c1, c2, held):
     e = held.shape[0]
-    held[...] = unpack(mine, 0, e // T) + unpack(along, 0, e // T)
+    tiles = e // T
+    held[...] = unpack(mine, 0, tiles) + unpack(along, 0, tiles)
     inverse_factor(held)
     b_out[...] = dot(b[...], held[...], NT)
-    factor = split(held[...])
-    c1_out[:e, :] = c1[:e, :]
-    c1_out[e:, :] = dot3(split(c1[e:, :]), factor, NT)
-    c2_out[...] = dot3(split(c2[...]), factor, NT)
-    same = place[0] == place[1]
-
-    @pl.when(same)
-    def _():
-        swap[: 2 * e, :] = c1_out[...]
-        swap[2 * e :, :] = c2_out[...]
-
-    @pl.when(jnp.logical_not(same))
-    def _():
-        swap[: outer1.shape[0], :T] = outer1[...]
-
-
-def gauge(place, mine, along, b, c1, c2, outer1):
+    scaled = dot3(split(c[e:, :]), split(held[...]), NT)
+    for at in range(3 * tiles * tiles):
+        r, k = at // tiles * T, at % tiles * T
+        tile = c[r : r + T, k : k + T] if r < e else scaled[r - e : r - e + T, k : k + T]
+        ref, spot = (c1, at * T) if at * T < c1.shape[0] else (c2, at * T - c1.shape[0])
+        ref[spot : spot + T, :] = tile
+
+
+def gauge(mine, along, b, c, last):
     e = b.shape[0]
     return call(
         gauge_kernel,
         "gauge_side",
-        [((e, e), F32), ((2 * e, e), F32), ((e, e), F32), ((3 * e, e), F32)],
-        [(SMEM, place)] + [(VMEM, x) for x in (mine, along, b, c1, c2, outer1)],
+        [((e, e), F32), ((3 * e * e // T - last, T), F32), ((last, T), F32)],
+        [(VMEM, x) for x in (mine, along, b, c)],
         [pltpu.VMEM((e, e), F32)],
-        5 * 10**9,
     )
 
 
@@ -293,13 +308,15 @@
     )
 
 
-def factor_start_kernel(a0, a1, a2, a3, b0, b1, b2, b3, side):
+def factor_start_kernel(a0, a1, hs, a3, b0, b1, b2, b3, side):
     e = b0.shape[0]
     tiles = e // T
     coup = couple((b0, b1, b2, b3))
     side[...] = -dot(coup, coup, NT)
     side[:e, :e] = side[:e, :e] + (unpack(a0, 0, tiles) + unpack(a1, 0, tiles))
-    side[e:, e:] = side[e:, e:] + (unpack(a2, 0, tiles) + unpack(a3, 0, tiles))
+    side[e:, e:] = side[e:, e:] + (
+        unpack(hs, len(upper(tiles)) * T, tiles) + unpack(a3, 0, tiles)
+    )
     sweep(side, 0, e)
 
 
@@ -311,7 +328,6 @@
         [((2 * e, 2 * e), F32)],
         [(VMEM, x) for x in (*a, *b)],
         [],
-        8 * 10**9,
     )[0]
 
 
@@ -352,18 +368,18 @@
         [((3 * e, 3 * e), BF16)] * 2,
         [(SMEM, place), (VMEM, side)] + [(VMEM, x) for x in b],
         [pltpu.VMEM((2 * e, 2 * e), F32), pltpu.VMEM((2 * e, 2 * e), F32)],
-        8 * 10**9,
-    )
-
-
-def cross_block(a, c):
-    e = c[0].shape[1]
-    n_sym = len(upper(e // T)) * T
-    c = jnp.concatenate([ref[...] for ref in c], axis=0)
+    )
+
+
+def cross_block(first, at, c1, c2):
+    rest = jnp.concatenate([c1[...], c2[...]], axis=0)
+    e = math.isqrt(rest.shape[0] * T // 3)
+    n = e * e // T
+    tiles = e // T
     return jnp.concatenate(
         [
-            jnp.concatenate([unpack_full(a, n_sym, e // T), c[e : 2 * e]], axis=1),
-            jnp.concatenate([c[:e], c[2 * e :]], axis=1),
+            jnp.concatenate([unpack_full(first, at, tiles), unpack_full(rest, n, tiles)], axis=1),
+            jnp.concatenate([unpack_full(rest, 0, tiles), unpack_full(rest, 2 * n, tiles)], axis=1),
         ],
         axis=0,
     )
@@ -376,8 +392,11 @@
     )
 
 
-def rows_kernel(place, leaf, high, low, a0, c01, c02, a2, swapped, top, bottom, block, col, own, sem):
-    e = c02.shape[0]
+def rows_kernel(
+    place, leaf, high, low, a0, c01, c02, swapped, c21, c22, top, bottom, block, col, own, sem
+):
+    e = leaf.shape[1] // 4
+    n_sym = len(upper(e // T)) * T
     ext, _ = sides(place)
     copies = []
     for r in range(2):
@@ -387,7 +406,7 @@
             copies.append(pltpu.make_async_copy(source, target, sem.at[2 * r + c]))
             copies[-1].start()
     same = place[0] == place[1]
-    mine = cross_block(a0, (c01, c02))
+    mine = cross_block(a0, n_sym, c01, c02)
 
     @pl.when(same)
     def _():
@@ -395,7 +414,7 @@
 
     @pl.when(jnp.logical_not(same))
     def _():
-        col[...] = cross_block(a2, (swapped,))
+        col[...] = cross_block(swapped, 0, c21, c22)
 
     left = split(times_inverse(mine, high[...], low[...], slice(e, 2 * e)))
     top[...], bottom[...] = left
@@ -409,19 +428,19 @@
         block[...] = block[...] + own[...]
 
 
-def own_rows(place, leaf, high, low, a0, c0, a2, swapped):
+def own_rows(place, leaf, high, low, a0, c01, c02, swapped, c21, c22):
     e = leaf.shape[1] // 4
     return call(
         rows_kernel,
         "own_rows",
         [((2 * e, 3 * e), BF16)] * 2 + [((2 * e, 2 * e), F32)],
-        [(SMEM, place), (HBM, leaf)] + [(VMEM, x) for x in (high, low, a0, *c0, a2, swapped)],
+        [(SMEM, place), (HBM, leaf)]
+        + [(VMEM, x) for x in (high, low, a0, c01, c02, swapped, c21, c22)],
         [
             pltpu.VMEM((2 * e, 2 * e), F32),
             pltpu.VMEM((2 * e, 2 * e), F32),
             pltpu.SemaphoreType.DMA((4,)),
         ],
-        3 * 10**9,
     )
 
 
@@ -430,90 +449,123 @@
     return pl.ds(pl.multiple_of((2 * side + x) * e, T), e)
 
 
+def write(out, place, value, a, b):
+    e = out.shape[1] // 4
+    for r in range(2):
+        for c in range(2):
+            out[0, spot(place, e, r, a), spot(place, e, c, b)] = value[
+                r * e : (r + 1) * e, c * e : (c + 1) * e
+            ]
+
+
+def pick(ref, rows, b):
+    e = ref.shape[1] // 3
+    return jnp.concatenate([ref[rows, :e], ref[rows, (1 + b) * e : (2 + b) * e]], axis=1)
+
+
 def products_kernel(
-    place, high, low, top, bottom, block, a0, c01, c02, a1, c11, c12, a2, swapped, a3, c31, c32, out, col
+    place, high, low, top, bottom, block, a0, c01, c02, a1, c11, c12, a3, c31, c32, out, part, scratch
 ):
-    e = c02.shape[0]
+    e = out.shape[1] // 4
+    n_sym = len(upper(e // T)) * T
     same = place[0] == place[1]
-    across = cross_block(a1, (c11, c12))
+    write(out, place, block[...], 0, 0)
+    everything = slice(0, 2 * e)
 
     @pl.when(same)
     def _():
-        col[0] = cross_block(a0, (c01, c02))
-        col[1] = across
+        across = cross_block(a1, n_sym, c11, c12)
+        right = split(across)
+        left = [pick(x, everything, 1) for x in (top, bottom)]
+        write(out, place, -dot3(left, right, NT), 0, 1)
+        scratch[...] = times_inverse(across, high[...], low[...], slice(2 * e, 3 * e))
+        left = split(pick(scratch, everything, 0))
+        write(out, place, -dot3(left, split(cross_block(a0, n_sym, c01, c02)), NT), 1, 0)
+        left = split(pick(scratch, everything, 1))
+        part[...] = -dot3(left, right, NT)
 
     @pl.when(jnp.logical_not(same))
     def _():
-        col[0] = cross_block(a2, (swapped,))
-        col[1] = cross_block(a3, (c31, c32))
-
-    def write(value, a, b):
-        for r in range(2):
-            for c in range(2):
-                out[0, spot(place, e, r, a), spot(place, e, c, b)] = value[
-                    r * e : (r + 1) * e, c * e : (c + 1) * e
-                ]
-
-    write(block[...], 0, 0)
-    rows = [
-        (top[...], bottom[...]),
-        split(times_inverse(across, high[...], low[...], slice(2 * e, 3 * e))),
-    ]
-    for a, b in ((1, 0), (0, 1), (1, 1)):
-        inner = slice((1 + b) * e, (2 + b) * e)
-        left = [jnp.concatenate([x[:, :e], x[:, inner]], axis=1) for x in rows[a]]
-        write(-dot3(left, split(col[b]), NT), a, b)
-
-
-def products(place, high, low, top, bottom, block, a, c0, c1, swapped, c3):
-    e = swapped.shape[1]
+        right = split(cross_block(a3, n_sym, c31, c32))
+        left = [pick(x, everything, 1) for x in (top, bottom)]
+        write(out, place, -dot3(left, right, NT), 0, 1)
+
+
+def products(place, high, low, top, bottom, block, mine, across, corner):
+    e = block.shape[0] // 2
     return call(
         products_kernel,
         "products",
-        [((1, 4 * e, 4 * e), F32)],
+        [((1, 4 * e, 4 * e), F32), ((2 * e, 2 * e), F32)],
         [(SMEM, place)]
-        + [(VMEM, x) for x in (high, low, top, bottom, block)]
-        + [(VMEM, x) for x in (a[0], *c0, a[1], *c1, a[2], swapped, a[3], *c3)],
-        [pltpu.VMEM((2, 2 * e, 2 * e), F32)],
-        4 * 10**9,
-    )[0]
-
-
-def add_outer_kernel(place, before, outer0, outer1, out, held, sem):
+        + [(VMEM, x) for x in (high, low, top, bottom, block, *mine, *across, *corner)],
+        [pltpu.VMEM((2 * e, 3 * e), F32)],
+    )
+
+
+def finish_kernel(
+    place, before, high, low, part, passed, last, a1, c11, swapped, c21, c22, a3, c31, out, held, scratch, sem
+):
     e = out.shape[1] // 4
     tiles = e // T
-    spots = [
-        (
-            out.at[0, spot(place, e, r, 1), spot(place, e, c, 1)],
-            held.at[pl.ds(r * e, e), pl.ds(c * e, e)],
-        )
-        for r in range(2)
-        for c in range(2)
-    ]
+    n_sym = len(upper(tiles)) * T
+
+    def targets(b):
+        return [
+            (
+                held.at[pl.ds(r * e, e), pl.ds((2 * b + c) * e, e)],
+                out.at[0, spot(place, e, r, 1), spot(place, e, c, b)],
+            )
+            for r in range(2)
+            for c in range(2)
+        ]
 
     @pl.when(place[0] == place[1])
     def _():
-        run_copies(spots, sem)
-        half = outer0.shape[0]
+        half = last.shape[0]
         for at, (i, j) in enumerate(upper(2 * tiles)):
-            ref, at = (outer0, at * T) if at * T < half else (outer1, at * T - half)
+            ref, at = (last, at * T) if at * T < half else (passed, at * T - half)
             piece = ref[at : at + T, :]
             r, c = slice(i * T, (i + 1) * T), slice(j * T, (j + 1) * T)
-            held[r, c] = held[r, c] + piece
+            shift = 2 * e
+            held[r, j * T + shift : (j + 1) * T + shift] = part[r, c] + piece
             if i != j:
-                held[c, r] = held[c, r] + piece.T
-        run_copies([(b, a) for a, b in spots], sem)
-
-
-def add_outer(place, before, outer0, outer1):
+                held[c, i * T + shift : (i + 1) * T + shift] = part[c, r] + piece.T
+        run_copies(targets(1), sem)
+
+    @pl.when(place[0] != place[1])
+    def _():
+        across = cross_block(a1, n_sym, c11, last)
+        scratch[...] = times_inverse(across, high[...], low[...], slice(2 * e, 3 * e))
+        everything = slice(0, 2 * e)
+        copies = []
+        for b in range(2):
+            col = cross_block(swapped, 0, c21, c22) if b == 0 else cross_block(a3, n_sym, c31, passed)
+            left = split(pick(scratch, everything, b))
+            held[:, 2 * e * b : 2 * e * (b + 1)] = -dot3(left, split(col), NT)
+            for i, (source, target) in enumerate(targets(b)):
+                copies.append(pltpu.make_async_copy(source, target, sem.at[4 * b + i]))
+                copies[-1].start()
+        for copy in copies:
+            copy.wait()
+
+
+def finish(place, before, high, low, part, passed, last, a1, c11, swapped, c21, c22, a3, c31):
     e = before.shape[1] // 4
     return call(
-        add_outer_kernel,
-        "add_outer",
+        finish_kernel,
+        "finish",
         [(before.shape, F32)],
-        [(SMEM, place), (HBM, before), (VMEM, outer0), (VMEM, outer1)],
-        [pltpu.VMEM((2 * e, 2 * e), F32), pltpu.SemaphoreType.DMA((4,))],
-        10**8,
+        [(SMEM, place), (HBM, before)]
+        + [
+            (VMEM, x)
+            for x in (high, low, part, passed, last, a1, c11, swapped, c21, c22, a3, c31)
+        ],
+        [
+            pltpu.VMEM((2 * e, 4 * e), F32),
+            pltpu.VMEM((2 * e, 3 * e), F32),
+            pltpu.SemaphoreType.DMA((8,)),
+        ],
         out_specs=[HBM],
         input_output_aliases={1: 0},
     )[0]
@@ -543,35 +595,38 @@
         v = lax.axis_index("gx") // (nx // 2)
         u = lax.axis_index("gy") // (ny // 2)
         place = jnp.stack([v, u]).astype(jnp.int32)
-        hh, a = cut_first(place, leaf)
-        hh_y = send(hh, True)
+        same = u == v
+        a, hs = cut_first(place, leaf)
         a_x = send(a, False)
-        a_y = send(a, True)
-        b, c1, c2, outer0, outer1 = cut_second(place, leaf)
-        b, c1, c2, swap = gauge(place, hh, hh_y, b, c1, c2, outer1)
+        hs_y = send(hs, True)
+        outer0, swap, b, c = cut_second(place, leaf)
+        swapped = send(swap, True)
+        b, c1, c2 = gauge(hs, hs_y, b, c, swap.shape[0])
         b_x = send(b, False)
         b_y = send(b, True)
-        a_x, b = tie(a_x, b)
+        a_x, b_y = tie(a_x, b_y)
         a_d = send(a_x, True)
         b_d = send(b_x, True)
-        c1, swap, b_x = tie(c1, swap, b_x)
+        c1, b_x = tie(c1, b_x)
         c1_x = send(c1, False)
-        swapped = send(swap, True)
-        side = factor_start((a, a_x, a_y, a_d), (b, b_x, b_y, b_d))
-        c2, c1_x, side = tie(c2, c1_x, side)
-        c2_x = send(c2, False)
+        c1, c2, b_d = tie(c1, c2, b_d)
+        c1_y = send(c1, True, only=True)
+        c2_y = send(c2, True, only=True)
+        side = factor_start((a, a_x, hs_y, a_d), (b, b_x, b_y, b_d))
+        third, c1_x, side = tie(jnp.where(same, swapped, c2), c1_x, side)
+        third = send(third, False)
         c1_d = send(c1_x, True, only=True)
         high, low = factor_end(place, side, (b, b_x, b_y, b_d))
-        passed = swapped[: outer0.shape[0], :T]
-        outer0, high = tie(jnp.where(u == v, passed, outer0), high)
-        outer0 = send(outer0, False)
-        c2_d = send(c2_x, True, only=True)
-        top, bottom, block = own_rows(place, leaf, high, low, a, (c1, c2), a_y, swapped)
-        outer1 = send(outer0, True, only=False)
-        out = products(
-            place, high, low, top, bottom, block, (a, a_x, a_y, a_d), (c1, c2), (c1_x, c2_x), swapped, (c1_d, c2_d)
+        last, high = tie(jnp.where(same, c2, outer0), high)
+        last = send(last, False)
+        passed = send(third, True)
+        top, bottom, block = own_rows(place, leaf, high, low, a, c1, c2, swapped, c1_y, c2_y)
+        out, part = products(
+            place, high, low, top, bottom, block, (a, c1, c2), (a_x, c1_x, third), (a_d, c1_d, passed)
         )
-        return add_outer(place, out, outer0, outer1)
+        return finish(
+            place, out, high, low, part, passed, last, a_x, c1_x, swapped, c1_y, c2_y, a_d, c1_d
+        )
 
     return jax.shard_map(
         body,

time: 112 us -> 117 us (1.045)
  the two profiles are of different devices: /device:TPU:0 before, /device:TPU:24 now
where the time goes in v4:
time: 117 us; the launch traced here: 116 us
  waiting for transfers between devices  47.8 us (41%)
  Pallas kernels  44.8 us (38%)
  starting transfers between devices  14.6 us (12%)
  local copies, waits for them, and re-layouts  7.19 us (6%)
    ppermute x14, waiting for transfers between devices, send(): return lax.ppermute(value, ('gx', 'gy'), pairs)  47.8 us
    pallas_call x8, Pallas kernels, call(): pl.pallas_call(kernel, out_shape=[jax.ShapeDtypeStruct(shape, dtype) for...  44.8 us
    ppermute x14, starting transfers between devices, send(): return lax.ppermute(value, ('gx', 'gy'), pairs)  14.6 us
    unnamed x16, local copies, waits for them, and re-layouts  7.19 us
  transfers between devices with their start and end apart: 14, of which 6 were waited for; matrix products, arithmetic and copies ran while one was open for 1% of the time, Pallas kernels for 34%

profile of v4, /device:TPU:24, one launch (start us, length us, event | category | flops | bytes accessed | tf_op | source)
XLA Modules:
  0.0 115.7 jit_solution(3177847592378250670)
XLA Ops:
  0.0 0.1 pad_add_fusion.place
  0.1 2.2 %copy-done = f32[1,1024,1024]{2,1,0:T(8,128)S(1)} copy-done((f32[1,1024,1024]{2,1,0:T(8,128)S(1)}, f32[1,1024,1024]{2,1,0:T(8,128)}, u32[]{:S(2)}) %copy-start) | copy-done | bytes 4194328
  2.3 0.8 cut_first.1
  3.1 1.6 %collective-permute-start = (f32[768,128]{1,0:T(8,128)S(1)}, f32[768,128]{1,0:T(8,128)S(1)}, u32[]{:S(2)}, u32[]{:S(2)}) collective-permute-start(f32[768,128]{1,0:T(8,128)S(1)} %get-tuple-element.33.mine), channel_id=1, source_target_pairs={{0,2},{1,3},{2,0},{3,1},{4,6},{5,7},{6,4},{7,5},{8,10},{9,11},{10,... | collective-permute-start | bytes 1179656 | tf_op jit(solution)/shard_map/ppermute | solution.py:591
  4.7 0.3 collective-permute-start.5
  5.0 1.6 %cut_second.1 = (f32[640,128]{1,0:T(8,128)S(1)}, f32[640,128]{1,0:T(8,128)}, f32[256,256]{1,0:T(8,128)S(1)}, f32[768,256]{1,0:T(8,128)S(1)}) custom-call(s32[2]{0:T(128)S(1)} %pad_add_fusion.place, f32[1,1024,1024]{2,1,0:T(8,128)S(1)} %copy-done), custom_call_target="tpu_custom_call" | custom-call | flops 1000 | bytes 1000 | tf_op jit(solution)/shard_map/cut_second/pallas_call | solution.py:186
  6.6 0.0 copy-start.7
  6.6 0.7 copy-done.7
  7.3 6.7 %collective-permute-done.along.hs = f32[768,128]{1,0:T(8,128)S(1)} collective-permute-done((f32[768,128]{1,0:T(8,128)S(1)}, f32[768,128]{1,0:T(8,128)S(1)}, u32[]{:S(2)}, u32[]{:S(2)}) %collective-permute-start) | collective-permute-done | bytes 393248 | tf_op jit(solution)/shard_map/ppermute | solution.py:591
  14.0 7.3 %gauge_side.1 = (f32[256,256]{1,0:T(8,128)S(1)}, f32[896,128]{1,0:T(8,128)S(1)}, f32[640,128]{1,0:T(8,128)S(1)}) custom-call(f32[768,128]{1,0:T(8,128)S(1)} %get-tuple-element.33.mine, f32[768,128]{1,0:T(8,128)S(1)} %collective-permute-done.along.hs, f32[256,256]{1,0:T(8,128)S(1)} %get-tuple-element.34.b, f32[768,256]{1,0:T(8,128)S(1)} %get-tuple-element.35.c), custom_call_target="tpu_custom_call" | custom-call | flops 1000 | bytes 1000 | tf_op jit(solution)/shard_map/gauge_side/pallas_call | solution.py:186
  21.3 0.4 collective-permute-start.1
  21.7 1.5 %collective-permute-start.6 = (f32[256,256]{1,0:T(8,128)S(1)}, f32[256,256]{1,0:T(8,128)S(1)}, u32[]{:S(2)}, u32[]{:S(2)}) collective-permute-start(f32[256,256]{1,0:T(8,128)S(1)} %get-tuple-element.37.b0), channel_id=1, source_target_pairs={{0,2},{1,3},{2,0},{3,1},{4,6},{5,7},{6,4},{7,5},{8,10},{9,11},{10,... | collective-permute-start | bytes 786440 | tf_op jit(solution)/shard_map/ppermute | solution.py:591
  23.2 0.7 copy-done.2
  24.0 0.5 collective-permute-start.3
  24.5 14.2 %collective-permute-done.1.b1 = f32[256,256]{1,0:T(8,128)} collective-permute-done((f32[256,256]{1,0:T(8,128)S(1)}, f32[256,256]{1,0:T(8,128)}, u32[]{:S(2)}, u32[]{:S(2)}) %collective-permute-start.1) | collective-permute-done | bytes 262176 | tf_op jit(solution)/shard_map/ppermute | solution.py:591
  38.6 0.5 collective-permute-start.2
  39.1 0.0 collective-permute-done.5.a1
  39.1 0.0 collective-permute-done.6.b2
  39.1 0.7 copy-done.5
  39.8 1.5 %collective-permute-start.7 = (f32[896,128]{1,0:T(8,128)S(1)}, f32[896,128]{1,0:T(8,128)S(1)}, u32[]{:S(2)}, u32[]{:S(2)}) collective-permute-start(f32[896,128]{1,0:T(8,128)S(1)} %collective-permute-done.5.a1), channel_id=1, source_target_pairs={{0,2},{1,3},{2,0},{3,1},{4,6},{5,7},{6,4},{7,5},{8,10},{9,11},{10,... | collective-permute-start | bytes 1376264 | tf_op jit(solution)/shard_map/ppermute | solution.py:591
  41.4 0.0 collective-permute-start.4
  41.4 6.7 %collective-permute-done.2.b3 = f32[256,256]{1,0:T(8,128)} collective-permute-done((f32[256,256]{1,0:T(8,128)}, f32[256,256]{1,0:T(8,128)}, u32[]{:S(2)}, u32[]{:S(2)}) %collective-permute-start.2) | collective-permute-done | bytes 262176 | tf_op jit(solution)/shard_map/ppermute | solution.py:591
  48.1 0.0 collective-permute-done.3.swapped
  48.1 1.0 broadcast_select_fusion
  49.1 7.8 %collective-permute-done.7.a3 = f32[896,128]{1,0:T(8,128)S(1)} collective-permute-done((f32[896,128]{1,0:T(8,128)S(1)}, f32[896,128]{1,0:T(8,128)S(1)}, u32[]{:S(2)}, u32[]{:S(2)}) %collective-permute-start.7) | collective-permute-done | bytes 458784 | tf_op jit(solution)/shard_map/ppermute | solution.py:591
  56.9 0.9 copy-done.3
  57.8 0.9 copy-done.6
  58.8 10.7 %factor_start.1.side_in = f32[512,512]{1,0:T(8,128)S(1)} custom-call(f32[896,128]{1,0:T(8,128)S(1)} %get-tuple-element.43.a0, f32[896,128]{1,0:T(8,128)S(1)} %collective-permute-done.5.a1, f32[768,128]{1,0:T(8,128)S(1)} %collective-permute-done.along.hs, f32[896,128]{1,0:T(8,128)S(1)} %collective-permute-done.7.a3, f32[256,256]{1,0:T(8,128)S(1)} %copy-done.3, ...), custom_call_target="tpu_custom_call" | custom-call | flops 1000 | bytes 1000 | tf_op jit(solution)/shard_map/factor_start/pallas_call | solution.py:186
  69.5 0.0 collective-permute-done.4.c11
  69.5 0.1 collective-permute-start.10
  69.5 1.3 %collective-permute-start.8 = (f32[896,128]{1,0:T(8,128)S(1)}, f32[896,128]{1,0:T(8,128)S(1)}, u32[]{:S(2)}, u32[]{:S(2)}) collective-permute-start(f32[896,128]{1,0:T(8,128)S(1)} %get-tuple-element.52.c01), channel_id=1, source_target_pairs={{0,2},{1,3},{4,6},{5,7},{8,10},{9,11},{12,14},{13,15},{18,16},{19,... | collective-permute-start | bytes 1376264 | tf_op jit(solution)/shard_map/ppermute | solution.py:591
  70.8 1.3 %collective-permute-start.11 = (f32[896,128]{1,0:T(8,128)S(1)}, f32[896,128]{1,0:T(8,128)S(1)}, u32[]{:S(2)}, u32[]{:S(2)}) collective-permute-start(f32[896,128]{1,0:T(8,128)S(1)} %collective-permute-done.4.c11), channel_id=1, source_target_pairs={{0,2},{1,3},{4,6},{5,7},{8,10},{9,11},{12,14},{13,15},{18,16},{19,... | collective-permute-start | bytes 1376264 | tf_op jit(solution)/shard_map/ppermute | solution.py:591
  72.1 1.3 %collective-permute-start.9 = (f32[640,128]{1,0:T(8,128)S(1)}, f32[640,128]{1,0:T(8,128)S(1)}, u32[]{:S(2)}, u32[]{:S(2)}) collective-permute-start(f32[640,128]{1,0:T(8,128)S(1)} %get-tuple-element.40.c02), channel_id=1, source_target_pairs={{0,2},{1,3},{4,6},{5,7},{8,10},{9,11},{12,14},{13,15},{18,16},{19,... | collective-permute-start | bytes 983048 | tf_op jit(solution)/shard_map/ppermute | solution.py:591
  73.4 0.0 copy-start.4
  73.5 0.9 copy-done.4
  74.4 11.4 %factor_end.1 = (bf16[768,768]{1,0:T(8,128)(2,1)S(1)}, bf16[768,768]{1,0:T(8,128)(2,1)S(1)}) custom-call(s32[2]{0:T(128)S(1)} %pad_add_fusion.place, f32[512,512]{1,0:T(8,128)S(1)} %factor_start.1.side_in, f32[256,256]{1,0:T(8,128)S(1)} %copy-done.4, f32[256,256]{1,0:T(8,128)} %collective-permute-done.1.b1, f32[256,256]{1,0:T(8,128)S(1)} %copy-done.6, ...), custom_call_target="tpu_custom_call" | custom-call | flops 1000 | bytes 1000 | tf_op jit(solution)/shard_map/factor_end/pallas_call | solution.py:186
  85.8 0.0 collective-permute-done.10.c12
  85.8 2.8 %collective-permute-start.12 = (f32[640,128]{1,0:T(8,128)S(1)}, f32[640,128]{1,0:T(8,128)S(1)}, u32[]{:S(2)}, u32[]{:S(2)}) collective-permute-start(f32[640,128]{1,0:T(8,128)S(1)} %collective-permute-done.10.c12), channel_id=1, source_target_pairs={{0,2},{1,3},{2,0},{3,1},{4,6},{5,7},{6,4},{7,5},{8,10},{9,11},{10,... | collective-permute-start | bytes 983048 | tf_op jit(solution)/shard_map/ppermute | solution.py:591
  88.6 1.5 %collective-permute-start.13 = (f32[640,128]{1,0:T(8,128)S(1)}, f32[640,128]{1,0:T(8,128)S(1)}, u32[]{:S(2)}, u32[]{:S(2)}) collective-permute-start(f32[640,128]{1,0:T(8,128)S(1)} %get-tuple-element.60), channel_id=1, source_target_pairs={{0,16},{1,17},{2,18},{3,19},{4,20},{5,21},{6,22},{7,23},{8,24},{9,... | collective-permute-start | bytes 983048 | tf_op jit(solution)/shard_map/ppermute | solution.py:591
  90.0 11.7 %collective-permute-done.9.c22 = f32[640,128]{1,0:T(8,128)S(1)} collective-permute-done((f32[640,128]{1,0:T(8,128)S(1)}, f32[640,128]{1,0:T(8,128)S(1)}, u32[]{:S(2)}, u32[]{:S(2)}) %collective-permute-start.9) | collective-permute-done | bytes 327712 | tf_op jit(solution)/shard_map/ppermute | solution.py:591
  101.7 0.0 collective-permute-done.8.c21
  101.8 0.0 copy-done.1
  101.8 4.5 %own_rows.1 = (bf16[512,768]{1,0:T(8,128)(2,1)S(1)}, bf16[512,768]{1,0:T(8,128)(2,1)S(1)}, f32[512,512]{1,0:T(8,128)S(1)}) custom-call(s32[2]{0:T(128)S(1)} %pad_add_fusion.place, f32[1,1024,1024]{2,1,0:T(8,128)S(1)} %copy-done.1, bf16[768,768]{1,0:T(8,128)(2,1)S(1)} %get-tuple-element.50.high, bf16[768,768]{1,0:T(8,128)(2,1)S(1)} %get-tuple-element.51.low, ...), custom_call_target="tpu_custom_call" | custom-call | flops 1000 | bytes 1000 | tf_op jit(solution)/shard_map/own_rows/pallas_call | solution.py:186
  106.2 0.0 collective-permute-done.11.c31
  106.2 0.7 collective-permute-done.12.c32.passed
  106.9 3.7 %products.1 = (f32[1,1024,1024]{2,1,0:T(8,128)}, f32[512,512]{1,0:T(8,128)S(1)}) custom-call(s32[2]{0:T(128)S(1)} %pad_add_fusion.place, bf16[768,768]{1,0:T(8,128)(2,1)S(1)} %get-tuple-element.50.high, bf16[768,768]{1,0:T(8,128)(2,1)S(1)} %get-tuple-element.51.low, bf16[512,768]{1,0:T(8,128)(2,1)S(1)} %get-tuple-element.53.top, ...), custom_call_target="tpu_custom_call" | custom-call | flops 1000 | bytes 1000 | tf_op jit(solution)/shard_map/products/pallas_call | solution.py:186
  110.6 0.0 collective-permute-done.13.last
  110.6 5.0 %finish.1 = f32[1,1024,1024]{2,1,0:T(8,128)} custom-call(s32[2]{0:T(128)S(1)} %pad_add_fusion.place, f32[1,1024,1024]{2,1,0:T(8,128)} %get-tuple-element.58.before, bf16[768,768]{1,0:T(8,128)(2,1)S(1)} %get-tuple-element.50.high, bf16[768,768]{1,0:T(8,128)(2,1)S(1)} %get-tuple-element.51.low, ...), custom_call_target="tpu_custom_call", output_to_operand_aliasing={{}: (1, {})} | custom-call | flops 1000 | bytes 1000 | tf_op jit(solution)/shard_map/finish/pallas_call | solution.py:186
  (6 shorter events, 0.0 us)
Async XLA Ops:
  0.1 2.2 %copy-start = (f32[1,1024,1024]{2,1,0:T(8,128)S(1)}, f32[1,1024,1024]{2,1,0:T(8,128)}, u32[]{:S(2)}) copy-start(f32[1,1024,1024]{2,1,0:T(8,128)} %leaf.5) | copy-start | bytes 12582916
  3.1 10.9 %collective-permute-start = (f32[768,128]{1,0:T(8,128)S(1)}, f32[768,128]{1,0:T(8,128)S(1)}, u32[]{:S(2)}, u32[]{:S(2)}) collective-permute-start(f32[768,128]{1,0:T(8,128)S(1)} %get-tuple-element.33.mine), channel_id=1, source_target_pairs={{0,2},{1,3},{2,0},{3,1},{4,6},{5,7},{6,4},{7,5},{8,10},{9,11},{10,... | collective-permute-start | bytes 1179656 | tf_op jit(solution)/shard_map/ppermute | solution.py:591
  4.7 34.4 %collective-permute-start.5 = (f32[896,128]{1,0:T(8,128)S(1)}, f32[896,128]{1,0:T(8,128)S(1)}, u32[]{:S(2)}, u32[]{:S(2)}) collective-permute-start(f32[896,128]{1,0:T(8,128)S(1)} %get-tuple-element.43.a0), channel_id=1, source_target_pairs={{0,16},{1,17},{2,18},{3,19},{4,20},{5,21},{6,22},{7,23},{8,24},{9,... | collective-permute-start | bytes 1376264 | tf_op jit(solution)/shard_map/ppermute | solution.py:591
  6.6 0.7 copy-start.7
  21.3 17.3 %collective-permute-start.1 = (f32[256,256]{1,0:T(8,128)S(1)}, f32[256,256]{1,0:T(8,128)}, u32[]{:S(2)}, u32[]{:S(2)}) collective-permute-start(f32[256,256]{1,0:T(8,128)S(1)} %get-tuple-element.37.b0), channel_id=1, source_target_pairs={{0,16},{1,17},{2,18},{3,19},{4,20},{5,21},{6,22},{7,23},{8,24},{9,... | collective-permute-start | bytes 786440 | tf_op jit(solution)/shard_map/ppermute | solution.py:591
  21.7 17.4 %collective-permute-start.6 = (f32[256,256]{1,0:T(8,128)S(1)}, f32[256,256]{1,0:T(8,128)S(1)}, u32[]{:S(2)}, u32[]{:S(2)}) collective-permute-start(f32[256,256]{1,0:T(8,128)S(1)} %get-tuple-element.37.b0), channel_id=1, source_target_pairs={{0,2},{1,3},{2,0},{3,1},{4,6},{5,7},{6,4},{7,5},{8,10},{9,11},{10,... | collective-permute-start | bytes 786440 | tf_op jit(solution)/shard_map/ppermute | solution.py:591
  23.2 0.7 copy-start.2
  24.0 24.2 %collective-permute-start.3 = (f32[640,128]{1,0:T(8,128)}, f32[640,128]{1,0:T(8,128)S(1)}, u32[]{:S(2)}, u32[]{:S(2)}) collective-permute-start(f32[640,128]{1,0:T(8,128)} %get-tuple-element.42), channel_id=1, source_target_pairs={{0,2},{1,3},{2,0},{3,1},{4,6},{5,7},{6,4},{7,5},{8,10},{9,11},{10,... | collective-permute-start | bytes 983048 | tf_op jit(solution)/shard_map/ppermute | solution.py:591
  38.6 9.5 %collective-permute-start.2 = (f32[256,256]{1,0:T(8,128)}, f32[256,256]{1,0:T(8,128)}, u32[]{:S(2)}, u32[]{:S(2)}) collective-permute-start(f32[256,256]{1,0:T(8,128)} %collective-permute-done.1.b1), channel_id=1, source_target_pairs={{0,2},{1,3},{2,0},{3,1},{4,6},{5,7},{6,4},{7,5},{8,10},{9,11},{10,... | collective-permute-start | bytes 786440 | tf_op jit(solution)/shard_map/ppermute | solution.py:591
  39.1 0.7 copy-start.5
  39.8 17.1 %collective-permute-start.7 = (f32[896,128]{1,0:T(8,128)S(1)}, f32[896,128]{1,0:T(8,128)S(1)}, u32[]{:S(2)}, u32[]{:S(2)}) collective-permute-start(f32[896,128]{1,0:T(8,128)S(1)} %collective-permute-done.5.a1), channel_id=1, source_target_pairs={{0,2},{1,3},{2,0},{3,1},{4,6},{5,7},{6,4},{7,5},{8,10},{9,11},{10,... | collective-permute-start | bytes 1376264 | tf_op jit(solution)/shard_map/ppermute | solution.py:591
  41.4 28.1 %collective-permute-start.4 = (f32[896,128]{1,0:T(8,128)S(1)}, f32[896,128]{1,0:T(8,128)S(1)}, u32[]{:S(2)}, u32[]{:S(2)}) collective-permute-start(f32[896,128]{1,0:T(8,128)S(1)} %get-tuple-element.52.c01), channel_id=1, source_target_pairs={{0,16},{1,17},{2,18},{3,19},{4,20},{5,21},{6,22},{7,23},{8,24},{9,... | collective-permute-start | bytes 1376264 | tf_op jit(solution)/shard_map/ppermute | solution.py:591
  41.4 60.4 %copy-start.1 = (f32[1,1024,1024]{2,1,0:T(8,128)S(1)}, f32[1,1024,1024]{2,1,0:T(8,128)}, u32[]{:S(2)}) copy-start(f32[1,1024,1024]{2,1,0:T(8,128)} %leaf.5) | copy-start | bytes 12582916
  56.9 1.0 copy-start.3
  57.8 0.9 copy-start.6
  69.5 16.3 %collective-permute-start.10 = (f32[640,128]{1,0:T(8,128)S(1)}, f32[640,128]{1,0:T(8,128)S(1)}, u32[]{:S(2)}, u32[]{:S(2)}) collective-permute-start(f32[640,128]{1,0:T(8,128)S(1)} %get-tuple-element.57), channel_id=1, source_target_pairs={{0,16},{1,17},{2,18},{3,19},{4,20},{5,21},{6,22},{7,23},{8,24},{9,... | collective-permute-start | bytes 983048 | tf_op jit(solution)/shard_map/ppermute | solution.py:591
  69.5 32.2 %collective-permute-start.8 = (f32[896,128]{1,0:T(8,128)S(1)}, f32[896,128]{1,0:T(8,128)S(1)}, u32[]{:S(2)}, u32[]{:S(2)}) collective-permute-start(f32[896,128]{1,0:T(8,128)S(1)} %get-tuple-element.52.c01), channel_id=1, source_target_pairs={{0,2},{1,3},{4,6},{5,7},{8,10},{9,11},{12,14},{13,15},{18,16},{19,... | collective-permute-start | bytes 1376264 | tf_op jit(solution)/shard_map/ppermute | solution.py:591
  70.8 35.4 %collective-permute-start.11 = (f32[896,128]{1,0:T(8,128)S(1)}, f32[896,128]{1,0:T(8,128)S(1)}, u32[]{:S(2)}, u32[]{:S(2)}) collective-permute-start(f32[896,128]{1,0:T(8,128)S(1)} %collective-permute-done.4.c11), channel_id=1, source_target_pairs={{0,2},{1,3},{4,6},{5,7},{8,10},{9,11},{12,14},{13,15},{18,16},{19,... | collective-permute-start | bytes 1376264 | tf_op jit(solution)/shard_map/ppermute | solution.py:591
  72.1 29.6 %collective-permute-start.9 = (f32[640,128]{1,0:T(8,128)S(1)}, f32[640,128]{1,0:T(8,128)S(1)}, u32[]{:S(2)}, u32[]{:S(2)}) collective-permute-start(f32[640,128]{1,0:T(8,128)S(1)} %get-tuple-element.40.c02), channel_id=1, source_target_pairs={{0,2},{1,3},{4,6},{5,7},{8,10},{9,11},{12,14},{13,15},{18,16},{19,... | collective-permute-start | bytes 983048 | tf_op jit(solution)/shard_map/ppermute | solution.py:591
  73.4 1.0 copy-start.4
  85.8 21.1 %collective-permute-start.12 = (f32[640,128]{1,0:T(8,128)S(1)}, f32[640,128]{1,0:T(8,128)S(1)}, u32[]{:S(2)}, u32[]{:S(2)}) collective-permute-start(f32[640,128]{1,0:T(8,128)S(1)} %collective-permute-done.10.c12), channel_id=1, source_target_pairs={{0,2},{1,3},{2,0},{3,1},{4,6},{5,7},{6,4},{7,5},{8,10},{9,11},{10,... | collective-permute-start | bytes 983048 | tf_op jit(solution)/shard_map/ppermute | solution.py:591
  88.6 22.0 %collective-permute-start.13 = (f32[640,128]{1,0:T(8,128)S(1)}, f32[640,128]{1,0:T(8,128)S(1)}, u32[]{:S(2)}, u32[]{:S(2)}) collective-permute-start(f32[640,128]{1,0:T(8,128)S(1)} %get-tuple-element.60), channel_id=1, source_target_pairs={{0,16},{1,17},{2,18},{3,19},{4,20},{5,21},{6,22},{7,23},{8,24},{9,... | collective-permute-start | bytes 983048 | tf_op jit(solution)/shard_map/ppermute | solution.py:591

commit v5 on v4

--- a/solution.py
+++ b/solution.py
@@ -11,7 +11,8 @@
 BF16 = jnp.bfloat16
 T = 128
 R = 16
-COST = 1000
+FIRST = 2
+COST = 10**10
 HBM = pl.BlockSpec(memory_space=pl.ANY)
 VMEM = pl.BlockSpec(memory_space=pltpu.VMEM)
 SMEM = pl.BlockSpec(memory_space=pltpu.SMEM)
@@ -174,14 +175,6 @@
     )
 
 
-def unpack_full(ref, at, tiles):
-    rows = []
-    for r in range(tiles):
-        spots = [at + (r * tiles + c) * T for c in range(tiles)]
-        rows.append(jnp.concatenate([ref[x : x + T, :] for x in spots], axis=1))
-    return jnp.concatenate(rows, axis=0)
-
-
 def call(kernel, name, outs, ins, scratch, **more):
     return pl.pallas_call(
         kernel,
@@ -201,17 +194,15 @@
     return leaf_block(leaf, side_r, side_c, at // tiles, at % tiles, T)
 
 
-def cut_first_kernel(place, leaf, a, hs, sem):
+def cut_first_kernel(place, leaf, a, hh, sem):
     tiles = leaf.shape[1] // 4 // T
     ext, inn = sides(place)
     n_sym = len(upper(tiles))
     pairs = []
     for at, (r, c) in enumerate(upper(tiles)):
-        source = leaf_block(leaf, inn[0], inn[0], r, c, T)
-        pairs.append((source, a.at[pl.ds(at * T, T)]))
-        pairs.append((source, hs.at[pl.ds((n_sym + at) * T, T)]))
-        pairs.append((leaf_block(leaf, inn[1], inn[1], r, c, T), hs.at[pl.ds(at * T, T)]))
-    for at in range(tiles * tiles):
+        pairs.append((leaf_block(leaf, inn[0], inn[0], r, c, T), a.at[pl.ds(at * T, T)]))
+        pairs.append((leaf_block(leaf, inn[1], inn[1], r, c, T), hh.at[pl.ds(at * T, T)]))
+    for at in range(FIRST):
         pairs.append(
             (block_tiles(leaf, ext[0], inn[0], at), a.at[pl.ds((n_sym + at) * T, T)])
         )
@@ -219,43 +210,46 @@
 
 
 def cut_first(place, leaf):
-    tiles = leaf.shape[1] // 4 // T
-    n_sym, n_full = len(upper(tiles)), tiles * tiles
+    n_sym = len(upper(leaf.shape[1] // 4 // T))
     return call(
         cut_first_kernel,
         "cut_first",
-        [(((n_sym + n_full) * T, T), F32), ((2 * n_sym * T, T), F32)],
+        [(((n_sym + FIRST) * T, T), F32), ((n_sym * T, T), F32)],
         [(SMEM, place), (HBM, leaf)],
-        [pltpu.SemaphoreType.DMA((3 * n_sym + n_full,))],
-    )
-
-
-def cut_second_kernel(place, leaf, outer0, swap, b, c, sem):
+        [pltpu.SemaphoreType.DMA((2 * n_sym + FIRST,))],
+    )
+
+
+def cut_second_kernel(place, leaf, swap, outer0, b, c, sem):
     e = leaf.shape[1] // 4
     tiles = e // T
     ext, inn = sides(place)
+    n_sym = len(upper(tiles))
     pairs = [
         (leaf_block(leaf, inn[0], inn[1], 0, 0, e), b),
-        (leaf_block(leaf, ext[1], inn[0], 0, 0, e), c.at[pl.ds(0, e)]),
-        (leaf_block(leaf, ext[0], inn[1], 0, 0, e), c.at[pl.ds(e, e)]),
-        (leaf_block(leaf, ext[1], inn[1], 0, 0, e), c.at[pl.ds(2 * e, e)]),
+        (leaf_block(leaf, ext[0], inn[0], 0, 0, e), c.at[pl.ds(0, e)]),
+        (leaf_block(leaf, ext[1], inn[0], 0, 0, e), c.at[pl.ds(e, e)]),
+        (leaf_block(leaf, ext[0], inn[1], 0, 0, e), c.at[pl.ds(2 * e, e)]),
+        (leaf_block(leaf, ext[1], inn[1], 0, 0, e), c.at[pl.ds(3 * e, e)]),
     ]
+    for at, (r, k) in enumerate(upper(tiles)):
+        pairs.append((leaf_block(leaf, inn[0], inn[0], r, k, T), swap.at[pl.ds(at * T, T)]))
     half = outer0.shape[0] // T
     second = []
-    for at, (r, c) in enumerate(upper(2 * tiles)):
-        source = leaf_block(leaf, ext[r // tiles], ext[c // tiles], r % tiles, c % tiles, T)
+    for at, (r, k) in enumerate(upper(2 * tiles)):
+        source = leaf_block(leaf, ext[r // tiles], ext[k // tiles], r % tiles, k % tiles, T)
         if at < half:
             pairs.append((source, outer0.at[pl.ds(at * T, T)]))
         else:
-            second.append((source, swap.at[pl.ds((at - half) * T, T)]))
+            second.append((source, swap.at[pl.ds((n_sym + at - half) * T, T)]))
     run_copies(pairs, sem)
     same = place[0] == place[1]
 
     @pl.when(same)
     def _():
         cross = [
-            (block_tiles(leaf, ext[0], inn[0], at), swap.at[pl.ds(at * T, T)])
-            for at in range(tiles * tiles)
+            (block_tiles(leaf, ext[0], inn[0], at), swap.at[pl.ds((n_sym + at) * T, T)])
+            for at in range(FIRST)
         ]
         run_copies(cross, sem)
 
@@ -266,13 +260,14 @@
 
 def cut_second(place, leaf):
     e = leaf.shape[1] // 4
-    n_outer = len(upper(2 * (e // T)))
+    n_sym = len(upper(e // T))
+    half = len(upper(2 * (e // T))) // 2
     return call(
         cut_second_kernel,
         "cut_second",
-        [((n_outer // 2 * T, T), F32)] * 2 + [((e, e), F32), ((3 * e, e), F32)],
+        [(((n_sym + half) * T, T), F32), ((half * T, T), F32), ((e, e), F32), ((4 * e, e), F32)],
         [(SMEM, place), (HBM, leaf)],
-        [pltpu.SemaphoreType.DMA((n_outer // 2 + 4,))],
+        [pltpu.SemaphoreType.DMA((n_sym + half + 5,))],
     )
 
 
@@ -282,11 +277,12 @@
     held[...] = unpack(mine, 0, tiles) + unpack(along, 0, tiles)
     inverse_factor(held)
     b_out[...] = dot(b[...], held[...], NT)
-    scaled = dot3(split(c[e:, :]), split(held[...]), NT)
-    for at in range(3 * tiles * tiles):
+    scaled = dot3(split(c[2 * e :, :]), split(held[...]), NT)
+    for at in range(FIRST, 4 * tiles * tiles):
         r, k = at // tiles * T, at % tiles * T
-        tile = c[r : r + T, k : k + T] if r < e else scaled[r - e : r - e + T, k : k + T]
-        ref, spot = (c1, at * T) if at * T < c1.shape[0] else (c2, at * T - c1.shape[0])
+        tile = c[r : r + T, k : k + T] if r < 2 * e else scaled[r - 2 * e : r - 2 * e + T, k : k + T]
+        spot = (at - FIRST) * T
+        ref, spot = (c1, spot) if spot < c1.shape[0] else (c2, spot - c1.shape[0])
         ref[spot : spot + T, :] = tile
 
 
@@ -295,7 +291,7 @@
     return call(
         gauge_kernel,
         "gauge_side",
-        [((e, e), F32), ((3 * e * e // T - last, T), F32), ((last, T), F32)],
+        [((e, e), F32), ((4 * e * e // T - FIRST * T - last, T), F32), ((last, T), F32)],
         [(VMEM, x) for x in (mine, along, b, c)],
         [pltpu.VMEM((e, e), F32)],
     )
@@ -308,15 +304,13 @@
     )
 
 
-def factor_start_kernel(a0, a1, hs, a3, b0, b1, b2, b3, side):
+def factor_start_kernel(a0, a1, a2, a3, b0, b1, b2, b3, side):
     e = b0.shape[0]
     tiles = e // T
     coup = couple((b0, b1, b2, b3))
     side[...] = -dot(coup, coup, NT)
     side[:e, :e] = side[:e, :e] + (unpack(a0, 0, tiles) + unpack(a1, 0, tiles))
-    side[e:, e:] = side[e:, e:] + (
-        unpack(hs, len(upper(tiles)) * T, tiles) + unpack(a3, 0, tiles)
-    )
+    side[e:, e:] = side[e:, e:] + (unpack(a2, 0, tiles) + unpack(a3, 0, tiles))
     sweep(side, 0, e)
 
 
@@ -371,18 +365,18 @@
     )
 
 
-def cross_block(first, at, c1, c2):
-    rest = jnp.concatenate([c1[...], c2[...]], axis=0)
-    e = math.isqrt(rest.shape[0] * T // 3)
-    n = e * e // T
-    tiles = e // T
-    return jnp.concatenate(
-        [
-            jnp.concatenate([unpack_full(first, at, tiles), unpack_full(rest, n, tiles)], axis=1),
-            jnp.concatenate([unpack_full(rest, 0, tiles), unpack_full(rest, 2 * n, tiles)], axis=1),
-        ],
-        axis=0,
-    )
+def cross_block(first, c1, c2):
+    n1, n2 = c1.shape[0] // T, c2.shape[0] // T
+    tiles = math.isqrt((FIRST + n1 + n2) // 4)
+    n_sym = len(upper(tiles))
+    held = [first[(n_sym + at) * T : (n_sym + at + 1) * T, :] for at in range(FIRST)]
+    held += [ref[at * T : (at + 1) * T, :] for ref, n in ((c1, n1), (c2, n2)) for at in range(n)]
+    rows = []
+    for r in range(2 * tiles):
+        side = r // tiles
+        row = [held[((side + 2 * c) * tiles + r % tiles) * tiles + k] for c in range(2) for k in range(tiles)]
+        rows.append(jnp.concatenate(row, axis=1))
+    return jnp.concatenate(rows, axis=0)
 
 
 def times_inverse(cross, high, low, inner):
@@ -396,7 +390,6 @@
     place, leaf, high, low, a0, c01, c02, swapped, c21, c22, top, bottom, block, col, own, sem
 ):
     e = leaf.shape[1] // 4
-    n_sym = len(upper(e // T)) * T
     ext, _ = sides(place)
     copies = []
     for r in range(2):
@@ -406,7 +399,7 @@
             copies.append(pltpu.make_async_copy(source, target, sem.at[2 * r + c]))
             copies[-1].start()
     same = place[0] == place[1]
-    mine = cross_block(a0, n_sym, c01, c02)
+    mine = cross_block(a0, c01, c02)
 
     @pl.when(same)
     def _():
@@ -414,7 +407,7 @@
 
     @pl.when(jnp.logical_not(same))
     def _():
-        col[...] = cross_block(swapped, 0, c21, c22)
+        col[...] = cross_block(swapped, c21, c22)
 
     left = split(times_inverse(mine, high[...], low[...], slice(e, 2 * e)))
     top[...], bottom[...] = left
@@ -467,26 +460,25 @@
     place, high, low, top, bottom, block, a0, c01, c02, a1, c11, c12, a3, c31, c32, out, part, scratch
 ):
     e = out.shape[1] // 4
-    n_sym = len(upper(e // T)) * T
     same = place[0] == place[1]
     write(out, place, block[...], 0, 0)
     everything = slice(0, 2 * e)
 
     @pl.when(same)
     def _():
-        across = cross_block(a1, n_sym, c11, c12)
+        across = cross_block(a1, c11, c12)
         right = split(across)
         left = [pick(x, everything, 1) for x in (top, bottom)]
         write(out, place, -dot3(left, right, NT), 0, 1)
         scratch[...] = times_inverse(across, high[...], low[...], slice(2 * e, 3 * e))
         left = split(pick(scratch, everything, 0))
-        write(out, place, -dot3(left, split(cross_block(a0, n_sym, c01, c02)), NT), 1, 0)
+        write(out, place, -dot3(left, split(cross_block(a0, c01, c02)), NT), 1, 0)
         left = split(pick(scratch, everything, 1))
         part[...] = -dot3(left, right, NT)
 
     @pl.when(jnp.logical_not(same))
     def _():
-        right = split(cross_block(a3, n_sym, c31, c32))
+        right = split(cross_block(a3, c31, c32))
         left = [pick(x, everything, 1) for x in (top, bottom)]
         write(out, place, -dot3(left, right, NT), 0, 1)
 
@@ -508,7 +500,6 @@
 ):
     e = out.shape[1] // 4
     tiles = e // T
-    n_sym = len(upper(tiles)) * T
 
     def targets(b):
         return [
@@ -535,12 +526,12 @@
 
     @pl.when(place[0] != place[1])
     def _():
-        across = cross_block(a1, n_sym, c11, last)
+        across = cross_block(a1, c11, last)
         scratch[...] = times_inverse(across, high[...], low[...], slice(2 * e, 3 * e))
         everything = slice(0, 2 * e)
         copies = []
         for b in range(2):
-            col = cross_block(swapped, 0, c21, c22) if b == 0 else cross_block(a3, n_sym, c31, passed)
+            col = cross_block(swapped, c21, c22) if b == 0 else cross_block(a3, c31, passed)
             left = split(pick(scratch, everything, b))
             held[:, 2 * e * b : 2 * e * (b + 1)] = -dot3(left, split(col), NT)
             for i, (source, target) in enumerate(targets(b)):
@@ -596,24 +587,25 @@
         u = lax.axis_index("gy") // (ny // 2)
         place = jnp.stack([v, u]).astype(jnp.int32)
         same = u == v
-        a, hs = cut_first(place, leaf)
+        a, hh = cut_first(place, leaf)
         a_x = send(a, False)
-        hs_y = send(hs, True)
-        outer0, swap, b, c = cut_second(place, leaf)
+        hh_y = send(hh, True)
+        swap, outer0, b, c = cut_second(place, leaf)
         swapped = send(swap, True)
-        b, c1, c2 = gauge(hs, hs_y, b, c, swap.shape[0])
+        b, c1, c2 = gauge(hh, hh_y, b, c, outer0.shape[0])
+        b, a_x, swapped = tie(b, a_x, swapped)
         b_x = send(b, False)
         b_y = send(b, True)
-        a_x, b_y = tie(a_x, b_y)
         a_d = send(a_x, True)
+        a_d, b_x, b_y = tie(a_d, b_x, b_y)
         b_d = send(b_x, True)
         c1, b_x = tie(c1, b_x)
         c1_x = send(c1, False)
         c1, c2, b_d = tie(c1, c2, b_d)
         c1_y = send(c1, True, only=True)
         c2_y = send(c2, True, only=True)
-        side = factor_start((a, a_x, hs_y, a_d), (b, b_x, b_y, b_d))
-        third, c1_x, side = tie(jnp.where(same, swapped, c2), c1_x, side)
+        side = factor_start((a, a_x, swapped, a_d), (b, b_x, b_y, b_d))
+        third, side = tie(jnp.where(same, swapped[-outer0.shape[0] :], c2), side)
         third = send(third, False)
         c1_d = send(c1_x, True, only=True)
         high, low = factor_end(place, side, (b, b_x, b_y, b_d))

time: 117 us -> 109 us (0.932)
  local copies, waits for them, and re-layouts: 7.19 us -> 2.19 us
  starting transfers between devices: 14.6 us -> 12.8 us
  waiting for transfers between devices: 47.8 us -> 49 us
    unnamed x16 -> x4, local copies, waits for them, and re-layouts: 7.19 us -> 2.19 us
    ppermute x14, starting transfers between devices: 14.6 us -> 12.8 us  [send(): return lax.ppermute(value, ('gx', 'gy'), pairs)]
    ppermute x14, waiting for transfers between devices: 47.8 us -> 49 us  [send(): return lax.ppermute(value, ('gx', 'gy'), pairs)]
  transfers between devices with their start and end apart: 14 -> 14, of which waited for: 6 -> 6; matrix products, arithmetic and copies ran while one was open for 1% -> 0% of each run, Pallas kernels for 34% -> 35%
where the time goes in v5:
time: 109 us; the launch traced here: 108 us
  waiting for transfers between devices  49 us (45%)
  Pallas kernels  43.9 us (40%)
  starting transfers between devices  12.8 us (12%)
  local copies, waits for them, and re-layouts  2.19 us (2%)
    ppermute x14, waiting for transfers between devices, send(): return lax.ppermute(value, ('gx', 'gy'), pairs)  49 us
    pallas_call x8, Pallas kernels, call(): pl.pallas_call(kernel, out_shape=[jax.ShapeDtypeStruct(shape, dtype) for...  43.9 us
    ppermute x14, starting transfers between devices, send(): return lax.ppermute(value, ('gx', 'gy'), pairs)  12.8 us
    unnamed x4, local copies, waits for them, and re-layouts  2.19 us
  transfers between devices with their start and end apart: 14, of which 6 were waited for; matrix products, arithmetic and copies ran while one was open for 0% of the time, Pallas kernels for 35%

profile of v5, /device:TPU:24, one launch (start us, length us, event | category | flops | bytes accessed | tf_op | source)
XLA Modules:
  0.0 108.3 jit_solution(1702845682836934877)
XLA Ops:
  0.0 0.1 pad_add_fusion.place
  0.1 0.0 copy-start
  0.1 2.2 %copy-done = f32[1,1024,1024]{2,1,0:T(8,128)S(1)} copy-done((f32[1,1024,1024]{2,1,0:T(8,128)S(1)}, f32[1,1024,1024]{2,1,0:T(8,128)}, u32[]{:S(2)}) %copy-start) | copy-done | bytes 4194328
  2.3 0.7 cut_first.1
  3.0 1.6 %collective-permute-start = (f32[384,128]{1,0:T(8,128)S(1)}, f32[384,128]{1,0:T(8,128)S(1)}, u32[]{:S(2)}, u32[]{:S(2)}) collective-permute-start(f32[384,128]{1,0:T(8,128)S(1)} %get-tuple-element.36.mine), channel_id=1, source_target_pairs={{0,2},{1,3},{2,0},{3,1},{4,6},{5,7},{6,4},{7,5},{8,10},{9,11},{10,... | collective-permute-start | bytes 589832 | tf_op jit(solution)/shard_map/ppermute | solution.py:582
  4.6 0.3 collective-permute-start.1
  4.9 0.9 cut_second.1
  5.9 0.5 collective-permute-start.2
  6.4 4.4 %collective-permute-done.along = f32[384,128]{1,0:T(8,128)S(1)} collective-permute-done((f32[384,128]{1,0:T(8,128)S(1)}, f32[384,128]{1,0:T(8,128)S(1)}, u32[]{:S(2)}, u32[]{:S(2)}) %collective-permute-start) | collective-permute-done | bytes 196640 | tf_op jit(solution)/shard_map/ppermute | solution.py:582
  10.8 7.3 %gauge_side.1 = (f32[256,256]{1,0:T(8,128)S(1)}, f32[1152,128]{1,0:T(8,128)S(1)}, f32[640,128]{1,0:T(8,128)S(1)}) custom-call(f32[384,128]{1,0:T(8,128)S(1)} %get-tuple-element.36.mine, f32[384,128]{1,0:T(8,128)S(1)} %collective-permute-done.along, f32[256,256]{1,0:T(8,128)S(1)} %get-tuple-element.37.b, f32[1024,256]{1,0:T(8,128)S(1)} %get-tuple-element.38.c), custom_call_target="tpu_custom_call" | custom-call | flops 10000000000 | bytes 10000000000 | tf_op jit(solution)/shard_map/gauge_side/pallas_call | solution.py:179
  18.1 3.4 %collective-permute-done.1.a1 = f32[640,128]{1,0:T(8,128)S(1)} collective-permute-done((f32[640,128]{1,0:T(8,128)S(1)}, f32[640,128]{1,0:T(8,128)S(1)}, u32[]{:S(2)}, u32[]{:S(2)}) %collective-permute-start.1) | collective-permute-done | bytes 327712 | tf_op jit(solution)/shard_map/ppermute | solution.py:582
  21.6 0.0 collective-permute-done.2.a2.swapped
  21.6 0.9 collective-permute-start.3
  22.5 1.1 %collective-permute-start.5 = (f32[256,256]{1,0:T(8,128)S(1)}, f32[256,256]{1,0:T(8,128)S(1)}, u32[]{:S(2)}, u32[]{:S(2)}) collective-permute-start(f32[256,256]{1,0:T(8,128)S(1)} %get-tuple-element.44.b0), channel_id=1, source_target_pairs={{0,2},{1,3},{2,0},{3,1},{4,6},{5,7},{6,4},{7,5},{8,10},{9,11},{10,... | collective-permute-start | bytes 786440 | tf_op jit(solution)/shard_map/ppermute | solution.py:582
  23.6 0.0 collective-permute-start.4
  23.6 13.2 %collective-permute-done.5.b2 = f32[256,256]{1,0:T(8,128)S(1)} collective-permute-done((f32[256,256]{1,0:T(8,128)S(1)}, f32[256,256]{1,0:T(8,128)S(1)}, u32[]{:S(2)}, u32[]{:S(2)}) %collective-permute-start.5) | collective-permute-done | bytes 262176 | tf_op jit(solution)/shard_map/ppermute | solution.py:582
  36.8 0.0 collective-permute-done.4.b1
  36.8 0.0 collective-permute-done.3.a3
  36.8 0.7 collective-permute-start.6
  37.5 0.0 collective-permute-start.9
  37.5 6.8 %collective-permute-done.6.b3 = f32[256,256]{1,0:T(8,128)} collective-permute-done((f32[256,256]{1,0:T(8,128)S(1)}, f32[256,256]{1,0:T(8,128)}, u32[]{:S(2)}, u32[]{:S(2)}) %collective-permute-start.6) | collective-permute-done | bytes 262176 | tf_op jit(solution)/shard_map/ppermute | solution.py:582
  44.3 1.3 %collective-permute-start.8 = (f32[640,128]{1,0:T(8,128)S(1)}, f32[640,128]{1,0:T(8,128)S(1)}, u32[]{:S(2)}, u32[]{:S(2)}) collective-permute-start(f32[640,128]{1,0:T(8,128)S(1)} %get-tuple-element.48.c02), channel_id=1, source_target_pairs={{0,2},{1,3},{4,6},{5,7},{8,10},{9,11},{12,14},{13,15},{18,16},{19,... | collective-permute-start | bytes 983048 | tf_op jit(solution)/shard_map/ppermute | solution.py:582
  45.6 1.5 %collective-permute-start.7 = (f32[1152,128]{1,0:T(8,128)S(1)}, f32[1152,128]{1,0:T(8,128)S(1)}, u32[]{:S(2)}, u32[]{:S(2)}) collective-permute-start(f32[1152,128]{1,0:T(8,128)S(1)} %get-tuple-element.59.c01), channel_id=1, source_target_pairs={{0,2},{1,3},{4,6},{5,7},{8,10},{9,11},{12,14},{13,15},{18,16},{19,... | collective-permute-start | bytes 1769480 | tf_op jit(solution)/shard_map/ppermute | solution.py:582
  47.1 0.1 slice_select_fusion
  47.2 10.4 %factor_start.1.side_in = f32[512,512]{1,0:T(8,128)S(1)} custom-call(f32[640,128]{1,0:T(8,128)S(1)} %get-tuple-element.41.a0, f32[640,128]{1,0:T(8,128)S(1)} %collective-permute-done.1.a1, f32[1024,128]{1,0:T(8,128)S(1)} %collective-permute-done.2.a2.swapped, f32[640,128]{1,0:T(8,128)S(1)} %collective-permute-done.3.a3, ...), custom_call_target="tpu_custom_call" | custom-call | flops 10000000000 | bytes 10000000000 | tf_op jit(solution)/shard_map/factor_start/pallas_call | solution.py:179
  57.6 0.0 copy-start.1
  57.6 1.8 %collective-permute-start.10 = (f32[640,128]{1,0:T(8,128)S(1)}, f32[640,128]{1,0:T(8,128)S(1)}, u32[]{:S(2)}, u32[]{:S(2)}) collective-permute-start(f32[640,128]{1,0:T(8,128)S(1)} %get-tuple-element.63), channel_id=1, source_target_pairs={{0,16},{1,17},{2,18},{3,19},{4,20},{5,21},{6,22},{7,23},{8,24},{9,... | collective-permute-start | bytes 983048 | tf_op jit(solution)/shard_map/ppermute | solution.py:582
  59.4 11.3 %factor_end.1 = (bf16[768,768]{1,0:T(8,128)(2,1)S(1)}, bf16[768,768]{1,0:T(8,128)(2,1)S(1)}) custom-call(s32[2]{0:T(128)S(1)} %pad_add_fusion.place, f32[512,512]{1,0:T(8,128)S(1)} %factor_start.1.side_in, f32[256,256]{1,0:T(8,128)S(1)} %get-tuple-element.44.b0, f32[256,256]{1,0:T(8,128)S(1)} %collective-permute-done.4.b1, ...), custom_call_target="tpu_custom_call" | custom-call | flops 10000000000 | bytes 10000000000 | tf_op jit(solution)/shard_map/factor_end/pallas_call | solution.py:179
  70.7 1.3 %collective-permute-start.13 = (f32[640,128]{1,0:T(8,128)S(1)}, f32[640,128]{1,0:T(8,128)S(1)}, u32[]{:S(2)}, u32[]{:S(2)}) collective-permute-start(f32[640,128]{1,0:T(8,128)S(1)} %get-tuple-element.66), channel_id=1, source_target_pairs={{0,16},{1,17},{2,18},{3,19},{4,20},{5,21},{6,22},{7,23},{8,24},{9,... | collective-permute-start | bytes 983048 | tf_op jit(solution)/shard_map/ppermute | solution.py:582
  71.9 0.0 collective-permute-done.9.c11
  72.0 1.3 %collective-permute-start.11 = (f32[1152,128]{1,0:T(8,128)S(1)}, f32[1152,128]{1,0:T(8,128)S(1)}, u32[]{:S(2)}, u32[]{:S(2)}) collective-permute-start(f32[1152,128]{1,0:T(8,128)S(1)} %collective-permute-done.9.c11), channel_id=1, source_target_pairs={{0,2},{1,3},{4,6},{5,7},{8,10},{9,11},{12,14},{13,15},{18,16},{19,... | collective-permute-start | bytes 1769480 | tf_op jit(solution)/shard_map/ppermute | solution.py:582
  73.2 11.0 %collective-permute-done.10.c12 = f32[640,128]{1,0:T(8,128)S(1)} collective-permute-done((f32[640,128]{1,0:T(8,128)S(1)}, f32[640,128]{1,0:T(8,128)S(1)}, u32[]{:S(2)}, u32[]{:S(2)}) %collective-permute-start.10) | collective-permute-done | bytes 327712 | tf_op jit(solution)/shard_map/ppermute | solution.py:582
  84.2 0.5 collective-permute-start.12
  84.7 0.0 collective-permute-done.8.c22
  84.8 0.0 collective-permute-done.7.c21
  84.8 0.0 copy-done.1
  84.8 4.5 %own_rows.1 = (bf16[512,768]{1,0:T(8,128)(2,1)S(1)}, bf16[512,768]{1,0:T(8,128)(2,1)S(1)}, f32[512,512]{1,0:T(8,128)S(1)}) custom-call(s32[2]{0:T(128)S(1)} %pad_add_fusion.place, f32[1,1024,1024]{2,1,0:T(8,128)S(1)} %copy-done.1, bf16[768,768]{1,0:T(8,128)(2,1)S(1)} %get-tuple-element.57.high, bf16[768,768]{1,0:T(8,128)(2,1)S(1)} %get-tuple-element.58.low, ...), custom_call_target="tpu_custom_call" | custom-call | flops 10000000000 | bytes 10000000000 | tf_op jit(solution)/shard_map/own_rows/pallas_call | solution.py:179
  89.3 10.1 %collective-permute-done.12.c32.passed = f32[640,128]{1,0:T(8,128)S(1)} collective-permute-done((f32[640,128]{1,0:T(8,128)S(1)}, f32[640,128]{1,0:T(8,128)S(1)}, u32[]{:S(2)}, u32[]{:S(2)}) %collective-permute-start.12) | collective-permute-done | bytes 327712 | tf_op jit(solution)/shard_map/ppermute | solution.py:582
  99.4 0.0 collective-permute-done.11.c31
  99.4 3.7 %products.1 = (f32[1,1024,1024]{2,1,0:T(8,128)}, f32[512,512]{1,0:T(8,128)S(1)}) custom-call(s32[2]{0:T(128)S(1)} %pad_add_fusion.place, bf16[768,768]{1,0:T(8,128)(2,1)S(1)} %get-tuple-element.57.high, bf16[768,768]{1,0:T(8,128)(2,1)S(1)} %get-tuple-element.58.low, bf16[512,768]{1,0:T(8,128)(2,1)S(1)} %get-tuple-element.60.top, ...), custom_call_target="tpu_custom_call" | custom-call | flops 10000000000 | bytes 10000000000 | tf_op jit(solution)/shard_map/products/pallas_call | solution.py:179
  103.1 0.0 collective-permute-done.13.last
  103.1 5.0 %finish.1 = f32[1,1024,1024]{2,1,0:T(8,128)} custom-call(s32[2]{0:T(128)S(1)} %pad_add_fusion.place, f32[1,1024,1024]{2,1,0:T(8,128)} %get-tuple-element.64.before, bf16[768,768]{1,0:T(8,128)(2,1)S(1)} %get-tuple-element.57.high, bf16[768,768]{1,0:T(8,128)(2,1)S(1)} %get-tuple-element.58.low, ...), custom_call_target="tpu_custom_call", output_to_operand_aliasing={{}: (1, {})} | custom-call | flops 10000000000 | bytes 10000000000 | tf_op jit(solution)/shard_map/finish/pallas_call | solution.py:179
Async XLA Ops:
  0.1 2.2 %copy-start = (f32[1,1024,1024]{2,1,0:T(8,128)S(1)}, f32[1,1024,1024]{2,1,0:T(8,128)}, u32[]{:S(2)}) copy-start(f32[1,1024,1024]{2,1,0:T(8,128)} %leaf.5) | copy-start | bytes 12582916
  3.0 7.9 %collective-permute-start = (f32[384,128]{1,0:T(8,128)S(1)}, f32[384,128]{1,0:T(8,128)S(1)}, u32[]{:S(2)}, u32[]{:S(2)}) collective-permute-start(f32[384,128]{1,0:T(8,128)S(1)} %get-tuple-element.36.mine), channel_id=1, source_target_pairs={{0,2},{1,3},{2,0},{3,1},{4,6},{5,7},{6,4},{7,5},{8,10},{9,11},{10,... | collective-permute-start | bytes 589832 | tf_op jit(solution)/shard_map/ppermute | solution.py:582
  4.6 17.0 %collective-permute-start.1 = (f32[640,128]{1,0:T(8,128)S(1)}, f32[640,128]{1,0:T(8,128)S(1)}, u32[]{:S(2)}, u32[]{:S(2)}) collective-permute-start(f32[640,128]{1,0:T(8,128)S(1)} %get-tuple-element.41.a0), channel_id=1, source_target_pairs={{0,16},{1,17},{2,18},{3,19},{4,20},{5,21},{6,22},{7,23},{8,24},{9,... | collective-permute-start | bytes 983048 | tf_op jit(solution)/shard_map/ppermute | solution.py:582
  5.9 15.7 %collective-permute-start.2 = (f32[1024,128]{1,0:T(8,128)S(1)}, f32[1024,128]{1,0:T(8,128)S(1)}, u32[]{:S(2)}, u32[]{:S(2)}) collective-permute-start(f32[1024,128]{1,0:T(8,128)S(1)} %get-tuple-element.42), channel_id=1, source_target_pairs={{0,2},{1,3},{2,0},{3,1},{4,6},{5,7},{6,4},{7,5},{8,10},{9,11},{10,... | collective-permute-start | bytes 1572872 | tf_op jit(solution)/shard_map/ppermute | solution.py:582
  21.6 15.3 %collective-permute-start.3 = (f32[640,128]{1,0:T(8,128)S(1)}, f32[640,128]{1,0:T(8,128)S(1)}, u32[]{:S(2)}, u32[]{:S(2)}) collective-permute-start(f32[640,128]{1,0:T(8,128)S(1)} %collective-permute-done.1.a1), channel_id=1, source_target_pairs={{0,2},{1,3},{2,0},{3,1},{4,6},{5,7},{6,4},{7,5},{8,10},{9,11},{10,... | collective-permute-start | bytes 983048 | tf_op jit(solution)/shard_map/ppermute | solution.py:582
  22.5 14.4 %collective-permute-start.5 = (f32[256,256]{1,0:T(8,128)S(1)}, f32[256,256]{1,0:T(8,128)S(1)}, u32[]{:S(2)}, u32[]{:S(2)}) collective-permute-start(f32[256,256]{1,0:T(8,128)S(1)} %get-tuple-element.44.b0), channel_id=1, source_target_pairs={{0,2},{1,3},{2,0},{3,1},{4,6},{5,7},{6,4},{7,5},{8,10},{9,11},{10,... | collective-permute-start | bytes 786440 | tf_op jit(solution)/shard_map/ppermute | solution.py:582
  23.6 13.2 %collective-permute-start.4 = (f32[256,256]{1,0:T(8,128)S(1)}, f32[256,256]{1,0:T(8,128)S(1)}, u32[]{:S(2)}, u32[]{:S(2)}) collective-permute-start(f32[256,256]{1,0:T(8,128)S(1)} %get-tuple-element.44.b0), channel_id=1, source_target_pairs={{0,16},{1,17},{2,18},{3,19},{4,20},{5,21},{6,22},{7,23},{8,24},{9,... | collective-permute-start | bytes 786440 | tf_op jit(solution)/shard_map/ppermute | solution.py:582
  36.8 7.5 %collective-permute-start.6 = (f32[256,256]{1,0:T(8,128)S(1)}, f32[256,256]{1,0:T(8,128)}, u32[]{:S(2)}, u32[]{:S(2)}) collective-permute-start(f32[256,256]{1,0:T(8,128)S(1)} %collective-permute-done.4.b1), channel_id=1, source_target_pairs={{0,2},{1,3},{2,0},{3,1},{4,6},{5,7},{6,4},{7,5},{8,10},{9,11},{10,... | collective-permute-start | bytes 786440 | tf_op jit(solution)/shard_map/ppermute | solution.py:582
  37.5 34.4 %collective-permute-start.9 = (f32[1152,128]{1,0:T(8,128)S(1)}, f32[1152,128]{1,0:T(8,128)S(1)}, u32[]{:S(2)}, u32[]{:S(2)}) collective-permute-start(f32[1152,128]{1,0:T(8,128)S(1)} %get-tuple-element.59.c01), channel_id=1, source_target_pairs={{0,16},{1,17},{2,18},{3,19},{4,20},{5,21},{6,22},{7,23},{8,24},{9,... | collective-permute-start | bytes 1769480 | tf_op jit(solution)/shard_map/ppermute | solution.py:582
  44.3 40.4 %collective-permute-start.8 = (f32[640,128]{1,0:T(8,128)S(1)}, f32[640,128]{1,0:T(8,128)S(1)}, u32[]{:S(2)}, u32[]{:S(2)}) collective-permute-start(f32[640,128]{1,0:T(8,128)S(1)} %get-tuple-element.48.c02), channel_id=1, source_target_pairs={{0,2},{1,3},{4,6},{5,7},{8,10},{9,11},{12,14},{13,15},{18,16},{19,... | collective-permute-start | bytes 983048 | tf_op jit(solution)/shard_map/ppermute | solution.py:582
  45.6 39.1 %collective-permute-start.7 = (f32[1152,128]{1,0:T(8,128)S(1)}, f32[1152,128]{1,0:T(8,128)S(1)}, u32[]{:S(2)}, u32[]{:S(2)}) collective-permute-start(f32[1152,128]{1,0:T(8,128)S(1)} %get-tuple-element.59.c01), channel_id=1, source_target_pairs={{0,2},{1,3},{4,6},{5,7},{8,10},{9,11},{12,14},{13,15},{18,16},{19,... | collective-permute-start | bytes 1769480 | tf_op jit(solution)/shard_map/ppermute | solution.py:582
  57.6 27.2 %copy-start.1 = (f32[1,1024,1024]{2,1,0:T(8,128)S(1)}, f32[1,1024,1024]{2,1,0:T(8,128)}, u32[]{:S(2)}) copy-start(f32[1,1024,1024]{2,1,0:T(8,128)} %leaf.5) | copy-start | bytes 12582916
  57.6 26.7 %collective-permute-start.10 = (f32[640,128]{1,0:T(8,128)S(1)}, f32[640,128]{1,0:T(8,128)S(1)}, u32[]{:S(2)}, u32[]{:S(2)}) collective-permute-start(f32[640,128]{1,0:T(8,128)S(1)} %get-tuple-element.63), channel_id=1, source_target_pairs={{0,16},{1,17},{2,18},{3,19},{4,20},{5,21},{6,22},{7,23},{8,24},{9,... | collective-permute-start | bytes 983048 | tf_op jit(solution)/shard_map/ppermute | solution.py:582
  70.7 32.5 %collective-permute-start.13 = (f32[640,128]{1,0:T(8,128)S(1)}, f32[640,128]{1,0:T(8,128)S(1)}, u32[]{:S(2)}, u32[]{:S(2)}) collective-permute-start(f32[640,128]{1,0:T(8,128)S(1)} %get-tuple-element.66), channel_id=1, source_target_pairs={{0,16},{1,17},{2,18},{3,19},{4,20},{5,21},{6,22},{7,23},{8,24},{9,... | collective-permute-start | bytes 983048 | tf_op jit(solution)/shard_map/ppermute | solution.py:582
  72.0 27.5 %collective-permute-start.11 = (f32[1152,128]{1,0:T(8,128)S(1)}, f32[1152,128]{1,0:T(8,128)S(1)}, u32[]{:S(2)}, u32[]{:S(2)}) collective-permute-start(f32[1152,128]{1,0:T(8,128)S(1)} %collective-permute-done.9.c11), channel_id=1, source_target_pairs={{0,2},{1,3},{4,6},{5,7},{8,10},{9,11},{12,14},{13,15},{18,16},{19,... | collective-permute-start | bytes 1769480 | tf_op jit(solution)/shard_map/ppermute | solution.py:582
  84.2 15.2 %collective-permute-start.12 = (f32[640,128]{1,0:T(8,128)S(1)}, f32[640,128]{1,0:T(8,128)S(1)}, u32[]{:S(2)}, u32[]{:S(2)}) collective-permute-start(f32[640,128]{1,0:T(8,128)S(1)} %collective-permute-done.10.c12), channel_id=1, source_target_pairs={{0,2},{1,3},{2,0},{3,1},{4,6},{5,7},{6,4},{7,5},{8,10},{9,11},{10,... | collective-permute-start | bytes 983048 | tf_op jit(solution)/shard_map/ppermute | solution.py:582

commit v6 on v5

--- a/solution.py
+++ b/solution.py
@@ -11,9 +11,9 @@
 BF16 = jnp.bfloat16
 T = 128
 R = 16
-FIRST = 2
-COST = 10**10
+FIRST = 1
 HBM = pl.BlockSpec(memory_space=pl.ANY)
+FAR = pl.BlockSpec(memory_space=pltpu.HBM)
 VMEM = pl.BlockSpec(memory_space=pltpu.VMEM)
 SMEM = pl.BlockSpec(memory_space=pltpu.SMEM)
 PARAMS = pltpu.CompilerParams(vmem_limit_bytes=32 * 2**20)
@@ -175,7 +175,7 @@
     )
 
 
-def call(kernel, name, outs, ins, scratch, **more):
+def call(kernel, name, cost, outs, ins, scratch, **more):
     return pl.pallas_call(
         kernel,
         out_shape=[jax.ShapeDtypeStruct(shape, dtype) for shape, dtype in outs],
@@ -183,7 +183,7 @@
         out_specs=more.pop("out_specs", [VMEM] * len(outs)),
         scratch_shapes=scratch,
         compiler_params=PARAMS,
-        cost_estimate=pl.CostEstimate(flops=COST, bytes_accessed=COST, transcendentals=0),
+        cost_estimate=pl.CostEstimate(flops=cost, bytes_accessed=cost, transcendentals=0),
         name=name,
         **more,
     )(*[value for _, value in ins])
@@ -194,14 +194,13 @@
     return leaf_block(leaf, side_r, side_c, at // tiles, at % tiles, T)
 
 
-def cut_first_kernel(place, leaf, a, hh, sem):
+def cut_first_kernel(place, leaf, a, sem):
     tiles = leaf.shape[1] // 4 // T
     ext, inn = sides(place)
     n_sym = len(upper(tiles))
     pairs = []
     for at, (r, c) in enumerate(upper(tiles)):
         pairs.append((leaf_block(leaf, inn[0], inn[0], r, c, T), a.at[pl.ds(at * T, T)]))
-        pairs.append((leaf_block(leaf, inn[1], inn[1], r, c, T), hh.at[pl.ds(at * T, T)]))
     for at in range(FIRST):
         pairs.append(
             (block_tiles(leaf, ext[0], inn[0], at), a.at[pl.ds((n_sym + at) * T, T)])
@@ -214,10 +213,32 @@
     return call(
         cut_first_kernel,
         "cut_first",
-        [(((n_sym + FIRST) * T, T), F32), ((n_sym * T, T), F32)],
-        [(SMEM, place), (HBM, leaf)],
-        [pltpu.SemaphoreType.DMA((2 * n_sym + FIRST,))],
-    )
+        1000 * 10**6,
+        [(((n_sym + FIRST) * T, T), F32)],
+        [(SMEM, place), (FAR, leaf)],
+        [pltpu.SemaphoreType.DMA((n_sym + FIRST,))],
+    )[0]
+
+
+def cut_side_kernel(place, leaf, hh, sem):
+    tiles = leaf.shape[1] // 4 // T
+    _, inn = sides(place)
+    pairs = []
+    for at, (r, c) in enumerate(upper(tiles)):
+        pairs.append((leaf_block(leaf, inn[1], inn[1], r, c, T), hh.at[pl.ds(at * T, T)]))
+    run_copies(pairs, sem)
+
+
+def cut_side(place, leaf):
+    n_sym = len(upper(leaf.shape[1] // 4 // T))
+    return call(
+        cut_side_kernel,
+        "cut_side",
+        1000 * 10**6,
+        [((n_sym * T, T), F32)],
+        [(SMEM, place), (FAR, leaf)],
+        [pltpu.SemaphoreType.DMA((n_sym,))],
+    )[0]
 
 
 def cut_second_kernel(place, leaf, swap, outer0, b, c, sem):
@@ -265,19 +286,37 @@
     return call(
         cut_second_kernel,
         "cut_second",
+        1000 * 10**6,
         [(((n_sym + half) * T, T), F32), ((half * T, T), F32), ((e, e), F32), ((4 * e, e), F32)],
         [(SMEM, place), (HBM, leaf)],
         [pltpu.SemaphoreType.DMA((n_sym + half + 5,))],
     )
 
 
-def gauge_kernel(mine, along, b, c, b_out, c1, c2, held):
-    e = held.shape[0]
+def gauge_kernel(mine, along, b, b_out, factor):
+    e = factor.shape[0]
     tiles = e // T
-    held[...] = unpack(mine, 0, tiles) + unpack(along, 0, tiles)
-    inverse_factor(held)
-    b_out[...] = dot(b[...], held[...], NT)
-    scaled = dot3(split(c[2 * e :, :]), split(held[...]), NT)
+    factor[...] = unpack(mine, 0, tiles) + unpack(along, 0, tiles)
+    inverse_factor(factor)
+    b_out[...] = dot(b[...], factor[...], NT)
+
+
+def gauge(mine, along, b):
+    e = b.shape[0]
+    return call(
+        gauge_kernel,
+        "gauge_side",
+        8000 * 10**6,
+        [((e, e), F32), ((e, e), F32)],
+        [(VMEM, x) for x in (mine, along, b)],
+        [],
+    )
+
+
+def scale_kernel(factor, c, c1, c2):
+    e = factor.shape[0]
+    tiles = e // T
+    scaled = dot3(split(c[2 * e :, :]), split(factor[...]), NT)
     for at in range(FIRST, 4 * tiles * tiles):
         r, k = at // tiles * T, at % tiles * T
         tile = c[r : r + T, k : k + T] if r < 2 * e else scaled[r - 2 * e : r - 2 * e + T, k : k + T]
@@ -286,14 +325,15 @@
         ref[spot : spot + T, :] = tile
 
 
-def gauge(mine, along, b, c, last):
-    e = b.shape[0]
-    return call(
-        gauge_kernel,
-        "gauge_side",
-        [((e, e), F32), ((4 * e * e // T - FIRST * T - last, T), F32), ((last, T), F32)],
-        [(VMEM, x) for x in (mine, along, b, c)],
-        [pltpu.VMEM((e, e), F32)],
+def scale_cross(factor, c, last):
+    e = factor.shape[0]
+    return call(
+        scale_kernel,
+        "scale_cross",
+        2000 * 10**6,
+        [((4 * e * e // T - FIRST * T - last, T), F32), ((last, T), F32)],
+        [(VMEM, x) for x in (factor, c)],
+        [],
     )
 
 
@@ -319,6 +359,7 @@
     return call(
         factor_start_kernel,
         "factor_start",
+        10000 * 10**6,
         [((2 * e, 2 * e), F32)],
         [(VMEM, x) for x in (*a, *b)],
         [],
@@ -359,6 +400,7 @@
     return call(
         factor_end_kernel,
         "factor_end",
+        10000 * 10**6,
         [((3 * e, 3 * e), BF16)] * 2,
         [(SMEM, place), (VMEM, side)] + [(VMEM, x) for x in b],
         [pltpu.VMEM((2 * e, 2 * e), F32), pltpu.VMEM((2 * e, 2 * e), F32)],
@@ -426,6 +468,7 @@
     return call(
         rows_kernel,
         "own_rows",
+        500 * 10**6,
         [((2 * e, 3 * e), BF16)] * 2 + [((2 * e, 2 * e), F32)],
         [(SMEM, place), (HBM, leaf)]
         + [(VMEM, x) for x in (high, low, a0, c01, c02, swapped, c21, c22)],
@@ -474,13 +517,15 @@
         left = split(pick(scratch, everything, 0))
         write(out, place, -dot3(left, split(cross_block(a0, c01, c02)), NT), 1, 0)
         left = split(pick(scratch, everything, 1))
-        part[...] = -dot3(left, right, NT)
+        part[:, : 2 * e] = -dot3(left, right, NT)
 
     @pl.when(jnp.logical_not(same))
     def _():
         right = split(cross_block(a3, c31, c32))
         left = [pick(x, everything, 1) for x in (top, bottom)]
         write(out, place, -dot3(left, right, NT), 0, 1)
+        across = cross_block(a1, c11, jnp.zeros_like(c12))
+        part[...] = times_inverse(across, high[...], low[...], slice(2 * e, 3 * e))
 
 
 def products(place, high, low, top, bottom, block, mine, across, corner):
@@ -488,7 +533,8 @@
     return call(
         products_kernel,
         "products",
-        [((1, 4 * e, 4 * e), F32), ((2 * e, 2 * e), F32)],
+        500 * 10**6,
+        [((1, 4 * e, 4 * e), F32), ((2 * e, 3 * e), F32)],
         [(SMEM, place)]
         + [(VMEM, x) for x in (high, low, top, bottom, block, *mine, *across, *corner)],
         [pltpu.VMEM((2 * e, 3 * e), F32)],
@@ -496,10 +542,11 @@
 
 
 def finish_kernel(
-    place, before, high, low, part, passed, last, a1, c11, swapped, c21, c22, a3, c31, out, held, scratch, sem
+    place, before, high, low, part, passed, last, c11, swapped, c21, c22, a3, c31, out, held, scratch, sem
 ):
     e = out.shape[1] // 4
     tiles = e // T
+    n_sym = len(upper(tiles))
 
     def targets(b):
         return [
@@ -526,8 +573,12 @@
 
     @pl.when(place[0] != place[1])
     def _():
-        across = cross_block(a1, c11, last)
-        scratch[...] = times_inverse(across, high[...], low[...], slice(2 * e, 3 * e))
+        nothing = jnp.zeros(((n_sym + FIRST) * T, T), F32)
+        late = cross_block(nothing, jnp.zeros_like(c11), last)[:, e:]
+        inner = slice(2 * e, 3 * e)
+        start = (2 * tiles * tiles - last.shape[0] // T) // tiles * T
+        scratch[:start, :] = part[:start, :]
+        scratch[start:, :] = part[start:, :] + dot3(split(late[start:]), (high[inner], low[inner]))
         everything = slice(0, 2 * e)
         copies = []
         for b in range(2):
@@ -541,16 +592,17 @@
             copy.wait()
 
 
-def finish(place, before, high, low, part, passed, last, a1, c11, swapped, c21, c22, a3, c31):
+def finish(place, before, high, low, part, passed, last, c11, swapped, c21, c22, a3, c31):
     e = before.shape[1] // 4
     return call(
         finish_kernel,
         "finish",
+        500 * 10**6,
         [(before.shape, F32)],
         [(SMEM, place), (HBM, before)]
         + [
             (VMEM, x)
-            for x in (high, low, part, passed, last, a1, c11, swapped, c21, c22, a3, c31)
+            for x in (high, low, part, passed, last, c11, swapped, c21, c22, a3, c31)
         ],
         [
             pltpu.VMEM((2 * e, 4 * e), F32),
@@ -587,14 +639,17 @@
         u = lax.axis_index("gy") // (ny // 2)
         place = jnp.stack([v, u]).astype(jnp.int32)
         same = u == v
-        a, hh = cut_first(place, leaf)
+        a = cut_first(place, leaf)
         a_x = send(a, False)
+        here, a = tie(place, a)
+        hh = cut_side(here, leaf)
         hh_y = send(hh, True)
         swap, outer0, b, c = cut_second(place, leaf)
         swapped = send(swap, True)
-        b, c1, c2 = gauge(hh, hh_y, b, c, outer0.shape[0])
-        b, a_x, swapped = tie(b, a_x, swapped)
+        b, factor = gauge(hh, hh_y, b)
         b_x = send(b, False)
+        c1, c2 = scale_cross(factor, c, outer0.shape[0])
+        b, a_x, c1, swapped = tie(b, a_x, c1, swapped)
         b_y = send(b, True)
         a_d = send(a_x, True)
         a_d, b_x, b_y = tie(a_d, b_x, b_y)
@@ -607,17 +662,18 @@
         side = factor_start((a, a_x, swapped, a_d), (b, b_x, b_y, b_d))
         third, side = tie(jnp.where(same, swapped[-outer0.shape[0] :], c2), side)
         third = send(third, False)
+        high, low = factor_end(place, side, (b, b_x, b_y, b_d))
+        c1_x, high = tie(c1_x, high)
         c1_d = send(c1_x, True, only=True)
-        high, low = factor_end(place, side, (b, b_x, b_y, b_d))
-        last, high = tie(jnp.where(same, c2, outer0), high)
+        top, bottom, block = own_rows(place, leaf, high, low, a, c1, c2, swapped, c1_y, c2_y)
+        last, third, block = tie(jnp.where(same, c2, outer0), third, block)
         last = send(last, False)
         passed = send(third, True)
-        top, bottom, block = own_rows(place, leaf, high, low, a, c1, c2, swapped, c1_y, c2_y)
         out, part = products(
             place, high, low, top, bottom, block, (a, c1, c2), (a_x, c1_x, third), (a_d, c1_d, passed)
         )
         return finish(
-            place, out, high, low, part, passed, last, a_x, c1_x, swapped, c1_y, c2_y, a_d, c1_d
+            place, out, high, low, part, passed, last, c1_x, swapped, c1_y, c2_y, a_d, c1_d
         )
 
     return jax.shard_map(

time: 109 us -> 107 us (0.982)
  waiting for transfers between devices: 49 us -> 44.3 us
  starting transfers between devices: 12.8 us -> 14.9 us
  Pallas kernels: 43.9 us -> 45.4 us
    ppermute x14, waiting for transfers between devices: 49 us -> 44.3 us  [send(): return lax.ppermute(value, ('gx', 'gy'), pairs)]
    ppermute x14, starting transfers between devices: 12.8 us -> 14.9 us  [send(): return lax.ppermute(value, ('gx', 'gy'), pairs)]
    pallas_call x8 -> x10, Pallas kernels: 43.9 us -> 45.4 us  [call(): pl.pallas_call(kernel, out_shape=[jax.ShapeDtypeStruct(shape, dtype) for...]
  transfers between devices with their start and end apart: 14 -> 14, of which waited for: 6 -> 9; matrix products, arithmetic and copies ran while one was open for 0% -> 0% of each run, Pallas kernels for 35% -> 37%
where the time goes in v6:
time: 107 us
  Pallas kernels  45.4 us (42%)
  waiting for transfers between devices  44.3 us (41%)
  starting transfers between devices  14.9 us (14%)
  local copies, waits for them, and re-layouts  2.19 us (2%)
    pallas_call x10, Pallas kernels, call(): pl.pallas_call(kernel, out_shape=[jax.ShapeDtypeStruct(shape, dtype) for...  45.4 us
    ppermute x14, waiting for transfers between devices, send(): return lax.ppermute(value, ('gx', 'gy'), pairs)  44.3 us
    ppermute x14, starting transfers between devices, send(): return lax.ppermute(value, ('gx', 'gy'), pairs)  14.9 us
    unnamed x4, local copies, waits for them, and re-layouts  2.19 us
  transfers between devices with their start and end apart: 14, of which 9 were waited for; matrix products, arithmetic and copies ran while one was open for 0% of the time, Pallas kernels for 37%

profile of v6, /device:TPU:24, one launch (start us, length us, event | category | flops | bytes accessed | tf_op | source)
XLA Modules:
  0.0 107.3 jit_solution(234328591775955436)
XLA Ops:
  0.0 0.1 pad_add_fusion.place
  0.1 0.0 copy-start
  0.1 2.2 %copy-done = f32[1,1024,1024]{2,1,0:T(8,128)S(1)} copy-done((f32[1,1024,1024]{2,1,0:T(8,128)S(1)}, f32[1,1024,1024]{2,1,0:T(8,128)}, u32[]{:S(2)}) %copy-start) | copy-done | bytes 4194328
  2.3 0.6 cut_first.1.a0
  2.9 0.6 cut_side.1.mine
  3.5 1.6 %collective-permute-start = (f32[384,128]{1,0:T(8,128)S(1)}, f32[384,128]{1,0:T(8,128)S(1)}, u32[]{:S(2)}, u32[]{:S(2)}) collective-permute-start(f32[384,128]{1,0:T(8,128)S(1)} %cut_side.1.mine), channel_id=1, source_target_pairs={{0,2},{1,3},{2,0},{3,1},{4,6},{5,7},{6,4},{7,5},{8,10},{9,11},{10,... | collective-permute-start | bytes 589832 | tf_op jit(solution)/shard_map/ppermute | solution.py:634
  5.1 0.3 collective-permute-start.1
  5.4 0.9 cut_second.1
  6.4 0.5 collective-permute-start.2
  6.9 4.5 %collective-permute-done.along = f32[384,128]{1,0:T(8,128)S(1)} collective-permute-done((f32[384,128]{1,0:T(8,128)S(1)}, f32[384,128]{1,0:T(8,128)S(1)}, u32[]{:S(2)}, u32[]{:S(2)}) %collective-permute-start) | collective-permute-done | bytes 196640 | tf_op jit(solution)/shard_map/ppermute | solution.py:634
  11.4 7.1 %gauge_side.1 = (f32[256,256]{1,0:T(8,128)S(1)}, f32[256,256]{1,0:T(8,128)S(1)}) custom-call(f32[384,128]{1,0:T(8,128)S(1)} %cut_side.1.mine, f32[384,128]{1,0:T(8,128)S(1)} %collective-permute-done.along, f32[256,256]{1,0:T(8,128)S(1)} %get-tuple-element.42.b), custom_call_target="tpu_custom_call" | custom-call | flops 8000000000 | bytes 8000000000 | tf_op jit(solution)/shard_map/gauge_side/pallas_call | solution.py:179
  18.4 0.1 collective-permute-start.4
  18.5 0.4 scale_cross.1
  18.9 0.3 collective-permute-done.1.a1
  19.3 2.2 %collective-permute-done.2.a2.swapped = f32[1024,128]{1,0:T(8,128)S(1)} collective-permute-done((f32[1024,128]{1,0:T(8,128)S(1)}, f32[1024,128]{1,0:T(8,128)S(1)}, u32[]{:S(2)}, u32[]{:S(2)}) %collective-permute-start.2) | collective-permute-done | bytes 524320 | tf_op jit(solution)/shard_map/ppermute | solution.py:634
  21.5 1.5 %collective-permute-start.3 = (f32[512,128]{1,0:T(8,128)S(1)}, f32[512,128]{1,0:T(8,128)S(1)}, u32[]{:S(2)}, u32[]{:S(2)}) collective-permute-start(f32[512,128]{1,0:T(8,128)S(1)} %collective-permute-done.1.a1), channel_id=1, source_target_pairs={{0,2},{1,3},{2,0},{3,1},{4,6},{5,7},{6,4},{7,5},{8,10},{9,11},{10,... | collective-permute-start | bytes 786440 | tf_op jit(solution)/shard_map/ppermute | solution.py:634
  23.0 0.5 collective-permute-start.5
  23.5 7.4 %collective-permute-done.4.b1 = f32[256,256]{1,0:T(8,128)S(1)} collective-permute-done((f32[256,256]{1,0:T(8,128)S(1)}, f32[256,256]{1,0:T(8,128)S(1)}, u32[]{:S(2)}, u32[]{:S(2)}) %collective-permute-start.4) | collective-permute-done | bytes 262176 | tf_op jit(solution)/shard_map/ppermute | solution.py:634
  30.9 0.0 collective-permute-done.3.a3
  30.9 3.3 %collective-permute-done.5.b2 = f32[256,256]{1,0:T(8,128)S(1)} collective-permute-done((f32[256,256]{1,0:T(8,128)S(1)}, f32[256,256]{1,0:T(8,128)S(1)}, u32[]{:S(2)}, u32[]{:S(2)}) %collective-permute-start.5) | collective-permute-done | bytes 262176 | tf_op jit(solution)/shard_map/ppermute | solution.py:634
  34.3 1.5 %collective-permute-start.7 = (f32[256,256]{1,0:T(8,128)S(1)}, f32[256,256]{1,0:T(8,128)}, u32[]{:S(2)}, u32[]{:S(2)}) collective-permute-start(f32[256,256]{1,0:T(8,128)S(1)} %collective-permute-done.4.b1), channel_id=1, source_target_pairs={{0,2},{1,3},{2,0},{3,1},{4,6},{5,7},{6,4},{7,5},{8,10},{9,11},{10,... | collective-permute-start | bytes 786440 | tf_op jit(solution)/shard_map/ppermute | solution.py:634
  35.8 0.4 collective-permute-start.6
  36.2 4.6 %collective-permute-done.7.b3 = f32[256,256]{1,0:T(8,128)} collective-permute-done((f32[256,256]{1,0:T(8,128)S(1)}, f32[256,256]{1,0:T(8,128)}, u32[]{:S(2)}, u32[]{:S(2)}) %collective-permute-start.7) | collective-permute-done | bytes 262176 | tf_op jit(solution)/shard_map/ppermute | solution.py:634
  40.7 1.3 %collective-permute-start.9 = (f32[640,128]{1,0:T(8,128)S(1)}, f32[640,128]{1,0:T(8,128)S(1)}, u32[]{:S(2)}, u32[]{:S(2)}) collective-permute-start(f32[640,128]{1,0:T(8,128)S(1)} %get-tuple-element.55.c02), channel_id=1, source_target_pairs={{0,2},{1,3},{4,6},{5,7},{8,10},{9,11},{12,14},{13,15},{18,16},{19,... | collective-permute-start | bytes 983048 | tf_op jit(solution)/shard_map/ppermute | solution.py:634
  42.0 1.5 %collective-permute-start.8 = (f32[1280,128]{1,0:T(8,128)S(1)}, f32[1280,128]{1,0:T(8,128)S(1)}, u32[]{:S(2)}, u32[]{:S(2)}) collective-permute-start(f32[1280,128]{1,0:T(8,128)S(1)} %get-tuple-element.65.c01), channel_id=1, source_target_pairs={{0,2},{1,3},{4,6},{5,7},{8,10},{9,11},{12,14},{13,15},{18,16},{19,... | collective-permute-start | bytes 1966088 | tf_op jit(solution)/shard_map/ppermute | solution.py:634
  43.5 0.1 broadcast_select_fusion
  43.6 10.4 %factor_start.1.side_in = f32[512,512]{1,0:T(8,128)S(1)} custom-call(f32[512,128]{1,0:T(8,128)S(1)} %cut_first.1.a0, f32[512,128]{1,0:T(8,128)S(1)} %collective-permute-done.1.a1, f32[1024,128]{1,0:T(8,128)S(1)} %collective-permute-done.2.a2.swapped, f32[512,128]{1,0:T(8,128)S(1)} %collective-permute-done.3.a3, f32[256,256]{1,0:T(8,128)S(1)} %get-tuple-element.50.b0, ...), custom_call_target="tpu_custom_call" | custom-call | flops 10000000000 | bytes 10000000000 | tf_op jit(solution)/shard_map/factor_start/pallas_call | solution.py:179
  54.0 0.0 copy-start.1
  54.0 2.6 %collective-permute-start.10 = (f32[640,128]{1,0:T(8,128)S(1)}, f32[640,128]{1,0:T(8,128)S(1)}, u32[]{:S(2)}, u32[]{:S(2)}) collective-permute-start(f32[640,128]{1,0:T(8,128)S(1)} %get-tuple-element.69), channel_id=1, source_target_pairs={{0,16},{1,17},{2,18},{3,19},{4,20},{5,21},{6,22},{7,23},{8,24},{9,... | collective-permute-start | bytes 983048 | tf_op jit(solution)/shard_map/ppermute | solution.py:634
  56.6 11.3 %factor_end.1 = (bf16[768,768]{1,0:T(8,128)(2,1)S(1)}, bf16[768,768]{1,0:T(8,128)(2,1)S(1)}) custom-call(s32[2]{0:T(128)S(1)} %pad_add_fusion.place, f32[512,512]{1,0:T(8,128)S(1)} %factor_start.1.side_in, f32[256,256]{1,0:T(8,128)S(1)} %get-tuple-element.50.b0, f32[256,256]{1,0:T(8,128)S(1)} %collective-permute-done.4.b1, ...), custom_call_target="tpu_custom_call" | custom-call | flops 10000000000 | bytes 10000000000 | tf_op jit(solution)/shard_map/factor_end/pallas_call | solution.py:179
  68.0 4.2 %collective-permute-done.6.c11 = f32[1280,128]{1,0:T(8,128)S(1)} collective-permute-done((f32[1280,128]{1,0:T(8,128)S(1)}, f32[1280,128]{1,0:T(8,128)S(1)}, u32[]{:S(2)}, u32[]{:S(2)}) %collective-permute-start.6) | collective-permute-done | bytes 655392 | tf_op jit(solution)/shard_map/ppermute | solution.py:634
  72.1 1.3 %collective-permute-start.11 = (f32[1280,128]{1,0:T(8,128)S(1)}, f32[1280,128]{1,0:T(8,128)S(1)}, u32[]{:S(2)}, u32[]{:S(2)}) collective-permute-start(f32[1280,128]{1,0:T(8,128)S(1)} %collective-permute-done.6.c11), channel_id=1, source_target_pairs={{0,2},{1,3},{4,6},{5,7},{8,10},{9,11},{12,14},{13,15},{18,16},{19,... | collective-permute-start | bytes 1966088 | tf_op jit(solution)/shard_map/ppermute | solution.py:634
  73.4 0.0 collective-permute-done.9.c22
  73.4 0.0 collective-permute-done.8.c21
  73.4 0.0 copy-done.1
  73.4 4.5 %own_rows.1 = (bf16[512,768]{1,0:T(8,128)(2,1)S(1)}, bf16[512,768]{1,0:T(8,128)(2,1)S(1)}, f32[512,512]{1,0:T(8,128)S(1)}) custom-call(s32[2]{0:T(128)S(1)} %pad_add_fusion.place, f32[1,1024,1024]{2,1,0:T(8,128)S(1)} %copy-done.1, bf16[768,768]{1,0:T(8,128)(2,1)S(1)} %get-tuple-element.63.high, bf16[768,768]{1,0:T(8,128)(2,1)S(1)} %get-tuple-element.64.low, ...), custom_call_target="tpu_custom_call" | custom-call | flops 500000000 | bytes 500000000 | tf_op jit(solution)/shard_map/own_rows/pallas_call | solution.py:179
  78.0 1.1 %collective-permute-done.10.c12 = f32[640,128]{1,0:T(8,128)S(1)} collective-permute-done((f32[640,128]{1,0:T(8,128)S(1)}, f32[640,128]{1,0:T(8,128)S(1)}, u32[]{:S(2)}, u32[]{:S(2)}) %collective-permute-start.10) | collective-permute-done | bytes 327712 | tf_op jit(solution)/shard_map/ppermute | solution.py:634
  79.1 1.8 %collective-permute-start.12 = (f32[640,128]{1,0:T(8,128)S(1)}, f32[640,128]{1,0:T(8,128)S(1)}, u32[]{:S(2)}, u32[]{:S(2)}) collective-permute-start(f32[640,128]{1,0:T(8,128)S(1)} %collective-permute-done.10.c12), channel_id=1, source_target_pairs={{0,2},{1,3},{2,0},{3,1},{4,6},{5,7},{6,4},{7,5},{8,10},{9,11},{10,... | collective-permute-start | bytes 983048 | tf_op jit(solution)/shard_map/ppermute | solution.py:634
  80.8 0.0 collective-permute-start.13
  80.8 16.8 %collective-permute-done.12.c32.passed = f32[640,128]{1,0:T(8,128)S(1)} collective-permute-done((f32[640,128]{1,0:T(8,128)S(1)}, f32[640,128]{1,0:T(8,128)S(1)}, u32[]{:S(2)}, u32[]{:S(2)}) %collective-permute-start.12) | collective-permute-done | bytes 327712 | tf_op jit(solution)/shard_map/ppermute | solution.py:634
  97.6 0.0 collective-permute-done.11.c31
  97.6 5.2 %products.1 = (f32[1,1024,1024]{2,1,0:T(8,128)}, f32[512,768]{1,0:T(8,128)S(1)}) custom-call(s32[2]{0:T(128)S(1)} %pad_add_fusion.place, bf16[768,768]{1,0:T(8,128)(2,1)S(1)} %get-tuple-element.63.high, bf16[768,768]{1,0:T(8,128)(2,1)S(1)} %get-tuple-element.64.low, bf16[512,768]{1,0:T(8,128)(2,1)S(1)} %get-tuple-element.66.top, ...), custom_call_target="tpu_custom_call" | custom-call | flops 500000000 | bytes 500000000 | tf_op jit(solution)/shard_map/products/pallas_call | solution.py:179
  102.8 0.0 collective-permute-done.13.last
  102.8 4.3 %finish.1 = f32[1,1024,1024]{2,1,0:T(8,128)} custom-call(s32[2]{0:T(128)S(1)} %pad_add_fusion.place, f32[1,1024,1024]{2,1,0:T(8,128)} %get-tuple-element.74.before, bf16[768,768]{1,0:T(8,128)(2,1)S(1)} %get-tuple-element.63.high, bf16[768,768]{1,0:T(8,128)(2,1)S(1)} %get-tuple-element.64.low, ...), custom_call_target="tpu_custom_call", output_to_operand_aliasing={{}: (1, {})} | custom-call | flops 500000000 | bytes 500000000 | tf_op jit(solution)/shard_map/finish/pallas_call | solution.py:179
Async XLA Ops:
  0.1 2.2 %copy-start = (f32[1,1024,1024]{2,1,0:T(8,128)S(1)}, f32[1,1024,1024]{2,1,0:T(8,128)}, u32[]{:S(2)}) copy-start(f32[1,1024,1024]{2,1,0:T(8,128)} %leaf.7) | copy-start | bytes 12582916
  3.5 7.9 %collective-permute-start = (f32[384,128]{1,0:T(8,128)S(1)}, f32[384,128]{1,0:T(8,128)S(1)}, u32[]{:S(2)}, u32[]{:S(2)}) collective-permute-start(f32[384,128]{1,0:T(8,128)S(1)} %cut_side.1.mine), channel_id=1, source_target_pairs={{0,2},{1,3},{2,0},{3,1},{4,6},{5,7},{6,4},{7,5},{8,10},{9,11},{10,... | collective-permute-start | bytes 589832 | tf_op jit(solution)/shard_map/ppermute | solution.py:634
  5.1 14.2 %collective-permute-start.1 = (f32[512,128]{1,0:T(8,128)S(1)}, f32[512,128]{1,0:T(8,128)S(1)}, u32[]{:S(2)}, u32[]{:S(2)}) collective-permute-start(f32[512,128]{1,0:T(8,128)S(1)} %cut_first.1.a0), channel_id=1, source_target_pairs={{0,16},{1,17},{2,18},{3,19},{4,20},{5,21},{6,22},{7,23},{8,24},{9,... | collective-permute-start | bytes 786440 | tf_op jit(solution)/shard_map/ppermute | solution.py:634
  6.4 15.1 %collective-permute-start.2 = (f32[1024,128]{1,0:T(8,128)S(1)}, f32[1024,128]{1,0:T(8,128)S(1)}, u32[]{:S(2)}, u32[]{:S(2)}) collective-permute-start(f32[1024,128]{1,0:T(8,128)S(1)} %get-tuple-element.47), channel_id=1, source_target_pairs={{0,2},{1,3},{2,0},{3,1},{4,6},{5,7},{6,4},{7,5},{8,10},{9,11},{10,... | collective-permute-start | bytes 1572872 | tf_op jit(solution)/shard_map/ppermute | solution.py:634
  18.4 12.5 %collective-permute-start.4 = (f32[256,256]{1,0:T(8,128)S(1)}, f32[256,256]{1,0:T(8,128)S(1)}, u32[]{:S(2)}, u32[]{:S(2)}) collective-permute-start(f32[256,256]{1,0:T(8,128)S(1)} %get-tuple-element.50.b0), channel_id=1, source_target_pairs={{0,16},{1,17},{2,18},{3,19},{4,20},{5,21},{6,22},{7,23},{8,24},{9,... | collective-permute-start | bytes 786440 | tf_op jit(solution)/shard_map/ppermute | solution.py:634
  21.5 9.5 %collective-permute-start.3 = (f32[512,128]{1,0:T(8,128)S(1)}, f32[512,128]{1,0:T(8,128)S(1)}, u32[]{:S(2)}, u32[]{:S(2)}) collective-permute-start(f32[512,128]{1,0:T(8,128)S(1)} %collective-permute-done.1.a1), channel_id=1, source_target_pairs={{0,2},{1,3},{2,0},{3,1},{4,6},{5,7},{6,4},{7,5},{8,10},{9,11},{10,... | collective-permute-start | bytes 786440 | tf_op jit(solution)/shard_map/ppermute | solution.py:634
  23.0 11.3 %collective-permute-start.5 = (f32[256,256]{1,0:T(8,128)S(1)}, f32[256,256]{1,0:T(8,128)S(1)}, u32[]{:S(2)}, u32[]{:S(2)}) collective-permute-start(f32[256,256]{1,0:T(8,128)S(1)} %get-tuple-element.50.b0), channel_id=1, source_target_pairs={{0,2},{1,3},{2,0},{3,1},{4,6},{5,7},{6,4},{7,5},{8,10},{9,11},{10,... | collective-permute-start | bytes 786440 | tf_op jit(solution)/shard_map/ppermute | solution.py:634
  34.3 6.5 %collective-permute-start.7 = (f32[256,256]{1,0:T(8,128)S(1)}, f32[256,256]{1,0:T(8,128)}, u32[]{:S(2)}, u32[]{:S(2)}) collective-permute-start(f32[256,256]{1,0:T(8,128)S(1)} %collective-permute-done.4.b1), channel_id=1, source_target_pairs={{0,2},{1,3},{2,0},{3,1},{4,6},{5,7},{6,4},{7,5},{8,10},{9,11},{10,... | collective-permute-start | bytes 786440 | tf_op jit(solution)/shard_map/ppermute | solution.py:634
  35.8 36.3 %collective-permute-start.6 = (f32[1280,128]{1,0:T(8,128)S(1)}, f32[1280,128]{1,0:T(8,128)S(1)}, u32[]{:S(2)}, u32[]{:S(2)}) collective-permute-start(f32[1280,128]{1,0:T(8,128)S(1)} %get-tuple-element.65.c01), channel_id=1, source_target_pairs={{0,16},{1,17},{2,18},{3,19},{4,20},{5,21},{6,22},{7,23},{8,24},{9,... | collective-permute-start | bytes 1966088 | tf_op jit(solution)/shard_map/ppermute | solution.py:634
  40.7 32.7 %collective-permute-start.9 = (f32[640,128]{1,0:T(8,128)S(1)}, f32[640,128]{1,0:T(8,128)S(1)}, u32[]{:S(2)}, u32[]{:S(2)}) collective-permute-start(f32[640,128]{1,0:T(8,128)S(1)} %get-tuple-element.55.c02), channel_id=1, source_target_pairs={{0,2},{1,3},{4,6},{5,7},{8,10},{9,11},{12,14},{13,15},{18,16},{19,... | collective-permute-start | bytes 983048 | tf_op jit(solution)/shard_map/ppermute | solution.py:634
  42.0 31.4 %collective-permute-start.8 = (f32[1280,128]{1,0:T(8,128)S(1)}, f32[1280,128]{1,0:T(8,128)S(1)}, u32[]{:S(2)}, u32[]{:S(2)}) collective-permute-start(f32[1280,128]{1,0:T(8,128)S(1)} %get-tuple-element.65.c01), channel_id=1, source_target_pairs={{0,2},{1,3},{4,6},{5,7},{8,10},{9,11},{12,14},{13,15},{18,16},{19,... | collective-permute-start | bytes 1966088 | tf_op jit(solution)/shard_map/ppermute | solution.py:634
  54.0 19.4 %copy-start.1 = (f32[1,1024,1024]{2,1,0:T(8,128)S(1)}, f32[1,1024,1024]{2,1,0:T(8,128)}, u32[]{:S(2)}) copy-start(f32[1,1024,1024]{2,1,0:T(8,128)} %leaf.7) | copy-start | bytes 12582916
  54.0 25.1 %collective-permute-start.10 = (f32[640,128]{1,0:T(8,128)S(1)}, f32[640,128]{1,0:T(8,128)S(1)}, u32[]{:S(2)}, u32[]{:S(2)}) collective-permute-start(f32[640,128]{1,0:T(8,128)S(1)} %get-tuple-element.69), channel_id=1, source_target_pairs={{0,16},{1,17},{2,18},{3,19},{4,20},{5,21},{6,22},{7,23},{8,24},{9,... | collective-permute-start | bytes 983048 | tf_op jit(solution)/shard_map/ppermute | solution.py:634
  72.1 25.5 %collective-permute-start.11 = (f32[1280,128]{1,0:T(8,128)S(1)}, f32[1280,128]{1,0:T(8,128)S(1)}, u32[]{:S(2)}, u32[]{:S(2)}) collective-permute-start(f32[1280,128]{1,0:T(8,128)S(1)} %collective-permute-done.6.c11), channel_id=1, source_target_pairs={{0,2},{1,3},{4,6},{5,7},{8,10},{9,11},{12,14},{13,15},{18,16},{19,... | collective-permute-start | bytes 1966088 | tf_op jit(solution)/shard_map/ppermute | solution.py:634
  79.1 18.5 %collective-permute-start.12 = (f32[640,128]{1,0:T(8,128)S(1)}, f32[640,128]{1,0:T(8,128)S(1)}, u32[]{:S(2)}, u32[]{:S(2)}) collective-permute-start(f32[640,128]{1,0:T(8,128)S(1)} %collective-permute-done.10.c12), channel_id=1, source_target_pairs={{0,2},{1,3},{2,0},{3,1},{4,6},{5,7},{6,4},{7,5},{8,10},{9,11},{10,... | collective-permute-start | bytes 983048 | tf_op jit(solution)/shard_map/ppermute | solution.py:634
  80.8 22.0 %collective-permute-start.13 = (f32[640,128]{1,0:T(8,128)S(1)}, f32[640,128]{1,0:T(8,128)S(1)}, u32[]{:S(2)}, u32[]{:S(2)}) collective-permute-start(f32[640,128]{1,0:T(8,128)S(1)} %get-tuple-element.76), channel_id=1, source_target_pairs={{0,16},{1,17},{2,18},{3,19},{4,20},{5,21},{6,22},{7,23},{8,24},{9,... | collective-permute-start | bytes 983048 | tf_op jit(solution)/shard_map/ppermute | solution.py:634

commit v7 on v6

--- a/solution.py
+++ b/solution.py
@@ -12,6 +12,7 @@
 T = 128
 R = 16
 FIRST = 1
+SECOND = 8
 HBM = pl.BlockSpec(memory_space=pl.ANY)
 FAR = pl.BlockSpec(memory_space=pltpu.HBM)
 VMEM = pl.BlockSpec(memory_space=pltpu.VMEM)
@@ -194,6 +195,11 @@
     return leaf_block(leaf, side_r, side_c, at // tiles, at % tiles, T)
 
 
+def cross_tile(leaf, ext, inn, at):
+    n = (leaf.shape[1] // 4 // T) ** 2
+    return block_tiles(leaf, ext[at // n % 2], inn[at // n // 2], at % n)
+
+
 def cut_first_kernel(place, leaf, a, sem):
     tiles = leaf.shape[1] // 4 // T
     ext, inn = sides(place)
@@ -203,7 +209,7 @@
         pairs.append((leaf_block(leaf, inn[0], inn[0], r, c, T), a.at[pl.ds(at * T, T)]))
     for at in range(FIRST):
         pairs.append(
-            (block_tiles(leaf, ext[0], inn[0], at), a.at[pl.ds((n_sym + at) * T, T)])
+            (cross_tile(leaf, ext, inn, at), a.at[pl.ds((n_sym + at) * T, T)])
         )
     run_copies(pairs, sem)
 
@@ -269,8 +275,8 @@
     @pl.when(same)
     def _():
         cross = [
-            (block_tiles(leaf, ext[0], inn[0], at), swap.at[pl.ds((n_sym + at) * T, T)])
-            for at in range(FIRST)
+            (cross_tile(leaf, ext, inn, at), swap.at[pl.ds((n_sym + at) * T, T)])
+            for at in range(half)
         ]
         run_copies(cross, sem)
 
@@ -313,25 +319,31 @@
     )
 
 
-def scale_kernel(factor, c, c1, c2):
+def scale_kernel(factor, c, c1, c2, rest):
     e = factor.shape[0]
     tiles = e // T
     scaled = dot3(split(c[2 * e :, :]), split(factor[...]), NT)
-    for at in range(FIRST, 4 * tiles * tiles):
+    total = 4 * tiles * tiles
+    for at in range(FIRST, total):
         r, k = at // tiles * T, at % tiles * T
         tile = c[r : r + T, k : k + T] if r < 2 * e else scaled[r - 2 * e : r - 2 * e + T, k : k + T]
-        spot = (at - FIRST) * T
-        ref, spot = (c1, spot) if spot < c1.shape[0] else (c2, spot - c1.shape[0])
-        ref[spot : spot + T, :] = tile
-
-
-def scale_cross(factor, c, last):
+        if at < FIRST + SECOND:
+            c1[(at - FIRST) * T : (at - FIRST + 1) * T, :] = tile
+        else:
+            c2[(at - FIRST - SECOND) * T : (at - FIRST - SECOND + 1) * T, :] = tile
+        spot = at * T - (total * T - rest.shape[0])
+        if spot >= 0:
+            rest[spot : spot + T, :] = tile
+
+
+def scale_cross(factor, c, swapped):
     e = factor.shape[0]
+    total = 4 * e * e // T
     return call(
         scale_kernel,
         "scale_cross",
         2000 * 10**6,
-        [((4 * e * e // T - FIRST * T - last, T), F32), ((last, T), F32)],
+        [((n, T), F32) for n in (SECOND * T, total - (FIRST + SECOND) * T, total - swapped * T)],
         [(VMEM, x) for x in (factor, c)],
         [],
     )
@@ -359,7 +371,7 @@
     return call(
         factor_start_kernel,
         "factor_start",
-        10000 * 10**6,
+        1000 * 10**6,
         [((2 * e, 2 * e), F32)],
         [(VMEM, x) for x in (*a, *b)],
         [],
@@ -407,12 +419,12 @@
     )
 
 
-def cross_block(first, c1, c2):
-    n1, n2 = c1.shape[0] // T, c2.shape[0] // T
-    tiles = math.isqrt((FIRST + n1 + n2) // 4)
-    n_sym = len(upper(tiles))
-    held = [first[(n_sym + at) * T : (n_sym + at + 1) * T, :] for at in range(FIRST)]
-    held += [ref[at * T : (at + 1) * T, :] for ref, n in ((c1, n1), (c2, n2)) for at in range(n)]
+def cross_block(*pieces):
+    held = []
+    for ref, skip in pieces:
+        for at in range(skip * T, ref.shape[0], T):
+            held.append(ref[at : at + T, :])
+    tiles = math.isqrt(len(held) // 4)
     rows = []
     for r in range(2 * tiles):
         side = r // tiles
@@ -421,6 +433,14 @@
     return jnp.concatenate(rows, axis=0)
 
 
+def symmetric_tiles(e):
+    return len(upper(e // T))
+
+
+def zeros(tiles):
+    return jnp.zeros((tiles * T, T), F32), 0
+
+
 def times_inverse(cross, high, low, inner):
     e = cross.shape[1] // 2
     return dot3(split(cross[:, :e]), (high[:e], low[:e])) + dot3(
@@ -429,9 +449,10 @@
 
 
 def rows_kernel(
-    place, leaf, high, low, a0, c01, c02, swapped, c21, c22, top, bottom, block, col, own, sem
+    place, leaf, high, low, a0, c01, c02, a1, c11, swapped, rest, top, bottom, block, part, col, own, sem
 ):
     e = leaf.shape[1] // 4
+    n_sym = symmetric_tiles(e)
     ext, _ = sides(place)
     copies = []
     for r in range(2):
@@ -441,7 +462,7 @@
             copies.append(pltpu.make_async_copy(source, target, sem.at[2 * r + c]))
             copies[-1].start()
     same = place[0] == place[1]
-    mine = cross_block(a0, c01, c02)
+    mine = cross_block((a0, n_sym), (c01, 0), (c02, 0))
 
     @pl.when(same)
     def _():
@@ -449,7 +470,9 @@
 
     @pl.when(jnp.logical_not(same))
     def _():
-        col[...] = cross_block(swapped, c21, c22)
+        col[...] = cross_block((swapped, n_sym), (rest, 0))
+        across = cross_block((a1, n_sym), (c11, 0), zeros(c02.shape[0] // T))
+        part[...] = times_inverse(across, high[...], low[...], slice(2 * e, 3 * e))
 
     left = split(times_inverse(mine, high[...], low[...], slice(e, 2 * e)))
     top[...], bottom[...] = left
@@ -463,15 +486,15 @@
         block[...] = block[...] + own[...]
 
 
-def own_rows(place, leaf, high, low, a0, c01, c02, swapped, c21, c22):
+def own_rows(place, leaf, high, low, a0, c01, c02, a1, c11, swapped, rest):
     e = leaf.shape[1] // 4
     return call(
         rows_kernel,
         "own_rows",
         500 * 10**6,
-        [((2 * e, 3 * e), BF16)] * 2 + [((2 * e, 2 * e), F32)],
+        [((2 * e, 3 * e), BF16)] * 2 + [((2 * e, 2 * e), F32), ((2 * e, 3 * e), F32)],
         [(SMEM, place), (HBM, leaf)]
-        + [(VMEM, x) for x in (high, low, a0, c01, c02, swapped, c21, c22)],
+        + [(VMEM, x) for x in (high, low, a0, c01, c02, a1, c11, swapped, rest)],
         [
             pltpu.VMEM((2 * e, 2 * e), F32),
             pltpu.VMEM((2 * e, 2 * e), F32),
@@ -500,32 +523,32 @@
 
 
 def products_kernel(
-    place, high, low, top, bottom, block, a0, c01, c02, a1, c11, c12, a3, c31, c32, out, part, scratch
+    place, high, low, top, bottom, block, a0, c01, c02, a1, c11, third, a3, c31, passed, out, part, scratch
 ):
     e = out.shape[1] // 4
+    n_sym = symmetric_tiles(e)
     same = place[0] == place[1]
     write(out, place, block[...], 0, 0)
     everything = slice(0, 2 * e)
 
     @pl.when(same)
     def _():
-        across = cross_block(a1, c11, c12)
+        across = cross_block((a1, n_sym), (c11, 0), (third, 0))
         right = split(across)
         left = [pick(x, everything, 1) for x in (top, bottom)]
         write(out, place, -dot3(left, right, NT), 0, 1)
         scratch[...] = times_inverse(across, high[...], low[...], slice(2 * e, 3 * e))
         left = split(pick(scratch, everything, 0))
-        write(out, place, -dot3(left, split(cross_block(a0, c01, c02)), NT), 1, 0)
+        mine = cross_block((a0, n_sym), (c01, 0), (c02, 0))
+        write(out, place, -dot3(left, split(mine), NT), 1, 0)
         left = split(pick(scratch, everything, 1))
-        part[:, : 2 * e] = -dot3(left, right, NT)
+        part[...] = -dot3(left, right, NT)
 
     @pl.when(jnp.logical_not(same))
     def _():
-        right = split(cross_block(a3, c31, c32))
+        right = split(cross_block((a3, n_sym), (c31, 0), (passed, 0)))
         left = [pick(x, everything, 1) for x in (top, bottom)]
         write(out, place, -dot3(left, right, NT), 0, 1)
-        across = cross_block(a1, c11, jnp.zeros_like(c12))
-        part[...] = times_inverse(across, high[...], low[...], slice(2 * e, 3 * e))
 
 
 def products(place, high, low, top, bottom, block, mine, across, corner):
@@ -534,7 +557,7 @@
         products_kernel,
         "products",
         500 * 10**6,
-        [((1, 4 * e, 4 * e), F32), ((2 * e, 3 * e), F32)],
+        [((1, 4 * e, 4 * e), F32), ((2 * e, 2 * e), F32)],
         [(SMEM, place)]
         + [(VMEM, x) for x in (high, low, top, bottom, block, *mine, *across, *corner)],
         [pltpu.VMEM((2 * e, 3 * e), F32)],
@@ -542,11 +565,11 @@
 
 
 def finish_kernel(
-    place, before, high, low, part, passed, last, c11, swapped, c21, c22, a3, c31, out, held, scratch, sem
+    place, before, high, low, block, part, third, passed, last, swapped, rest, a3, c31, out, held, scratch, sem
 ):
     e = out.shape[1] // 4
     tiles = e // T
-    n_sym = len(upper(tiles))
+    n_sym = symmetric_tiles(e)
 
     def targets(b):
         return [
@@ -558,31 +581,34 @@
             for c in range(2)
         ]
 
+    n_last = last.shape[0] // T
+
     @pl.when(place[0] == place[1])
     def _():
-        half = last.shape[0]
+        skip = passed.shape[0] // T - n_last
         for at, (i, j) in enumerate(upper(2 * tiles)):
-            ref, at = (last, at * T) if at * T < half else (passed, at * T - half)
-            piece = ref[at : at + T, :]
+            ref, at = (last, at) if at < n_last else (passed, at - n_last + skip)
+            piece = ref[at * T : (at + 1) * T, :]
             r, c = slice(i * T, (i + 1) * T), slice(j * T, (j + 1) * T)
             shift = 2 * e
-            held[r, j * T + shift : (j + 1) * T + shift] = part[r, c] + piece
+            held[r, j * T + shift : (j + 1) * T + shift] = block[r, c] + piece
             if i != j:
-                held[c, i * T + shift : (i + 1) * T + shift] = part[c, r] + piece.T
+                held[c, i * T + shift : (i + 1) * T + shift] = block[c, r] + piece.T
         run_copies(targets(1), sem)
 
     @pl.when(place[0] != place[1])
     def _():
-        nothing = jnp.zeros(((n_sym + FIRST) * T, T), F32)
-        late = cross_block(nothing, jnp.zeros_like(c11), last)[:, e:]
+        first = third[: third.shape[0] - n_last * T, :]
+        late = cross_block(zeros(FIRST + SECOND), (first, 0), (last, 0))[:, e:]
         inner = slice(2 * e, 3 * e)
-        start = (2 * tiles * tiles - last.shape[0] // T) // tiles * T
-        scratch[:start, :] = part[:start, :]
-        scratch[start:, :] = part[start:, :] + dot3(split(late[start:]), (high[inner], low[inner]))
+        scratch[...] = part[...] + dot3(split(late), (high[inner], low[inner]))
         everything = slice(0, 2 * e)
         copies = []
         for b in range(2):
-            col = cross_block(swapped, c21, c22) if b == 0 else cross_block(a3, c31, passed)
+            if b == 0:
+                col = cross_block((swapped, n_sym), (rest, 0))
+            else:
+                col = cross_block((a3, n_sym), (c31, 0), (passed, 0))
             left = split(pick(scratch, everything, b))
             held[:, 2 * e * b : 2 * e * (b + 1)] = -dot3(left, split(col), NT)
             for i, (source, target) in enumerate(targets(b)):
@@ -592,7 +618,7 @@
             copy.wait()
 
 
-def finish(place, before, high, low, part, passed, last, c11, swapped, c21, c22, a3, c31):
+def finish(place, before, high, low, block, part, third, passed, last, swapped, rest, a3, c31):
     e = before.shape[1] // 4
     return call(
         finish_kernel,
@@ -602,7 +628,7 @@
         [(SMEM, place), (HBM, before)]
         + [
             (VMEM, x)
-            for x in (high, low, part, passed, last, c11, swapped, c21, c22, a3, c31)
+            for x in (high, low, block, part, third, passed, last, swapped, rest, a3, c31)
         ],
         [
             pltpu.VMEM((2 * e, 4 * e), F32),
@@ -648,32 +674,36 @@
         swapped = send(swap, True)
         b, factor = gauge(hh, hh_y, b)
         b_x = send(b, False)
-        c1, c2 = scale_cross(factor, c, outer0.shape[0])
+        n_last = outer0.shape[0] // T
+        c1, c2, rest = scale_cross(factor, c, n_last)
         b, a_x, c1, swapped = tie(b, a_x, c1, swapped)
         b_y = send(b, True)
+        a_x, b_y = tie(a_x, b_y)
         a_d = send(a_x, True)
-        a_d, b_x, b_y = tie(a_d, b_x, b_y)
-        b_d = send(b_x, True)
         c1, b_x = tie(c1, b_x)
         c1_x = send(c1, False)
-        c1, c2, b_d = tie(c1, c2, b_d)
-        c1_y = send(c1, True, only=True)
-        c2_y = send(c2, True, only=True)
+        b_x, b_y = tie(b_x, b_y)
+        b_d = send(b_x, True)
+        rest, b_d = tie(rest, b_d)
+        rest = send(rest, True, only=True)
         side = factor_start((a, a_x, swapped, a_d), (b, b_x, b_y, b_d))
-        third, side = tie(jnp.where(same, swapped[-outer0.shape[0] :], c2), side)
+        n_mid = c2.shape[0] // T - n_last
+        theirs = jnp.concatenate([c2[: n_mid * T], swapped[-n_last * T :]])
+        third, side = tie(jnp.where(same, theirs, c2), side)
         third = send(third, False)
+        c1_d = send(c1_x, True, only=True)
         high, low = factor_end(place, side, (b, b_x, b_y, b_d))
-        c1_x, high = tie(c1_x, high)
-        c1_d = send(c1_x, True, only=True)
-        top, bottom, block = own_rows(place, leaf, high, low, a, c1, c2, swapped, c1_y, c2_y)
-        last, third, block = tie(jnp.where(same, c2, outer0), third, block)
+        top, bottom, block, part = own_rows(
+            place, leaf, high, low, a, c1, c2, a_x, c1_x, swapped, rest
+        )
+        last, third, block = tie(jnp.where(same, c2[n_mid * T :], outer0), third, block)
         last = send(last, False)
         passed = send(third, True)
-        out, part = products(
+        out, block = products(
             place, high, low, top, bottom, block, (a, c1, c2), (a_x, c1_x, third), (a_d, c1_d, passed)
         )
         return finish(
-            place, out, high, low, part, passed, last, c1_x, swapped, c1_y, c2_y, a_d, c1_d
+            place, out, high, low, block, part, third, passed, last, swapped, rest, a_d, c1_d
         )
 
     return jax.shard_map(

time: 107 us -> 97.5 us (0.911); the launches traced: 107 us -> 96.6 us
  waiting for transfers between devices: 44.3 us -> 34.2 us
    ppermute x14 -> x13, waiting for transfers between devices: 44.3 us -> 34.2 us  [send(): return lax.ppermute(value, ('gx', 'gy'), pairs)]
    ppermute x14 -> x13, starting transfers between devices: 14.9 us -> 14 us  [send(): return lax.ppermute(value, ('gx', 'gy'), pairs)]
  transfers between devices with their start and end apart: 14 -> 13, of which waited for: 9 -> 7; matrix products, arithmetic and copies ran while one was open for 0% -> 0% of each run, Pallas kernels for 37% -> 41%
where the time goes in v7:
time: 97.5 us; the launch traced here: 96.6 us
  Pallas kernels  45.7 us (47%)
  waiting for transfers between devices  34.2 us (35%)
  starting transfers between devices  14 us (14%)
  local copies, waits for them, and re-layouts  2.23 us (2%)
    pallas_call x10, Pallas kernels, call(): pl.pallas_call(kernel, out_shape=[jax.ShapeDtypeStruct(shape, dtype) for...  45.7 us
    ppermute x13, waiting for transfers between devices, send(): return lax.ppermute(value, ('gx', 'gy'), pairs)  34.2 us
    ppermute x13, starting transfers between devices, send(): return lax.ppermute(value, ('gx', 'gy'), pairs)  14 us
    unnamed x4, local copies, waits for them, and re-layouts  2.19 us
  transfers between devices with their start and end apart: 13, of which 7 were waited for; matrix products, arithmetic and copies ran while one was open for 0% of the time, Pallas kernels for 41%

profile of v7, /device:TPU:24, one launch (start us, length us, event | category | flops | bytes accessed | tf_op | source)
XLA Modules:
  0.0 96.6 jit_solution(17550639722008780323)
XLA Ops:
  0.0 0.1 pad_add_fusion.place
  0.1 0.0 copy-start
  0.1 2.2 %copy-done = f32[1,1024,1024]{2,1,0:T(8,128)S(1)} copy-done((f32[1,1024,1024]{2,1,0:T(8,128)S(1)}, f32[1,1024,1024]{2,1,0:T(8,128)}, u32[]{:S(2)}) %copy-start) | copy-done | bytes 4194328
  2.3 0.6 cut_first.1.a0
  2.9 0.6 cut_side.1.mine
  3.5 1.6 %collective-permute-start = (f32[384,128]{1,0:T(8,128)S(1)}, f32[384,128]{1,0:T(8,128)S(1)}, u32[]{:S(2)}, u32[]{:S(2)}) collective-permute-start(f32[384,128]{1,0:T(8,128)S(1)} %cut_side.1.mine), channel_id=1, source_target_pairs={{0,2},{1,3},{2,0},{3,1},{4,6},{5,7},{6,4},{7,5},{8,10},{9,11},{10,... | collective-permute-start | bytes 589832 | tf_op jit(solution)/shard_map/ppermute | solution.py:660
  5.1 0.3 collective-permute-start.1
  5.4 0.9 cut_second.1
  6.4 0.6 collective-permute-start.2
  7.0 4.4 %collective-permute-done.along = f32[384,128]{1,0:T(8,128)S(1)} collective-permute-done((f32[384,128]{1,0:T(8,128)S(1)}, f32[384,128]{1,0:T(8,128)S(1)}, u32[]{:S(2)}, u32[]{:S(2)}) %collective-permute-start) | collective-permute-done | bytes 196640 | tf_op jit(solution)/shard_map/ppermute | solution.py:660
  11.4 7.0 %gauge_side.1 = (f32[256,256]{1,0:T(8,128)S(1)}, f32[256,256]{1,0:T(8,128)S(1)}) custom-call(f32[384,128]{1,0:T(8,128)S(1)} %cut_side.1.mine, f32[384,128]{1,0:T(8,128)S(1)} %collective-permute-done.along, f32[256,256]{1,0:T(8,128)S(1)} %get-tuple-element.42.b), custom_call_target="tpu_custom_call" | custom-call | flops 8000000000 | bytes 8000000000 | tf_op jit(solution)/shard_map/gauge_side/pallas_call | solution.py:180
  18.4 0.1 collective-permute-start.5
  18.5 0.4 scale_cross.1
  18.9 0.3 collective-permute-done.1.a1
  19.3 2.2 %collective-permute-done.2.a2.swapped = f32[1024,128]{1,0:T(8,128)S(1)} collective-permute-done((f32[1024,128]{1,0:T(8,128)S(1)}, f32[1024,128]{1,0:T(8,128)S(1)}, u32[]{:S(2)}, u32[]{:S(2)}) %collective-permute-start.2) | collective-permute-done | bytes 524320 | tf_op jit(solution)/shard_map/ppermute | solution.py:660
  21.5 1.5 %collective-permute-start.3 = (f32[256,256]{1,0:T(8,128)S(1)}, f32[256,256]{1,0:T(8,128)}, u32[]{:S(2)}, u32[]{:S(2)}) collective-permute-start(f32[256,256]{1,0:T(8,128)S(1)} %get-tuple-element.52.b0), channel_id=1, source_target_pairs={{0,2},{1,3},{2,0},{3,1},{4,6},{5,7},{6,4},{7,5},{8,10},{9,11},{10,... | collective-permute-start | bytes 786440 | tf_op jit(solution)/shard_map/ppermute | solution.py:660
  23.0 8.0 %collective-permute-done.5.b1 = f32[256,256]{1,0:T(8,128)} collective-permute-done((f32[256,256]{1,0:T(8,128)S(1)}, f32[256,256]{1,0:T(8,128)}, u32[]{:S(2)}, u32[]{:S(2)}) %collective-permute-start.5) | collective-permute-done | bytes 262176 | tf_op jit(solution)/shard_map/ppermute | solution.py:660
  31.0 0.0 collective-permute-start.7
  31.0 0.0 collective-permute-done.3.b2
  31.0 1.5 %collective-permute-start.6 = (f32[256,256]{1,0:T(8,128)}, f32[256,256]{1,0:T(8,128)S(1)}, u32[]{:S(2)}, u32[]{:S(2)}) collective-permute-start(f32[256,256]{1,0:T(8,128)} %collective-permute-done.5.b1), channel_id=1, source_target_pairs={{0,2},{1,3},{2,0},{3,1},{4,6},{5,7},{6,4},{7,5},{8,10},{9,11},{10,... | collective-permute-start | bytes 786440 | tf_op jit(solution)/shard_map/ppermute | solution.py:660
  32.6 0.5 collective-permute-start.4
  33.2 0.1 maximum_select_fusion
  33.2 7.3 %collective-permute-done.6.b3 = f32[256,256]{1,0:T(8,128)S(1)} collective-permute-done((f32[256,256]{1,0:T(8,128)}, f32[256,256]{1,0:T(8,128)S(1)}, u32[]{:S(2)}, u32[]{:S(2)}) %collective-permute-start.6) | collective-permute-done | bytes 262176 | tf_op jit(solution)/shard_map/ppermute | solution.py:660
  40.5 1.5 %collective-permute-start.8 = (f32[1408,128]{1,0:T(8,128)S(1)}, f32[1408,128]{1,0:T(8,128)S(1)}, u32[]{:S(2)}, u32[]{:S(2)}) collective-permute-start(f32[1408,128]{1,0:T(8,128)S(1)} %get-tuple-element.65), channel_id=1, source_target_pairs={{0,2},{1,3},{4,6},{5,7},{8,10},{9,11},{12,14},{13,15},{18,16},{19,... | collective-permute-start | bytes 2162696 | tf_op jit(solution)/shard_map/ppermute | solution.py:660
  41.9 4.1 %collective-permute-done.4.a3 = f32[512,128]{1,0:T(8,128)S(1)} collective-permute-done((f32[512,128]{1,0:T(8,128)S(1)}, f32[512,128]{1,0:T(8,128)S(1)}, u32[]{:S(2)}, u32[]{:S(2)}) %collective-permute-start.4) | collective-permute-done | bytes 262176 | tf_op jit(solution)/shard_map/ppermute | solution.py:660
  46.1 10.5 %factor_start.1.side_in = f32[512,512]{1,0:T(8,128)S(1)} custom-call(f32[512,128]{1,0:T(8,128)S(1)} %cut_first.1.a0, f32[512,128]{1,0:T(8,128)S(1)} %collective-permute-done.1.a1, f32[1024,128]{1,0:T(8,128)S(1)} %collective-permute-done.2.a2.swapped, f32[512,128]{1,0:T(8,128)S(1)} %collective-permute-done.4.a3, f32[256,256]{1,0:T(8,128)S(1)} %get-tuple-element.52.b0, ...), custom_call_target="tpu_custom_call" | custom-call | flops 1000000000 | bytes 1000000000 | tf_op jit(solution)/shard_map/factor_start/pallas_call | solution.py:180
  56.6 0.0 copy-start.1
  56.6 2.0 %collective-permute-start.9 = (f32[896,128]{1,0:T(8,128)S(1)}, f32[896,128]{1,0:T(8,128)S(1)}, u32[]{:S(2)}, u32[]{:S(2)}) collective-permute-start(f32[896,128]{1,0:T(8,128)S(1)} %maximum_select_fusion), channel_id=1, source_target_pairs={{0,16},{1,17},{2,18},{3,19},{4,20},{5,21},{6,22},{7,23},{8,24},{9,... | collective-permute-start | bytes 1376264 | tf_op jit(solution)/shard_map/ppermute | solution.py:660
  58.6 0.0 collective-permute-done.7.c11
  58.6 1.5 %collective-permute-start.10 = (f32[1024,128]{1,0:T(8,128)S(1)}, f32[1024,128]{1,0:T(8,128)S(1)}, u32[]{:S(2)}, u32[]{:S(2)}) collective-permute-start(f32[1024,128]{1,0:T(8,128)S(1)} %collective-permute-done.7.c11), channel_id=1, source_target_pairs={{0,2},{1,3},{4,6},{5,7},{8,10},{9,11},{12,14},{13,15},{18,16},{19,... | collective-permute-start | bytes 1572872 | tf_op jit(solution)/shard_map/ppermute | solution.py:660
  60.2 11.2 %factor_end.1 = (bf16[768,768]{1,0:T(8,128)(2,1)S(1)}, bf16[768,768]{1,0:T(8,128)(2,1)S(1)}) custom-call(s32[2]{0:T(128)S(1)} %pad_add_fusion.place, f32[512,512]{1,0:T(8,128)S(1)} %factor_start.1.side_in, f32[256,256]{1,0:T(8,128)S(1)} %get-tuple-element.52.b0, f32[256,256]{1,0:T(8,128)} %collective-permute-done.5.b1, ...), custom_call_target="tpu_custom_call" | custom-call | flops 10000000000 | bytes 10000000000 | tf_op jit(solution)/shard_map/factor_end/pallas_call | solution.py:180
  71.3 0.0 collective-permute-done.8.rest
  71.3 0.0 copy-done.1
  71.4 6.2 %own_rows.1 = (bf16[512,768]{1,0:T(8,128)(2,1)S(1)}, bf16[512,768]{1,0:T(8,128)(2,1)S(1)}, f32[512,512]{1,0:T(8,128)S(1)}, f32[512,768]{1,0:T(8,128)S(1)}) custom-call(s32[2]{0:T(128)S(1)} %pad_add_fusion.place, f32[1,1024,1024]{2,1,0:T(8,128)S(1)} %copy-done.1, bf16[768,768]{1,0:T(8,128)(2,1)S(1)} %get-tuple-element.62.high, ...), custom_call_target="tpu_custom_call" | custom-call | flops 500000000 | bytes 500000000 | tf_op jit(solution)/shard_map/own_rows/pallas_call | solution.py:180
  77.6 0.0 collective-permute-done.9.third
  77.6 1.4 %collective-permute-start.11 = (f32[896,128]{1,0:T(8,128)S(1)}, f32[896,128]{1,0:T(8,128)S(1)}, u32[]{:S(2)}, u32[]{:S(2)}) collective-permute-start(f32[896,128]{1,0:T(8,128)S(1)} %collective-permute-done.9.third), channel_id=1, source_target_pairs={{0,2},{1,3},{2,0},{3,1},{4,6},{5,7},{6,4},{7,5},{8,10},{9,11},{10,... | collective-permute-start | bytes 1376264 | tf_op jit(solution)/shard_map/ppermute | solution.py:660
  79.0 1.4 %collective-permute-start.12 = (f32[640,128]{1,0:T(8,128)S(1)}, f32[640,128]{1,0:T(8,128)S(1)}, u32[]{:S(2)}, u32[]{:S(2)}) collective-permute-start(f32[640,128]{1,0:T(8,128)S(1)} %slice_select_fusion), channel_id=1, source_target_pairs={{0,16},{1,17},{2,18},{3,19},{4,20},{5,21},{6,22},{7,23},{8,24},{9,... | collective-permute-start | bytes 983048 | tf_op jit(solution)/shard_map/ppermute | solution.py:660
  80.4 0.0 collective-permute-done.10.c31
  80.5 7.8 %collective-permute-done.11.passed = f32[896,128]{1,0:T(8,128)S(1)} collective-permute-done((f32[896,128]{1,0:T(8,128)S(1)}, f32[896,128]{1,0:T(8,128)S(1)}, u32[]{:S(2)}, u32[]{:S(2)}) %collective-permute-start.11) | collective-permute-done | bytes 458784 | tf_op jit(solution)/shard_map/ppermute | solution.py:660
  88.3 3.7 %products.1 = (f32[1,1024,1024]{2,1,0:T(8,128)}, f32[512,512]{1,0:T(8,128)S(1)}) custom-call(s32[2]{0:T(128)S(1)} %pad_add_fusion.place, bf16[768,768]{1,0:T(8,128)(2,1)S(1)} %get-tuple-element.62.high, bf16[768,768]{1,0:T(8,128)(2,1)S(1)} %get-tuple-element.63.low, bf16[512,768]{1,0:T(8,128)(2,1)S(1)} %get-tuple-element.66.top, ...), custom_call_target="tpu_custom_call" | custom-call | flops 500000000 | bytes 500000000 | tf_op jit(solution)/shard_map/products/pallas_call | solution.py:180
  92.0 0.0 collective-permute-done.12.last
  92.0 4.5 %finish.1 = f32[1,1024,1024]{2,1,0:T(8,128)} custom-call(s32[2]{0:T(128)S(1)} %pad_add_fusion.place, f32[1,1024,1024]{2,1,0:T(8,128)} %get-tuple-element.73.before, bf16[768,768]{1,0:T(8,128)(2,1)S(1)} %get-tuple-element.62.high, bf16[768,768]{1,0:T(8,128)(2,1)S(1)} %get-tuple-element.63.low, ...), custom_call_target="tpu_custom_call", output_to_operand_aliasing={{}: (1, {})} | custom-call | flops 500000000 | bytes 500000000 | tf_op jit(solution)/shard_map/finish/pallas_call | solution.py:180
  (3 shorter events, 0.1 us)
Async XLA Ops:
  0.1 2.2 %copy-start = (f32[1,1024,1024]{2,1,0:T(8,128)S(1)}, f32[1,1024,1024]{2,1,0:T(8,128)}, u32[]{:S(2)}) copy-start(f32[1,1024,1024]{2,1,0:T(8,128)} %leaf.7) | copy-start | bytes 12582916
  3.5 7.9 %collective-permute-start = (f32[384,128]{1,0:T(8,128)S(1)}, f32[384,128]{1,0:T(8,128)S(1)}, u32[]{:S(2)}, u32[]{:S(2)}) collective-permute-start(f32[384,128]{1,0:T(8,128)S(1)} %cut_side.1.mine), channel_id=1, source_target_pairs={{0,2},{1,3},{2,0},{3,1},{4,6},{5,7},{6,4},{7,5},{8,10},{9,11},{10,... | collective-permute-start | bytes 589832 | tf_op jit(solution)/shard_map/ppermute | solution.py:660
  5.1 14.2 %collective-permute-start.1 = (f32[512,128]{1,0:T(8,128)S(1)}, f32[512,128]{1,0:T(8,128)S(1)}, u32[]{:S(2)}, u32[]{:S(2)}) collective-permute-start(f32[512,128]{1,0:T(8,128)S(1)} %cut_first.1.a0), channel_id=1, source_target_pairs={{0,16},{1,17},{2,18},{3,19},{4,20},{5,21},{6,22},{7,23},{8,24},{9,... | collective-permute-start | bytes 786440 | tf_op jit(solution)/shard_map/ppermute | solution.py:660
  6.4 15.1 %collective-permute-start.2 = (f32[1024,128]{1,0:T(8,128)S(1)}, f32[1024,128]{1,0:T(8,128)S(1)}, u32[]{:S(2)}, u32[]{:S(2)}) collective-permute-start(f32[1024,128]{1,0:T(8,128)S(1)} %get-tuple-element.48), channel_id=1, source_target_pairs={{0,2},{1,3},{2,0},{3,1},{4,6},{5,7},{6,4},{7,5},{8,10},{9,11},{10,... | collective-permute-start | bytes 1572872 | tf_op jit(solution)/shard_map/ppermute | solution.py:660
  18.4 12.6 %collective-permute-start.5 = (f32[256,256]{1,0:T(8,128)S(1)}, f32[256,256]{1,0:T(8,128)}, u32[]{:S(2)}, u32[]{:S(2)}) collective-permute-start(f32[256,256]{1,0:T(8,128)S(1)} %get-tuple-element.52.b0), channel_id=1, source_target_pairs={{0,16},{1,17},{2,18},{3,19},{4,20},{5,21},{6,22},{7,23},{8,24},{9,... | collective-permute-start | bytes 786440 | tf_op jit(solution)/shard_map/ppermute | solution.py:660
  21.5 9.6 %collective-permute-start.3 = (f32[256,256]{1,0:T(8,128)S(1)}, f32[256,256]{1,0:T(8,128)}, u32[]{:S(2)}, u32[]{:S(2)}) collective-permute-start(f32[256,256]{1,0:T(8,128)S(1)} %get-tuple-element.52.b0), channel_id=1, source_target_pairs={{0,2},{1,3},{2,0},{3,1},{4,6},{5,7},{6,4},{7,5},{8,10},{9,11},{10,... | collective-permute-start | bytes 786440 | tf_op jit(solution)/shard_map/ppermute | solution.py:660
  31.0 27.6 %collective-permute-start.7 = (f32[1024,128]{1,0:T(8,128)S(1)}, f32[1024,128]{1,0:T(8,128)S(1)}, u32[]{:S(2)}, u32[]{:S(2)}) collective-permute-start(f32[1024,128]{1,0:T(8,128)S(1)} %get-tuple-element.64.c01), channel_id=1, source_target_pairs={{0,16},{1,17},{2,18},{3,19},{4,20},{5,21},{6,22},{7,23},{8,24},{9,... | collective-permute-start | bytes 1572872 | tf_op jit(solution)/shard_map/ppermute | solution.py:660
  31.0 9.4 %collective-permute-start.6 = (f32[256,256]{1,0:T(8,128)}, f32[256,256]{1,0:T(8,128)S(1)}, u32[]{:S(2)}, u32[]{:S(2)}) collective-permute-start(f32[256,256]{1,0:T(8,128)} %collective-permute-done.5.b1), channel_id=1, source_target_pairs={{0,2},{1,3},{2,0},{3,1},{4,6},{5,7},{6,4},{7,5},{8,10},{9,11},{10,... | collective-permute-start | bytes 786440 | tf_op jit(solution)/shard_map/ppermute | solution.py:660
  32.6 13.5 %collective-permute-start.4 = (f32[512,128]{1,0:T(8,128)S(1)}, f32[512,128]{1,0:T(8,128)S(1)}, u32[]{:S(2)}, u32[]{:S(2)}) collective-permute-start(f32[512,128]{1,0:T(8,128)S(1)} %collective-permute-done.1.a1), channel_id=1, source_target_pairs={{0,2},{1,3},{2,0},{3,1},{4,6},{5,7},{6,4},{7,5},{8,10},{9,11},{10,... | collective-permute-start | bytes 786440 | tf_op jit(solution)/shard_map/ppermute | solution.py:660
  40.5 30.9 %collective-permute-start.8 = (f32[1408,128]{1,0:T(8,128)S(1)}, f32[1408,128]{1,0:T(8,128)S(1)}, u32[]{:S(2)}, u32[]{:S(2)}) collective-permute-start(f32[1408,128]{1,0:T(8,128)S(1)} %get-tuple-element.65), channel_id=1, source_target_pairs={{0,2},{1,3},{4,6},{5,7},{8,10},{9,11},{12,14},{13,15},{18,16},{19,... | collective-permute-start | bytes 2162696 | tf_op jit(solution)/shard_map/ppermute | solution.py:660
  56.6 14.8 %copy-start.1 = (f32[1,1024,1024]{2,1,0:T(8,128)S(1)}, f32[1,1024,1024]{2,1,0:T(8,128)}, u32[]{:S(2)}) copy-start(f32[1,1024,1024]{2,1,0:T(8,128)} %leaf.7) | copy-start | bytes 12582916
  56.6 21.0 %collective-permute-start.9 = (f32[896,128]{1,0:T(8,128)S(1)}, f32[896,128]{1,0:T(8,128)S(1)}, u32[]{:S(2)}, u32[]{:S(2)}) collective-permute-start(f32[896,128]{1,0:T(8,128)S(1)} %maximum_select_fusion), channel_id=1, source_target_pairs={{0,16},{1,17},{2,18},{3,19},{4,20},{5,21},{6,22},{7,23},{8,24},{9,... | collective-permute-start | bytes 1376264 | tf_op jit(solution)/shard_map/ppermute | solution.py:660
  58.6 21.8 %collective-permute-start.10 = (f32[1024,128]{1,0:T(8,128)S(1)}, f32[1024,128]{1,0:T(8,128)S(1)}, u32[]{:S(2)}, u32[]{:S(2)}) collective-permute-start(f32[1024,128]{1,0:T(8,128)S(1)} %collective-permute-done.7.c11), channel_id=1, source_target_pairs={{0,2},{1,3},{4,6},{5,7},{8,10},{9,11},{12,14},{13,15},{18,16},{19,... | collective-permute-start | bytes 1572872 | tf_op jit(solution)/shard_map/ppermute | solution.py:660
  77.6 10.7 %collective-permute-start.11 = (f32[896,128]{1,0:T(8,128)S(1)}, f32[896,128]{1,0:T(8,128)S(1)}, u32[]{:S(2)}, u32[]{:S(2)}) collective-permute-start(f32[896,128]{1,0:T(8,128)S(1)} %collective-permute-done.9.third), channel_id=1, source_target_pairs={{0,2},{1,3},{2,0},{3,1},{4,6},{5,7},{6,4},{7,5},{8,10},{9,11},{10,... | collective-permute-start | bytes 1376264 | tf_op jit(solution)/shard_map/ppermute | solution.py:660
  79.0 13.0 %collective-permute-start.12 = (f32[640,128]{1,0:T(8,128)S(1)}, f32[640,128]{1,0:T(8,128)S(1)}, u32[]{:S(2)}, u32[]{:S(2)}) collective-permute-start(f32[640,128]{1,0:T(8,128)S(1)} %slice_select_fusion), channel_id=1, source_target_pairs={{0,16},{1,17},{2,18},{3,19},{4,20},{5,21},{6,22},{7,23},{8,24},{9,... | collective-permute-start | bytes 983048 | tf_op jit(solution)/shard_map/ppermute | solution.py:660

commit v8 on v7

--- a/solution.py
+++ b/solution.py
@@ -1,3 +1,4 @@
+import functools
 import math
 
 import jax
@@ -294,7 +295,7 @@
         "cut_second",
         1000 * 10**6,
         [(((n_sym + half) * T, T), F32), ((half * T, T), F32), ((e, e), F32), ((4 * e, e), F32)],
-        [(SMEM, place), (HBM, leaf)],
+        [(SMEM, place), (FAR, leaf)],
         [pltpu.SemaphoreType.DMA((n_sym + half + 5,))],
     )
 
@@ -493,7 +494,7 @@
         "own_rows",
         500 * 10**6,
         [((2 * e, 3 * e), BF16)] * 2 + [((2 * e, 2 * e), F32), ((2 * e, 3 * e), F32)],
-        [(SMEM, place), (HBM, leaf)]
+        [(SMEM, place), (FAR, leaf)]
         + [(VMEM, x) for x in (high, low, a0, c01, c02, a1, c11, swapped, rest)],
         [
             pltpu.VMEM((2 * e, 2 * e), F32),
@@ -522,8 +523,14 @@
     return jnp.concatenate([ref[rows, :e], ref[rows, (1 + b) * e : (2 + b) * e]], axis=1)
 
 
+def late_row(e):
+    tiles = e // T
+    return (2 * tiles * tiles - len(upper(2 * tiles)) // 2) // tiles * T
+
+
 def products_kernel(
-    place, high, low, top, bottom, block, a0, c01, c02, a1, c11, third, a3, c31, passed, out, part, scratch
+    n_mid, place, high, low, top, bottom, block, before, swapped, rest, a0, c01, c02, a1, c11, third,
+    a3, c31, passed, out, part, scratch
 ):
     e = out.shape[1] // 4
     n_sym = symmetric_tiles(e)
@@ -542,44 +549,63 @@
         mine = cross_block((a0, n_sym), (c01, 0), (c02, 0))
         write(out, place, -dot3(left, split(mine), NT), 1, 0)
         left = split(pick(scratch, everything, 1))
-        part[...] = -dot3(left, right, NT)
+        part[:, : 2 * e] = -dot3(left, right, NT)
 
     @pl.when(jnp.logical_not(same))
     def _():
-        right = split(cross_block((a3, n_sym), (c31, 0), (passed, 0)))
+        cols = [
+            split(cross_block((swapped, n_sym), (rest, 0))),
+            split(cross_block((a3, n_sym), (c31, 0), (passed, 0))),
+        ]
         left = [pick(x, everything, 1) for x in (top, bottom)]
-        write(out, place, -dot3(left, right, NT), 0, 1)
-
-
-def products(place, high, low, top, bottom, block, mine, across, corner):
+        write(out, place, -dot3(left, cols[1], NT), 0, 1)
+        n_last = 4 * (e // T) ** 2 - FIRST - SECOND - n_mid
+        middle = cross_block(zeros(FIRST + SECOND), (third[: n_mid * T, :], 0), zeros(n_last))
+        inner = slice(2 * e, 3 * e)
+        part[:e, :] = before[:e, :] + dot3(split(middle[:e, e:]), (high[inner], low[inner]))
+        part[e:, :] = before[e:, :]
+        start = late_row(e)
+        for b in range(2):
+            value = -dot3(split(pick(part, slice(0, start), b)), cols[b], NT)
+            for c in range(2):
+                rows = pl.ds(spot(place, e, 0, 1).start, start)
+                out[0, rows, spot(place, e, c, b)] = value[:, c * e : (c + 1) * e]
+
+
+def products(n_mid, place, high, low, top, bottom, block, part, swapped, rest, mine, across, corner):
     e = block.shape[0] // 2
     return call(
-        products_kernel,
+        functools.partial(products_kernel, n_mid),
         "products",
         500 * 10**6,
-        [((1, 4 * e, 4 * e), F32), ((2 * e, 2 * e), F32)],
+        [((1, 4 * e, 4 * e), F32), ((2 * e, 3 * e), F32)],
         [(SMEM, place)]
-        + [(VMEM, x) for x in (high, low, top, bottom, block, *mine, *across, *corner)],
+        + [(VMEM, x) for x in (high, low, top, bottom, block, part, swapped, rest)]
+        + [(VMEM, x) for x in (*mine, *across, *corner)],
         [pltpu.VMEM((2 * e, 3 * e), F32)],
     )
 
 
 def finish_kernel(
-    place, before, high, low, block, part, third, passed, last, swapped, rest, a3, c31, out, held, scratch, sem
+    place, before, high, low, part, passed, last, swapped, rest, a3, c31, out, held, scratch, sem
 ):
     e = out.shape[1] // 4
     tiles = e // T
     n_sym = symmetric_tiles(e)
 
-    def targets(b):
-        return [
-            (
-                held.at[pl.ds(r * e, e), pl.ds((2 * b + c) * e, e)],
-                out.at[0, spot(place, e, r, 1), spot(place, e, c, b)],
-            )
-            for r in range(2)
-            for c in range(2)
-        ]
+    def targets(b, start):
+        pairs = []
+        for r in range(2):
+            skip = start if r == 0 else 0
+            rows = pl.multiple_of(spot(place, e, r, 1).start + skip, T)
+            for c in range(2):
+                pairs.append(
+                    (
+                        held.at[pl.ds(r * e + skip, e - skip), pl.ds((2 * b + c) * e, e)],
+                        out.at[0, pl.ds(rows, e - skip), spot(place, e, c, b)],
+                    )
+                )
+        return pairs
 
     n_last = last.shape[0] // T
 
@@ -591,34 +617,33 @@
             piece = ref[at * T : (at + 1) * T, :]
             r, c = slice(i * T, (i + 1) * T), slice(j * T, (j + 1) * T)
             shift = 2 * e
-            held[r, j * T + shift : (j + 1) * T + shift] = block[r, c] + piece
+            held[r, j * T + shift : (j + 1) * T + shift] = part[r, c] + piece
             if i != j:
-                held[c, i * T + shift : (i + 1) * T + shift] = block[c, r] + piece.T
-        run_copies(targets(1), sem)
+                held[c, i * T + shift : (i + 1) * T + shift] = part[c, r] + piece.T
+        run_copies(targets(1, 0), sem)
 
     @pl.when(place[0] != place[1])
     def _():
-        first = third[: third.shape[0] - n_last * T, :]
-        late = cross_block(zeros(FIRST + SECOND), (first, 0), (last, 0))[:, e:]
+        start = late_row(e)
+        late = cross_block(zeros(4 * tiles * tiles - n_last), (last, 0))[start:, e:]
         inner = slice(2 * e, 3 * e)
-        scratch[...] = part[...] + dot3(split(late), (high[inner], low[inner]))
-        everything = slice(0, 2 * e)
+        scratch[start:, :] = part[start:, :] + dot3(split(late), (high[inner], low[inner]))
         copies = []
         for b in range(2):
             if b == 0:
                 col = cross_block((swapped, n_sym), (rest, 0))
             else:
                 col = cross_block((a3, n_sym), (c31, 0), (passed, 0))
-            left = split(pick(scratch, everything, b))
-            held[:, 2 * e * b : 2 * e * (b + 1)] = -dot3(left, split(col), NT)
-            for i, (source, target) in enumerate(targets(b)):
+            left = split(pick(scratch, slice(start, 2 * e), b))
+            held[start:, 2 * e * b : 2 * e * (b + 1)] = -dot3(left, split(col), NT)
+            for i, (source, target) in enumerate(targets(b, start)):
                 copies.append(pltpu.make_async_copy(source, target, sem.at[4 * b + i]))
                 copies[-1].start()
         for copy in copies:
             copy.wait()
 
 
-def finish(place, before, high, low, block, part, third, passed, last, swapped, rest, a3, c31):
+def finish(place, before, high, low, part, passed, last, swapped, rest, a3, c31):
     e = before.shape[1] // 4
     return call(
         finish_kernel,
@@ -626,10 +651,7 @@
         500 * 10**6,
         [(before.shape, F32)],
         [(SMEM, place), (HBM, before)]
-        + [
-            (VMEM, x)
-            for x in (high, low, block, part, third, passed, last, swapped, rest, a3, c31)
-        ],
+        + [(VMEM, x) for x in (high, low, part, passed, last, swapped, rest, a3, c31)],
         [
             pltpu.VMEM((2 * e, 4 * e), F32),
             pltpu.VMEM((2 * e, 3 * e), F32),
@@ -671,6 +693,7 @@
         hh = cut_side(here, leaf)
         hh_y = send(hh, True)
         swap, outer0, b, c = cut_second(place, leaf)
+        swap, hh_y = tie(swap, hh_y)
         swapped = send(swap, True)
         b, factor = gauge(hh, hh_y, b)
         b_x = send(b, False)
@@ -684,7 +707,7 @@
         c1_x = send(c1, False)
         b_x, b_y = tie(b_x, b_y)
         b_d = send(b_x, True)
-        rest, b_d = tie(rest, b_d)
+        rest, b_d, a_d = tie(rest, b_d, a_d)
         rest = send(rest, True, only=True)
         side = factor_start((a, a_x, swapped, a_d), (b, b_x, b_y, b_d))
         n_mid = c2.shape[0] // T - n_last
@@ -696,15 +719,15 @@
         top, bottom, block, part = own_rows(
             place, leaf, high, low, a, c1, c2, a_x, c1_x, swapped, rest
         )
-        last, third, block = tie(jnp.where(same, c2[n_mid * T :], outer0), third, block)
+        last, block = tie(jnp.where(same, c2[n_mid * T :], outer0), block)
         last = send(last, False)
+        third, block = tie(third, block)
         passed = send(third, True)
-        out, block = products(
-            place, high, low, top, bottom, block, (a, c1, c2), (a_x, c1_x, third), (a_d, c1_d, passed)
+        mine, across, corner = (a, c1, c2), (a_x, c1_x, third), (a_d, c1_d, passed)
+        out, part = products(
+            n_mid, place, high, low, top, bottom, block, part, swapped, rest, mine, across, corner
         )
-        return finish(
-            place, out, high, low, block, part, third, passed, last, swapped, rest, a_d, c1_d
-        )
+        return finish(place, out, high, low, part, passed, last, swapped, rest, a_d, c1_d)
 
     return jax.shard_map(
         body,

time: 97.5 us -> 102 us (1.046)
  starting transfers between devices: 14 us -> 16.1 us
  waiting for transfers between devices: 34.2 us -> 35.8 us
    ppermute x13, starting transfers between devices: 14 us -> 16.1 us  [send(): return lax.ppermute(value, ('gx', 'gy'), pairs)]
    ppermute x13, waiting for transfers between devices: 34.2 us -> 35.8 us  [send(): return lax.ppermute(value, ('gx', 'gy'), pairs)]
  transfers between devices with their start and end apart: 13 -> 13, of which waited for: 7 -> 6; matrix products, arithmetic and copies ran while one was open for 0% -> 0% of each run, Pallas kernels for 41% -> 41%
where the time goes in v8:
time: 102 us; the launch traced here: 101 us
  Pallas kernels  46.5 us (46%)
  waiting for transfers between devices  35.8 us (35%)
  starting transfers between devices  16.1 us (16%)
  local copies, waits for them, and re-layouts  2.23 us (2%)
    pallas_call x10, Pallas kernels, call(): pl.pallas_call(kernel, out_shape=[jax.ShapeDtypeStruct(shape, dtype) for...  46.5 us
    ppermute x13, waiting for transfers between devices, send(): return lax.ppermute(value, ('gx', 'gy'), pairs)  35.8 us
    ppermute x13, starting transfers between devices, send(): return lax.ppermute(value, ('gx', 'gy'), pairs)  16.1 us
    unnamed x4, local copies, waits for them, and re-layouts  2.19 us
  transfers between devices with their start and end apart: 13, of which 6 were waited for; matrix products, arithmetic and copies ran while one was open for 0% of the time, Pallas kernels for 41%

profile of v8, /device:TPU:24, one launch (start us, length us, event | category | flops | bytes accessed | tf_op | source)
XLA Modules:
  0.0 101.0 jit_solution(11810304642938441809)
XLA Ops:
  0.0 0.1 pad_add_fusion.place
  0.1 0.0 copy-start
  0.1 2.2 %copy-done = f32[1,1024,1024]{2,1,0:T(8,128)S(1)} copy-done((f32[1,1024,1024]{2,1,0:T(8,128)S(1)}, f32[1,1024,1024]{2,1,0:T(8,128)}, u32[]{:S(2)}) %copy-start) | copy-done | bytes 4194328
  2.3 0.6 cut_first.1.a0
  2.9 0.6 cut_side.1.mine
  3.5 1.6 %collective-permute-start = (f32[384,128]{1,0:T(8,128)S(1)}, f32[384,128]{1,0:T(8,128)S(1)}, u32[]{:S(2)}, u32[]{:S(2)}) collective-permute-start(f32[384,128]{1,0:T(8,128)S(1)} %cut_side.1.mine), channel_id=1, source_target_pairs={{0,2},{1,3},{2,0},{3,1},{4,6},{5,7},{6,4},{7,5},{8,10},{9,11},{10,... | collective-permute-start | bytes 589832 | tf_op jit(solution)/shard_map/ppermute | solution.py:682
  5.1 0.3 collective-permute-start.1
  5.4 0.9 cut_second.1
  6.4 3.8 %collective-permute-done.along = f32[384,128]{1,0:T(8,128)S(1)} collective-permute-done((f32[384,128]{1,0:T(8,128)S(1)}, f32[384,128]{1,0:T(8,128)S(1)}, u32[]{:S(2)}, u32[]{:S(2)}) %collective-permute-start) | collective-permute-done | bytes 196640 | tf_op jit(solution)/shard_map/ppermute | solution.py:682
  10.2 1.5 %collective-permute-start.2 = (f32[1024,128]{1,0:T(8,128)S(1)}, f32[1024,128]{1,0:T(8,128)S(1)}, u32[]{:S(2)}, u32[]{:S(2)}) collective-permute-start(f32[1024,128]{1,0:T(8,128)S(1)} %get-tuple-element.54), channel_id=1, source_target_pairs={{0,2},{1,3},{2,0},{3,1},{4,6},{5,7},{6,4},{7,5},{8,10},{9,11},{10,... | collective-permute-start | bytes 1572872 | tf_op jit(solution)/shard_map/ppermute | solution.py:682
  11.8 7.0 %gauge_side.1 = (f32[256,256]{1,0:T(8,128)S(1)}, f32[256,256]{1,0:T(8,128)S(1)}) custom-call(f32[384,128]{1,0:T(8,128)S(1)} %cut_side.1.mine, f32[384,128]{1,0:T(8,128)S(1)} %collective-permute-done.along, f32[256,256]{1,0:T(8,128)S(1)} %get-tuple-element.48.b), custom_call_target="tpu_custom_call" | custom-call | flops 8000000000 | bytes 8000000000 | tf_op jit(solution)/shard_map/gauge_side/pallas_call | solution.py:181
  18.8 0.4 collective-permute-start.4
  19.2 0.4 scale_cross.1
  19.6 0.0 collective-permute-done.1.a1
  19.6 3.4 %collective-permute-done.2.a2.swapped = f32[1024,128]{1,0:T(8,128)S(1)} collective-permute-done((f32[1024,128]{1,0:T(8,128)S(1)}, f32[1024,128]{1,0:T(8,128)S(1)}, u32[]{:S(2)}, u32[]{:S(2)}) %collective-permute-start.2) | collective-permute-done | bytes 524320 | tf_op jit(solution)/shard_map/ppermute | solution.py:682
  23.0 1.5 %collective-permute-start.3 = (f32[256,256]{1,0:T(8,128)S(1)}, f32[256,256]{1,0:T(8,128)}, u32[]{:S(2)}, u32[]{:S(2)}) collective-permute-start(f32[256,256]{1,0:T(8,128)S(1)} %get-tuple-element.58.b0), channel_id=1, source_target_pairs={{0,2},{1,3},{2,0},{3,1},{4,6},{5,7},{6,4},{7,5},{8,10},{9,11},{10,... | collective-permute-start | bytes 786440 | tf_op jit(solution)/shard_map/ppermute | solution.py:682
  24.5 7.7 %collective-permute-done.4.b1 = f32[256,256]{1,0:T(8,128)} collective-permute-done((f32[256,256]{1,0:T(8,128)S(1)}, f32[256,256]{1,0:T(8,128)}, u32[]{:S(2)}, u32[]{:S(2)}) %collective-permute-start.4) | collective-permute-done | bytes 262176 | tf_op jit(solution)/shard_map/ppermute | solution.py:682
  32.3 0.0 collective-permute-start.7
  32.3 0.0 collective-permute-done.3.b2
  32.3 0.5 collective-permute-start.5
  32.8 1.5 %collective-permute-start.6 = (f32[512,128]{1,0:T(8,128)S(1)}, f32[512,128]{1,0:T(8,128)S(1)}, u32[]{:S(2)}, u32[]{:S(2)}) collective-permute-start(f32[512,128]{1,0:T(8,128)S(1)} %collective-permute-done.1.a1), channel_id=1, source_target_pairs={{0,2},{1,3},{2,0},{3,1},{4,6},{5,7},{6,4},{7,5},{8,10},{9,11},{10,... | collective-permute-start | bytes 786440 | tf_op jit(solution)/shard_map/ppermute | solution.py:682
  34.4 0.1 maximum_select_fusion
  34.5 7.2 %collective-permute-done.5.b3 = f32[256,256]{1,0:T(8,128)S(1)} collective-permute-done((f32[256,256]{1,0:T(8,128)}, f32[256,256]{1,0:T(8,128)S(1)}, u32[]{:S(2)}, u32[]{:S(2)}) %collective-permute-start.5) | collective-permute-done | bytes 262176 | tf_op jit(solution)/shard_map/ppermute | solution.py:682
  41.7 4.7 %collective-permute-done.6.a3 = f32[512,128]{1,0:T(8,128)S(1)} collective-permute-done((f32[512,128]{1,0:T(8,128)S(1)}, f32[512,128]{1,0:T(8,128)S(1)}, u32[]{:S(2)}, u32[]{:S(2)}) %collective-permute-start.6) | collective-permute-done | bytes 262176 | tf_op jit(solution)/shard_map/ppermute | solution.py:682
  46.3 1.5 %collective-permute-start.8 = (f32[1408,128]{1,0:T(8,128)S(1)}, f32[1408,128]{1,0:T(8,128)S(1)}, u32[]{:S(2)}, u32[]{:S(2)}) collective-permute-start(f32[1408,128]{1,0:T(8,128)S(1)} %get-tuple-element.72), channel_id=1, source_target_pairs={{0,2},{1,3},{4,6},{5,7},{8,10},{9,11},{12,14},{13,15},{18,16},{19,... | collective-permute-start | bytes 2162696 | tf_op jit(solution)/shard_map/ppermute | solution.py:682
  47.8 10.5 %factor_start.1.side_in = f32[512,512]{1,0:T(8,128)S(1)} custom-call(f32[512,128]{1,0:T(8,128)S(1)} %cut_first.1.a0, f32[512,128]{1,0:T(8,128)S(1)} %collective-permute-done.1.a1, f32[1024,128]{1,0:T(8,128)S(1)} %collective-permute-done.2.a2.swapped, f32[512,128]{1,0:T(8,128)S(1)} %collective-permute-done.6.a3, f32[256,256]{1,0:T(8,128)S(1)} %get-tuple-element.58.b0, ...), custom_call_target="tpu_custom_call" | custom-call | flops 1000000000 | bytes 1000000000 | tf_op jit(solution)/shard_map/factor_start/pallas_call | solution.py:181
  58.3 3.9 %collective-permute-start.9 = (f32[896,128]{1,0:T(8,128)S(1)}, f32[896,128]{1,0:T(8,128)S(1)}, u32[]{:S(2)}, u32[]{:S(2)}) collective-permute-start(f32[896,128]{1,0:T(8,128)S(1)} %maximum_select_fusion), channel_id=1, source_target_pairs={{0,16},{1,17},{2,18},{3,19},{4,20},{5,21},{6,22},{7,23},{8,24},{9,... | collective-permute-start | bytes 1376264 | tf_op jit(solution)/shard_map/ppermute | solution.py:682
  62.2 0.0 collective-permute-done.7.c11
  62.2 1.5 %collective-permute-start.10 = (f32[1024,128]{1,0:T(8,128)S(1)}, f32[1024,128]{1,0:T(8,128)S(1)}, u32[]{:S(2)}, u32[]{:S(2)}) collective-permute-start(f32[1024,128]{1,0:T(8,128)S(1)} %collective-permute-done.7.c11), channel_id=1, source_target_pairs={{0,2},{1,3},{4,6},{5,7},{8,10},{9,11},{12,14},{13,15},{18,16},{19,... | collective-permute-start | bytes 1572872 | tf_op jit(solution)/shard_map/ppermute | solution.py:682
  63.7 0.0 copy-start.1
  63.7 11.4 %factor_end.1 = (bf16[768,768]{1,0:T(8,128)(2,1)S(1)}, bf16[768,768]{1,0:T(8,128)(2,1)S(1)}) custom-call(s32[2]{0:T(128)S(1)} %pad_add_fusion.place, f32[512,512]{1,0:T(8,128)S(1)} %factor_start.1.side_in, f32[256,256]{1,0:T(8,128)S(1)} %get-tuple-element.58.b0, f32[256,256]{1,0:T(8,128)} %collective-permute-done.4.b1, ...), custom_call_target="tpu_custom_call" | custom-call | flops 10000000000 | bytes 10000000000 | tf_op jit(solution)/shard_map/factor_end/pallas_call | solution.py:181
  75.1 0.0 collective-permute-done.8.rest
  75.1 0.0 copy-done.1
  75.1 6.2 %own_rows.1 = (bf16[512,768]{1,0:T(8,128)(2,1)S(1)}, bf16[512,768]{1,0:T(8,128)(2,1)S(1)}, f32[512,512]{1,0:T(8,128)S(1)}, f32[512,768]{1,0:T(8,128)S(1)}) custom-call(s32[2]{0:T(128)S(1)} %pad_add_fusion.place, f32[1,1024,1024]{2,1,0:T(8,128)S(1)} %copy-done.1, bf16[768,768]{1,0:T(8,128)(2,1)S(1)} %get-tuple-element.69.high, ...), custom_call_target="tpu_custom_call" | custom-call | flops 500000000 | bytes 500000000 | tf_op jit(solution)/shard_map/own_rows/pallas_call | solution.py:181
  81.3 0.0 collective-permute-done.9.third
  81.3 1.4 %collective-permute-start.11 = (f32[896,128]{1,0:T(8,128)S(1)}, f32[896,128]{1,0:T(8,128)S(1)}, u32[]{:S(2)}, u32[]{:S(2)}) collective-permute-start(f32[896,128]{1,0:T(8,128)S(1)} %collective-permute-done.9.third), channel_id=1, source_target_pairs={{0,2},{1,3},{2,0},{3,1},{4,6},{5,7},{6,4},{7,5},{8,10},{9,11},{10,... | collective-permute-start | bytes 1376264 | tf_op jit(solution)/shard_map/ppermute | solution.py:682
  82.7 0.5 collective-permute-start.12
  83.2 0.0 collective-permute-done.10.c31
  83.2 8.9 %collective-permute-done.11.passed = f32[896,128]{1,0:T(8,128)S(1)} collective-permute-done((f32[896,128]{1,0:T(8,128)S(1)}, f32[896,128]{1,0:T(8,128)S(1)}, u32[]{:S(2)}, u32[]{:S(2)}) %collective-permute-start.11) | collective-permute-done | bytes 458784 | tf_op jit(solution)/shard_map/ppermute | solution.py:682
  92.1 5.0 %products.1 = (f32[1,1024,1024]{2,1,0:T(8,128)}, f32[512,768]{1,0:T(8,128)S(1)}) custom-call(s32[2]{0:T(128)S(1)} %pad_add_fusion.place, bf16[768,768]{1,0:T(8,128)(2,1)S(1)} %get-tuple-element.69.high, bf16[768,768]{1,0:T(8,128)(2,1)S(1)} %get-tuple-element.70.low, bf16[512,768]{1,0:T(8,128)(2,1)S(1)} %get-tuple-element.73.top, ...), custom_call_target="tpu_custom_call" | custom-call | flops 500000000 | bytes 500000000 | tf_op jit(solution)/shard_map/products/pallas_call | solution.py:181
  97.1 0.0 collective-permute-done.12.last
  97.1 3.7 %finish.1 = f32[1,1024,1024]{2,1,0:T(8,128)} custom-call(s32[2]{0:T(128)S(1)} %pad_add_fusion.place, f32[1,1024,1024]{2,1,0:T(8,128)} %get-tuple-element.82.before, bf16[768,768]{1,0:T(8,128)(2,1)S(1)} %get-tuple-element.69.high, bf16[768,768]{1,0:T(8,128)(2,1)S(1)} %get-tuple-element.70.low, ...), custom_call_target="tpu_custom_call", output_to_operand_aliasing={{}: (1, {})} | custom-call | flops 500000000 | bytes 500000000 | tf_op jit(solution)/shard_map/finish/pallas_call | solution.py:181
  (3 shorter events, 0.1 us)
Async XLA Ops:
  0.1 2.2 %copy-start = (f32[1,1024,1024]{2,1,0:T(8,128)S(1)}, f32[1,1024,1024]{2,1,0:T(8,128)}, u32[]{:S(2)}) copy-start(f32[1,1024,1024]{2,1,0:T(8,128)} %leaf.7) | copy-start | bytes 12582916
  3.5 6.7 %collective-permute-start = (f32[384,128]{1,0:T(8,128)S(1)}, f32[384,128]{1,0:T(8,128)S(1)}, u32[]{:S(2)}, u32[]{:S(2)}) collective-permute-start(f32[384,128]{1,0:T(8,128)S(1)} %cut_side.1.mine), channel_id=1, source_target_pairs={{0,2},{1,3},{2,0},{3,1},{4,6},{5,7},{6,4},{7,5},{8,10},{9,11},{10,... | collective-permute-start | bytes 589832 | tf_op jit(solution)/shard_map/ppermute | solution.py:682
  5.1 14.5 %collective-permute-start.1 = (f32[512,128]{1,0:T(8,128)S(1)}, f32[512,128]{1,0:T(8,128)S(1)}, u32[]{:S(2)}, u32[]{:S(2)}) collective-permute-start(f32[512,128]{1,0:T(8,128)S(1)} %cut_first.1.a0), channel_id=1, source_target_pairs={{0,16},{1,17},{2,18},{3,19},{4,20},{5,21},{6,22},{7,23},{8,24},{9,... | collective-permute-start | bytes 786440 | tf_op jit(solution)/shard_map/ppermute | solution.py:682
  10.2 12.8 %collective-permute-start.2 = (f32[1024,128]{1,0:T(8,128)S(1)}, f32[1024,128]{1,0:T(8,128)S(1)}, u32[]{:S(2)}, u32[]{:S(2)}) collective-permute-start(f32[1024,128]{1,0:T(8,128)S(1)} %get-tuple-element.54), channel_id=1, source_target_pairs={{0,2},{1,3},{2,0},{3,1},{4,6},{5,7},{6,4},{7,5},{8,10},{9,11},{10,... | collective-permute-start | bytes 1572872 | tf_op jit(solution)/shard_map/ppermute | solution.py:682
  18.8 13.5 %collective-permute-start.4 = (f32[256,256]{1,0:T(8,128)S(1)}, f32[256,256]{1,0:T(8,128)}, u32[]{:S(2)}, u32[]{:S(2)}) collective-permute-start(f32[256,256]{1,0:T(8,128)S(1)} %get-tuple-element.58.b0), channel_id=1, source_target_pairs={{0,16},{1,17},{2,18},{3,19},{4,20},{5,21},{6,22},{7,23},{8,24},{9,... | collective-permute-start | bytes 786440 | tf_op jit(solution)/shard_map/ppermute | solution.py:682
  23.0 9.2 %collective-permute-start.3 = (f32[256,256]{1,0:T(8,128)S(1)}, f32[256,256]{1,0:T(8,128)}, u32[]{:S(2)}, u32[]{:S(2)}) collective-permute-start(f32[256,256]{1,0:T(8,128)S(1)} %get-tuple-element.58.b0), channel_id=1, source_target_pairs={{0,2},{1,3},{2,0},{3,1},{4,6},{5,7},{6,4},{7,5},{8,10},{9,11},{10,... | collective-permute-start | bytes 786440 | tf_op jit(solution)/shard_map/ppermute | solution.py:682
  32.3 29.9 %collective-permute-start.7 = (f32[1024,128]{1,0:T(8,128)S(1)}, f32[1024,128]{1,0:T(8,128)S(1)}, u32[]{:S(2)}, u32[]{:S(2)}) collective-permute-start(f32[1024,128]{1,0:T(8,128)S(1)} %get-tuple-element.71.c01), channel_id=1, source_target_pairs={{0,16},{1,17},{2,18},{3,19},{4,20},{5,21},{6,22},{7,23},{8,24},{9,... | collective-permute-start | bytes 1572872 | tf_op jit(solution)/shard_map/ppermute | solution.py:682
  32.3 9.4 %collective-permute-start.5 = (f32[256,256]{1,0:T(8,128)}, f32[256,256]{1,0:T(8,128)S(1)}, u32[]{:S(2)}, u32[]{:S(2)}) collective-permute-start(f32[256,256]{1,0:T(8,128)} %collective-permute-done.4.b1), channel_id=1, source_target_pairs={{0,2},{1,3},{2,0},{3,1},{4,6},{5,7},{6,4},{7,5},{8,10},{9,11},{10,... | collective-permute-start | bytes 786440 | tf_op jit(solution)/shard_map/ppermute | solution.py:682
  32.8 13.5 %collective-permute-start.6 = (f32[512,128]{1,0:T(8,128)S(1)}, f32[512,128]{1,0:T(8,128)S(1)}, u32[]{:S(2)}, u32[]{:S(2)}) collective-permute-start(f32[512,128]{1,0:T(8,128)S(1)} %collective-permute-done.1.a1), channel_id=1, source_target_pairs={{0,2},{1,3},{2,0},{3,1},{4,6},{5,7},{6,4},{7,5},{8,10},{9,11},{10,... | collective-permute-start | bytes 786440 | tf_op jit(solution)/shard_map/ppermute | solution.py:682
  46.3 28.8 %collective-permute-start.8 = (f32[1408,128]{1,0:T(8,128)S(1)}, f32[1408,128]{1,0:T(8,128)S(1)}, u32[]{:S(2)}, u32[]{:S(2)}) collective-permute-start(f32[1408,128]{1,0:T(8,128)S(1)} %get-tuple-element.72), channel_id=1, source_target_pairs={{0,2},{1,3},{4,6},{5,7},{8,10},{9,11},{12,14},{13,15},{18,16},{19,... | collective-permute-start | bytes 2162696 | tf_op jit(solution)/shard_map/ppermute | solution.py:682
  58.3 23.0 %collective-permute-start.9 = (f32[896,128]{1,0:T(8,128)S(1)}, f32[896,128]{1,0:T(8,128)S(1)}, u32[]{:S(2)}, u32[]{:S(2)}) collective-permute-start(f32[896,128]{1,0:T(8,128)S(1)} %maximum_select_fusion), channel_id=1, source_target_pairs={{0,16},{1,17},{2,18},{3,19},{4,20},{5,21},{6,22},{7,23},{8,24},{9,... | collective-permute-start | bytes 1376264 | tf_op jit(solution)/shard_map/ppermute | solution.py:682
  62.2 21.0 %collective-permute-start.10 = (f32[1024,128]{1,0:T(8,128)S(1)}, f32[1024,128]{1,0:T(8,128)S(1)}, u32[]{:S(2)}, u32[]{:S(2)}) collective-permute-start(f32[1024,128]{1,0:T(8,128)S(1)} %collective-permute-done.7.c11), channel_id=1, source_target_pairs={{0,2},{1,3},{4,6},{5,7},{8,10},{9,11},{12,14},{13,15},{18,16},{19,... | collective-permute-start | bytes 1572872 | tf_op jit(solution)/shard_map/ppermute | solution.py:682
  63.7 11.4 %copy-start.1 = (f32[1,1024,1024]{2,1,0:T(8,128)S(1)}, f32[1,1024,1024]{2,1,0:T(8,128)}, u32[]{:S(2)}) copy-start(f32[1,1024,1024]{2,1,0:T(8,128)} %leaf.7) | copy-start | bytes 12582916
  81.3 10.8 %collective-permute-start.11 = (f32[896,128]{1,0:T(8,128)S(1)}, f32[896,128]{1,0:T(8,128)S(1)}, u32[]{:S(2)}, u32[]{:S(2)}) collective-permute-start(f32[896,128]{1,0:T(8,128)S(1)} %collective-permute-done.9.third), channel_id=1, source_target_pairs={{0,2},{1,3},{2,0},{3,1},{4,6},{5,7},{6,4},{7,5},{8,10},{9,11},{10,... | collective-permute-start | bytes 1376264 | tf_op jit(solution)/shard_map/ppermute | solution.py:682
  82.7 14.4 %collective-permute-start.12 = (f32[640,128]{1,0:T(8,128)S(1)}, f32[640,128]{1,0:T(8,128)S(1)}, u32[]{:S(2)}, u32[]{:S(2)}) collective-permute-start(f32[640,128]{1,0:T(8,128)S(1)} %slice_select_fusion), channel_id=1, source_target_pairs={{0,16},{1,17},{2,18},{3,19},{4,20},{5,21},{6,22},{7,23},{8,24},{9,... | collective-permute-start | bytes 983048 | tf_op jit(solution)/shard_map/ppermute | solution.py:682

commit v9 on v7

--- a/solution.py
+++ b/solution.py
@@ -10,14 +10,14 @@
 F32 = jnp.float32
 BF16 = jnp.bfloat16
 T = 128
+ALONE = 59
 R = 16
 FIRST = 1
-SECOND = 8
+SECOND = 10
 HBM = pl.BlockSpec(memory_space=pl.ANY)
 FAR = pl.BlockSpec(memory_space=pltpu.HBM)
 VMEM = pl.BlockSpec(memory_space=pltpu.VMEM)
 SMEM = pl.BlockSpec(memory_space=pltpu.SMEM)
-PARAMS = pltpu.CompilerParams(vmem_limit_bytes=32 * 2**20)
 
 
 def dot(a, b, dims=((1,), (0,))):
@@ -176,14 +176,14 @@
     )
 
 
-def call(kernel, name, cost, outs, ins, scratch, **more):
+def call(kernel, name, cost, outs, ins, scratch, room=32, **more):
     return pl.pallas_call(
         kernel,
         out_shape=[jax.ShapeDtypeStruct(shape, dtype) for shape, dtype in outs],
         in_specs=[spec for spec, _ in ins],
         out_specs=more.pop("out_specs", [VMEM] * len(outs)),
         scratch_shapes=scratch,
-        compiler_params=PARAMS,
+        compiler_params=pltpu.CompilerParams(vmem_limit_bytes=room * 2**20),
         cost_estimate=pl.CostEstimate(flops=cost, bytes_accessed=cost, transcendentals=0),
         name=name,
         **more,
@@ -223,6 +223,7 @@
         [(((n_sym + FIRST) * T, T), F32)],
         [(SMEM, place), (FAR, leaf)],
         [pltpu.SemaphoreType.DMA((n_sym + FIRST,))],
+        room=ALONE,
     )[0]
 
 
@@ -244,6 +245,7 @@
         [((n_sym * T, T), F32)],
         [(SMEM, place), (FAR, leaf)],
         [pltpu.SemaphoreType.DMA((n_sym,))],
+        room=ALONE,
     )[0]
 
 
@@ -371,7 +373,7 @@
     return call(
         factor_start_kernel,
         "factor_start",
-        1000 * 10**6,
+        3500 * 10**6,
         [((2 * e, 2 * e), F32)],
         [(VMEM, x) for x in (*a, *b)],
         [],
@@ -448,177 +450,155 @@
     )
 
 
+def spot(place, e, side, which):
+    x = place[0] if which == 0 else 1 - place[0]
+    return pl.ds(pl.multiple_of((2 * side + x) * e, T), e)
+
+
+def put(out, place, held, a, b, sem):
+    e = out.shape[1] // 4
+    copies = []
+    for r in range(2):
+        for c in range(2):
+            source = held.at[pl.ds(r * e, e), pl.ds(c * e, e)]
+            target = out.at[0, spot(place, e, r, a), spot(place, e, c, b)]
+            copies.append(pltpu.make_async_copy(source, target, sem.at[2 * r + c]))
+            copies[-1].start()
+    return copies
+
+
+def wait(copies):
+    for copy in copies:
+        copy.wait()
+
+
+def pick(ref, b):
+    e = ref.shape[1] // 3
+    return jnp.concatenate([ref[:, :e], ref[:, (1 + b) * e : (2 + b) * e]], axis=1)
+
+
 def rows_kernel(
-    place, leaf, high, low, a0, c01, c02, a1, c11, swapped, rest, top, bottom, block, part, col, own, sem
+    place, leaf, high, low, a0, c01, c02, a1, c11, third, swapped, rest, out, top, bottom, part, col, own, held, sem
 ):
     e = leaf.shape[1] // 4
     n_sym = symmetric_tiles(e)
     ext, _ = sides(place)
-    copies = []
+    fetch = []
     for r in range(2):
         for c in range(2):
             target = own.at[pl.ds(r * e, e), pl.ds(c * e, e)]
             source = leaf_block(leaf, ext[r], ext[c], 0, 0, e)
-            copies.append(pltpu.make_async_copy(source, target, sem.at[2 * r + c]))
-            copies[-1].start()
+            fetch.append(pltpu.make_async_copy(source, target, sem.at[3, 2 * r + c]))
+            fetch[-1].start()
     same = place[0] == place[1]
     mine = cross_block((a0, n_sym), (c01, 0), (c02, 0))
-
-    @pl.when(same)
-    def _():
-        col[...] = mine
-
-    @pl.when(jnp.logical_not(same))
-    def _():
-        col[...] = cross_block((swapped, n_sym), (rest, 0))
-        across = cross_block((a1, n_sym), (c11, 0), zeros(c02.shape[0] // T))
-        part[...] = times_inverse(across, high[...], low[...], slice(2 * e, 3 * e))
-
     left = split(times_inverse(mine, high[...], low[...], slice(e, 2 * e)))
     top[...], bottom[...] = left
-    left = [x[:, : 2 * e] for x in left]
-    block[...] = -dot3(left, split(col[...]), NT)
-    for copy in copies:
-        copy.wait()
+    left = [[pick(x, b) for x in left] for b in range(2)]
+    wait(fetch)
 
     @pl.when(same)
     def _():
-        block[...] = block[...] + own[...]
-
-
-def own_rows(place, leaf, high, low, a0, c01, c02, a1, c11, swapped, rest):
+        right = split(mine)
+        held[0] = own[...] - dot3(left[0], right, NT)
+        copies = put(out, place, held.at[0], 0, 0, sem.at[0])
+        across = cross_block((a1, n_sym), (c11, 0), (third, 0))
+        other = split(across)
+        held[1] = -dot3(left[1], other, NT)
+        copies += put(out, place, held.at[1], 0, 1, sem.at[1])
+        value = times_inverse(across, high[...], low[...], slice(2 * e, 3 * e))
+        held[2] = -dot3(split(pick(value, 0)), right, NT)
+        copies += put(out, place, held.at[2], 1, 0, sem.at[2])
+        part[:, : 2 * e] = -dot3(split(pick(value, 1)), other, NT)
+        wait(copies)
+
+    @pl.when(jnp.logical_not(same))
+    def _():
+        col[...] = cross_block((swapped, n_sym), (rest, 0))
+        held[0] = -dot3(left[0], split(col[...]), NT)
+        copies = put(out, place, held.at[0], 0, 0, sem.at[0])
+        across = cross_block((a1, n_sym), (c11, 0), zeros(third.shape[0] // T))
+        part[...] = times_inverse(across, high[...], low[...], slice(2 * e, 3 * e))
+        wait(copies)
+
+
+def first_rows(place, leaf, high, low, mine, across, swapped, rest):
     e = leaf.shape[1] // 4
+    block = pltpu.VMEM((2 * e, 2 * e), F32)
     return call(
         rows_kernel,
-        "own_rows",
+        "first_rows",
         500 * 10**6,
-        [((2 * e, 3 * e), BF16)] * 2 + [((2 * e, 2 * e), F32), ((2 * e, 3 * e), F32)],
+        [(leaf.shape, F32)] + [((2 * e, 3 * e), BF16)] * 2 + [((2 * e, 3 * e), F32)],
         [(SMEM, place), (HBM, leaf)]
-        + [(VMEM, x) for x in (high, low, a0, c01, c02, a1, c11, swapped, rest)],
-        [
-            pltpu.VMEM((2 * e, 2 * e), F32),
-            pltpu.VMEM((2 * e, 2 * e), F32),
-            pltpu.SemaphoreType.DMA((4,)),
-        ],
-    )
-
-
-def spot(place, e, side, which):
-    x = place[0] if which == 0 else 1 - place[0]
-    return pl.ds(pl.multiple_of((2 * side + x) * e, T), e)
-
-
-def write(out, place, value, a, b):
-    e = out.shape[1] // 4
-    for r in range(2):
-        for c in range(2):
-            out[0, spot(place, e, r, a), spot(place, e, c, b)] = value[
-                r * e : (r + 1) * e, c * e : (c + 1) * e
-            ]
-
-
-def pick(ref, rows, b):
-    e = ref.shape[1] // 3
-    return jnp.concatenate([ref[rows, :e], ref[rows, (1 + b) * e : (2 + b) * e]], axis=1)
-
-
-def products_kernel(
-    place, high, low, top, bottom, block, a0, c01, c02, a1, c11, third, a3, c31, passed, out, part, scratch
-):
-    e = out.shape[1] // 4
-    n_sym = symmetric_tiles(e)
-    same = place[0] == place[1]
-    write(out, place, block[...], 0, 0)
-    everything = slice(0, 2 * e)
-
-    @pl.when(same)
-    def _():
-        across = cross_block((a1, n_sym), (c11, 0), (third, 0))
-        right = split(across)
-        left = [pick(x, everything, 1) for x in (top, bottom)]
-        write(out, place, -dot3(left, right, NT), 0, 1)
-        scratch[...] = times_inverse(across, high[...], low[...], slice(2 * e, 3 * e))
-        left = split(pick(scratch, everything, 0))
-        mine = cross_block((a0, n_sym), (c01, 0), (c02, 0))
-        write(out, place, -dot3(left, split(mine), NT), 1, 0)
-        left = split(pick(scratch, everything, 1))
-        part[...] = -dot3(left, right, NT)
-
-    @pl.when(jnp.logical_not(same))
+        + [(VMEM, x) for x in (high, low, *mine, *across, swapped, rest)],
+        [block, block, pltpu.VMEM((3, 2 * e, 2 * e), F32), pltpu.SemaphoreType.DMA((4, 4))],
+        out_specs=[HBM] + [VMEM] * 3,
+    )
+
+
+def corner_kernel(place, before, top, bottom, a3, c31, passed, out, held, sem):
+    n_sym = symmetric_tiles(out.shape[1] // 4)
+
+    @pl.when(place[0] != place[1])
     def _():
         right = split(cross_block((a3, n_sym), (c31, 0), (passed, 0)))
-        left = [pick(x, everything, 1) for x in (top, bottom)]
-        write(out, place, -dot3(left, right, NT), 0, 1)
-
-
-def products(place, high, low, top, bottom, block, mine, across, corner):
-    e = block.shape[0] // 2
-    return call(
-        products_kernel,
-        "products",
+        held[...] = -dot3([pick(x, 1) for x in (top, bottom)], right, NT)
+        wait(put(out, place, held, 0, 1, sem))
+
+
+def corner_block(place, before, top, bottom, a3, c31, passed):
+    e = before.shape[1] // 4
+    return call(
+        corner_kernel,
+        "corner_block",
         500 * 10**6,
-        [((1, 4 * e, 4 * e), F32), ((2 * e, 2 * e), F32)],
-        [(SMEM, place)]
-        + [(VMEM, x) for x in (high, low, top, bottom, block, *mine, *across, *corner)],
-        [pltpu.VMEM((2 * e, 3 * e), F32)],
-    )
+        [(before.shape, F32)],
+        [(SMEM, place), (HBM, before)] + [(VMEM, x) for x in (top, bottom, a3, c31, passed)],
+        [pltpu.VMEM((2 * e, 2 * e), F32), pltpu.SemaphoreType.DMA((4,))],
+        out_specs=[HBM],
+        input_output_aliases={1: 0},
+    )[0]
 
 
 def finish_kernel(
-    place, before, high, low, block, part, third, passed, last, swapped, rest, a3, c31, out, held, scratch, sem
+    place, before, high, low, part, passed, last, swapped, rest, a3, c31, out, held, scratch, sem
 ):
     e = out.shape[1] // 4
     tiles = e // T
     n_sym = symmetric_tiles(e)
-
-    def targets(b):
-        return [
-            (
-                held.at[pl.ds(r * e, e), pl.ds((2 * b + c) * e, e)],
-                out.at[0, spot(place, e, r, 1), spot(place, e, c, b)],
-            )
-            for r in range(2)
-            for c in range(2)
-        ]
-
     n_last = last.shape[0] // T
 
     @pl.when(place[0] == place[1])
     def _():
-        skip = passed.shape[0] // T - n_last
         for at, (i, j) in enumerate(upper(2 * tiles)):
-            ref, at = (last, at) if at < n_last else (passed, at - n_last + skip)
+            ref, at = (last, at) if at < n_last else (passed, at - n_last)
             piece = ref[at * T : (at + 1) * T, :]
             r, c = slice(i * T, (i + 1) * T), slice(j * T, (j + 1) * T)
-            shift = 2 * e
-            held[r, j * T + shift : (j + 1) * T + shift] = block[r, c] + piece
+            held[0, r, c] = part[r, c] + piece
             if i != j:
-                held[c, i * T + shift : (i + 1) * T + shift] = block[c, r] + piece.T
-        run_copies(targets(1), sem)
+                held[0, c, r] = part[c, r] + piece.T
+        wait(put(out, place, held.at[0], 1, 1, sem.at[0]))
 
     @pl.when(place[0] != place[1])
     def _():
-        first = third[: third.shape[0] - n_last * T, :]
-        late = cross_block(zeros(FIRST + SECOND), (first, 0), (last, 0))[:, e:]
+        late = cross_block(zeros(FIRST + SECOND), (last, 0))[:, e:]
         inner = slice(2 * e, 3 * e)
-        scratch[...] = part[...] + dot3(split(late), (high[inner], low[inner]))
-        everything = slice(0, 2 * e)
+        start = (2 * tiles * tiles - n_last) // tiles * T
+        scratch[:start, :] = part[:start, :]
+        scratch[start:, :] = part[start:, :] + dot3(split(late[start:]), (high[inner], low[inner]))
         copies = []
         for b in range(2):
             if b == 0:
                 col = cross_block((swapped, n_sym), (rest, 0))
             else:
                 col = cross_block((a3, n_sym), (c31, 0), (passed, 0))
-            left = split(pick(scratch, everything, b))
-            held[:, 2 * e * b : 2 * e * (b + 1)] = -dot3(left, split(col), NT)
-            for i, (source, target) in enumerate(targets(b)):
-                copies.append(pltpu.make_async_copy(source, target, sem.at[4 * b + i]))
-                copies[-1].start()
-        for copy in copies:
-            copy.wait()
-
-
-def finish(place, before, high, low, block, part, third, passed, last, swapped, rest, a3, c31):
+            held[b] = -dot3(split(pick(scratch, b)), split(col), NT)
+            copies += put(out, place, held.at[b], 1, b, sem.at[b])
+        wait(copies)
+
+
+def finish(place, before, high, low, part, passed, last, swapped, rest, a3, c31):
     e = before.shape[1] // 4
     return call(
         finish_kernel,
@@ -626,14 +606,11 @@
         500 * 10**6,
         [(before.shape, F32)],
         [(SMEM, place), (HBM, before)]
-        + [
-            (VMEM, x)
-            for x in (high, low, block, part, third, passed, last, swapped, rest, a3, c31)
-        ],
+        + [(VMEM, x) for x in (high, low, part, passed, last, swapped, rest, a3, c31)],
         [
-            pltpu.VMEM((2 * e, 4 * e), F32),
+            pltpu.VMEM((2, 2 * e, 2 * e), F32),
             pltpu.VMEM((2 * e, 3 * e), F32),
-            pltpu.SemaphoreType.DMA((8,)),
+            pltpu.SemaphoreType.DMA((2, 4)),
         ],
         out_specs=[HBM],
         input_output_aliases={1: 0},
@@ -687,24 +664,18 @@
         rest, b_d = tie(rest, b_d)
         rest = send(rest, True, only=True)
         side = factor_start((a, a_x, swapped, a_d), (b, b_x, b_y, b_d))
-        n_mid = c2.shape[0] // T - n_last
-        theirs = jnp.concatenate([c2[: n_mid * T], swapped[-n_last * T :]])
-        third, side = tie(jnp.where(same, theirs, c2), side)
+        third, side = tie(jnp.where(same, swapped[-n_last * T :], c2), side)
         third = send(third, False)
         c1_d = send(c1_x, True, only=True)
         high, low = factor_end(place, side, (b, b_x, b_y, b_d))
-        top, bottom, block, part = own_rows(
-            place, leaf, high, low, a, c1, c2, a_x, c1_x, swapped, rest
-        )
-        last, third, block = tie(jnp.where(same, c2[n_mid * T :], outer0), third, block)
+        last, third, high = tie(jnp.where(same, c2, outer0), third, high)
         last = send(last, False)
         passed = send(third, True)
-        out, block = products(
-            place, high, low, top, bottom, block, (a, c1, c2), (a_x, c1_x, third), (a_d, c1_d, passed)
+        out, top, bottom, part = first_rows(
+            place, leaf, high, low, (a, c1, c2), (a_x, c1_x, third), swapped, rest
         )
-        return finish(
-            place, out, high, low, block, part, third, passed, last, swapped, rest, a_d, c1_d
-        )
+        out = corner_block(place, out, top, bottom, a_d, c1_d, passed)
+        return finish(place, out, high, low, part, passed, last, swapped, rest, a_d, c1_d)
 
     return jax.shard_map(
         body,

time: 97.5 us -> 104 us (1.067)
  waiting for transfers between devices: 34.2 us -> 40.4 us
  Pallas kernels: 45.7 us -> 47.1 us
  local copies, waits for them, and re-layouts: 2.23 us -> 0.98 us
    ppermute x13, waiting for transfers between devices: 34.2 us -> 40.4 us  [send(): return lax.ppermute(value, ('gx', 'gy'), pairs)]
    pallas_call x10, Pallas kernels: 45.7 us -> 47.1 us  [call(): pl.pallas_call(kernel, out_shape=[jax.ShapeDtypeStruct(shape, dtype) for...]
    unnamed x4 -> x16, local copies, waits for them, and re-layouts: 2.19 us -> 0.98 us
  transfers between devices with their start and end apart: 13 -> 13, of which waited for: 7 -> 9; matrix products, arithmetic and copies ran while one was open for 0% -> 0% of each run, Pallas kernels for 41% -> 36%
where the time goes in v9:
time: 104 us; the launch traced here: 103 us
  Pallas kernels  47.1 us (45%)
  waiting for transfers between devices  40.4 us (39%)
  starting transfers between devices  13.9 us (13%)
    pallas_call x10, Pallas kernels, call(): pl.pallas_call(kernel, out_shape=[jax.ShapeDtypeStruct(shape, dtype) for...  47.1 us
    ppermute x13, waiting for transfers between devices, send(): return lax.ppermute(value, ('gx', 'gy'), pairs)  40.4 us
    ppermute x13, starting transfers between devices, send(): return lax.ppermute(value, ('gx', 'gy'), pairs)  13.9 us
  transfers between devices with their start and end apart: 13, of which 9 were waited for; matrix products, arithmetic and copies ran while one was open for 0% of the time, Pallas kernels for 36%

profile of v9, /device:TPU:24, one launch (start us, length us, event | category | flops | bytes accessed | tf_op | source)
XLA Modules:
  0.0 103.4 jit_solution(5024765207938160132)
XLA Ops:
  0.0 0.6 pad_add_fusion.place
  0.6 2.9 %cut_first.1.a0 = f32[512,128]{1,0:T(8,128)} custom-call(s32[2]{0:T(128)} %pad_add_fusion.place, f32[1,1024,1024]{2,1,0:T(8,128)} %leaf.7), custom_call_target="tpu_custom_call" | custom-call | flops 1000000000 | bytes 1000000000 | tf_op jit(solution)/shard_map/cut_first/pallas_call | solution.py:180
  3.4 0.0 copy-start.2
  3.5 2.4 %cut_side.1.mine = f32[384,128]{1,0:T(8,128)} custom-call(s32[2]{0:T(128)} %pad_add_fusion.place, f32[1,1024,1024]{2,1,0:T(8,128)} %leaf.7), custom_call_target="tpu_custom_call" | custom-call | flops 1000000000 | bytes 1000000000 | tf_op jit(solution)/shard_map/cut_side/pallas_call | solution.py:180
  5.9 0.0 copy-start.3
  5.9 1.6 %collective-permute-start = (f32[384,128]{1,0:T(8,128)}, f32[384,128]{1,0:T(8,128)S(1)}, u32[]{:S(2)}, u32[]{:S(2)}) collective-permute-start(f32[384,128]{1,0:T(8,128)} %cut_side.1.mine), channel_id=1, source_target_pairs={{0,2},{1,3},{2,0},{3,1},{4,6},{5,7},{6,4},{7,5},{8,10},{9,11},{10,... | collective-permute-start | bytes 589832 | tf_op jit(solution)/shard_map/ppermute | solution.py:637
  7.5 0.0 copy-done.2
  7.5 0.3 collective-permute-start.1
  7.8 0.0 copy-done.4
  7.8 0.9 cut_second.1
  8.8 0.6 collective-permute-start.2
  9.3 4.6 %collective-permute-done.along = f32[384,128]{1,0:T(8,128)S(1)} collective-permute-done((f32[384,128]{1,0:T(8,128)}, f32[384,128]{1,0:T(8,128)S(1)}, u32[]{:S(2)}, u32[]{:S(2)}) %collective-permute-start) | collective-permute-done | bytes 196640 | tf_op jit(solution)/shard_map/ppermute | solution.py:637
  14.0 7.0 %gauge_side.1 = (f32[256,256]{1,0:T(8,128)S(1)}, f32[256,256]{1,0:T(8,128)S(1)}) custom-call(f32[384,128]{1,0:T(8,128)S(1)} %copy-done.3, f32[384,128]{1,0:T(8,128)S(1)} %collective-permute-done.along, f32[256,256]{1,0:T(8,128)S(1)} %get-tuple-element.40.b), custom_call_target="tpu_custom_call" | custom-call | flops 8000000000 | bytes 8000000000 | tf_op jit(solution)/shard_map/gauge_side/pallas_call | solution.py:180
  21.0 0.0 copy-start.6
  21.0 0.1 collective-permute-start.5
  21.1 0.4 scale_cross.1
  21.5 0.0 copy-start.5
  21.5 0.1 collective-permute-done.1.a1
  21.6 2.4 %collective-permute-done.2.a2.swapped = f32[1024,128]{1,0:T(8,128)S(1)} collective-permute-done((f32[1024,128]{1,0:T(8,128)S(1)}, f32[1024,128]{1,0:T(8,128)S(1)}, u32[]{:S(2)}, u32[]{:S(2)}) %collective-permute-start.2) | collective-permute-done | bytes 524320 | tf_op jit(solution)/shard_map/ppermute | solution.py:637
  24.0 1.5 %collective-permute-start.3 = (f32[256,256]{1,0:T(8,128)S(1)}, f32[256,256]{1,0:T(8,128)}, u32[]{:S(2)}, u32[]{:S(2)}) collective-permute-start(f32[256,256]{1,0:T(8,128)S(1)} %get-tuple-element.51.b0), channel_id=1, source_target_pairs={{0,2},{1,3},{2,0},{3,1},{4,6},{5,7},{6,4},{7,5},{8,10},{9,11},{10,... | collective-permute-start | bytes 786440 | tf_op jit(solution)/shard_map/ppermute | solution.py:637
  25.6 8.1 %collective-permute-done.5.b1 = f32[256,256]{1,0:T(8,128)} collective-permute-done((f32[256,256]{1,0:T(8,128)S(1)}, f32[256,256]{1,0:T(8,128)}, u32[]{:S(2)}, u32[]{:S(2)}) %collective-permute-start.5) | collective-permute-done | bytes 262176 | tf_op jit(solution)/shard_map/ppermute | solution.py:637
  33.6 0.0 collective-permute-start.8
  33.6 0.0 collective-permute-done.3.b2
  33.6 1.5 %collective-permute-start.6 = (f32[256,256]{1,0:T(8,128)}, f32[256,256]{1,0:T(8,128)S(1)}, u32[]{:S(2)}, u32[]{:S(2)}) collective-permute-start(f32[256,256]{1,0:T(8,128)} %collective-permute-done.5.b1), channel_id=1, source_target_pairs={{0,2},{1,3},{2,0},{3,1},{4,6},{5,7},{6,4},{7,5},{8,10},{9,11},{10,... | collective-permute-start | bytes 786440 | tf_op jit(solution)/shard_map/ppermute | solution.py:637
  35.1 0.5 collective-permute-start.4
  35.7 0.1 slice_select_fusion
  35.7 7.3 %collective-permute-done.6.b3 = f32[256,256]{1,0:T(8,128)S(1)} collective-permute-done((f32[256,256]{1,0:T(8,128)}, f32[256,256]{1,0:T(8,128)S(1)}, u32[]{:S(2)}, u32[]{:S(2)}) %collective-permute-start.6) | collective-permute-done | bytes 262176 | tf_op jit(solution)/shard_map/ppermute | solution.py:637
  43.0 1.5 %collective-permute-start.9 = (f32[1408,128]{1,0:T(8,128)}, f32[1408,128]{1,0:T(8,128)S(1)}, u32[]{:S(2)}, u32[]{:S(2)}) collective-permute-start(f32[1408,128]{1,0:T(8,128)} %copy-done.5), channel_id=1, source_target_pairs={{0,2},{1,3},{4,6},{5,7},{8,10},{9,11},{12,14},{13,15},{18,16},{19,... | collective-permute-start | bytes 2162696 | tf_op jit(solution)/shard_map/ppermute | solution.py:637
  44.5 4.1 %collective-permute-done.4.a3 = f32[512,128]{1,0:T(8,128)S(1)} collective-permute-done((f32[512,128]{1,0:T(8,128)S(1)}, f32[512,128]{1,0:T(8,128)S(1)}, u32[]{:S(2)}, u32[]{:S(2)}) %collective-permute-start.4) | collective-permute-done | bytes 262176 | tf_op jit(solution)/shard_map/ppermute | solution.py:637
  48.7 0.0 copy-done.6
  48.7 10.5 %factor_start.1.side_in = f32[512,512]{1,0:T(8,128)S(1)} custom-call(f32[512,128]{1,0:T(8,128)S(1)} %copy-done.2, f32[512,128]{1,0:T(8,128)S(1)} %collective-permute-done.1.a1, f32[1024,128]{1,0:T(8,128)S(1)} %collective-permute-done.2.a2.swapped, f32[512,128]{1,0:T(8,128)S(1)} %collective-permute-done.4.a3, f32[256,256]{1,0:T(8,128)S(1)} %get-tuple-element.51.b0, ...), custom_call_target="tpu_custom_call" | custom-call | flops 3500000000 | bytes 3500000000 | tf_op jit(solution)/shard_map/factor_start/pallas_call | solution.py:180
  59.2 0.0 copy-start.1
  59.2 2.1 %collective-permute-start.7 = (f32[640,128]{1,0:T(8,128)S(1)}, f32[640,128]{1,0:T(8,128)S(1)}, u32[]{:S(2)}, u32[]{:S(2)}) collective-permute-start(f32[640,128]{1,0:T(8,128)S(1)} %get-tuple-element.60), channel_id=1, source_target_pairs={{0,16},{1,17},{2,18},{3,19},{4,20},{5,21},{6,22},{7,23},{8,24},{9,... | collective-permute-start | bytes 983048 | tf_op jit(solution)/shard_map/ppermute | solution.py:637
  61.2 7.9 %collective-permute-done.8.c11 = f32[1280,128]{1,0:T(8,128)S(1)} collective-permute-done((f32[1280,128]{1,0:T(8,128)S(1)}, f32[1280,128]{1,0:T(8,128)S(1)}, u32[]{:S(2)}, u32[]{:S(2)}) %collective-permute-start.8) | collective-permute-done | bytes 655392 | tf_op jit(solution)/shard_map/ppermute | solution.py:637
  69.1 1.5 %collective-permute-start.10 = (f32[1280,128]{1,0:T(8,128)S(1)}, f32[1280,128]{1,0:T(8,128)S(1)}, u32[]{:S(2)}, u32[]{:S(2)}) collective-permute-start(f32[1280,128]{1,0:T(8,128)S(1)} %collective-permute-done.8.c11), channel_id=1, source_target_pairs={{0,2},{1,3},{4,6},{5,7},{8,10},{9,11},{12,14},{13,15},{18,16},{19,... | collective-permute-start | bytes 1966088 | tf_op jit(solution)/shard_map/ppermute | solution.py:637
  70.6 0.0 copy-start.7
  70.6 0.9 copy-done.7
  71.6 11.2 %factor_end.1 = (bf16[768,768]{1,0:T(8,128)(2,1)S(1)}, bf16[768,768]{1,0:T(8,128)(2,1)S(1)}) custom-call(s32[2]{0:T(128)S(1)} %copy-done.4, f32[512,512]{1,0:T(8,128)S(1)} %factor_start.1.side_in, f32[256,256]{1,0:T(8,128)S(1)} %copy-done.7, f32[256,256]{1,0:T(8,128)} %collective-permute-done.5.b1, f32[256,256]{1,0:T(8,128)} %collective-permute-done.3.b2, ...), custom_call_target="tpu_custom_call" | custom-call | flops 10000000000 | bytes 10000000000 | tf_op jit(solution)/shard_map/factor_end/pallas_call | solution.py:180
  82.8 0.0 collective-permute-done.7.third
  82.8 2.7 %collective-permute-start.11 = (f32[640,128]{1,0:T(8,128)S(1)}, f32[640,128]{1,0:T(8,128)S(1)}, u32[]{:S(2)}, u32[]{:S(2)}) collective-permute-start(f32[640,128]{1,0:T(8,128)S(1)} %collective-permute-done.7.third), channel_id=1, source_target_pairs={{0,2},{1,3},{2,0},{3,1},{4,6},{5,7},{6,4},{7,5},{8,10},{9,11},{10,... | collective-permute-start | bytes 983048 | tf_op jit(solution)/shard_map/ppermute | solution.py:637
  85.5 0.0 collective-permute-start.12
  85.5 0.0 collective-permute-done.9.rest
  85.5 4.9 %first_rows.1 = (f32[1,1024,1024]{2,1,0:T(8,128)}, bf16[512,768]{1,0:T(8,128)(2,1)S(1)}, bf16[512,768]{1,0:T(8,128)(2,1)S(1)}, f32[512,768]{1,0:T(8,128)S(1)}) custom-call(s32[2]{0:T(128)S(1)} %copy-done.4, f32[1,1024,1024]{2,1,0:T(8,128)S(1)} %copy-done.1, bf16[768,768]{1,0:T(8,128)(2,1)S(1)} %get-tuple-element.63.high, ...), custom_call_target="tpu_custom_call" | custom-call | flops 500000000 | bytes 500000000 | tf_op jit(solution)/shard_map/first_rows/pallas_call | solution.py:180
  90.5 4.1 %collective-permute-done.11.passed = f32[640,128]{1,0:T(8,128)S(1)} collective-permute-done((f32[640,128]{1,0:T(8,128)S(1)}, f32[640,128]{1,0:T(8,128)S(1)}, u32[]{:S(2)}, u32[]{:S(2)}) %collective-permute-start.11) | collective-permute-done | bytes 327712 | tf_op jit(solution)/shard_map/ppermute | solution.py:637
  94.6 0.0 collective-permute-done.10.c31
  94.6 2.6 %corner_block.1.before = f32[1,1024,1024]{2,1,0:T(8,128)} custom-call(s32[2]{0:T(128)S(1)} %copy-done.4, f32[1,1024,1024]{2,1,0:T(8,128)} %get-tuple-element.68.before, bf16[512,768]{1,0:T(8,128)(2,1)S(1)} %get-tuple-element.69.top, bf16[512,768]{1,0:T(8,128)(2,1)S(1)} %get-tuple-element.70.bottom, ...), custom_call_target="tpu_custom_call", output_to_operand_aliasing={{}: (1, {})} | custom-call | flops 500000000 | bytes 500000000 | tf_op jit(solution)/shard_map/corner_block/pallas_call | solution.py:180
  97.2 1.7 %collective-permute-done.12.last = f32[640,128]{1,0:T(8,128)S(1)} collective-permute-done((f32[640,128]{1,0:T(8,128)S(1)}, f32[640,128]{1,0:T(8,128)S(1)}, u32[]{:S(2)}, u32[]{:S(2)}) %collective-permute-start.12) | collective-permute-done | bytes 327712 | tf_op jit(solution)/shard_map/ppermute | solution.py:637
  98.9 4.3 %finish.1 = f32[1,1024,1024]{2,1,0:T(8,128)} custom-call(s32[2]{0:T(128)S(1)} %copy-done.4, f32[1,1024,1024]{2,1,0:T(8,128)} %corner_block.1.before, bf16[768,768]{1,0:T(8,128)(2,1)S(1)} %get-tuple-element.63.high, bf16[768,768]{1,0:T(8,128)(2,1)S(1)} %get-tuple-element.64.low, ...), custom_call_target="tpu_custom_call", output_to_operand_aliasing={{}: (1, {})} | custom-call | flops 500000000 | bytes 500000000 | tf_op jit(solution)/shard_map/finish/pallas_call | solution.py:180
  (6 shorter events, 0.0 us)
Async XLA Ops:
  0.6 7.2 %copy-start = (f32[1,1024,1024]{2,1,0:T(8,128)S(1)}, f32[1,1024,1024]{2,1,0:T(8,128)}, u32[]{:S(2)}) copy-start(f32[1,1024,1024]{2,1,0:T(8,128)} %leaf.7) | copy-start | bytes 12582916
  0.6 7.2 %copy-start.4 = (s32[2]{0:T(128)S(1)}, s32[2]{0:T(128)}, u32[]{:S(2)}) copy-start(s32[2]{0:T(128)} %pad_add_fusion.place) | copy-start | bytes 28
  3.4 4.0 %copy-start.2 = (f32[512,128]{1,0:T(8,128)S(1)}, f32[512,128]{1,0:T(8,128)}, u32[]{:S(2)}) copy-start(f32[512,128]{1,0:T(8,128)} %cut_first.1.a0) | copy-start | bytes 786436
  5.9 8.1 %copy-start.3 = (f32[384,128]{1,0:T(8,128)S(1)}, f32[384,128]{1,0:T(8,128)}, u32[]{:S(2)}) copy-start(f32[384,128]{1,0:T(8,128)} %cut_side.1.mine) | copy-start | bytes 589828
  5.9 8.1 %collective-permute-start = (f32[384,128]{1,0:T(8,128)}, f32[384,128]{1,0:T(8,128)S(1)}, u32[]{:S(2)}, u32[]{:S(2)}) collective-permute-start(f32[384,128]{1,0:T(8,128)} %cut_side.1.mine), channel_id=1, source_target_pairs={{0,2},{1,3},{2,0},{3,1},{4,6},{5,7},{6,4},{7,5},{8,10},{9,11},{10,... | collective-permute-start | bytes 589832 | tf_op jit(solution)/shard_map/ppermute | solution.py:637
  7.5 14.2 %collective-permute-start.1 = (f32[512,128]{1,0:T(8,128)S(1)}, f32[512,128]{1,0:T(8,128)S(1)}, u32[]{:S(2)}, u32[]{:S(2)}) collective-permute-start(f32[512,128]{1,0:T(8,128)S(1)} %copy-done.2), channel_id=1, source_target_pairs={{0,16},{1,17},{2,18},{3,19},{4,20},{5,21},{6,22},{7,23},{8,24},{9,... | collective-permute-start | bytes 786440 | tf_op jit(solution)/shard_map/ppermute | solution.py:637
  8.8 15.3 %collective-permute-start.2 = (f32[1024,128]{1,0:T(8,128)S(1)}, f32[1024,128]{1,0:T(8,128)S(1)}, u32[]{:S(2)}, u32[]{:S(2)}) collective-permute-start(f32[1024,128]{1,0:T(8,128)S(1)} %get-tuple-element.47), channel_id=1, source_target_pairs={{0,2},{1,3},{2,0},{3,1},{4,6},{5,7},{6,4},{7,5},{8,10},{9,11},{10,... | collective-permute-start | bytes 1572872 | tf_op jit(solution)/shard_map/ppermute | solution.py:637
  21.0 27.7 %copy-start.6 = (f32[256,256]{1,0:T(8,128)}, f32[256,256]{1,0:T(8,128)S(1)}, u32[]{:S(2)}) copy-start(f32[256,256]{1,0:T(8,128)S(1)} %get-tuple-element.51.b0) | copy-start | bytes 786436
  21.0 12.6 %collective-permute-start.5 = (f32[256,256]{1,0:T(8,128)S(1)}, f32[256,256]{1,0:T(8,128)}, u32[]{:S(2)}, u32[]{:S(2)}) collective-permute-start(f32[256,256]{1,0:T(8,128)S(1)} %get-tuple-element.51.b0), channel_id=1, source_target_pairs={{0,16},{1,17},{2,18},{3,19},{4,20},{5,21},{6,22},{7,23},{8,24},{9,... | collective-permute-start | bytes 786440 | tf_op jit(solution)/shard_map/ppermute | solution.py:637
  21.5 4.1 %copy-start.5 = (f32[1408,128]{1,0:T(8,128)}, f32[1408,128]{1,0:T(8,128)S(1)}, u32[]{:S(2)}) copy-start(f32[1408,128]{1,0:T(8,128)S(1)} %get-tuple-element.67) | copy-start | bytes 2162692
  24.0 9.6 %collective-permute-start.3 = (f32[256,256]{1,0:T(8,128)S(1)}, f32[256,256]{1,0:T(8,128)}, u32[]{:S(2)}, u32[]{:S(2)}) collective-permute-start(f32[256,256]{1,0:T(8,128)S(1)} %get-tuple-element.51.b0), channel_id=1, source_target_pairs={{0,2},{1,3},{2,0},{3,1},{4,6},{5,7},{6,4},{7,5},{8,10},{9,11},{10,... | collective-permute-start | bytes 786440 | tf_op jit(solution)/shard_map/ppermute | solution.py:637
  33.6 35.5 %collective-permute-start.8 = (f32[1280,128]{1,0:T(8,128)S(1)}, f32[1280,128]{1,0:T(8,128)S(1)}, u32[]{:S(2)}, u32[]{:S(2)}) collective-permute-start(f32[1280,128]{1,0:T(8,128)S(1)} %get-tuple-element.65.c01), channel_id=1, source_target_pairs={{0,16},{1,17},{2,18},{3,19},{4,20},{5,21},{6,22},{7,23},{8,24},{9,... | collective-permute-start | bytes 1966088 | tf_op jit(solution)/shard_map/ppermute | solution.py:637
  33.6 9.4 %collective-permute-start.6 = (f32[256,256]{1,0:T(8,128)}, f32[256,256]{1,0:T(8,128)S(1)}, u32[]{:S(2)}, u32[]{:S(2)}) collective-permute-start(f32[256,256]{1,0:T(8,128)} %collective-permute-done.5.b1), channel_id=1, source_target_pairs={{0,2},{1,3},{2,0},{3,1},{4,6},{5,7},{6,4},{7,5},{8,10},{9,11},{10,... | collective-permute-start | bytes 786440 | tf_op jit(solution)/shard_map/ppermute | solution.py:637
  35.1 13.5 %collective-permute-start.4 = (f32[512,128]{1,0:T(8,128)S(1)}, f32[512,128]{1,0:T(8,128)S(1)}, u32[]{:S(2)}, u32[]{:S(2)}) collective-permute-start(f32[512,128]{1,0:T(8,128)S(1)} %collective-permute-done.1.a1), channel_id=1, source_target_pairs={{0,2},{1,3},{2,0},{3,1},{4,6},{5,7},{6,4},{7,5},{8,10},{9,11},{10,... | collective-permute-start | bytes 786440 | tf_op jit(solution)/shard_map/ppermute | solution.py:637
  43.0 42.5 %collective-permute-start.9 = (f32[1408,128]{1,0:T(8,128)}, f32[1408,128]{1,0:T(8,128)S(1)}, u32[]{:S(2)}, u32[]{:S(2)}) collective-permute-start(f32[1408,128]{1,0:T(8,128)} %copy-done.5), channel_id=1, source_target_pairs={{0,2},{1,3},{4,6},{5,7},{8,10},{9,11},{12,14},{13,15},{18,16},{19,... | collective-permute-start | bytes 2162696 | tf_op jit(solution)/shard_map/ppermute | solution.py:637
  59.2 26.4 %copy-start.1 = (f32[1,1024,1024]{2,1,0:T(8,128)S(1)}, f32[1,1024,1024]{2,1,0:T(8,128)}, u32[]{:S(2)}) copy-start(f32[1,1024,1024]{2,1,0:T(8,128)} %leaf.7) | copy-start | bytes 12582916
  59.2 23.6 %collective-permute-start.7 = (f32[640,128]{1,0:T(8,128)S(1)}, f32[640,128]{1,0:T(8,128)S(1)}, u32[]{:S(2)}, u32[]{:S(2)}) collective-permute-start(f32[640,128]{1,0:T(8,128)S(1)} %get-tuple-element.60), channel_id=1, source_target_pairs={{0,16},{1,17},{2,18},{3,19},{4,20},{5,21},{6,22},{7,23},{8,24},{9,... | collective-permute-start | bytes 983048 | tf_op jit(solution)/shard_map/ppermute | solution.py:637
  69.1 25.5 %collective-permute-start.10 = (f32[1280,128]{1,0:T(8,128)S(1)}, f32[1280,128]{1,0:T(8,128)S(1)}, u32[]{:S(2)}, u32[]{:S(2)}) collective-permute-start(f32[1280,128]{1,0:T(8,128)S(1)} %collective-permute-done.8.c11), channel_id=1, source_target_pairs={{0,2},{1,3},{4,6},{5,7},{8,10},{9,11},{12,14},{13,15},{18,16},{19,... | collective-permute-start | bytes 1966088 | tf_op jit(solution)/shard_map/ppermute | solution.py:637
  70.6 1.0 copy-start.7
  82.8 11.8 %collective-permute-start.11 = (f32[640,128]{1,0:T(8,128)S(1)}, f32[640,128]{1,0:T(8,128)S(1)}, u32[]{:S(2)}, u32[]{:S(2)}) collective-permute-start(f32[640,128]{1,0:T(8,128)S(1)} %collective-permute-done.7.third), channel_id=1, source_target_pairs={{0,2},{1,3},{2,0},{3,1},{4,6},{5,7},{6,4},{7,5},{8,10},{9,11},{10,... | collective-permute-start | bytes 983048 | tf_op jit(solution)/shard_map/ppermute | solution.py:637
  85.5 13.4 %collective-permute-start.12 = (f32[640,128]{1,0:T(8,128)S(1)}, f32[640,128]{1,0:T(8,128)S(1)}, u32[]{:S(2)}, u32[]{:S(2)}) collective-permute-start(f32[640,128]{1,0:T(8,128)S(1)} %get-tuple-element.72), channel_id=1, source_target_pairs={{0,16},{1,17},{2,18},{3,19},{4,20},{5,21},{6,22},{7,23},{8,24},{9,... | collective-permute-start | bytes 983048 | tf_op jit(solution)/shard_map/ppermute | solution.py:637

commit v10 on v9

--- a/solution.py
+++ b/solution.py
@@ -10,7 +10,6 @@
 F32 = jnp.float32
 BF16 = jnp.bfloat16
 T = 128
-ALONE = 59
 R = 16
 FIRST = 1
 SECOND = 10
@@ -176,14 +175,14 @@
     )
 
 
-def call(kernel, name, cost, outs, ins, scratch, room=32, **more):
+def call(kernel, name, cost, outs, ins, scratch, **more):
     return pl.pallas_call(
         kernel,
         out_shape=[jax.ShapeDtypeStruct(shape, dtype) for shape, dtype in outs],
         in_specs=[spec for spec, _ in ins],
         out_specs=more.pop("out_specs", [VMEM] * len(outs)),
         scratch_shapes=scratch,
-        compiler_params=pltpu.CompilerParams(vmem_limit_bytes=room * 2**20),
+        compiler_params=pltpu.CompilerParams(vmem_limit_bytes=32 * 2**20),
         cost_estimate=pl.CostEstimate(flops=cost, bytes_accessed=cost, transcendentals=0),
         name=name,
         **more,
@@ -223,7 +222,6 @@
         [(((n_sym + FIRST) * T, T), F32)],
         [(SMEM, place), (FAR, leaf)],
         [pltpu.SemaphoreType.DMA((n_sym + FIRST,))],
-        room=ALONE,
     )[0]
 
 
@@ -245,7 +243,6 @@
         [((n_sym * T, T), F32)],
         [(SMEM, place), (FAR, leaf)],
         [pltpu.SemaphoreType.DMA((n_sym,))],
-        room=ALONE,
     )[0]
 
 
@@ -380,10 +377,27 @@
     )[0]
 
 
+def factor_middle_kernel(before, side):
+    side[...] = before[...]
+    half = side.shape[0] // 2
+    sweep(side, half, half + T)
+
+
+def factor_middle(side):
+    return call(
+        factor_middle_kernel,
+        "factor_middle",
+        4000 * 10**6,
+        [(side.shape, F32)],
+        [(VMEM, side)],
+        [],
+    )[0]
+
+
 def factor_end_kernel(place, side_in, b0, b1, b2, b3, high, low, side, full):
     e = b0.shape[0]
     side[...] = side_in[...]
-    sweep(side, e, 2 * e)
+    sweep(side, e + T, 2 * e)
     coup = split(couple((b0, b1, b2, b3)))
     away = dot3(split(side[...]), coup)
     shape = full.shape
@@ -414,7 +428,7 @@
     return call(
         factor_end_kernel,
         "factor_end",
-        10000 * 10**6,
+        3000 * 10**6,
         [((3 * e, 3 * e), BF16)] * 2,
         [(SMEM, place), (VMEM, side)] + [(VMEM, x) for x in b],
         [pltpu.VMEM((2 * e, 2 * e), F32), pltpu.VMEM((2 * e, 2 * e), F32)],
@@ -655,17 +669,18 @@
         c1, c2, rest = scale_cross(factor, c, n_last)
         b, a_x, c1, swapped = tie(b, a_x, c1, swapped)
         b_y = send(b, True)
-        a_x, b_y = tie(a_x, b_y)
         a_d = send(a_x, True)
         c1, b_x = tie(c1, b_x)
         c1_x = send(c1, False)
-        b_x, b_y = tie(b_x, b_y)
+        b_x, b_y, a_d = tie(b_x, b_y, a_d)
         b_d = send(b_x, True)
         rest, b_d = tie(rest, b_d)
         rest = send(rest, True, only=True)
         side = factor_start((a, a_x, swapped, a_d), (b, b_x, b_y, b_d))
+        side = factor_middle(side)
         third, side = tie(jnp.where(same, swapped[-n_last * T :], c2), side)
         third = send(third, False)
+        c1_x, side = tie(c1_x, side)
         c1_d = send(c1_x, True, only=True)
         high, low = factor_end(place, side, (b, b_x, b_y, b_d))
         last, third, high = tie(jnp.where(same, c2, outer0), third, high)

time: 104 us -> 100 us (0.962)
  Pallas kernels: 47.1 us -> 43.9 us
  waiting for transfers between devices: 40.4 us -> 37.9 us
  starting transfers between devices: 13.9 us -> 15.7 us
  local copies, waits for them, and re-layouts: 0.98 us -> 2.19 us
    pallas_call x10 -> x11, Pallas kernels: 47.1 us -> 43.9 us  [call(): pl.pallas_call(kernel, out_shape=[jax.ShapeDtypeStruct(shape, dtype) for...]
    ppermute x13, waiting for transfers between devices: 40.4 us -> 37.9 us  [send(): return lax.ppermute(value, ('gx', 'gy'), pairs)]
    ppermute x13, starting transfers between devices: 13.9 us -> 15.7 us  [send(): return lax.ppermute(value, ('gx', 'gy'), pairs)]
    unnamed x16 -> x4, local copies, waits for them, and re-layouts: 0.98 us -> 2.19 us
  transfers between devices with their start and end apart: 13 -> 13, of which waited for: 9 -> 7; matrix products, arithmetic and copies ran while one was open for 0% -> 0% of each run, Pallas kernels for 36% -> 38%
where the time goes in v10:
time: 100 us
  Pallas kernels  43.9 us (44%)
  waiting for transfers between devices  37.9 us (38%)
  starting transfers between devices  15.7 us (16%)
  local copies, waits for them, and re-layouts  2.19 us (2%)
    pallas_call x11, Pallas kernels, call(): pl.pallas_call(kernel, out_shape=[jax.ShapeDtypeStruct(shape, dtype) for...  43.9 us
    ppermute x13, waiting for transfers between devices, send(): return lax.ppermute(value, ('gx', 'gy'), pairs)  37.9 us
    ppermute x13, starting transfers between devices, send(): return lax.ppermute(value, ('gx', 'gy'), pairs)  15.7 us
    unnamed x4, local copies, waits for them, and re-layouts  2.19 us
  transfers between devices with their start and end apart: 13, of which 7 were waited for; matrix products, arithmetic and copies ran while one was open for 0% of the time, Pallas kernels for 38%

profile of v10, /device:TPU:24, one launch (start us, length us, event | category | flops | bytes accessed | tf_op | source)
XLA Modules:
  0.0 100.2 jit_solution(4949771975626587646)
XLA Ops:
  0.0 0.1 pad_add_fusion.place
  0.1 0.0 copy-start
  0.1 2.2 %copy-done = f32[1,1024,1024]{2,1,0:T(8,128)S(1)} copy-done((f32[1,1024,1024]{2,1,0:T(8,128)S(1)}, f32[1,1024,1024]{2,1,0:T(8,128)}, u32[]{:S(2)}) %copy-start) | copy-done | bytes 4194328
  2.3 0.6 cut_first.1.a0
  2.9 0.6 cut_side.1.mine
  3.5 1.6 %collective-permute-start = (f32[384,128]{1,0:T(8,128)S(1)}, f32[384,128]{1,0:T(8,128)S(1)}, u32[]{:S(2)}, u32[]{:S(2)}) collective-permute-start(f32[384,128]{1,0:T(8,128)S(1)} %cut_side.1.mine), channel_id=1, source_target_pairs={{0,2},{1,3},{2,0},{3,1},{4,6},{5,7},{6,4},{7,5},{8,10},{9,11},{10,... | collective-permute-start | bytes 589832 | tf_op jit(solution)/shard_map/ppermute | solution.py:651
  5.1 0.3 collective-permute-start.1
  5.4 0.9 cut_second.1
  6.4 0.6 collective-permute-start.2
  7.0 4.4 %collective-permute-done.along = f32[384,128]{1,0:T(8,128)S(1)} collective-permute-done((f32[384,128]{1,0:T(8,128)S(1)}, f32[384,128]{1,0:T(8,128)S(1)}, u32[]{:S(2)}, u32[]{:S(2)}) %collective-permute-start) | collective-permute-done | bytes 196640 | tf_op jit(solution)/shard_map/ppermute | solution.py:651
  11.4 7.8 %gauge_side.1 = (f32[256,256]{1,0:T(8,128)}, f32[256,256]{1,0:T(8,128)S(1)}) custom-call(f32[384,128]{1,0:T(8,128)S(1)} %cut_side.1.mine, f32[384,128]{1,0:T(8,128)S(1)} %collective-permute-done.along, f32[256,256]{1,0:T(8,128)S(1)} %get-tuple-element.41.b), custom_call_target="tpu_custom_call" | custom-call | flops 8000000000 | bytes 8000000000 | tf_op jit(solution)/shard_map/gauge_side/pallas_call | solution.py:179
  19.1 0.0 collective-permute-start.3
  19.1 0.4 scale_cross.1
  19.6 0.0 collective-permute-done.1.a1
  19.6 1.9 %collective-permute-done.2.a2.swapped = f32[1024,128]{1,0:T(8,128)S(1)} collective-permute-done((f32[1024,128]{1,0:T(8,128)S(1)}, f32[1024,128]{1,0:T(8,128)S(1)}, u32[]{:S(2)}, u32[]{:S(2)}) %collective-permute-start.2) | collective-permute-done | bytes 524320 | tf_op jit(solution)/shard_map/ppermute | solution.py:651
  21.5 1.5 %collective-permute-start.5 = (f32[512,128]{1,0:T(8,128)S(1)}, f32[512,128]{1,0:T(8,128)S(1)}, u32[]{:S(2)}, u32[]{:S(2)}) collective-permute-start(f32[512,128]{1,0:T(8,128)S(1)} %collective-permute-done.1.a1), channel_id=1, source_target_pairs={{0,2},{1,3},{2,0},{3,1},{4,6},{5,7},{6,4},{7,5},{8,10},{9,11},{10,... | collective-permute-start | bytes 786440 | tf_op jit(solution)/shard_map/ppermute | solution.py:651
  23.0 0.5 collective-permute-start.4
  23.5 8.4 %collective-permute-done.3.b1 = f32[256,256]{1,0:T(8,128)} collective-permute-done((f32[256,256]{1,0:T(8,128)}, f32[256,256]{1,0:T(8,128)}, u32[]{:S(2)}, u32[]{:S(2)}) %collective-permute-start.3) | collective-permute-done | bytes 262176 | tf_op jit(solution)/shard_map/ppermute | solution.py:651
  31.9 0.0 collective-permute-start.8
  31.9 0.0 collective-permute-done.5.a3
  31.9 2.5 %collective-permute-done.4.b2 = f32[256,256]{1,0:T(8,128)} collective-permute-done((f32[256,256]{1,0:T(8,128)}, f32[256,256]{1,0:T(8,128)}, u32[]{:S(2)}, u32[]{:S(2)}) %collective-permute-start.4) | collective-permute-done | bytes 262176 | tf_op jit(solution)/shard_map/ppermute | solution.py:651
  34.4 1.5 %collective-permute-start.6 = (f32[256,256]{1,0:T(8,128)}, f32[256,256]{1,0:T(8,128)S(1)}, u32[]{:S(2)}, u32[]{:S(2)}) collective-permute-start(f32[256,256]{1,0:T(8,128)} %collective-permute-done.3.b1), channel_id=1, source_target_pairs={{0,2},{1,3},{2,0},{3,1},{4,6},{5,7},{6,4},{7,5},{8,10},{9,11},{10,... | collective-permute-start | bytes 786440 | tf_op jit(solution)/shard_map/ppermute | solution.py:651
  35.9 0.1 slice_select_fusion
  35.9 5.0 %collective-permute-done.6.b3 = f32[256,256]{1,0:T(8,128)S(1)} collective-permute-done((f32[256,256]{1,0:T(8,128)}, f32[256,256]{1,0:T(8,128)S(1)}, u32[]{:S(2)}, u32[]{:S(2)}) %collective-permute-start.6) | collective-permute-done | bytes 262176 | tf_op jit(solution)/shard_map/ppermute | solution.py:651
  40.9 1.5 %collective-permute-start.9 = (f32[1408,128]{1,0:T(8,128)S(1)}, f32[1408,128]{1,0:T(8,128)S(1)}, u32[]{:S(2)}, u32[]{:S(2)}) collective-permute-start(f32[1408,128]{1,0:T(8,128)S(1)} %get-tuple-element.69), channel_id=1, source_target_pairs={{0,2},{1,3},{4,6},{5,7},{8,10},{9,11},{12,14},{13,15},{18,16},{19,... | collective-permute-start | bytes 2162696 | tf_op jit(solution)/shard_map/ppermute | solution.py:651
  42.4 10.6 %factor_start.1.before = f32[512,512]{1,0:T(8,128)S(1)} custom-call(f32[512,128]{1,0:T(8,128)S(1)} %cut_first.1.a0, f32[512,128]{1,0:T(8,128)S(1)} %collective-permute-done.1.a1, f32[1024,128]{1,0:T(8,128)S(1)} %collective-permute-done.2.a2.swapped, f32[512,128]{1,0:T(8,128)S(1)} %collective-permute-done.5.a3, f32[256,256]{1,0:T(8,128)} %get-tuple-element.54.b0, ...), custom_call_target="tpu_custom_call" | custom-call | flops 3500000000 | bytes 3500000000 | tf_op jit(solution)/shard_map/factor_start/pallas_call | solution.py:179
  53.0 4.0 %factor_middle.1.side_in = f32[512,512]{1,0:T(8,128)S(1)} custom-call(f32[512,512]{1,0:T(8,128)S(1)} %factor_start.1.before), custom_call_target="tpu_custom_call" | custom-call | flops 4000000000 | bytes 4000000000 | tf_op jit(solution)/shard_map/factor_middle/pallas_call | solution.py:179
  57.0 0.0 copy-start.1
  57.0 3.9 %collective-permute-start.7 = (f32[640,128]{1,0:T(8,128)S(1)}, f32[640,128]{1,0:T(8,128)S(1)}, u32[]{:S(2)}, u32[]{:S(2)}) collective-permute-start(f32[640,128]{1,0:T(8,128)S(1)} %get-tuple-element.60), channel_id=1, source_target_pairs={{0,16},{1,17},{2,18},{3,19},{4,20},{5,21},{6,22},{7,23},{8,24},{9,... | collective-permute-start | bytes 983048 | tf_op jit(solution)/shard_map/ppermute | solution.py:651
  61.0 6.4 %collective-permute-done.8.c11 = f32[1280,128]{1,0:T(8,128)S(1)} collective-permute-done((f32[1280,128]{1,0:T(8,128)S(1)}, f32[1280,128]{1,0:T(8,128)S(1)}, u32[]{:S(2)}, u32[]{:S(2)}) %collective-permute-start.8) | collective-permute-done | bytes 655392 | tf_op jit(solution)/shard_map/ppermute | solution.py:651
  67.4 1.5 %collective-permute-start.10 = (f32[1280,128]{1,0:T(8,128)S(1)}, f32[1280,128]{1,0:T(8,128)S(1)}, u32[]{:S(2)}, u32[]{:S(2)}) collective-permute-start(f32[1280,128]{1,0:T(8,128)S(1)} %collective-permute-done.8.c11), channel_id=1, source_target_pairs={{0,2},{1,3},{4,6},{5,7},{8,10},{9,11},{12,14},{13,15},{18,16},{19,... | collective-permute-start | bytes 1966088 | tf_op jit(solution)/shard_map/ppermute | solution.py:651
  68.9 7.2 %factor_end.1 = (bf16[768,768]{1,0:T(8,128)(2,1)S(1)}, bf16[768,768]{1,0:T(8,128)(2,1)S(1)}) custom-call(s32[2]{0:T(128)S(1)} %pad_add_fusion.place, f32[512,512]{1,0:T(8,128)S(1)} %factor_middle.1.side_in, f32[256,256]{1,0:T(8,128)} %get-tuple-element.54.b0, f32[256,256]{1,0:T(8,128)} %collective-permute-done.3.b1, f32[256,256]{1,0:T(8,128)} %collective-permute-done.4.b2, ...), custom_call_target="tpu_custom_call" | custom-call | flops 3000000000 | bytes 3000000000 | tf_op jit(solution)/shard_map/factor_end/pallas_call | solution.py:179
  76.2 0.0 collective-permute-done.7.third
  76.2 2.8 %collective-permute-start.11 = (f32[640,128]{1,0:T(8,128)S(1)}, f32[640,128]{1,0:T(8,128)S(1)}, u32[]{:S(2)}, u32[]{:S(2)}) collective-permute-start(f32[640,128]{1,0:T(8,128)S(1)} %collective-permute-done.7.third), channel_id=1, source_target_pairs={{0,2},{1,3},{2,0},{3,1},{4,6},{5,7},{6,4},{7,5},{8,10},{9,11},{10,... | collective-permute-start | bytes 983048 | tf_op jit(solution)/shard_map/ppermute | solution.py:651
  78.9 0.0 collective-permute-start.12
  78.9 0.0 collective-permute-done.9.rest
  78.9 0.0 copy-done.1
  78.9 4.7 %first_rows.1 = (f32[1,1024,1024]{2,1,0:T(8,128)}, bf16[512,768]{1,0:T(8,128)(2,1)S(1)}, bf16[512,768]{1,0:T(8,128)(2,1)S(1)}, f32[512,768]{1,0:T(8,128)S(1)}) custom-call(s32[2]{0:T(128)S(1)} %pad_add_fusion.place, f32[1,1024,1024]{2,1,0:T(8,128)S(1)} %copy-done.1, bf16[768,768]{1,0:T(8,128)(2,1)S(1)} %get-tuple-element.65.high, ...), custom_call_target="tpu_custom_call" | custom-call | flops 500000000 | bytes 500000000 | tf_op jit(solution)/shard_map/first_rows/pallas_call | solution.py:179
  83.6 9.3 %collective-permute-done.11.passed = f32[640,128]{1,0:T(8,128)S(1)} collective-permute-done((f32[640,128]{1,0:T(8,128)S(1)}, f32[640,128]{1,0:T(8,128)S(1)}, u32[]{:S(2)}, u32[]{:S(2)}) %collective-permute-start.11) | collective-permute-done | bytes 327712 | tf_op jit(solution)/shard_map/ppermute | solution.py:651
  92.9 0.0 collective-permute-done.10.c31
  92.9 2.8 %corner_block.1.before = f32[1,1024,1024]{2,1,0:T(8,128)} custom-call(s32[2]{0:T(128)S(1)} %pad_add_fusion.place, f32[1,1024,1024]{2,1,0:T(8,128)} %get-tuple-element.70.before, bf16[512,768]{1,0:T(8,128)(2,1)S(1)} %get-tuple-element.71.top, bf16[512,768]{1,0:T(8,128)(2,1)S(1)} %get-tuple-element.72.bottom, ...), custom_call_target="tpu_custom_call", output_to_operand_aliasing={{}: (1, {})} | custom-call | flops 500000000 | bytes 500000000 | tf_op jit(solution)/shard_map/corner_block/pallas_call | solution.py:179
  95.7 0.0 collective-permute-done.12.last
  95.7 4.3 %finish.1 = f32[1,1024,1024]{2,1,0:T(8,128)} custom-call(s32[2]{0:T(128)S(1)} %pad_add_fusion.place, f32[1,1024,1024]{2,1,0:T(8,128)} %corner_block.1.before, bf16[768,768]{1,0:T(8,128)(2,1)S(1)} %get-tuple-element.65.high, bf16[768,768]{1,0:T(8,128)(2,1)S(1)} %get-tuple-element.66.low, ...), custom_call_target="tpu_custom_call", output_to_operand_aliasing={{}: (1, {})} | custom-call | flops 500000000 | bytes 500000000 | tf_op jit(solution)/shard_map/finish/pallas_call | solution.py:179
Async XLA Ops:
  0.1 2.2 %copy-start = (f32[1,1024,1024]{2,1,0:T(8,128)S(1)}, f32[1,1024,1024]{2,1,0:T(8,128)}, u32[]{:S(2)}) copy-start(f32[1,1024,1024]{2,1,0:T(8,128)} %leaf.7) | copy-start | bytes 12582916
  3.5 7.9 %collective-permute-start = (f32[384,128]{1,0:T(8,128)S(1)}, f32[384,128]{1,0:T(8,128)S(1)}, u32[]{:S(2)}, u32[]{:S(2)}) collective-permute-start(f32[384,128]{1,0:T(8,128)S(1)} %cut_side.1.mine), channel_id=1, source_target_pairs={{0,2},{1,3},{2,0},{3,1},{4,6},{5,7},{6,4},{7,5},{8,10},{9,11},{10,... | collective-permute-start | bytes 589832 | tf_op jit(solution)/shard_map/ppermute | solution.py:651
  5.1 14.4 %collective-permute-start.1 = (f32[512,128]{1,0:T(8,128)S(1)}, f32[512,128]{1,0:T(8,128)S(1)}, u32[]{:S(2)}, u32[]{:S(2)}) collective-permute-start(f32[512,128]{1,0:T(8,128)S(1)} %cut_first.1.a0), channel_id=1, source_target_pairs={{0,16},{1,17},{2,18},{3,19},{4,20},{5,21},{6,22},{7,23},{8,24},{9,... | collective-permute-start | bytes 786440 | tf_op jit(solution)/shard_map/ppermute | solution.py:651
  6.4 15.1 %collective-permute-start.2 = (f32[1024,128]{1,0:T(8,128)S(1)}, f32[1024,128]{1,0:T(8,128)S(1)}, u32[]{:S(2)}, u32[]{:S(2)}) collective-permute-start(f32[1024,128]{1,0:T(8,128)S(1)} %get-tuple-element.48), channel_id=1, source_target_pairs={{0,2},{1,3},{2,0},{3,1},{4,6},{5,7},{6,4},{7,5},{8,10},{9,11},{10,... | collective-permute-start | bytes 1572872 | tf_op jit(solution)/shard_map/ppermute | solution.py:651
  19.1 12.7 %collective-permute-start.3 = (f32[256,256]{1,0:T(8,128)}, f32[256,256]{1,0:T(8,128)}, u32[]{:S(2)}, u32[]{:S(2)}) collective-permute-start(f32[256,256]{1,0:T(8,128)} %get-tuple-element.54.b0), channel_id=1, source_target_pairs={{0,16},{1,17},{2,18},{3,19},{4,20},{5,21},{6,22},{7,23},{8,24},{9,... | collective-permute-start | bytes 786440 | tf_op jit(solution)/shard_map/ppermute | solution.py:651
  21.5 10.4 %collective-permute-start.5 = (f32[512,128]{1,0:T(8,128)S(1)}, f32[512,128]{1,0:T(8,128)S(1)}, u32[]{:S(2)}, u32[]{:S(2)}) collective-permute-start(f32[512,128]{1,0:T(8,128)S(1)} %collective-permute-done.1.a1), channel_id=1, source_target_pairs={{0,2},{1,3},{2,0},{3,1},{4,6},{5,7},{6,4},{7,5},{8,10},{9,11},{10,... | collective-permute-start | bytes 786440 | tf_op jit(solution)/shard_map/ppermute | solution.py:651
  23.0 11.4 %collective-permute-start.4 = (f32[256,256]{1,0:T(8,128)}, f32[256,256]{1,0:T(8,128)}, u32[]{:S(2)}, u32[]{:S(2)}) collective-permute-start(f32[256,256]{1,0:T(8,128)} %get-tuple-element.54.b0), channel_id=1, source_target_pairs={{0,2},{1,3},{2,0},{3,1},{4,6},{5,7},{6,4},{7,5},{8,10},{9,11},{10,... | collective-permute-start | bytes 786440 | tf_op jit(solution)/shard_map/ppermute | solution.py:651
  31.9 35.5 %collective-permute-start.8 = (f32[1280,128]{1,0:T(8,128)S(1)}, f32[1280,128]{1,0:T(8,128)S(1)}, u32[]{:S(2)}, u32[]{:S(2)}) collective-permute-start(f32[1280,128]{1,0:T(8,128)S(1)} %get-tuple-element.61.c01), channel_id=1, source_target_pairs={{0,16},{1,17},{2,18},{3,19},{4,20},{5,21},{6,22},{7,23},{8,24},{9,... | collective-permute-start | bytes 1966088 | tf_op jit(solution)/shard_map/ppermute | solution.py:651
  34.4 6.6 %collective-permute-start.6 = (f32[256,256]{1,0:T(8,128)}, f32[256,256]{1,0:T(8,128)S(1)}, u32[]{:S(2)}, u32[]{:S(2)}) collective-permute-start(f32[256,256]{1,0:T(8,128)} %collective-permute-done.3.b1), channel_id=1, source_target_pairs={{0,2},{1,3},{2,0},{3,1},{4,6},{5,7},{6,4},{7,5},{8,10},{9,11},{10,... | collective-permute-start | bytes 786440 | tf_op jit(solution)/shard_map/ppermute | solution.py:651
  40.9 38.0 %collective-permute-start.9 = (f32[1408,128]{1,0:T(8,128)S(1)}, f32[1408,128]{1,0:T(8,128)S(1)}, u32[]{:S(2)}, u32[]{:S(2)}) collective-permute-start(f32[1408,128]{1,0:T(8,128)S(1)} %get-tuple-element.69), channel_id=1, source_target_pairs={{0,2},{1,3},{4,6},{5,7},{8,10},{9,11},{12,14},{13,15},{18,16},{19,... | collective-permute-start | bytes 2162696 | tf_op jit(solution)/shard_map/ppermute | solution.py:651
  57.0 21.9 %copy-start.1 = (f32[1,1024,1024]{2,1,0:T(8,128)S(1)}, f32[1,1024,1024]{2,1,0:T(8,128)}, u32[]{:S(2)}) copy-start(f32[1,1024,1024]{2,1,0:T(8,128)} %leaf.7) | copy-start | bytes 12582916
  57.0 19.1 %collective-permute-start.7 = (f32[640,128]{1,0:T(8,128)S(1)}, f32[640,128]{1,0:T(8,128)S(1)}, u32[]{:S(2)}, u32[]{:S(2)}) collective-permute-start(f32[640,128]{1,0:T(8,128)S(1)} %get-tuple-element.60), channel_id=1, source_target_pairs={{0,16},{1,17},{2,18},{3,19},{4,20},{5,21},{6,22},{7,23},{8,24},{9,... | collective-permute-start | bytes 983048 | tf_op jit(solution)/shard_map/ppermute | solution.py:651
  67.4 25.5 %collective-permute-start.10 = (f32[1280,128]{1,0:T(8,128)S(1)}, f32[1280,128]{1,0:T(8,128)S(1)}, u32[]{:S(2)}, u32[]{:S(2)}) collective-permute-start(f32[1280,128]{1,0:T(8,128)S(1)} %collective-permute-done.8.c11), channel_id=1, source_target_pairs={{0,2},{1,3},{4,6},{5,7},{8,10},{9,11},{12,14},{13,15},{18,16},{19,... | collective-permute-start | bytes 1966088 | tf_op jit(solution)/shard_map/ppermute | solution.py:651
  76.2 16.7 %collective-permute-start.11 = (f32[640,128]{1,0:T(8,128)S(1)}, f32[640,128]{1,0:T(8,128)S(1)}, u32[]{:S(2)}, u32[]{:S(2)}) collective-permute-start(f32[640,128]{1,0:T(8,128)S(1)} %collective-permute-done.7.third), channel_id=1, source_target_pairs={{0,2},{1,3},{2,0},{3,1},{4,6},{5,7},{6,4},{7,5},{8,10},{9,11},{10,... | collective-permute-start | bytes 983048 | tf_op jit(solution)/shard_map/ppermute | solution.py:651
  78.9 16.8 %collective-permute-start.12 = (f32[640,128]{1,0:T(8,128)S(1)}, f32[640,128]{1,0:T(8,128)S(1)}, u32[]{:S(2)}, u32[]{:S(2)}) collective-permute-start(f32[640,128]{1,0:T(8,128)S(1)} %get-tuple-element.74), channel_id=1, source_target_pairs={{0,16},{1,17},{2,18},{3,19},{4,20},{5,21},{6,22},{7,23},{8,24},{9,... | collective-permute-start | bytes 983048 | tf_op jit(solution)/shard_map/ppermute | solution.py:651

commit v11 on v10

--- a/solution.py
+++ b/solution.py
@@ -1,3 +1,4 @@
+import functools
 import math
 
 import jax
@@ -12,7 +13,7 @@
 T = 128
 R = 16
 FIRST = 1
-SECOND = 10
+SECOND = 9
 HBM = pl.BlockSpec(memory_space=pl.ANY)
 FAR = pl.BlockSpec(memory_space=pltpu.HBM)
 VMEM = pl.BlockSpec(memory_space=pltpu.VMEM)
@@ -97,9 +98,11 @@
         if c0 + R < T:
             old = m[c0 + R : c0 + 2 * R]
             inside = (lane[:R] >= c0) & (lane[:R] < c0 + R)
-            rows = jnp.where(inside, 0.0, old)
+            sums = [jnp.where(inside, 0.0, old)] + [None] * 3
             for k in range(R):
-                rows = rows - across_lanes(old, c0 + k) * across_rows(swept, k)
+                term = across_lanes(old, c0 + k) * across_rows(swept, k)
+                sums[k % 4] = -term if sums[k % 4] is None else sums[k % 4] - term
+            rows = (sums[0] + sums[1]) + (sums[2] + sums[3])
         wide = put_rows(jnp.zeros((T, T), F32), swept, c0)
         rest = jnp.where((lane >= c0) & (lane < c0 + R), 0.0, m) - dot(m, wide)
         if lower:
@@ -370,7 +373,7 @@
     return call(
         factor_start_kernel,
         "factor_start",
-        3500 * 10**6,
+        100 * 10**6,
         [((2 * e, 2 * e), F32)],
         [(VMEM, x) for x in (*a, *b)],
         [],
@@ -387,7 +390,7 @@
     return call(
         factor_middle_kernel,
         "factor_middle",
-        4000 * 10**6,
+        100 * 10**6,
         [(side.shape, F32)],
         [(VMEM, side)],
         [],
@@ -492,7 +495,7 @@
 
 
 def rows_kernel(
-    place, leaf, high, low, a0, c01, c02, a1, c11, third, swapped, rest, out, top, bottom, part, col, own, held, sem
+    n_mid, place, leaf, high, low, a0, c01, c02, a1, c11, third, swapped, rest, out, top, bottom, part, col, own, held, sem
 ):
     e = leaf.shape[1] // 4
     n_sym = symmetric_tiles(e)
@@ -531,16 +534,18 @@
         col[...] = cross_block((swapped, n_sym), (rest, 0))
         held[0] = -dot3(left[0], split(col[...]), NT)
         copies = put(out, place, held.at[0], 0, 0, sem.at[0])
-        across = cross_block((a1, n_sym), (c11, 0), zeros(third.shape[0] // T))
+        across = cross_block(
+            (a1, n_sym), (c11, 0), (third[: n_mid * T, :], 0), zeros(third.shape[0] // T - n_mid)
+        )
         part[...] = times_inverse(across, high[...], low[...], slice(2 * e, 3 * e))
         wait(copies)
 
 
-def first_rows(place, leaf, high, low, mine, across, swapped, rest):
+def first_rows(n_mid, place, leaf, high, low, mine, across, swapped, rest):
     e = leaf.shape[1] // 4
     block = pltpu.VMEM((2 * e, 2 * e), F32)
     return call(
-        rows_kernel,
+        functools.partial(rows_kernel, n_mid),
         "first_rows",
         500 * 10**6,
         [(leaf.shape, F32)] + [((2 * e, 3 * e), BF16)] * 2 + [((2 * e, 3 * e), F32)],
@@ -582,11 +587,12 @@
     tiles = e // T
     n_sym = symmetric_tiles(e)
     n_last = last.shape[0] // T
+    n_mid = passed.shape[0] // T - n_last
 
     @pl.when(place[0] == place[1])
     def _():
         for at, (i, j) in enumerate(upper(2 * tiles)):
-            ref, at = (last, at) if at < n_last else (passed, at - n_last)
+            ref, at = (last, at) if at < n_last else (passed, at - n_last + n_mid)
             piece = ref[at * T : (at + 1) * T, :]
             r, c = slice(i * T, (i + 1) * T), slice(j * T, (j + 1) * T)
             held[0, r, c] = part[r, c] + piece
@@ -596,7 +602,7 @@
 
     @pl.when(place[0] != place[1])
     def _():
-        late = cross_block(zeros(FIRST + SECOND), (last, 0))[:, e:]
+        late = cross_block(zeros(4 * tiles * tiles - n_last), (last, 0))[:, e:]
         inner = slice(2 * e, 3 * e)
         start = (2 * tiles * tiles - n_last) // tiles * T
         scratch[:start, :] = part[:start, :]
@@ -678,16 +684,18 @@
         rest = send(rest, True, only=True)
         side = factor_start((a, a_x, swapped, a_d), (b, b_x, b_y, b_d))
         side = factor_middle(side)
-        third, side = tie(jnp.where(same, swapped[-n_last * T :], c2), side)
+        n_mid = c2.shape[0] // T - n_last
+        theirs = jnp.concatenate([c2[: n_mid * T], swapped[-n_last * T :]])
+        third, side = tie(jnp.where(same, theirs, c2), side)
         third = send(third, False)
         c1_x, side = tie(c1_x, side)
         c1_d = send(c1_x, True, only=True)
         high, low = factor_end(place, side, (b, b_x, b_y, b_d))
-        last, third, high = tie(jnp.where(same, c2, outer0), third, high)
+        last, third, high = tie(jnp.where(same, c2[n_mid * T :], outer0), third, high)
         last = send(last, False)
         passed = send(third, True)
         out, top, bottom, part = first_rows(
-            place, leaf, high, low, (a, c1, c2), (a_x, c1_x, third), swapped, rest
+            n_mid, place, leaf, high, low, (a, c1, c2), (a_x, c1_x, third), swapped, rest
         )
         out = corner_block(place, out, top, bottom, a_d, c1_d, passed)
         return finish(place, out, high, low, part, passed, last, swapped, rest, a_d, c1_d)

time: 100 us -> 102 us (1.020)
  starting transfers between devices: 15.7 us -> 21.9 us
  waiting for transfers between devices: 37.9 us -> 31.8 us
  local copies, waits for them, and re-layouts: 2.19 us -> 4.71 us
    ppermute x13, starting transfers between devices: 15.7 us -> 21.9 us  [send(): return lax.ppermute(value, ('gx', 'gy'), pairs)]
    ppermute x13, waiting for transfers between devices: 37.9 us -> 31.8 us  [send(): return lax.ppermute(value, ('gx', 'gy'), pairs)]
    unnamed x4 -> x12, local copies, waits for them, and re-layouts: 2.19 us -> 4.69 us
    pallas_call x11, Pallas kernels: 43.9 us -> 42.9 us  [call(): pl.pallas_call(kernel, out_shape=[jax.ShapeDtypeStruct(shape, dtype) for...]
  transfers between devices with their start and end apart: 13 -> 13, of which waited for: 7 -> 7; matrix products, arithmetic and copies ran while one was open for 0% -> 0% of each run, Pallas kernels for 38% -> 37%
where the time goes in v11:
time: 102 us
  Pallas kernels  42.9 us (42%)
  waiting for transfers between devices  31.8 us (31%)
  starting transfers between devices  21.9 us (21%)
  local copies, waits for them, and re-layouts  4.71 us (5%)
    pallas_call x11, Pallas kernels, call(): pl.pallas_call(kernel, out_shape=[jax.ShapeDtypeStruct(shape, dtype) for...  42.9 us
    ppermute x13, waiting for transfers between devices, send(): return lax.ppermute(value, ('gx', 'gy'), pairs)  31.8 us
    ppermute x13, starting transfers between devices, send(): return lax.ppermute(value, ('gx', 'gy'), pairs)  21.9 us
    unnamed x12, local copies, waits for them, and re-layouts  4.69 us
  transfers between devices with their start and end apart: 13, of which 7 were waited for; matrix products, arithmetic and copies ran while one was open for 0% of the time, Pallas kernels for 37%

profile of v11, /device:TPU:24, one launch (start us, length us, event | category | flops | bytes accessed | tf_op | source)
XLA Modules:
  0.0 101.8 jit_solution(2878132619791014962)
XLA Ops:
  0.0 0.1 pad_add_fusion.place
  0.1 0.0 copy-start
  0.1 2.2 %copy-done = f32[1,1024,1024]{2,1,0:T(8,128)S(1)} copy-done((f32[1,1024,1024]{2,1,0:T(8,128)S(1)}, f32[1,1024,1024]{2,1,0:T(8,128)}, u32[]{:S(2)}) %copy-start) | copy-done | bytes 4194328
  2.3 0.6 cut_first.1.a0
  2.9 0.6 cut_side.1.mine
  3.5 1.6 %collective-permute-start = (f32[384,128]{1,0:T(8,128)S(1)}, f32[384,128]{1,0:T(8,128)S(1)}, u32[]{:S(2)}, u32[]{:S(2)}) collective-permute-start(f32[384,128]{1,0:T(8,128)S(1)} %cut_side.1.mine), channel_id=1, source_target_pairs={{0,2},{1,3},{2,0},{3,1},{4,6},{5,7},{6,4},{7,5},{8,10},{9,11},{10,... | collective-permute-start | bytes 589832 | tf_op jit(solution)/shard_map/ppermute | solution.py:657
  5.1 0.3 collective-permute-start.1
  5.4 0.9 cut_second.1
  6.4 0.6 collective-permute-start.2
  7.0 4.4 %collective-permute-done.along = f32[384,128]{1,0:T(8,128)S(1)} collective-permute-done((f32[384,128]{1,0:T(8,128)S(1)}, f32[384,128]{1,0:T(8,128)S(1)}, u32[]{:S(2)}, u32[]{:S(2)}) %collective-permute-start) | collective-permute-done | bytes 196640 | tf_op jit(solution)/shard_map/ppermute | solution.py:657
  11.4 7.0 %gauge_side.1 = (f32[256,256]{1,0:T(8,128)S(1)}, f32[256,256]{1,0:T(8,128)S(1)}) custom-call(f32[384,128]{1,0:T(8,128)S(1)} %cut_side.1.mine, f32[384,128]{1,0:T(8,128)S(1)} %collective-permute-done.along, f32[256,256]{1,0:T(8,128)S(1)} %get-tuple-element.41.b), custom_call_target="tpu_custom_call" | custom-call | flops 8000000000 | bytes 8000000000 | tf_op jit(solution)/shard_map/gauge_side/pallas_call | solution.py:182
  18.4 0.1 collective-permute-start.3
  18.5 0.4 scale_cross.1
  18.9 0.0 copy-start.5
  18.9 0.8 copy-done.5
  19.7 0.0 collective-permute-done.1.a1
  19.7 1.7 %collective-permute-done.2.a2.swapped = f32[1024,128]{1,0:T(8,128)S(1)} collective-permute-done((f32[1024,128]{1,0:T(8,128)S(1)}, f32[1024,128]{1,0:T(8,128)S(1)}, u32[]{:S(2)}, u32[]{:S(2)}) %collective-permute-start.2) | collective-permute-done | bytes 524320 | tf_op jit(solution)/shard_map/ppermute | solution.py:657
  21.5 1.5 %collective-permute-start.5 = (f32[512,128]{1,0:T(8,128)S(1)}, f32[512,128]{1,0:T(8,128)S(1)}, u32[]{:S(2)}, u32[]{:S(2)}) collective-permute-start(f32[512,128]{1,0:T(8,128)S(1)} %collective-permute-done.1.a1), channel_id=1, source_target_pairs={{0,2},{1,3},{2,0},{3,1},{4,6},{5,7},{6,4},{7,5},{8,10},{9,11},{10,... | collective-permute-start | bytes 786440 | tf_op jit(solution)/shard_map/ppermute | solution.py:657
  23.0 0.5 collective-permute-start.4
  23.5 7.5 %collective-permute-done.3.b1 = f32[256,256]{1,0:T(8,128)} collective-permute-done((f32[256,256]{1,0:T(8,128)S(1)}, f32[256,256]{1,0:T(8,128)}, u32[]{:S(2)}, u32[]{:S(2)}) %collective-permute-start.3) | collective-permute-done | bytes 262176 | tf_op jit(solution)/shard_map/ppermute | solution.py:657
  31.0 0.0 collective-permute-start.8
  31.0 0.0 collective-permute-done.5.a3
  31.0 3.3 %collective-permute-done.4.b2 = f32[256,256]{1,0:T(8,128)S(1)} collective-permute-done((f32[256,256]{1,0:T(8,128)S(1)}, f32[256,256]{1,0:T(8,128)S(1)}, u32[]{:S(2)}, u32[]{:S(2)}) %collective-permute-start.4) | collective-permute-done | bytes 262176 | tf_op jit(solution)/shard_map/ppermute | solution.py:657
  34.3 0.7 copy-done.2
  35.0 1.5 %collective-permute-start.6 = (f32[256,256]{1,0:T(8,128)}, f32[256,256]{1,0:T(8,128)}, u32[]{:S(2)}, u32[]{:S(2)}) collective-permute-start(f32[256,256]{1,0:T(8,128)} %collective-permute-done.3.b1), channel_id=1, source_target_pairs={{0,2},{1,3},{2,0},{3,1},{4,6},{5,7},{6,4},{7,5},{8,10},{9,11},{10,... | collective-permute-start | bytes 786440 | tf_op jit(solution)/shard_map/ppermute | solution.py:657
  36.6 5.1 %collective-permute-done.6.b3 = f32[256,256]{1,0:T(8,128)} collective-permute-done((f32[256,256]{1,0:T(8,128)}, f32[256,256]{1,0:T(8,128)}, u32[]{:S(2)}, u32[]{:S(2)}) %collective-permute-start.6) | collective-permute-done | bytes 262176 | tf_op jit(solution)/shard_map/ppermute | solution.py:657
  41.6 1.5 %collective-permute-start.9 = (f32[1408,128]{1,0:T(8,128)}, f32[1408,128]{1,0:T(8,128)S(1)}, u32[]{:S(2)}, u32[]{:S(2)}) collective-permute-start(f32[1408,128]{1,0:T(8,128)} %copy-done.5), channel_id=1, source_target_pairs={{0,2},{1,3},{4,6},{5,7},{8,10},{9,11},{12,14},{13,15},{18,16},{19,... | collective-permute-start | bytes 2162696 | tf_op jit(solution)/shard_map/ppermute | solution.py:657
  43.1 0.0 copy-start.3
  43.1 0.9 copy-done.3
  44.1 10.4 %factor_start.1.before = f32[512,512]{1,0:T(8,128)S(1)} custom-call(f32[512,128]{1,0:T(8,128)S(1)} %cut_first.1.a0, f32[512,128]{1,0:T(8,128)S(1)} %collective-permute-done.1.a1, f32[1024,128]{1,0:T(8,128)S(1)} %collective-permute-done.2.a2.swapped, f32[512,128]{1,0:T(8,128)S(1)} %collective-permute-done.5.a3, f32[256,256]{1,0:T(8,128)S(1)} %get-tuple-element.54.b0, ...), custom_call_target="tpu_custom_call" | custom-call | flops 100000000 | bytes 100000000 | tf_op jit(solution)/shard_map/factor_start/pallas_call | solution.py:182
  54.5 4.0 %factor_middle.1.side_in = f32[512,512]{1,0:T(8,128)S(1)} custom-call(f32[512,512]{1,0:T(8,128)S(1)} %factor_start.1.before), custom_call_target="tpu_custom_call" | custom-call | flops 100000000 | bytes 100000000 | tf_op jit(solution)/shard_map/factor_middle/pallas_call | solution.py:182
  58.5 3.2 %collective-permute-start.7 = (f32[768,128]{1,0:T(8,128)S(1)}, f32[768,128]{1,0:T(8,128)S(1)}, u32[]{:S(2)}, u32[]{:S(2)}) collective-permute-start(f32[768,128]{1,0:T(8,128)S(1)} %maximum_select_fusion), channel_id=1, source_target_pairs={{0,16},{1,17},{2,18},{3,19},{4,20},{5,21},{6,22},{7,23},{8,24},{9,... | collective-permute-start | bytes 1179656 | tf_op jit(solution)/shard_map/ppermute | solution.py:657
  61.7 0.0 copy-start.1
  61.7 0.0 collective-permute-done.8.c11
  61.8 1.8 %collective-permute-start.10 = (f32[1152,128]{1,0:T(8,128)S(1)}, f32[1152,128]{1,0:T(8,128)S(1)}, u32[]{:S(2)}, u32[]{:S(2)}) collective-permute-start(f32[1152,128]{1,0:T(8,128)S(1)} %collective-permute-done.8.c11), channel_id=1, source_target_pairs={{0,2},{1,3},{4,6},{5,7},{8,10},{9,11},{12,14},{13,15},{18,16},{19,... | collective-permute-start | bytes 1769480 | tf_op jit(solution)/shard_map/ppermute | solution.py:657
  63.5 0.0 copy-done.4
  63.6 7.1 %factor_end.1 = (bf16[768,768]{1,0:T(8,128)(2,1)S(1)}, bf16[768,768]{1,0:T(8,128)(2,1)S(1)}) custom-call(s32[2]{0:T(128)S(1)} %pad_add_fusion.place, f32[512,512]{1,0:T(8,128)S(1)} %factor_middle.1.side_in, f32[256,256]{1,0:T(8,128)S(1)} %get-tuple-element.54.b0, f32[256,256]{1,0:T(8,128)} %collective-permute-done.3.b1, f32[256,256]{1,0:T(8,128)S(1)} %copy-done.4, ...), custom_call_target="tpu_custom_call" | custom-call | flops 3000000000 | bytes 3000000000 | tf_op jit(solution)/shard_map/factor_end/pallas_call | solution.py:182
  70.7 5.2 %collective-permute-done.7.third = f32[768,128]{1,0:T(8,128)S(1)} collective-permute-done((f32[768,128]{1,0:T(8,128)S(1)}, f32[768,128]{1,0:T(8,128)S(1)}, u32[]{:S(2)}, u32[]{:S(2)}) %collective-permute-start.7) | collective-permute-done | bytes 393248 | tf_op jit(solution)/shard_map/ppermute | solution.py:657
  75.9 9.4 %collective-permute-start.11 = (f32[768,128]{1,0:T(8,128)S(1)}, f32[768,128]{1,0:T(8,128)S(1)}, u32[]{:S(2)}, u32[]{:S(2)}) collective-permute-start(f32[768,128]{1,0:T(8,128)S(1)} %collective-permute-done.7.third), channel_id=1, source_target_pairs={{0,2},{1,3},{2,0},{3,1},{4,6},{5,7},{6,4},{7,5},{8,10},{9,11},{10,... | collective-permute-start | bytes 1179656 | tf_op jit(solution)/shard_map/ppermute | solution.py:657
  85.3 0.0 collective-permute-start.12
  85.3 0.0 collective-permute-done.9.rest
  85.3 0.0 copy-done.1
  85.3 4.6 %first_rows.1 = (f32[1,1024,1024]{2,1,0:T(8,128)}, bf16[512,768]{1,0:T(8,128)(2,1)S(1)}, bf16[512,768]{1,0:T(8,128)(2,1)S(1)}, f32[512,768]{1,0:T(8,128)S(1)}) custom-call(s32[2]{0:T(128)S(1)} %pad_add_fusion.place, f32[1,1024,1024]{2,1,0:T(8,128)S(1)} %copy-done.1, bf16[768,768]{1,0:T(8,128)(2,1)S(1)} %get-tuple-element.65.high, ...), custom_call_target="tpu_custom_call" | custom-call | flops 500000000 | bytes 500000000 | tf_op jit(solution)/shard_map/first_rows/pallas_call | solution.py:182
  89.9 0.0 collective-permute-done.10.c31
  90.0 4.6 %collective-permute-done.11.passed = f32[768,128]{1,0:T(8,128)S(1)} collective-permute-done((f32[768,128]{1,0:T(8,128)S(1)}, f32[768,128]{1,0:T(8,128)S(1)}, u32[]{:S(2)}, u32[]{:S(2)}) %collective-permute-start.11) | collective-permute-done | bytes 393248 | tf_op jit(solution)/shard_map/ppermute | solution.py:657
  94.5 2.8 %corner_block.1.before = f32[1,1024,1024]{2,1,0:T(8,128)} custom-call(s32[2]{0:T(128)S(1)} %pad_add_fusion.place, f32[1,1024,1024]{2,1,0:T(8,128)} %get-tuple-element.70.before, bf16[512,768]{1,0:T(8,128)(2,1)S(1)} %get-tuple-element.71.top, bf16[512,768]{1,0:T(8,128)(2,1)S(1)} %get-tuple-element.72.bottom, ...), custom_call_target="tpu_custom_call", output_to_operand_aliasing={{}: (1, {})} | custom-call | flops 500000000 | bytes 500000000 | tf_op jit(solution)/shard_map/corner_block/pallas_call | solution.py:182
  97.3 0.0 collective-permute-done.12.last
  97.4 4.3 %finish.1 = f32[1,1024,1024]{2,1,0:T(8,128)} custom-call(s32[2]{0:T(128)S(1)} %pad_add_fusion.place, f32[1,1024,1024]{2,1,0:T(8,128)} %corner_block.1.before, bf16[768,768]{1,0:T(8,128)(2,1)S(1)} %get-tuple-element.65.high, bf16[768,768]{1,0:T(8,128)(2,1)S(1)} %get-tuple-element.66.low, ...), custom_call_target="tpu_custom_call", output_to_operand_aliasing={{}: (1, {})} | custom-call | flops 500000000 | bytes 500000000 | tf_op jit(solution)/shard_map/finish/pallas_call | solution.py:182
  (6 shorter events, 0.1 us)
Async XLA Ops:
  0.1 2.2 %copy-start = (f32[1,1024,1024]{2,1,0:T(8,128)S(1)}, f32[1,1024,1024]{2,1,0:T(8,128)}, u32[]{:S(2)}) copy-start(f32[1,1024,1024]{2,1,0:T(8,128)} %leaf.7) | copy-start | bytes 12582916
  3.5 7.9 %collective-permute-start = (f32[384,128]{1,0:T(8,128)S(1)}, f32[384,128]{1,0:T(8,128)S(1)}, u32[]{:S(2)}, u32[]{:S(2)}) collective-permute-start(f32[384,128]{1,0:T(8,128)S(1)} %cut_side.1.mine), channel_id=1, source_target_pairs={{0,2},{1,3},{2,0},{3,1},{4,6},{5,7},{6,4},{7,5},{8,10},{9,11},{10,... | collective-permute-start | bytes 589832 | tf_op jit(solution)/shard_map/ppermute | solution.py:657
  5.1 14.6 %collective-permute-start.1 = (f32[512,128]{1,0:T(8,128)S(1)}, f32[512,128]{1,0:T(8,128)S(1)}, u32[]{:S(2)}, u32[]{:S(2)}) collective-permute-start(f32[512,128]{1,0:T(8,128)S(1)} %cut_first.1.a0), channel_id=1, source_target_pairs={{0,16},{1,17},{2,18},{3,19},{4,20},{5,21},{6,22},{7,23},{8,24},{9,... | collective-permute-start | bytes 786440 | tf_op jit(solution)/shard_map/ppermute | solution.py:657
  6.4 15.1 %collective-permute-start.2 = (f32[1024,128]{1,0:T(8,128)S(1)}, f32[1024,128]{1,0:T(8,128)S(1)}, u32[]{:S(2)}, u32[]{:S(2)}) collective-permute-start(f32[1024,128]{1,0:T(8,128)S(1)} %get-tuple-element.48), channel_id=1, source_target_pairs={{0,2},{1,3},{2,0},{3,1},{4,6},{5,7},{6,4},{7,5},{8,10},{9,11},{10,... | collective-permute-start | bytes 1572872 | tf_op jit(solution)/shard_map/ppermute | solution.py:657
  18.4 12.6 %collective-permute-start.3 = (f32[256,256]{1,0:T(8,128)S(1)}, f32[256,256]{1,0:T(8,128)}, u32[]{:S(2)}, u32[]{:S(2)}) collective-permute-start(f32[256,256]{1,0:T(8,128)S(1)} %get-tuple-element.54.b0), channel_id=1, source_target_pairs={{0,16},{1,17},{2,18},{3,19},{4,20},{5,21},{6,22},{7,23},{8,24},{9,... | collective-permute-start | bytes 786440 | tf_op jit(solution)/shard_map/ppermute | solution.py:657
  18.9 0.9 copy-start.5
  21.5 9.5 %collective-permute-start.5 = (f32[512,128]{1,0:T(8,128)S(1)}, f32[512,128]{1,0:T(8,128)S(1)}, u32[]{:S(2)}, u32[]{:S(2)}) collective-permute-start(f32[512,128]{1,0:T(8,128)S(1)} %collective-permute-done.1.a1), channel_id=1, source_target_pairs={{0,2},{1,3},{2,0},{3,1},{4,6},{5,7},{6,4},{7,5},{8,10},{9,11},{10,... | collective-permute-start | bytes 786440 | tf_op jit(solution)/shard_map/ppermute | solution.py:657
  23.0 11.3 %collective-permute-start.4 = (f32[256,256]{1,0:T(8,128)S(1)}, f32[256,256]{1,0:T(8,128)S(1)}, u32[]{:S(2)}, u32[]{:S(2)}) collective-permute-start(f32[256,256]{1,0:T(8,128)S(1)} %get-tuple-element.54.b0), channel_id=1, source_target_pairs={{0,2},{1,3},{2,0},{3,1},{4,6},{5,7},{6,4},{7,5},{8,10},{9,11},{10,... | collective-permute-start | bytes 786440 | tf_op jit(solution)/shard_map/ppermute | solution.py:657
  31.0 30.8 %collective-permute-start.8 = (f32[1152,128]{1,0:T(8,128)S(1)}, f32[1152,128]{1,0:T(8,128)S(1)}, u32[]{:S(2)}, u32[]{:S(2)}) collective-permute-start(f32[1152,128]{1,0:T(8,128)S(1)} %get-tuple-element.61.c01), channel_id=1, source_target_pairs={{0,16},{1,17},{2,18},{3,19},{4,20},{5,21},{6,22},{7,23},{8,24},{9,... | collective-permute-start | bytes 1769480 | tf_op jit(solution)/shard_map/ppermute | solution.py:657
  34.3 0.7 copy-start.2
  35.0 6.7 %collective-permute-start.6 = (f32[256,256]{1,0:T(8,128)}, f32[256,256]{1,0:T(8,128)}, u32[]{:S(2)}, u32[]{:S(2)}) collective-permute-start(f32[256,256]{1,0:T(8,128)} %collective-permute-done.3.b1), channel_id=1, source_target_pairs={{0,2},{1,3},{2,0},{3,1},{4,6},{5,7},{6,4},{7,5},{8,10},{9,11},{10,... | collective-permute-start | bytes 786440 | tf_op jit(solution)/shard_map/ppermute | solution.py:657
  36.5 27.1 %copy-start.4 = (f32[256,256]{1,0:T(8,128)S(1)}, f32[256,256]{1,0:T(8,128)}, u32[]{:S(2)}) copy-start(f32[256,256]{1,0:T(8,128)} %copy-done.2) | copy-start | bytes 786436
  41.6 43.6 %collective-permute-start.9 = (f32[1408,128]{1,0:T(8,128)}, f32[1408,128]{1,0:T(8,128)S(1)}, u32[]{:S(2)}, u32[]{:S(2)}) collective-permute-start(f32[1408,128]{1,0:T(8,128)} %copy-done.5), channel_id=1, source_target_pairs={{0,2},{1,3},{4,6},{5,7},{8,10},{9,11},{12,14},{13,15},{18,16},{19,... | collective-permute-start | bytes 2162696 | tf_op jit(solution)/shard_map/ppermute | solution.py:657
  43.1 1.0 copy-start.3
  58.5 17.4 %collective-permute-start.7 = (f32[768,128]{1,0:T(8,128)S(1)}, f32[768,128]{1,0:T(8,128)S(1)}, u32[]{:S(2)}, u32[]{:S(2)}) collective-permute-start(f32[768,128]{1,0:T(8,128)S(1)} %maximum_select_fusion), channel_id=1, source_target_pairs={{0,16},{1,17},{2,18},{3,19},{4,20},{5,21},{6,22},{7,23},{8,24},{9,... | collective-permute-start | bytes 1179656 | tf_op jit(solution)/shard_map/ppermute | solution.py:657
  61.7 23.6 %copy-start.1 = (f32[1,1024,1024]{2,1,0:T(8,128)S(1)}, f32[1,1024,1024]{2,1,0:T(8,128)}, u32[]{:S(2)}) copy-start(f32[1,1024,1024]{2,1,0:T(8,128)} %leaf.7) | copy-start | bytes 12582916
  61.8 28.2 %collective-permute-start.10 = (f32[1152,128]{1,0:T(8,128)S(1)}, f32[1152,128]{1,0:T(8,128)S(1)}, u32[]{:S(2)}, u32[]{:S(2)}) collective-permute-start(f32[1152,128]{1,0:T(8,128)S(1)} %collective-permute-done.8.c11), channel_id=1, source_target_pairs={{0,2},{1,3},{4,6},{5,7},{8,10},{9,11},{12,14},{13,15},{18,16},{19,... | collective-permute-start | bytes 1769480 | tf_op jit(solution)/shard_map/ppermute | solution.py:657
  75.9 18.6 %collective-permute-start.11 = (f32[768,128]{1,0:T(8,128)S(1)}, f32[768,128]{1,0:T(8,128)S(1)}, u32[]{:S(2)}, u32[]{:S(2)}) collective-permute-start(f32[768,128]{1,0:T(8,128)S(1)} %collective-permute-done.7.third), channel_id=1, source_target_pairs={{0,2},{1,3},{2,0},{3,1},{4,6},{5,7},{6,4},{7,5},{8,10},{9,11},{10,... | collective-permute-start | bytes 1179656 | tf_op jit(solution)/shard_map/ppermute | solution.py:657
  85.3 12.1 %collective-permute-start.12 = (f32[640,128]{1,0:T(8,128)S(1)}, f32[640,128]{1,0:T(8,128)S(1)}, u32[]{:S(2)}, u32[]{:S(2)}) collective-permute-start(f32[640,128]{1,0:T(8,128)S(1)} %slice_select_fusion), channel_id=1, source_target_pairs={{0,16},{1,17},{2,18},{3,19},{4,20},{5,21},{6,22},{7,23},{8,24},{9,... | collective-permute-start | bytes 983048 | tf_op jit(solution)/shard_map/ppermute | solution.py:657

commit v12 on v11

--- a/solution.py
+++ b/solution.py
@@ -13,7 +13,7 @@
 T = 128
 R = 16
 FIRST = 1
-SECOND = 9
+SECOND = 8
 HBM = pl.BlockSpec(memory_space=pl.ANY)
 FAR = pl.BlockSpec(memory_space=pltpu.HBM)
 VMEM = pl.BlockSpec(memory_space=pltpu.VMEM)
@@ -373,34 +373,17 @@
     return call(
         factor_start_kernel,
         "factor_start",
-        100 * 10**6,
+        1000 * 10**6,
         [((2 * e, 2 * e), F32)],
         [(VMEM, x) for x in (*a, *b)],
         [],
     )[0]
 
 
-def factor_middle_kernel(before, side):
-    side[...] = before[...]
-    half = side.shape[0] // 2
-    sweep(side, half, half + T)
-
-
-def factor_middle(side):
-    return call(
-        factor_middle_kernel,
-        "factor_middle",
-        100 * 10**6,
-        [(side.shape, F32)],
-        [(VMEM, side)],
-        [],
-    )[0]
-
-
 def factor_end_kernel(place, side_in, b0, b1, b2, b3, high, low, side, full):
     e = b0.shape[0]
     side[...] = side_in[...]
-    sweep(side, e + T, 2 * e)
+    sweep(side, e, 2 * e)
     coup = split(couple((b0, b1, b2, b3)))
     away = dot3(split(side[...]), coup)
     shape = full.shape
@@ -431,7 +414,7 @@
     return call(
         factor_end_kernel,
         "factor_end",
-        3000 * 10**6,
+        10000 * 10**6,
         [((3 * e, 3 * e), BF16)] * 2,
         [(SMEM, place), (VMEM, side)] + [(VMEM, x) for x in b],
         [pltpu.VMEM((2 * e, 2 * e), F32), pltpu.VMEM((2 * e, 2 * e), F32)],
@@ -683,7 +666,6 @@
         rest, b_d = tie(rest, b_d)
         rest = send(rest, True, only=True)
         side = factor_start((a, a_x, swapped, a_d), (b, b_x, b_y, b_d))
-        side = factor_middle(side)
         n_mid = c2.shape[0] // T - n_last
         theirs = jnp.concatenate([c2[: n_mid * T], swapped[-n_last * T :]])
         third, side = tie(jnp.where(same, theirs, c2), side)

time: 102 us -> 99.8 us (0.978)
  starting transfers between devices: 21.9 us -> 12.4 us
  waiting for transfers between devices: 31.8 us -> 40 us
  local copies, waits for them, and re-layouts: 4.71 us -> 2.23 us
    ppermute x13, starting transfers between devices: 21.9 us -> 12.4 us  [send(): return lax.ppermute(value, ('gx', 'gy'), pairs)]
    ppermute x13, waiting for transfers between devices: 31.8 us -> 40 us  [send(): return lax.ppermute(value, ('gx', 'gy'), pairs)]
    unnamed x12 -> x4, local copies, waits for them, and re-layouts: 4.69 us -> 2.19 us
    pallas_call x11 -> x10, Pallas kernels: 42.9 us -> 43.8 us  [call(): pl.pallas_call(kernel, out_shape=[jax.ShapeDtypeStruct(shape, dtype) for...]
  transfers between devices with their start and end apart: 13 -> 13, of which waited for: 7 -> 9; matrix products, arithmetic and copies ran while one was open for 0% -> 0% of each run, Pallas kernels for 37% -> 39%
where the time goes in v12:
time: 99.8 us; the launch traced here: 98.9 us
  Pallas kernels  43.8 us (44%)
  waiting for transfers between devices  40 us (40%)
  starting transfers between devices  12.4 us (12%)
  local copies, waits for them, and re-layouts  2.23 us (2%)
    pallas_call x10, Pallas kernels, call(): pl.pallas_call(kernel, out_shape=[jax.ShapeDtypeStruct(shape, dtype) for...  43.8 us
    ppermute x13, waiting for transfers between devices, send(): return lax.ppermute(value, ('gx', 'gy'), pairs)  40 us
    ppermute x13, starting transfers between devices, send(): return lax.ppermute(value, ('gx', 'gy'), pairs)  12.4 us
    unnamed x4, local copies, waits for them, and re-layouts  2.19 us
  transfers between devices with their start and end apart: 13, of which 9 were waited for; matrix products, arithmetic and copies ran while one was open for 0% of the time, Pallas kernels for 39%

profile of v12, /device:TPU:24, one launch (start us, length us, event | category | flops | bytes accessed | tf_op | source)
XLA Modules:
  0.0 98.9 jit_solution(11018027973264339403)
XLA Ops:
  0.0 0.1 pad_add_fusion.place
  0.1 0.0 copy-start
  0.1 2.2 %copy-done = f32[1,1024,1024]{2,1,0:T(8,128)S(1)} copy-done((f32[1,1024,1024]{2,1,0:T(8,128)S(1)}, f32[1,1024,1024]{2,1,0:T(8,128)}, u32[]{:S(2)}) %copy-start) | copy-done | bytes 4194328
  2.3 0.6 cut_first.1.a0
  2.9 0.6 cut_side.1.mine
  3.5 1.6 %collective-permute-start = (f32[384,128]{1,0:T(8,128)S(1)}, f32[384,128]{1,0:T(8,128)S(1)}, u32[]{:S(2)}, u32[]{:S(2)}) collective-permute-start(f32[384,128]{1,0:T(8,128)S(1)} %cut_side.1.mine), channel_id=1, source_target_pairs={{0,2},{1,3},{2,0},{3,1},{4,6},{5,7},{6,4},{7,5},{8,10},{9,11},{10,... | collective-permute-start | bytes 589832 | tf_op jit(solution)/shard_map/ppermute | solution.py:640
  5.1 0.3 collective-permute-start.1
  5.4 0.9 cut_second.1
  6.4 0.6 collective-permute-start.2
  7.0 4.4 %collective-permute-done.along = f32[384,128]{1,0:T(8,128)S(1)} collective-permute-done((f32[384,128]{1,0:T(8,128)S(1)}, f32[384,128]{1,0:T(8,128)S(1)}, u32[]{:S(2)}, u32[]{:S(2)}) %collective-permute-start) | collective-permute-done | bytes 196640 | tf_op jit(solution)/shard_map/ppermute | solution.py:640
  11.4 7.7 %gauge_side.1 = (f32[256,256]{1,0:T(8,128)}, f32[256,256]{1,0:T(8,128)S(1)}) custom-call(f32[384,128]{1,0:T(8,128)S(1)} %cut_side.1.mine, f32[384,128]{1,0:T(8,128)S(1)} %collective-permute-done.along, f32[256,256]{1,0:T(8,128)S(1)} %get-tuple-element.41.b), custom_call_target="tpu_custom_call" | custom-call | flops 8000000000 | bytes 8000000000 | tf_op jit(solution)/shard_map/gauge_side/pallas_call | solution.py:182
  19.1 0.0 collective-permute-start.3
  19.1 0.4 scale_cross.1
  19.5 0.0 collective-permute-done.1.a1
  19.5 2.0 %collective-permute-done.2.a2.swapped = f32[1024,128]{1,0:T(8,128)S(1)} collective-permute-done((f32[1024,128]{1,0:T(8,128)S(1)}, f32[1024,128]{1,0:T(8,128)S(1)}, u32[]{:S(2)}, u32[]{:S(2)}) %collective-permute-start.2) | collective-permute-done | bytes 524320 | tf_op jit(solution)/shard_map/ppermute | solution.py:640
  21.5 1.5 %collective-permute-start.5 = (f32[512,128]{1,0:T(8,128)S(1)}, f32[512,128]{1,0:T(8,128)S(1)}, u32[]{:S(2)}, u32[]{:S(2)}) collective-permute-start(f32[512,128]{1,0:T(8,128)S(1)} %collective-permute-done.1.a1), channel_id=1, source_target_pairs={{0,2},{1,3},{2,0},{3,1},{4,6},{5,7},{6,4},{7,5},{8,10},{9,11},{10,... | collective-permute-start | bytes 786440 | tf_op jit(solution)/shard_map/ppermute | solution.py:640
  23.0 0.5 collective-permute-start.4
  23.5 8.3 %collective-permute-done.3.b1 = f32[256,256]{1,0:T(8,128)} collective-permute-done((f32[256,256]{1,0:T(8,128)}, f32[256,256]{1,0:T(8,128)}, u32[]{:S(2)}, u32[]{:S(2)}) %collective-permute-start.3) | collective-permute-done | bytes 262176 | tf_op jit(solution)/shard_map/ppermute | solution.py:640
  31.8 0.0 collective-permute-start.8
  31.8 0.0 collective-permute-done.5.a3
  31.8 2.5 %collective-permute-done.4.b2 = f32[256,256]{1,0:T(8,128)} collective-permute-done((f32[256,256]{1,0:T(8,128)}, f32[256,256]{1,0:T(8,128)}, u32[]{:S(2)}, u32[]{:S(2)}) %collective-permute-start.4) | collective-permute-done | bytes 262176 | tf_op jit(solution)/shard_map/ppermute | solution.py:640
  34.4 1.5 %collective-permute-start.6 = (f32[256,256]{1,0:T(8,128)}, f32[256,256]{1,0:T(8,128)S(1)}, u32[]{:S(2)}, u32[]{:S(2)}) collective-permute-start(f32[256,256]{1,0:T(8,128)} %collective-permute-done.3.b1), channel_id=1, source_target_pairs={{0,2},{1,3},{2,0},{3,1},{4,6},{5,7},{6,4},{7,5},{8,10},{9,11},{10,... | collective-permute-start | bytes 786440 | tf_op jit(solution)/shard_map/ppermute | solution.py:640
  36.0 0.1 maximum_select_fusion
  36.0 4.9 %collective-permute-done.6.b3 = f32[256,256]{1,0:T(8,128)S(1)} collective-permute-done((f32[256,256]{1,0:T(8,128)}, f32[256,256]{1,0:T(8,128)S(1)}, u32[]{:S(2)}, u32[]{:S(2)}) %collective-permute-start.6) | collective-permute-done | bytes 262176 | tf_op jit(solution)/shard_map/ppermute | solution.py:640
  40.9 1.5 %collective-permute-start.9 = (f32[1408,128]{1,0:T(8,128)S(1)}, f32[1408,128]{1,0:T(8,128)S(1)}, u32[]{:S(2)}, u32[]{:S(2)}) collective-permute-start(f32[1408,128]{1,0:T(8,128)S(1)} %get-tuple-element.69), channel_id=1, source_target_pairs={{0,2},{1,3},{4,6},{5,7},{8,10},{9,11},{12,14},{13,15},{18,16},{19,... | collective-permute-start | bytes 2162696 | tf_op jit(solution)/shard_map/ppermute | solution.py:640
  42.4 10.5 %factor_start.1.side_in = f32[512,512]{1,0:T(8,128)S(1)} custom-call(f32[512,128]{1,0:T(8,128)S(1)} %cut_first.1.a0, f32[512,128]{1,0:T(8,128)S(1)} %collective-permute-done.1.a1, f32[1024,128]{1,0:T(8,128)S(1)} %collective-permute-done.2.a2.swapped, f32[512,128]{1,0:T(8,128)S(1)} %collective-permute-done.5.a3, f32[256,256]{1,0:T(8,128)} %get-tuple-element.54.b0, ...), custom_call_target="tpu_custom_call" | custom-call | flops 1000000000 | bytes 1000000000 | tf_op jit(solution)/shard_map/factor_start/pallas_call | solution.py:182
  52.9 0.0 copy-start.1
  53.0 1.6 %collective-permute-done.8.c11 = f32[1024,128]{1,0:T(8,128)S(1)} collective-permute-done((f32[1024,128]{1,0:T(8,128)S(1)}, f32[1024,128]{1,0:T(8,128)S(1)}, u32[]{:S(2)}, u32[]{:S(2)}) %collective-permute-start.8) | collective-permute-done | bytes 524320 | tf_op jit(solution)/shard_map/ppermute | solution.py:640
  54.6 2.2 %collective-permute-start.7 = (f32[896,128]{1,0:T(8,128)S(1)}, f32[896,128]{1,0:T(8,128)S(1)}, u32[]{:S(2)}, u32[]{:S(2)}) collective-permute-start(f32[896,128]{1,0:T(8,128)S(1)} %maximum_select_fusion), channel_id=1, source_target_pairs={{0,16},{1,17},{2,18},{3,19},{4,20},{5,21},{6,22},{7,23},{8,24},{9,... | collective-permute-start | bytes 1376264 | tf_op jit(solution)/shard_map/ppermute | solution.py:640
  56.8 1.5 %collective-permute-start.10 = (f32[1024,128]{1,0:T(8,128)S(1)}, f32[1024,128]{1,0:T(8,128)S(1)}, u32[]{:S(2)}, u32[]{:S(2)}) collective-permute-start(f32[1024,128]{1,0:T(8,128)S(1)} %collective-permute-done.8.c11), channel_id=1, source_target_pairs={{0,2},{1,3},{4,6},{5,7},{8,10},{9,11},{12,14},{13,15},{18,16},{19,... | collective-permute-start | bytes 1572872 | tf_op jit(solution)/shard_map/ppermute | solution.py:640
  58.4 11.2 %factor_end.1 = (bf16[768,768]{1,0:T(8,128)(2,1)S(1)}, bf16[768,768]{1,0:T(8,128)(2,1)S(1)}) custom-call(s32[2]{0:T(128)S(1)} %pad_add_fusion.place, f32[512,512]{1,0:T(8,128)S(1)} %factor_start.1.side_in, f32[256,256]{1,0:T(8,128)} %get-tuple-element.54.b0, f32[256,256]{1,0:T(8,128)} %collective-permute-done.3.b1, f32[256,256]{1,0:T(8,128)} %collective-permute-done.4.b2, ...), custom_call_target="tpu_custom_call" | custom-call | flops 10000000000 | bytes 10000000000 | tf_op jit(solution)/shard_map/factor_end/pallas_call | solution.py:182
  69.6 6.7 %collective-permute-done.7.third = f32[896,128]{1,0:T(8,128)S(1)} collective-permute-done((f32[896,128]{1,0:T(8,128)S(1)}, f32[896,128]{1,0:T(8,128)S(1)}, u32[]{:S(2)}, u32[]{:S(2)}) %collective-permute-start.7) | collective-permute-done | bytes 458784 | tf_op jit(solution)/shard_map/ppermute | solution.py:640
  76.2 1.2 %collective-permute-start.11 = (f32[896,128]{1,0:T(8,128)S(1)}, f32[896,128]{1,0:T(8,128)S(1)}, u32[]{:S(2)}, u32[]{:S(2)}) collective-permute-start(f32[896,128]{1,0:T(8,128)S(1)} %collective-permute-done.7.third), channel_id=1, source_target_pairs={{0,2},{1,3},{2,0},{3,1},{4,6},{5,7},{6,4},{7,5},{8,10},{9,11},{10,... | collective-permute-start | bytes 1376264 | tf_op jit(solution)/shard_map/ppermute | solution.py:640
  77.4 0.0 collective-permute-start.12
  77.4 0.0 collective-permute-done.9.rest
  77.4 0.0 copy-done.1
  77.4 4.9 %first_rows.1 = (f32[1,1024,1024]{2,1,0:T(8,128)}, bf16[512,768]{1,0:T(8,128)(2,1)S(1)}, bf16[512,768]{1,0:T(8,128)(2,1)S(1)}, f32[512,768]{1,0:T(8,128)S(1)}) custom-call(s32[2]{0:T(128)S(1)} %pad_add_fusion.place, f32[1,1024,1024]{2,1,0:T(8,128)S(1)} %copy-done.1, bf16[768,768]{1,0:T(8,128)(2,1)S(1)} %get-tuple-element.65.high, ...), custom_call_target="tpu_custom_call" | custom-call | flops 500000000 | bytes 500000000 | tf_op jit(solution)/shard_map/first_rows/pallas_call | solution.py:182
  82.4 0.0 collective-permute-done.10.c31
  82.4 6.3 %collective-permute-done.11.passed = f32[896,128]{1,0:T(8,128)S(1)} collective-permute-done((f32[896,128]{1,0:T(8,128)S(1)}, f32[896,128]{1,0:T(8,128)S(1)}, u32[]{:S(2)}, u32[]{:S(2)}) %collective-permute-start.11) | collective-permute-done | bytes 458784 | tf_op jit(solution)/shard_map/ppermute | solution.py:640
  88.7 2.6 %corner_block.1.before = f32[1,1024,1024]{2,1,0:T(8,128)} custom-call(s32[2]{0:T(128)S(1)} %pad_add_fusion.place, f32[1,1024,1024]{2,1,0:T(8,128)} %get-tuple-element.70.before, bf16[512,768]{1,0:T(8,128)(2,1)S(1)} %get-tuple-element.71.top, bf16[512,768]{1,0:T(8,128)(2,1)S(1)} %get-tuple-element.72.bottom, ...), custom_call_target="tpu_custom_call", output_to_operand_aliasing={{}: (1, {})} | custom-call | flops 500000000 | bytes 500000000 | tf_op jit(solution)/shard_map/corner_block/pallas_call | solution.py:182
  91.3 3.2 %collective-permute-done.12.last = f32[640,128]{1,0:T(8,128)S(1)} collective-permute-done((f32[640,128]{1,0:T(8,128)S(1)}, f32[640,128]{1,0:T(8,128)S(1)}, u32[]{:S(2)}, u32[]{:S(2)}) %collective-permute-start.12) | collective-permute-done | bytes 327712 | tf_op jit(solution)/shard_map/ppermute | solution.py:640
  94.5 4.3 %finish.1 = f32[1,1024,1024]{2,1,0:T(8,128)} custom-call(s32[2]{0:T(128)S(1)} %pad_add_fusion.place, f32[1,1024,1024]{2,1,0:T(8,128)} %corner_block.1.before, bf16[768,768]{1,0:T(8,128)(2,1)S(1)} %get-tuple-element.65.high, bf16[768,768]{1,0:T(8,128)(2,1)S(1)} %get-tuple-element.66.low, ...), custom_call_target="tpu_custom_call", output_to_operand_aliasing={{}: (1, {})} | custom-call | flops 500000000 | bytes 500000000 | tf_op jit(solution)/shard_map/finish/pallas_call | solution.py:182
  (3 shorter events, 0.1 us)
Async XLA Ops:
  0.1 2.2 %copy-start = (f32[1,1024,1024]{2,1,0:T(8,128)S(1)}, f32[1,1024,1024]{2,1,0:T(8,128)}, u32[]{:S(2)}) copy-start(f32[1,1024,1024]{2,1,0:T(8,128)} %leaf.7) | copy-start | bytes 12582916
  3.5 7.9 %collective-permute-start = (f32[384,128]{1,0:T(8,128)S(1)}, f32[384,128]{1,0:T(8,128)S(1)}, u32[]{:S(2)}, u32[]{:S(2)}) collective-permute-start(f32[384,128]{1,0:T(8,128)S(1)} %cut_side.1.mine), channel_id=1, source_target_pairs={{0,2},{1,3},{2,0},{3,1},{4,6},{5,7},{6,4},{7,5},{8,10},{9,11},{10,... | collective-permute-start | bytes 589832 | tf_op jit(solution)/shard_map/ppermute | solution.py:640
  5.1 14.4 %collective-permute-start.1 = (f32[512,128]{1,0:T(8,128)S(1)}, f32[512,128]{1,0:T(8,128)S(1)}, u32[]{:S(2)}, u32[]{:S(2)}) collective-permute-start(f32[512,128]{1,0:T(8,128)S(1)} %cut_first.1.a0), channel_id=1, source_target_pairs={{0,16},{1,17},{2,18},{3,19},{4,20},{5,21},{6,22},{7,23},{8,24},{9,... | collective-permute-start | bytes 786440 | tf_op jit(solution)/shard_map/ppermute | solution.py:640
  6.4 15.1 %collective-permute-start.2 = (f32[1024,128]{1,0:T(8,128)S(1)}, f32[1024,128]{1,0:T(8,128)S(1)}, u32[]{:S(2)}, u32[]{:S(2)}) collective-permute-start(f32[1024,128]{1,0:T(8,128)S(1)} %get-tuple-element.48), channel_id=1, source_target_pairs={{0,2},{1,3},{2,0},{3,1},{4,6},{5,7},{6,4},{7,5},{8,10},{9,11},{10,... | collective-permute-start | bytes 1572872 | tf_op jit(solution)/shard_map/ppermute | solution.py:640
  19.1 12.7 %collective-permute-start.3 = (f32[256,256]{1,0:T(8,128)}, f32[256,256]{1,0:T(8,128)}, u32[]{:S(2)}, u32[]{:S(2)}) collective-permute-start(f32[256,256]{1,0:T(8,128)} %get-tuple-element.54.b0), channel_id=1, source_target_pairs={{0,16},{1,17},{2,18},{3,19},{4,20},{5,21},{6,22},{7,23},{8,24},{9,... | collective-permute-start | bytes 786440 | tf_op jit(solution)/shard_map/ppermute | solution.py:640
  21.5 10.4 %collective-permute-start.5 = (f32[512,128]{1,0:T(8,128)S(1)}, f32[512,128]{1,0:T(8,128)S(1)}, u32[]{:S(2)}, u32[]{:S(2)}) collective-permute-start(f32[512,128]{1,0:T(8,128)S(1)} %collective-permute-done.1.a1), channel_id=1, source_target_pairs={{0,2},{1,3},{2,0},{3,1},{4,6},{5,7},{6,4},{7,5},{8,10},{9,11},{10,... | collective-permute-start | bytes 786440 | tf_op jit(solution)/shard_map/ppermute | solution.py:640
  23.0 11.4 %collective-permute-start.4 = (f32[256,256]{1,0:T(8,128)}, f32[256,256]{1,0:T(8,128)}, u32[]{:S(2)}, u32[]{:S(2)}) collective-permute-start(f32[256,256]{1,0:T(8,128)} %get-tuple-element.54.b0), channel_id=1, source_target_pairs={{0,2},{1,3},{2,0},{3,1},{4,6},{5,7},{6,4},{7,5},{8,10},{9,11},{10,... | collective-permute-start | bytes 786440 | tf_op jit(solution)/shard_map/ppermute | solution.py:640
  31.8 22.8 %collective-permute-start.8 = (f32[1024,128]{1,0:T(8,128)S(1)}, f32[1024,128]{1,0:T(8,128)S(1)}, u32[]{:S(2)}, u32[]{:S(2)}) collective-permute-start(f32[1024,128]{1,0:T(8,128)S(1)} %get-tuple-element.61.c01), channel_id=1, source_target_pairs={{0,16},{1,17},{2,18},{3,19},{4,20},{5,21},{6,22},{7,23},{8,24},{9,... | collective-permute-start | bytes 1572872 | tf_op jit(solution)/shard_map/ppermute | solution.py:640
  34.4 6.6 %collective-permute-start.6 = (f32[256,256]{1,0:T(8,128)}, f32[256,256]{1,0:T(8,128)S(1)}, u32[]{:S(2)}, u32[]{:S(2)}) collective-permute-start(f32[256,256]{1,0:T(8,128)} %collective-permute-done.3.b1), channel_id=1, source_target_pairs={{0,2},{1,3},{2,0},{3,1},{4,6},{5,7},{6,4},{7,5},{8,10},{9,11},{10,... | collective-permute-start | bytes 786440 | tf_op jit(solution)/shard_map/ppermute | solution.py:640
  40.9 36.5 %collective-permute-start.9 = (f32[1408,128]{1,0:T(8,128)S(1)}, f32[1408,128]{1,0:T(8,128)S(1)}, u32[]{:S(2)}, u32[]{:S(2)}) collective-permute-start(f32[1408,128]{1,0:T(8,128)S(1)} %get-tuple-element.69), channel_id=1, source_target_pairs={{0,2},{1,3},{4,6},{5,7},{8,10},{9,11},{12,14},{13,15},{18,16},{19,... | collective-permute-start | bytes 2162696 | tf_op jit(solution)/shard_map/ppermute | solution.py:640
  52.9 24.5 %copy-start.1 = (f32[1,1024,1024]{2,1,0:T(8,128)S(1)}, f32[1,1024,1024]{2,1,0:T(8,128)}, u32[]{:S(2)}) copy-start(f32[1,1024,1024]{2,1,0:T(8,128)} %leaf.7) | copy-start | bytes 12582916
  54.6 21.6 %collective-permute-start.7 = (f32[896,128]{1,0:T(8,128)S(1)}, f32[896,128]{1,0:T(8,128)S(1)}, u32[]{:S(2)}, u32[]{:S(2)}) collective-permute-start(f32[896,128]{1,0:T(8,128)S(1)} %maximum_select_fusion), channel_id=1, source_target_pairs={{0,16},{1,17},{2,18},{3,19},{4,20},{5,21},{6,22},{7,23},{8,24},{9,... | collective-permute-start | bytes 1376264 | tf_op jit(solution)/shard_map/ppermute | solution.py:640
  56.8 25.5 %collective-permute-start.10 = (f32[1024,128]{1,0:T(8,128)S(1)}, f32[1024,128]{1,0:T(8,128)S(1)}, u32[]{:S(2)}, u32[]{:S(2)}) collective-permute-start(f32[1024,128]{1,0:T(8,128)S(1)} %collective-permute-done.8.c11), channel_id=1, source_target_pairs={{0,2},{1,3},{4,6},{5,7},{8,10},{9,11},{12,14},{13,15},{18,16},{19,... | collective-permute-start | bytes 1572872 | tf_op jit(solution)/shard_map/ppermute | solution.py:640
  76.2 12.4 %collective-permute-start.11 = (f32[896,128]{1,0:T(8,128)S(1)}, f32[896,128]{1,0:T(8,128)S(1)}, u32[]{:S(2)}, u32[]{:S(2)}) collective-permute-start(f32[896,128]{1,0:T(8,128)S(1)} %collective-permute-done.7.third), channel_id=1, source_target_pairs={{0,2},{1,3},{2,0},{3,1},{4,6},{5,7},{6,4},{7,5},{8,10},{9,11},{10,... | collective-permute-start | bytes 1376264 | tf_op jit(solution)/shard_map/ppermute | solution.py:640
  77.4 17.1 %collective-permute-start.12 = (f32[640,128]{1,0:T(8,128)S(1)}, f32[640,128]{1,0:T(8,128)S(1)}, u32[]{:S(2)}, u32[]{:S(2)}) collective-permute-start(f32[640,128]{1,0:T(8,128)S(1)} %slice_select_fusion), channel_id=1, source_target_pairs={{0,16},{1,17},{2,18},{3,19},{4,20},{5,21},{6,22},{7,23},{8,24},{9,... | collective-permute-start | bytes 983048 | tf_op jit(solution)/shard_map/ppermute | solution.py:640

commit v13 on v7

--- a/solution.py
+++ b/solution.py
@@ -98,9 +98,11 @@
         if c0 + R < T:
             old = m[c0 + R : c0 + 2 * R]
             inside = (lane[:R] >= c0) & (lane[:R] < c0 + R)
-            rows = jnp.where(inside, 0.0, old)
+            sums = [jnp.where(inside, 0.0, old)] + [None] * 3
             for k in range(R):
-                rows = rows - across_lanes(old, c0 + k) * across_rows(swept, k)
+                term = across_lanes(old, c0 + k) * across_rows(swept, k)
+                sums[k % 4] = -term if sums[k % 4] is None else sums[k % 4] - term
+            rows = (sums[0] + sums[1]) + (sums[2] + sums[3])
         wide = put_rows(jnp.zeros((T, T), F32), swept, c0)
         rest = jnp.where((lane >= c0) & (lane < c0 + R), 0.0, m) - dot(m, wide)
         if lower:
@@ -678,11 +680,10 @@
         c1, c2, rest = scale_cross(factor, c, n_last)
         b, a_x, c1, swapped = tie(b, a_x, c1, swapped)
         b_y = send(b, True)
-        a_x, b_y = tie(a_x, b_y)
         a_d = send(a_x, True)
         c1, b_x = tie(c1, b_x)
         c1_x = send(c1, False)
-        b_x, b_y = tie(b_x, b_y)
+        b_x, b_y, a_d = tie(b_x, b_y, a_d)
         b_d = send(b_x, True)
         rest, b_d = tie(rest, b_d)
         rest = send(rest, True, only=True)

time: 97.5 us -> 107 us (1.097)
  the two profiles are of different devices: /device:TPU:24 before, /device:TPU:0 now
where the time goes in v13:
time: 107 us
  Pallas kernels  45.2 us (42%)
  starting transfers between devices  32.5 us (30%)
  waiting for transfers between devices  26.3 us (25%)
  local copies, waits for them, and re-layouts  2.23 us (2%)
    pallas_call x10, Pallas kernels, call(): pl.pallas_call(kernel, out_shape=[jax.ShapeDtypeStruct(shape, dtype) for...  45.2 us
    ppermute x13, starting transfers between devices, send(): return lax.ppermute(value, ('gx', 'gy'), pairs)  32.5 us
    ppermute x13, waiting for transfers between devices, send(): return lax.ppermute(value, ('gx', 'gy'), pairs)  26.3 us
    unnamed x4, local copies, waits for them, and re-layouts  2.19 us
  transfers between devices with their start and end apart: 13, of which 6 were waited for; matrix products, arithmetic and copies ran while one was open for 0% of the time, Pallas kernels for 40%

profile of v13, /device:TPU:0, one launch (start us, length us, event | category | flops | bytes accessed | tf_op | source)
XLA Modules:
  0.0 106.7 jit_solution(13201055281187412987)
XLA Ops:
  0.0 0.1 pad_add_fusion.place
  0.1 0.0 copy-start
  0.1 2.2 %copy-done = f32[1,1024,1024]{2,1,0:T(8,128)S(1)} copy-done((f32[1,1024,1024]{2,1,0:T(8,128)S(1)}, f32[1,1024,1024]{2,1,0:T(8,128)}, u32[]{:S(2)}) %copy-start) | copy-done | bytes 4194328
  2.3 0.6 cut_first.1.a0
  2.9 0.6 cut_side.1.mine
  3.5 3.0 %collective-permute-start = (f32[384,128]{1,0:T(8,128)S(1)}, f32[384,128]{1,0:T(8,128)S(1)}, u32[]{:S(2)}, u32[]{:S(2)}) collective-permute-start(f32[384,128]{1,0:T(8,128)S(1)} %cut_side.1.mine), channel_id=1, source_target_pairs={{0,2},{1,3},{2,0},{3,1},{4,6},{5,7},{6,4},{7,5},{8,10},{9,11},{10,... | collective-permute-start | bytes 589832 | tf_op jit(solution)/shard_map/ppermute | solution.py:662
  6.6 2.6 %collective-permute-start.1 = (f32[512,128]{1,0:T(8,128)S(1)}, f32[512,128]{1,0:T(8,128)S(1)}, u32[]{:S(2)}, u32[]{:S(2)}) collective-permute-start(f32[512,128]{1,0:T(8,128)S(1)} %cut_first.1.a0), channel_id=1, source_target_pairs={{0,16},{1,17},{2,18},{3,19},{4,20},{5,21},{6,22},{7,23},{8,24},{9,... | collective-permute-start | bytes 786440 | tf_op jit(solution)/shard_map/ppermute | solution.py:662
  9.1 0.9 cut_second.1
  10.1 0.6 collective-permute-start.2
  10.7 0.8 collective-permute-done.along
  11.5 7.7 %gauge_side.1 = (f32[256,256]{1,0:T(8,128)}, f32[256,256]{1,0:T(8,128)S(1)}) custom-call(f32[384,128]{1,0:T(8,128)S(1)} %cut_side.1.mine, f32[384,128]{1,0:T(8,128)S(1)} %collective-permute-done.along, f32[256,256]{1,0:T(8,128)S(1)} %get-tuple-element.41.b), custom_call_target="tpu_custom_call" | custom-call | flops 8000000000 | bytes 8000000000 | tf_op jit(solution)/shard_map/gauge_side/pallas_call | solution.py:182
  19.1 4.0 %collective-permute-start.3 = (f32[256,256]{1,0:T(8,128)}, f32[256,256]{1,0:T(8,128)}, u32[]{:S(2)}, u32[]{:S(2)}) collective-permute-start(f32[256,256]{1,0:T(8,128)} %get-tuple-element.53.b0), channel_id=1, source_target_pairs={{0,16},{1,17},{2,18},{3,19},{4,20},{5,21},{6,22},{7,23},{8,24},{9,... | collective-permute-start | bytes 786440 | tf_op jit(solution)/shard_map/ppermute | solution.py:662
  23.1 0.4 scale_cross.1
  23.5 0.0 collective-permute-done.1.a1
  23.5 0.0 collective-permute-done.2.a2.swapped
  23.5 1.6 %collective-permute-start.4 = (f32[256,256]{1,0:T(8,128)}, f32[256,256]{1,0:T(8,128)}, u32[]{:S(2)}, u32[]{:S(2)}) collective-permute-start(f32[256,256]{1,0:T(8,128)} %get-tuple-element.53.b0), channel_id=1, source_target_pairs={{0,2},{1,3},{2,0},{3,1},{4,6},{5,7},{6,4},{7,5},{8,10},{9,11},{10,... | collective-permute-start | bytes 786440 | tf_op jit(solution)/shard_map/ppermute | solution.py:662
  25.1 0.5 collective-permute-start.5
  25.6 7.8 %collective-permute-done.3.b1 = f32[256,256]{1,0:T(8,128)} collective-permute-done((f32[256,256]{1,0:T(8,128)}, f32[256,256]{1,0:T(8,128)}, u32[]{:S(2)}, u32[]{:S(2)}) %collective-permute-start.3) | collective-permute-done | bytes 262176 | tf_op jit(solution)/shard_map/ppermute | solution.py:662
  33.5 0.0 collective-permute-start.7
  33.5 0.0 collective-permute-done.4.b2
  33.5 2.3 %collective-permute-done.5.a3 = f32[512,128]{1,0:T(8,128)S(1)} collective-permute-done((f32[512,128]{1,0:T(8,128)S(1)}, f32[512,128]{1,0:T(8,128)S(1)}, u32[]{:S(2)}, u32[]{:S(2)}) %collective-permute-start.5) | collective-permute-done | bytes 262176 | tf_op jit(solution)/shard_map/ppermute | solution.py:662
  35.7 1.7 %collective-permute-start.6 = (f32[256,256]{1,0:T(8,128)}, f32[256,256]{1,0:T(8,128)S(1)}, u32[]{:S(2)}, u32[]{:S(2)}) collective-permute-start(f32[256,256]{1,0:T(8,128)} %collective-permute-done.3.b1), channel_id=1, source_target_pairs={{0,2},{1,3},{2,0},{3,1},{4,6},{5,7},{6,4},{7,5},{8,10},{9,11},{10,... | collective-permute-start | bytes 786440 | tf_op jit(solution)/shard_map/ppermute | solution.py:662
  37.6 0.1 maximum_select_fusion
  37.6 4.7 %collective-permute-done.6.b3 = f32[256,256]{1,0:T(8,128)S(1)} collective-permute-done((f32[256,256]{1,0:T(8,128)}, f32[256,256]{1,0:T(8,128)S(1)}, u32[]{:S(2)}, u32[]{:S(2)}) %collective-permute-start.6) | collective-permute-done | bytes 262176 | tf_op jit(solution)/shard_map/ppermute | solution.py:662
  42.3 3.9 %collective-permute-start.8 = (f32[1408,128]{1,0:T(8,128)S(1)}, f32[1408,128]{1,0:T(8,128)S(1)}, u32[]{:S(2)}, u32[]{:S(2)}) collective-permute-start(f32[1408,128]{1,0:T(8,128)S(1)} %get-tuple-element.63), channel_id=1, source_target_pairs={{0,2},{1,3},{4,6},{5,7},{8,10},{9,11},{12,14},{13,15},{18,16},{19,... | collective-permute-start | bytes 2162696 | tf_op jit(solution)/shard_map/ppermute | solution.py:662
  46.2 10.5 %factor_start.1.side_in = f32[512,512]{1,0:T(8,128)S(1)} custom-call(f32[512,128]{1,0:T(8,128)S(1)} %cut_first.1.a0, f32[512,128]{1,0:T(8,128)S(1)} %collective-permute-done.1.a1, f32[1024,128]{1,0:T(8,128)S(1)} %collective-permute-done.2.a2.swapped, f32[512,128]{1,0:T(8,128)S(1)} %collective-permute-done.5.a3, f32[256,256]{1,0:T(8,128)} %get-tuple-element.53.b0, ...), custom_call_target="tpu_custom_call" | custom-call | flops 1000000000 | bytes 1000000000 | tf_op jit(solution)/shard_map/factor_start/pallas_call | solution.py:182
  56.7 0.0 copy-start.1
  56.7 0.4 collective-permute-start.9
  57.2 3.0 %collective-permute-done.7.c11 = f32[1024,128]{1,0:T(8,128)S(1)} collective-permute-done((f32[1024,128]{1,0:T(8,128)S(1)}, f32[1024,128]{1,0:T(8,128)S(1)}, u32[]{:S(2)}, u32[]{:S(2)}) %collective-permute-start.7) | collective-permute-done | bytes 524320 | tf_op jit(solution)/shard_map/ppermute | solution.py:662
  60.1 13.4 %collective-permute-start.10 = (f32[1024,128]{1,0:T(8,128)S(1)}, f32[1024,128]{1,0:T(8,128)S(1)}, u32[]{:S(2)}, u32[]{:S(2)}) collective-permute-start(f32[1024,128]{1,0:T(8,128)S(1)} %collective-permute-done.7.c11), channel_id=1, source_target_pairs={{0,2},{1,3},{4,6},{5,7},{8,10},{9,11},{12,14},{13,15},{18,16},{19,... | collective-permute-start | bytes 1572872 | tf_op jit(solution)/shard_map/ppermute | solution.py:662
  73.5 11.2 %factor_end.1 = (bf16[768,768]{1,0:T(8,128)(2,1)S(1)}, bf16[768,768]{1,0:T(8,128)(2,1)S(1)}) custom-call(s32[2]{0:T(128)S(1)} %pad_add_fusion.place, f32[512,512]{1,0:T(8,128)S(1)} %factor_start.1.side_in, f32[256,256]{1,0:T(8,128)} %get-tuple-element.53.b0, f32[256,256]{1,0:T(8,128)} %collective-permute-done.3.b1, f32[256,256]{1,0:T(8,128)} %collective-permute-done.4.b2, ...), custom_call_target="tpu_custom_call" | custom-call | flops 10000000000 | bytes 10000000000 | tf_op jit(solution)/shard_map/factor_end/pallas_call | solution.py:182
  84.8 0.0 collective-permute-done.8.rest
  84.8 0.0 copy-done.1
  84.8 4.9 %own_rows.1 = (bf16[512,768]{1,0:T(8,128)(2,1)S(1)}, bf16[512,768]{1,0:T(8,128)(2,1)S(1)}, f32[512,512]{1,0:T(8,128)S(1)}, f32[512,768]{1,0:T(8,128)S(1)}) custom-call(s32[2]{0:T(128)S(1)} %pad_add_fusion.place, f32[1,1024,1024]{2,1,0:T(8,128)S(1)} %copy-done.1, bf16[768,768]{1,0:T(8,128)(2,1)S(1)} %get-tuple-element.60.high, ...), custom_call_target="tpu_custom_call" | custom-call | flops 500000000 | bytes 500000000 | tf_op jit(solution)/shard_map/own_rows/pallas_call | solution.py:182
  89.7 0.0 collective-permute-done.9.third
  89.7 0.7 collective-permute-start.11
  90.4 0.0 collective-permute-start.12
  90.4 0.0 collective-permute-done.10.c31
  90.4 7.8 %collective-permute-done.11.passed = f32[896,128]{1,0:T(8,128)S(1)} collective-permute-done((f32[896,128]{1,0:T(8,128)S(1)}, f32[896,128]{1,0:T(8,128)S(1)}, u32[]{:S(2)}, u32[]{:S(2)}) %collective-permute-start.11) | collective-permute-done | bytes 458784 | tf_op jit(solution)/shard_map/ppermute | solution.py:662
  98.2 6.6 %products.1 = (f32[1,1024,1024]{2,1,0:T(8,128)}, f32[512,512]{1,0:T(8,128)S(1)}) custom-call(s32[2]{0:T(128)S(1)} %pad_add_fusion.place, bf16[768,768]{1,0:T(8,128)(2,1)S(1)} %get-tuple-element.60.high, bf16[768,768]{1,0:T(8,128)(2,1)S(1)} %get-tuple-element.61.low, bf16[512,768]{1,0:T(8,128)(2,1)S(1)} %get-tuple-element.64.top, ...), custom_call_target="tpu_custom_call" | custom-call | flops 500000000 | bytes 500000000 | tf_op jit(solution)/shard_map/products/pallas_call | solution.py:182
  104.8 0.0 collective-permute-done.12.last
  104.8 1.8 %finish.1 = f32[1,1024,1024]{2,1,0:T(8,128)} custom-call(s32[2]{0:T(128)S(1)} %pad_add_fusion.place, f32[1,1024,1024]{2,1,0:T(8,128)} %get-tuple-element.71.before, bf16[768,768]{1,0:T(8,128)(2,1)S(1)} %get-tuple-element.60.high, bf16[768,768]{1,0:T(8,128)(2,1)S(1)} %get-tuple-element.61.low, ...), custom_call_target="tpu_custom_call", output_to_operand_aliasing={{}: (1, {})} | custom-call | flops 500000000 | bytes 500000000 | tf_op jit(solution)/shard_map/finish/pallas_call | solution.py:182
  (3 shorter events, 0.1 us)
Async XLA Ops:
  0.1 2.2 %copy-start = (f32[1,1024,1024]{2,1,0:T(8,128)S(1)}, f32[1,1024,1024]{2,1,0:T(8,128)}, u32[]{:S(2)}) copy-start(f32[1,1024,1024]{2,1,0:T(8,128)} %leaf.7) | copy-start | bytes 12582916
  3.5 7.9 %collective-permute-start = (f32[384,128]{1,0:T(8,128)S(1)}, f32[384,128]{1,0:T(8,128)S(1)}, u32[]{:S(2)}, u32[]{:S(2)}) collective-permute-start(f32[384,128]{1,0:T(8,128)S(1)} %cut_side.1.mine), channel_id=1, source_target_pairs={{0,2},{1,3},{2,0},{3,1},{4,6},{5,7},{6,4},{7,5},{8,10},{9,11},{10,... | collective-permute-start | bytes 589832 | tf_op jit(solution)/shard_map/ppermute | solution.py:662
  6.6 17.0 %collective-permute-start.1 = (f32[512,128]{1,0:T(8,128)S(1)}, f32[512,128]{1,0:T(8,128)S(1)}, u32[]{:S(2)}, u32[]{:S(2)}) collective-permute-start(f32[512,128]{1,0:T(8,128)S(1)} %cut_first.1.a0), channel_id=1, source_target_pairs={{0,16},{1,17},{2,18},{3,19},{4,20},{5,21},{6,22},{7,23},{8,24},{9,... | collective-permute-start | bytes 786440 | tf_op jit(solution)/shard_map/ppermute | solution.py:662
  10.1 13.4 %collective-permute-start.2 = (f32[1024,128]{1,0:T(8,128)S(1)}, f32[1024,128]{1,0:T(8,128)S(1)}, u32[]{:S(2)}, u32[]{:S(2)}) collective-permute-start(f32[1024,128]{1,0:T(8,128)S(1)} %get-tuple-element.47), channel_id=1, source_target_pairs={{0,2},{1,3},{2,0},{3,1},{4,6},{5,7},{6,4},{7,5},{8,10},{9,11},{10,... | collective-permute-start | bytes 1572872 | tf_op jit(solution)/shard_map/ppermute | solution.py:662
  19.1 14.3 %collective-permute-start.3 = (f32[256,256]{1,0:T(8,128)}, f32[256,256]{1,0:T(8,128)}, u32[]{:S(2)}, u32[]{:S(2)}) collective-permute-start(f32[256,256]{1,0:T(8,128)} %get-tuple-element.53.b0), channel_id=1, source_target_pairs={{0,16},{1,17},{2,18},{3,19},{4,20},{5,21},{6,22},{7,23},{8,24},{9,... | collective-permute-start | bytes 786440 | tf_op jit(solution)/shard_map/ppermute | solution.py:662
  23.5 9.9 %collective-permute-start.4 = (f32[256,256]{1,0:T(8,128)}, f32[256,256]{1,0:T(8,128)}, u32[]{:S(2)}, u32[]{:S(2)}) collective-permute-start(f32[256,256]{1,0:T(8,128)} %get-tuple-element.53.b0), channel_id=1, source_target_pairs={{0,2},{1,3},{2,0},{3,1},{4,6},{5,7},{6,4},{7,5},{8,10},{9,11},{10,... | collective-permute-start | bytes 786440 | tf_op jit(solution)/shard_map/ppermute | solution.py:662
  25.1 10.6 %collective-permute-start.5 = (f32[512,128]{1,0:T(8,128)S(1)}, f32[512,128]{1,0:T(8,128)S(1)}, u32[]{:S(2)}, u32[]{:S(2)}) collective-permute-start(f32[512,128]{1,0:T(8,128)S(1)} %collective-permute-done.1.a1), channel_id=1, source_target_pairs={{0,2},{1,3},{2,0},{3,1},{4,6},{5,7},{6,4},{7,5},{8,10},{9,11},{10,... | collective-permute-start | bytes 786440 | tf_op jit(solution)/shard_map/ppermute | solution.py:662
  33.5 26.6 %collective-permute-start.7 = (f32[1024,128]{1,0:T(8,128)S(1)}, f32[1024,128]{1,0:T(8,128)S(1)}, u32[]{:S(2)}, u32[]{:S(2)}) collective-permute-start(f32[1024,128]{1,0:T(8,128)S(1)} %get-tuple-element.62.c01), channel_id=1, source_target_pairs={{0,16},{1,17},{2,18},{3,19},{4,20},{5,21},{6,22},{7,23},{8,24},{9,... | collective-permute-start | bytes 1572872 | tf_op jit(solution)/shard_map/ppermute | solution.py:662
  35.7 6.6 %collective-permute-start.6 = (f32[256,256]{1,0:T(8,128)}, f32[256,256]{1,0:T(8,128)S(1)}, u32[]{:S(2)}, u32[]{:S(2)}) collective-permute-start(f32[256,256]{1,0:T(8,128)} %collective-permute-done.3.b1), channel_id=1, source_target_pairs={{0,2},{1,3},{2,0},{3,1},{4,6},{5,7},{6,4},{7,5},{8,10},{9,11},{10,... | collective-permute-start | bytes 786440 | tf_op jit(solution)/shard_map/ppermute | solution.py:662
  42.3 42.4 %collective-permute-start.8 = (f32[1408,128]{1,0:T(8,128)S(1)}, f32[1408,128]{1,0:T(8,128)S(1)}, u32[]{:S(2)}, u32[]{:S(2)}) collective-permute-start(f32[1408,128]{1,0:T(8,128)S(1)} %get-tuple-element.63), channel_id=1, source_target_pairs={{0,2},{1,3},{4,6},{5,7},{8,10},{9,11},{12,14},{13,15},{18,16},{19,... | collective-permute-start | bytes 2162696 | tf_op jit(solution)/shard_map/ppermute | solution.py:662
  56.7 28.0 %copy-start.1 = (f32[1,1024,1024]{2,1,0:T(8,128)S(1)}, f32[1,1024,1024]{2,1,0:T(8,128)}, u32[]{:S(2)}) copy-start(f32[1,1024,1024]{2,1,0:T(8,128)} %leaf.7) | copy-start | bytes 12582916
  56.7 32.9 %collective-permute-start.9 = (f32[896,128]{1,0:T(8,128)S(1)}, f32[896,128]{1,0:T(8,128)S(1)}, u32[]{:S(2)}, u32[]{:S(2)}) collective-permute-start(f32[896,128]{1,0:T(8,128)S(1)} %maximum_select_fusion), channel_id=1, source_target_pairs={{0,16},{1,17},{2,18},{3,19},{4,20},{5,21},{6,22},{7,23},{8,24},{9,... | collective-permute-start | bytes 1376264 | tf_op jit(solution)/shard_map/ppermute | solution.py:662
  60.1 30.3 %collective-permute-start.10 = (f32[1024,128]{1,0:T(8,128)S(1)}, f32[1024,128]{1,0:T(8,128)S(1)}, u32[]{:S(2)}, u32[]{:S(2)}) collective-permute-start(f32[1024,128]{1,0:T(8,128)S(1)} %collective-permute-done.7.c11), channel_id=1, source_target_pairs={{0,2},{1,3},{4,6},{5,7},{8,10},{9,11},{12,14},{13,15},{18,16},{19,... | collective-permute-start | bytes 1572872 | tf_op jit(solution)/shard_map/ppermute | solution.py:662
  89.7 8.5 %collective-permute-start.11 = (f32[896,128]{1,0:T(8,128)S(1)}, f32[896,128]{1,0:T(8,128)S(1)}, u32[]{:S(2)}, u32[]{:S(2)}) collective-permute-start(f32[896,128]{1,0:T(8,128)S(1)} %collective-permute-done.9.third), channel_id=1, source_target_pairs={{0,2},{1,3},{2,0},{3,1},{4,6},{5,7},{6,4},{7,5},{8,10},{9,11},{10,... | collective-permute-start | bytes 1376264 | tf_op jit(solution)/shard_map/ppermute | solution.py:662
  90.4 14.4 %collective-permute-start.12 = (f32[640,128]{1,0:T(8,128)S(1)}, f32[640,128]{1,0:T(8,128)S(1)}, u32[]{:S(2)}, u32[]{:S(2)}) collective-permute-start(f32[640,128]{1,0:T(8,128)S(1)} %slice_select_fusion), channel_id=1, source_target_pairs={{0,16},{1,17},{2,18},{3,19},{4,20},{5,21},{6,22},{7,23},{8,24},{9,... | collective-permute-start | bytes 983048 | tf_op jit(solution)/shard_map/ppermute | solution.py:662

commit v14 on v13

--- a/solution.py
+++ b/solution.py
@@ -510,13 +510,21 @@
     return pl.ds(pl.multiple_of((2 * side + x) * e, T), e)
 
 
-def write(out, place, value, a, b):
+def put(out, place, held, a, b, sem):
     e = out.shape[1] // 4
+    copies = []
     for r in range(2):
         for c in range(2):
-            out[0, spot(place, e, r, a), spot(place, e, c, b)] = value[
-                r * e : (r + 1) * e, c * e : (c + 1) * e
-            ]
+            source = held.at[pl.ds(r * e, e), pl.ds(c * e, e)]
+            target = out.at[0, spot(place, e, r, a), spot(place, e, c, b)]
+            copies.append(pltpu.make_async_copy(source, target, sem.at[2 * r + c]))
+            copies[-1].start()
+    return copies
+
+
+def wait(copies):
+    for copy in copies:
+        copy.wait()
 
 
 def pick(ref, rows, b):
@@ -525,12 +533,12 @@
 
 
 def products_kernel(
-    place, high, low, top, bottom, block, a0, c01, c02, a1, c11, third, a3, c31, passed, out, part, scratch
+    place, high, low, top, bottom, block, a0, c01, c02, a1, c11, third, a3, c31, passed, out, part, held, scratch, sem
 ):
     e = out.shape[1] // 4
     n_sym = symmetric_tiles(e)
     same = place[0] == place[1]
-    write(out, place, block[...], 0, 0)
+    first = put(out, place, block, 0, 0, sem.at[0])
     everything = slice(0, 2 * e)
 
     @pl.when(same)
@@ -538,19 +546,25 @@
         across = cross_block((a1, n_sym), (c11, 0), (third, 0))
         right = split(across)
         left = [pick(x, everything, 1) for x in (top, bottom)]
-        write(out, place, -dot3(left, right, NT), 0, 1)
+        held[0] = -dot3(left, right, NT)
+        copies = put(out, place, held.at[0], 0, 1, sem.at[1])
         scratch[...] = times_inverse(across, high[...], low[...], slice(2 * e, 3 * e))
         left = split(pick(scratch, everything, 0))
         mine = cross_block((a0, n_sym), (c01, 0), (c02, 0))
-        write(out, place, -dot3(left, split(mine), NT), 1, 0)
+        held[1] = -dot3(left, split(mine), NT)
+        copies += put(out, place, held.at[1], 1, 0, sem.at[2])
         left = split(pick(scratch, everything, 1))
         part[...] = -dot3(left, right, NT)
+        wait(copies)
 
     @pl.when(jnp.logical_not(same))
     def _():
         right = split(cross_block((a3, n_sym), (c31, 0), (passed, 0)))
         left = [pick(x, everything, 1) for x in (top, bottom)]
-        write(out, place, -dot3(left, right, NT), 0, 1)
+        held[0] = -dot3(left, right, NT)
+        wait(put(out, place, held.at[0], 0, 1, sem.at[1]))
+
+    wait(first)
 
 
 def products(place, high, low, top, bottom, block, mine, across, corner):
@@ -562,7 +576,12 @@
         [((1, 4 * e, 4 * e), F32), ((2 * e, 2 * e), F32)],
         [(SMEM, place)]
         + [(VMEM, x) for x in (high, low, top, bottom, block, *mine, *across, *corner)],
-        [pltpu.VMEM((2 * e, 3 * e), F32)],
+        [
+            pltpu.VMEM((2, 2 * e, 2 * e), F32),
+            pltpu.VMEM((2 * e, 3 * e), F32),
+            pltpu.SemaphoreType.DMA((3, 4)),
+        ],
+        out_specs=[HBM, VMEM],
     )
 
 
@@ -680,10 +699,11 @@
         c1, c2, rest = scale_cross(factor, c, n_last)
         b, a_x, c1, swapped = tie(b, a_x, c1, swapped)
         b_y = send(b, True)
+        a_x, b_y = tie(a_x, b_y)
         a_d = send(a_x, True)
         c1, b_x = tie(c1, b_x)
         c1_x = send(c1, False)
-        b_x, b_y, a_d = tie(b_x, b_y, a_d)
+        b_x, b_y = tie(b_x, b_y)
         b_d = send(b_x, True)
         rest, b_d = tie(rest, b_d)
         rest = send(rest, True, only=True)

time: 107 us -> 96.8 us (0.905)
  the two profiles are of different devices: /device:TPU:0 before, /device:TPU:24 now
where the time goes in v14:
time: 96.8 us; the launch traced here: 95.5 us
  Pallas kernels  44.5 us (46%)
  waiting for transfers between devices  34.3 us (35%)
  starting transfers between devices  14 us (14%)
  local copies, waits for them, and re-layouts  2.23 us (2%)
    pallas_call x10, Pallas kernels, call(): pl.pallas_call(kernel, out_shape=[jax.ShapeDtypeStruct(shape, dtype) for...  44.5 us
    ppermute x13, waiting for transfers between devices, send(): return lax.ppermute(value, ('gx', 'gy'), pairs)  34.3 us
    ppermute x13, starting transfers between devices, send(): return lax.ppermute(value, ('gx', 'gy'), pairs)  14 us
    unnamed x4, local copies, waits for them, and re-layouts  2.19 us
  transfers between devices with their start and end apart: 13, of which 7 were waited for; matrix products, arithmetic and copies ran while one was open for 0% of the time, Pallas kernels for 41%

profile of v14, /device:TPU:24, one launch (start us, length us, event | category | flops | bytes accessed | tf_op | source)
XLA Modules:
  0.0 95.5 jit_solution(5115013407667999841)
XLA Ops:
  0.0 0.1 pad_add_fusion.place
  0.1 0.0 copy-start
  0.1 2.2 %copy-done = f32[1,1024,1024]{2,1,0:T(8,128)S(1)} copy-done((f32[1,1024,1024]{2,1,0:T(8,128)S(1)}, f32[1,1024,1024]{2,1,0:T(8,128)}, u32[]{:S(2)}) %copy-start) | copy-done | bytes 4194328
  2.3 0.6 cut_first.1.a0
  2.9 0.6 cut_side.1.mine
  3.5 1.6 %collective-permute-start = (f32[384,128]{1,0:T(8,128)S(1)}, f32[384,128]{1,0:T(8,128)S(1)}, u32[]{:S(2)}, u32[]{:S(2)}) collective-permute-start(f32[384,128]{1,0:T(8,128)S(1)} %cut_side.1.mine), channel_id=1, source_target_pairs={{0,2},{1,3},{2,0},{3,1},{4,6},{5,7},{6,4},{7,5},{8,10},{9,11},{10,... | collective-permute-start | bytes 589832 | tf_op jit(solution)/shard_map/ppermute | solution.py:681
  5.1 0.3 collective-permute-start.1
  5.4 0.9 cut_second.1
  6.4 0.6 collective-permute-start.2
  7.0 4.4 %collective-permute-done.along = f32[384,128]{1,0:T(8,128)S(1)} collective-permute-done((f32[384,128]{1,0:T(8,128)S(1)}, f32[384,128]{1,0:T(8,128)S(1)}, u32[]{:S(2)}, u32[]{:S(2)}) %collective-permute-start) | collective-permute-done | bytes 196640 | tf_op jit(solution)/shard_map/ppermute | solution.py:681
  11.4 7.0 %gauge_side.1 = (f32[256,256]{1,0:T(8,128)S(1)}, f32[256,256]{1,0:T(8,128)S(1)}) custom-call(f32[384,128]{1,0:T(8,128)S(1)} %cut_side.1.mine, f32[384,128]{1,0:T(8,128)S(1)} %collective-permute-done.along, f32[256,256]{1,0:T(8,128)S(1)} %get-tuple-element.42.b), custom_call_target="tpu_custom_call" | custom-call | flops 8000000000 | bytes 8000000000 | tf_op jit(solution)/shard_map/gauge_side/pallas_call | solution.py:182
  18.4 0.1 collective-permute-start.5
  18.4 0.4 scale_cross.1
  18.9 0.4 collective-permute-done.1.a1
  19.3 2.2 %collective-permute-done.2.a2.swapped = f32[1024,128]{1,0:T(8,128)S(1)} collective-permute-done((f32[1024,128]{1,0:T(8,128)S(1)}, f32[1024,128]{1,0:T(8,128)S(1)}, u32[]{:S(2)}, u32[]{:S(2)}) %collective-permute-start.2) | collective-permute-done | bytes 524320 | tf_op jit(solution)/shard_map/ppermute | solution.py:681
  21.5 1.5 %collective-permute-start.3 = (f32[256,256]{1,0:T(8,128)S(1)}, f32[256,256]{1,0:T(8,128)}, u32[]{:S(2)}, u32[]{:S(2)}) collective-permute-start(f32[256,256]{1,0:T(8,128)S(1)} %get-tuple-element.52.b0), channel_id=1, source_target_pairs={{0,2},{1,3},{2,0},{3,1},{4,6},{5,7},{6,4},{7,5},{8,10},{9,11},{10,... | collective-permute-start | bytes 786440 | tf_op jit(solution)/shard_map/ppermute | solution.py:681
  23.0 8.0 %collective-permute-done.5.b1 = f32[256,256]{1,0:T(8,128)} collective-permute-done((f32[256,256]{1,0:T(8,128)S(1)}, f32[256,256]{1,0:T(8,128)}, u32[]{:S(2)}, u32[]{:S(2)}) %collective-permute-start.5) | collective-permute-done | bytes 262176 | tf_op jit(solution)/shard_map/ppermute | solution.py:681
  31.0 0.0 collective-permute-start.7
  31.0 0.0 collective-permute-done.3.b2
  31.0 1.5 %collective-permute-start.6 = (f32[256,256]{1,0:T(8,128)}, f32[256,256]{1,0:T(8,128)S(1)}, u32[]{:S(2)}, u32[]{:S(2)}) collective-permute-start(f32[256,256]{1,0:T(8,128)} %collective-permute-done.5.b1), channel_id=1, source_target_pairs={{0,2},{1,3},{2,0},{3,1},{4,6},{5,7},{6,4},{7,5},{8,10},{9,11},{10,... | collective-permute-start | bytes 786440 | tf_op jit(solution)/shard_map/ppermute | solution.py:681
  32.5 0.5 collective-permute-start.4
  33.1 0.1 maximum_select_fusion
  33.2 7.2 %collective-permute-done.6.b3 = f32[256,256]{1,0:T(8,128)S(1)} collective-permute-done((f32[256,256]{1,0:T(8,128)}, f32[256,256]{1,0:T(8,128)S(1)}, u32[]{:S(2)}, u32[]{:S(2)}) %collective-permute-start.6) | collective-permute-done | bytes 262176 | tf_op jit(solution)/shard_map/ppermute | solution.py:681
  40.4 1.5 %collective-permute-start.8 = (f32[1408,128]{1,0:T(8,128)S(1)}, f32[1408,128]{1,0:T(8,128)S(1)}, u32[]{:S(2)}, u32[]{:S(2)}) collective-permute-start(f32[1408,128]{1,0:T(8,128)S(1)} %get-tuple-element.65), channel_id=1, source_target_pairs={{0,2},{1,3},{4,6},{5,7},{8,10},{9,11},{12,14},{13,15},{18,16},{19,... | collective-permute-start | bytes 2162696 | tf_op jit(solution)/shard_map/ppermute | solution.py:681
  41.9 4.1 %collective-permute-done.4.a3 = f32[512,128]{1,0:T(8,128)S(1)} collective-permute-done((f32[512,128]{1,0:T(8,128)S(1)}, f32[512,128]{1,0:T(8,128)S(1)}, u32[]{:S(2)}, u32[]{:S(2)}) %collective-permute-start.4) | collective-permute-done | bytes 262176 | tf_op jit(solution)/shard_map/ppermute | solution.py:681
  46.0 10.4 %factor_start.1.side_in = f32[512,512]{1,0:T(8,128)S(1)} custom-call(f32[512,128]{1,0:T(8,128)S(1)} %cut_first.1.a0, f32[512,128]{1,0:T(8,128)S(1)} %collective-permute-done.1.a1, f32[1024,128]{1,0:T(8,128)S(1)} %collective-permute-done.2.a2.swapped, f32[512,128]{1,0:T(8,128)S(1)} %collective-permute-done.4.a3, f32[256,256]{1,0:T(8,128)S(1)} %get-tuple-element.52.b0, ...), custom_call_target="tpu_custom_call" | custom-call | flops 1000000000 | bytes 1000000000 | tf_op jit(solution)/shard_map/factor_start/pallas_call | solution.py:182
  56.5 0.0 copy-start.1
  56.5 2.1 %collective-permute-start.9 = (f32[896,128]{1,0:T(8,128)S(1)}, f32[896,128]{1,0:T(8,128)S(1)}, u32[]{:S(2)}, u32[]{:S(2)}) collective-permute-start(f32[896,128]{1,0:T(8,128)S(1)} %maximum_select_fusion), channel_id=1, source_target_pairs={{0,16},{1,17},{2,18},{3,19},{4,20},{5,21},{6,22},{7,23},{8,24},{9,... | collective-permute-start | bytes 1376264 | tf_op jit(solution)/shard_map/ppermute | solution.py:681
  58.5 0.0 collective-permute-done.7.c11
  58.5 1.5 %collective-permute-start.10 = (f32[1024,128]{1,0:T(8,128)S(1)}, f32[1024,128]{1,0:T(8,128)S(1)}, u32[]{:S(2)}, u32[]{:S(2)}) collective-permute-start(f32[1024,128]{1,0:T(8,128)S(1)} %collective-permute-done.7.c11), channel_id=1, source_target_pairs={{0,2},{1,3},{4,6},{5,7},{8,10},{9,11},{12,14},{13,15},{18,16},{19,... | collective-permute-start | bytes 1572872 | tf_op jit(solution)/shard_map/ppermute | solution.py:681
  60.0 11.1 %factor_end.1 = (bf16[768,768]{1,0:T(8,128)(2,1)S(1)}, bf16[768,768]{1,0:T(8,128)(2,1)S(1)}) custom-call(s32[2]{0:T(128)S(1)} %pad_add_fusion.place, f32[512,512]{1,0:T(8,128)S(1)} %factor_start.1.side_in, f32[256,256]{1,0:T(8,128)S(1)} %get-tuple-element.52.b0, f32[256,256]{1,0:T(8,128)} %collective-permute-done.5.b1, ...), custom_call_target="tpu_custom_call" | custom-call | flops 10000000000 | bytes 10000000000 | tf_op jit(solution)/shard_map/factor_end/pallas_call | solution.py:182
  71.2 0.0 collective-permute-done.8.rest
  71.2 0.0 copy-done.1
  71.2 6.2 %own_rows.1 = (bf16[512,768]{1,0:T(8,128)(2,1)S(1)}, bf16[512,768]{1,0:T(8,128)(2,1)S(1)}, f32[512,512]{1,0:T(8,128)S(1)}, f32[512,768]{1,0:T(8,128)S(1)}) custom-call(s32[2]{0:T(128)S(1)} %pad_add_fusion.place, f32[1,1024,1024]{2,1,0:T(8,128)S(1)} %copy-done.1, bf16[768,768]{1,0:T(8,128)(2,1)S(1)} %get-tuple-element.62.high, ...), custom_call_target="tpu_custom_call" | custom-call | flops 500000000 | bytes 500000000 | tf_op jit(solution)/shard_map/own_rows/pallas_call | solution.py:182
  77.4 0.0 collective-permute-done.9.third
  77.4 1.4 %collective-permute-start.11 = (f32[896,128]{1,0:T(8,128)S(1)}, f32[896,128]{1,0:T(8,128)S(1)}, u32[]{:S(2)}, u32[]{:S(2)}) collective-permute-start(f32[896,128]{1,0:T(8,128)S(1)} %collective-permute-done.9.third), channel_id=1, source_target_pairs={{0,2},{1,3},{2,0},{3,1},{4,6},{5,7},{6,4},{7,5},{8,10},{9,11},{10,... | collective-permute-start | bytes 1376264 | tf_op jit(solution)/shard_map/ppermute | solution.py:681
  78.8 1.4 %collective-permute-start.12 = (f32[640,128]{1,0:T(8,128)S(1)}, f32[640,128]{1,0:T(8,128)S(1)}, u32[]{:S(2)}, u32[]{:S(2)}) collective-permute-start(f32[640,128]{1,0:T(8,128)S(1)} %slice_select_fusion), channel_id=1, source_target_pairs={{0,16},{1,17},{2,18},{3,19},{4,20},{5,21},{6,22},{7,23},{8,24},{9,... | collective-permute-start | bytes 983048 | tf_op jit(solution)/shard_map/ppermute | solution.py:681
  80.3 0.0 collective-permute-done.10.c31
  80.3 7.9 %collective-permute-done.11.passed = f32[896,128]{1,0:T(8,128)S(1)} collective-permute-done((f32[896,128]{1,0:T(8,128)S(1)}, f32[896,128]{1,0:T(8,128)S(1)}, u32[]{:S(2)}, u32[]{:S(2)}) %collective-permute-start.11) | collective-permute-done | bytes 458784 | tf_op jit(solution)/shard_map/ppermute | solution.py:681
  88.1 2.7 %products.1 = (f32[1,1024,1024]{2,1,0:T(8,128)}, f32[512,512]{1,0:T(8,128)S(1)}) custom-call(s32[2]{0:T(128)S(1)} %pad_add_fusion.place, bf16[768,768]{1,0:T(8,128)(2,1)S(1)} %get-tuple-element.62.high, bf16[768,768]{1,0:T(8,128)(2,1)S(1)} %get-tuple-element.63.low, bf16[512,768]{1,0:T(8,128)(2,1)S(1)} %get-tuple-element.66.top, ...), custom_call_target="tpu_custom_call" | custom-call | flops 500000000 | bytes 500000000 | tf_op jit(solution)/shard_map/products/pallas_call | solution.py:182
  90.8 0.0 collective-permute-done.12.last
  90.8 4.5 %finish.1 = f32[1,1024,1024]{2,1,0:T(8,128)} custom-call(s32[2]{0:T(128)S(1)} %pad_add_fusion.place, f32[1,1024,1024]{2,1,0:T(8,128)} %get-tuple-element.73.before, bf16[768,768]{1,0:T(8,128)(2,1)S(1)} %get-tuple-element.62.high, bf16[768,768]{1,0:T(8,128)(2,1)S(1)} %get-tuple-element.63.low, ...), custom_call_target="tpu_custom_call", output_to_operand_aliasing={{}: (1, {})} | custom-call | flops 500000000 | bytes 500000000 | tf_op jit(solution)/shard_map/finish/pallas_call | solution.py:182
  (3 shorter events, 0.1 us)
Async XLA Ops:
  0.1 2.2 %copy-start = (f32[1,1024,1024]{2,1,0:T(8,128)S(1)}, f32[1,1024,1024]{2,1,0:T(8,128)}, u32[]{:S(2)}) copy-start(f32[1,1024,1024]{2,1,0:T(8,128)} %leaf.7) | copy-start | bytes 12582916
  3.5 7.9 %collective-permute-start = (f32[384,128]{1,0:T(8,128)S(1)}, f32[384,128]{1,0:T(8,128)S(1)}, u32[]{:S(2)}, u32[]{:S(2)}) collective-permute-start(f32[384,128]{1,0:T(8,128)S(1)} %cut_side.1.mine), channel_id=1, source_target_pairs={{0,2},{1,3},{2,0},{3,1},{4,6},{5,7},{6,4},{7,5},{8,10},{9,11},{10,... | collective-permute-start | bytes 589832 | tf_op jit(solution)/shard_map/ppermute | solution.py:681
  5.1 14.2 %collective-permute-start.1 = (f32[512,128]{1,0:T(8,128)S(1)}, f32[512,128]{1,0:T(8,128)S(1)}, u32[]{:S(2)}, u32[]{:S(2)}) collective-permute-start(f32[512,128]{1,0:T(8,128)S(1)} %cut_first.1.a0), channel_id=1, source_target_pairs={{0,16},{1,17},{2,18},{3,19},{4,20},{5,21},{6,22},{7,23},{8,24},{9,... | collective-permute-start | bytes 786440 | tf_op jit(solution)/shard_map/ppermute | solution.py:681
  6.4 15.1 %collective-permute-start.2 = (f32[1024,128]{1,0:T(8,128)S(1)}, f32[1024,128]{1,0:T(8,128)S(1)}, u32[]{:S(2)}, u32[]{:S(2)}) collective-permute-start(f32[1024,128]{1,0:T(8,128)S(1)} %get-tuple-element.48), channel_id=1, source_target_pairs={{0,2},{1,3},{2,0},{3,1},{4,6},{5,7},{6,4},{7,5},{8,10},{9,11},{10,... | collective-permute-start | bytes 1572872 | tf_op jit(solution)/shard_map/ppermute | solution.py:681
  18.4 12.6 %collective-permute-start.5 = (f32[256,256]{1,0:T(8,128)S(1)}, f32[256,256]{1,0:T(8,128)}, u32[]{:S(2)}, u32[]{:S(2)}) collective-permute-start(f32[256,256]{1,0:T(8,128)S(1)} %get-tuple-element.52.b0), channel_id=1, source_target_pairs={{0,16},{1,17},{2,18},{3,19},{4,20},{5,21},{6,22},{7,23},{8,24},{9,... | collective-permute-start | bytes 786440 | tf_op jit(solution)/shard_map/ppermute | solution.py:681
  21.5 9.5 %collective-permute-start.3 = (f32[256,256]{1,0:T(8,128)S(1)}, f32[256,256]{1,0:T(8,128)}, u32[]{:S(2)}, u32[]{:S(2)}) collective-permute-start(f32[256,256]{1,0:T(8,128)S(1)} %get-tuple-element.52.b0), channel_id=1, source_target_pairs={{0,2},{1,3},{2,0},{3,1},{4,6},{5,7},{6,4},{7,5},{8,10},{9,11},{10,... | collective-permute-start | bytes 786440 | tf_op jit(solution)/shard_map/ppermute | solution.py:681
  31.0 27.5 %collective-permute-start.7 = (f32[1024,128]{1,0:T(8,128)S(1)}, f32[1024,128]{1,0:T(8,128)S(1)}, u32[]{:S(2)}, u32[]{:S(2)}) collective-permute-start(f32[1024,128]{1,0:T(8,128)S(1)} %get-tuple-element.64.c01), channel_id=1, source_target_pairs={{0,16},{1,17},{2,18},{3,19},{4,20},{5,21},{6,22},{7,23},{8,24},{9,... | collective-permute-start | bytes 1572872 | tf_op jit(solution)/shard_map/ppermute | solution.py:681
  31.0 9.4 %collective-permute-start.6 = (f32[256,256]{1,0:T(8,128)}, f32[256,256]{1,0:T(8,128)S(1)}, u32[]{:S(2)}, u32[]{:S(2)}) collective-permute-start(f32[256,256]{1,0:T(8,128)} %collective-permute-done.5.b1), channel_id=1, source_target_pairs={{0,2},{1,3},{2,0},{3,1},{4,6},{5,7},{6,4},{7,5},{8,10},{9,11},{10,... | collective-permute-start | bytes 786440 | tf_op jit(solution)/shard_map/ppermute | solution.py:681
  32.5 13.5 %collective-permute-start.4 = (f32[512,128]{1,0:T(8,128)S(1)}, f32[512,128]{1,0:T(8,128)S(1)}, u32[]{:S(2)}, u32[]{:S(2)}) collective-permute-start(f32[512,128]{1,0:T(8,128)S(1)} %collective-permute-done.1.a1), channel_id=1, source_target_pairs={{0,2},{1,3},{2,0},{3,1},{4,6},{5,7},{6,4},{7,5},{8,10},{9,11},{10,... | collective-permute-start | bytes 786440 | tf_op jit(solution)/shard_map/ppermute | solution.py:681
  40.4 30.8 %collective-permute-start.8 = (f32[1408,128]{1,0:T(8,128)S(1)}, f32[1408,128]{1,0:T(8,128)S(1)}, u32[]{:S(2)}, u32[]{:S(2)}) collective-permute-start(f32[1408,128]{1,0:T(8,128)S(1)} %get-tuple-element.65), channel_id=1, source_target_pairs={{0,2},{1,3},{4,6},{5,7},{8,10},{9,11},{12,14},{13,15},{18,16},{19,... | collective-permute-start | bytes 2162696 | tf_op jit(solution)/shard_map/ppermute | solution.py:681
  56.5 14.7 %copy-start.1 = (f32[1,1024,1024]{2,1,0:T(8,128)S(1)}, f32[1,1024,1024]{2,1,0:T(8,128)}, u32[]{:S(2)}) copy-start(f32[1,1024,1024]{2,1,0:T(8,128)} %leaf.7) | copy-start | bytes 12582916
  56.5 21.0 %collective-permute-start.9 = (f32[896,128]{1,0:T(8,128)S(1)}, f32[896,128]{1,0:T(8,128)S(1)}, u32[]{:S(2)}, u32[]{:S(2)}) collective-permute-start(f32[896,128]{1,0:T(8,128)S(1)} %maximum_select_fusion), channel_id=1, source_target_pairs={{0,16},{1,17},{2,18},{3,19},{4,20},{5,21},{6,22},{7,23},{8,24},{9,... | collective-permute-start | bytes 1376264 | tf_op jit(solution)/shard_map/ppermute | solution.py:681
  58.5 21.7 %collective-permute-start.10 = (f32[1024,128]{1,0:T(8,128)S(1)}, f32[1024,128]{1,0:T(8,128)S(1)}, u32[]{:S(2)}, u32[]{:S(2)}) collective-permute-start(f32[1024,128]{1,0:T(8,128)S(1)} %collective-permute-done.7.c11), channel_id=1, source_target_pairs={{0,2},{1,3},{4,6},{5,7},{8,10},{9,11},{12,14},{13,15},{18,16},{19,... | collective-permute-start | bytes 1572872 | tf_op jit(solution)/shard_map/ppermute | solution.py:681
  77.4 10.7 %collective-permute-start.11 = (f32[896,128]{1,0:T(8,128)S(1)}, f32[896,128]{1,0:T(8,128)S(1)}, u32[]{:S(2)}, u32[]{:S(2)}) collective-permute-start(f32[896,128]{1,0:T(8,128)S(1)} %collective-permute-done.9.third), channel_id=1, source_target_pairs={{0,2},{1,3},{2,0},{3,1},{4,6},{5,7},{6,4},{7,5},{8,10},{9,11},{10,... | collective-permute-start | bytes 1376264 | tf_op jit(solution)/shard_map/ppermute | solution.py:681
  78.8 12.0 %collective-permute-start.12 = (f32[640,128]{1,0:T(8,128)S(1)}, f32[640,128]{1,0:T(8,128)S(1)}, u32[]{:S(2)}, u32[]{:S(2)}) collective-permute-start(f32[640,128]{1,0:T(8,128)S(1)} %slice_select_fusion), channel_id=1, source_target_pairs={{0,16},{1,17},{2,18},{3,19},{4,20},{5,21},{6,22},{7,23},{8,24},{9,... | collective-permute-start | bytes 983048 | tf_op jit(solution)/shard_map/ppermute | solution.py:681

commit v15 on v14

--- a/solution.py
+++ b/solution.py
@@ -11,7 +11,7 @@
 BF16 = jnp.bfloat16
 T = 128
 R = 16
-FIRST = 1
+FIRST = 2
 SECOND = 8
 HBM = pl.BlockSpec(memory_space=pl.ANY)
 FAR = pl.BlockSpec(memory_space=pltpu.HBM)
@@ -700,7 +700,7 @@
         b, a_x, c1, swapped = tie(b, a_x, c1, swapped)
         b_y = send(b, True)
         a_x, b_y = tie(a_x, b_y)
-        a_d = send(a_x, True)
+        a_d = send(a_x[: a_x.shape[0] - T], True)
         c1, b_x = tie(c1, b_x)
         c1_x = send(c1, False)
         b_x, b_y = tie(b_x, b_y)
@@ -712,7 +712,8 @@
         theirs = jnp.concatenate([c2[: n_mid * T], swapped[-n_last * T :]])
         third, side = tie(jnp.where(same, theirs, c2), side)
         third = send(third, False)
-        c1_d = send(c1_x, True, only=True)
+        c1_x, side = tie(c1_x, side)
+        c1_d = send(jnp.concatenate([a_x[-T:], c1_x]), True, only=True)
         high, low = factor_end(place, side, (b, b_x, b_y, b_d))
         top, bottom, block, part = own_rows(
             place, leaf, high, low, a, c1, c2, a_x, c1_x, swapped, rest

time: 96.8 us -> 102 us (1.054)
  the two profiles are of different devices: /device:TPU:24 before, /device:TPU:4 now
where the time goes in v15:
time: 102 us
  Pallas kernels  44.5 us (44%)
  waiting for transfers between devices  33.7 us (33%)
  starting transfers between devices  21.1 us (21%)
  local copies, waits for them, and re-layouts  2.25 us (2%)
    pallas_call x10, Pallas kernels, call(): pl.pallas_call(kernel, out_shape=[jax.ShapeDtypeStruct(shape, dtype) for...  44.5 us
    ppermute x13, waiting for transfers between devices, send(): return lax.ppermute(value, ('gx', 'gy'), pairs)  33.7 us
    ppermute x13, starting transfers between devices, send(): return lax.ppermute(value, ('gx', 'gy'), pairs)  21.1 us
    unnamed x4, local copies, waits for them, and re-layouts  2.19 us
  transfers between devices with their start and end apart: 13, of which 7 were waited for; matrix products, arithmetic and copies ran while one was open for 0% of the time, Pallas kernels for 38%

profile of v15, /device:TPU:4, one launch (start us, length us, event | category | flops | bytes accessed | tf_op | source)
XLA Modules:
  0.0 102.1 jit_solution(15120469411091157379)
XLA Ops:
  0.0 0.1 pad_add_fusion.place
  0.1 0.0 copy-start
  0.1 2.2 %copy-done = f32[1,1024,1024]{2,1,0:T(8,128)S(1)} copy-done((f32[1,1024,1024]{2,1,0:T(8,128)S(1)}, f32[1,1024,1024]{2,1,0:T(8,128)}, u32[]{:S(2)}) %copy-start) | copy-done | bytes 4194328
  2.3 0.7 cut_first.1.a0
  2.9 0.6 cut_side.1.mine
  3.5 0.1 collective-permute-start
  3.6 3.1 %collective-permute-start.1 = (f32[640,128]{1,0:T(8,128)S(1)}, f32[640,128]{1,0:T(8,128)S(1)}, u32[]{:S(2)}, u32[]{:S(2)}) collective-permute-start(f32[640,128]{1,0:T(8,128)S(1)} %cut_first.1.a0), channel_id=1, source_target_pairs={{0,16},{1,17},{2,18},{3,19},{4,20},{5,21},{6,22},{7,23},{8,24},{9,... | collective-permute-start | bytes 983048 | tf_op jit(solution)/shard_map/ppermute | solution.py:681
  6.7 0.9 cut_second.1
  7.7 1.6 %collective-permute-start.2 = (f32[1024,128]{1,0:T(8,128)S(1)}, f32[1024,128]{1,0:T(8,128)S(1)}, u32[]{:S(2)}, u32[]{:S(2)}) collective-permute-start(f32[1024,128]{1,0:T(8,128)S(1)} %get-tuple-element.49), channel_id=1, source_target_pairs={{0,2},{1,3},{2,0},{3,1},{4,6},{5,7},{6,4},{7,5},{8,10},{9,11},{10,... | collective-permute-start | bytes 1572872 | tf_op jit(solution)/shard_map/ppermute | solution.py:681
  9.2 1.6 %collective-permute-done.along = f32[384,128]{1,0:T(8,128)S(1)} collective-permute-done((f32[384,128]{1,0:T(8,128)S(1)}, f32[384,128]{1,0:T(8,128)S(1)}, u32[]{:S(2)}, u32[]{:S(2)}) %collective-permute-start) | collective-permute-done | bytes 196640 | tf_op jit(solution)/shard_map/ppermute | solution.py:681
  10.8 7.0 %gauge_side.1 = (f32[256,256]{1,0:T(8,128)S(1)}, f32[256,256]{1,0:T(8,128)S(1)}) custom-call(f32[384,128]{1,0:T(8,128)S(1)} %cut_side.1.mine, f32[384,128]{1,0:T(8,128)S(1)} %collective-permute-done.along, f32[256,256]{1,0:T(8,128)S(1)} %get-tuple-element.44.b), custom_call_target="tpu_custom_call" | custom-call | flops 8000000000 | bytes 8000000000 | tf_op jit(solution)/shard_map/gauge_side/pallas_call | solution.py:182
  17.8 3.2 %collective-permute-start.3 = (f32[256,256]{1,0:T(8,128)S(1)}, f32[256,256]{1,0:T(8,128)}, u32[]{:S(2)}, u32[]{:S(2)}) collective-permute-start(f32[256,256]{1,0:T(8,128)S(1)} %get-tuple-element.56.b0), channel_id=1, source_target_pairs={{0,16},{1,17},{2,18},{3,19},{4,20},{5,21},{6,22},{7,23},{8,24},{9,... | collective-permute-start | bytes 786440 | tf_op jit(solution)/shard_map/ppermute | solution.py:681
  21.1 0.4 scale_cross.1
  21.5 6.4 %collective-permute-done.1.a1 = f32[640,128]{1,0:T(8,128)S(1)} collective-permute-done((f32[640,128]{1,0:T(8,128)S(1)}, f32[640,128]{1,0:T(8,128)S(1)}, u32[]{:S(2)}, u32[]{:S(2)}) %collective-permute-start.1) | collective-permute-done | bytes 327712 | tf_op jit(solution)/shard_map/ppermute | solution.py:681
  27.9 0.0 collective-permute-done.2.a2.swapped
  27.9 1.6 %collective-permute-start.5 = (f32[256,256]{1,0:T(8,128)S(1)}, f32[256,256]{1,0:T(8,128)}, u32[]{:S(2)}, u32[]{:S(2)}) collective-permute-start(f32[256,256]{1,0:T(8,128)S(1)} %get-tuple-element.56.b0), channel_id=1, source_target_pairs={{0,2},{1,3},{2,0},{3,1},{4,6},{5,7},{6,4},{7,5},{8,10},{9,11},{10,... | collective-permute-start | bytes 786440 | tf_op jit(solution)/shard_map/ppermute | solution.py:681
  29.5 3.0 %collective-permute-done.3.b1 = f32[256,256]{1,0:T(8,128)} collective-permute-done((f32[256,256]{1,0:T(8,128)S(1)}, f32[256,256]{1,0:T(8,128)}, u32[]{:S(2)}, u32[]{:S(2)}) %collective-permute-start.3) | collective-permute-done | bytes 262176 | tf_op jit(solution)/shard_map/ppermute | solution.py:681
  32.5 0.0 collective-permute-start.4
  32.5 2.0 %collective-permute-done.5.b2 = f32[256,256]{1,0:T(8,128)} collective-permute-done((f32[256,256]{1,0:T(8,128)S(1)}, f32[256,256]{1,0:T(8,128)}, u32[]{:S(2)}, u32[]{:S(2)}) %collective-permute-start.5) | collective-permute-done | bytes 262176 | tf_op jit(solution)/shard_map/ppermute | solution.py:681
  34.5 1.7 %collective-permute-start.6 = (f32[512,128]{1,0:T(8,128)S(1)}, f32[512,128]{1,0:T(8,128)S(1)}, u32[]{:S(2)}, u32[]{:S(2)}) collective-permute-start(f32[512,128]{1,0:T(8,128)S(1)} %slice.17), channel_id=1, source_target_pairs={{0,2},{1,3},{2,0},{3,1},{4,6},{5,7},{6,4},{7,5},{8,10},{9,11},{10,... | collective-permute-start | bytes 786440 | tf_op jit(solution)/shard_map/ppermute | solution.py:681
  36.2 0.4 collective-permute-start.7
  36.7 8.8 %collective-permute-done.7.b3 = f32[256,256]{1,0:T(8,128)S(1)} collective-permute-done((f32[256,256]{1,0:T(8,128)}, f32[256,256]{1,0:T(8,128)S(1)}, u32[]{:S(2)}, u32[]{:S(2)}) %collective-permute-start.7) | collective-permute-done | bytes 262176 | tf_op jit(solution)/shard_map/ppermute | solution.py:681
  45.5 1.5 %collective-permute-start.8 = (f32[1408,128]{1,0:T(8,128)S(1)}, f32[1408,128]{1,0:T(8,128)S(1)}, u32[]{:S(2)}, u32[]{:S(2)}) collective-permute-start(f32[1408,128]{1,0:T(8,128)S(1)} %get-tuple-element.69), channel_id=1, source_target_pairs={{0,2},{1,3},{4,6},{5,7},{8,10},{9,11},{12,14},{13,15},{18,16},{19,... | collective-permute-start | bytes 2162696 | tf_op jit(solution)/shard_map/ppermute | solution.py:681
  47.0 0.0 collective-permute-done.6.a3
  47.0 10.4 %factor_start.1.side_in = f32[512,512]{1,0:T(8,128)S(1)} custom-call(f32[640,128]{1,0:T(8,128)S(1)} %cut_first.1.a0, f32[640,128]{1,0:T(8,128)S(1)} %collective-permute-done.1.a1, f32[1024,128]{1,0:T(8,128)S(1)} %collective-permute-done.2.a2.swapped, f32[512,128]{1,0:T(8,128)S(1)} %collective-permute-done.6.a3, f32[256,256]{1,0:T(8,128)S(1)} %get-tuple-element.56.b0, ...), custom_call_target="tpu_custom_call" | custom-call | flops 1000000000 | bytes 1000000000 | tf_op jit(solution)/shard_map/factor_start/pallas_call | solution.py:182
  57.5 0.0 collective-permute-done.4.c11
  57.5 4.8 %collective-permute-start.9 = (f32[768,128]{1,0:T(8,128)S(1)}, f32[768,128]{1,0:T(8,128)S(1)}, u32[]{:S(2)}, u32[]{:S(2)}) collective-permute-start(f32[768,128]{1,0:T(8,128)S(1)} %maximum_select_fusion), channel_id=1, source_target_pairs={{0,16},{1,17},{2,18},{3,19},{4,20},{5,21},{6,22},{7,23},{8,24},{9,... | collective-permute-start | bytes 1179656 | tf_op jit(solution)/shard_map/ppermute | solution.py:681
  62.3 0.0 copy-start.1
  62.3 1.8 %collective-permute-start.10 = (f32[1152,128]{1,0:T(8,128)S(1)}, f32[1152,128]{1,0:T(8,128)S(1)}, u32[]{:S(2)}, u32[]{:S(2)}) collective-permute-start(f32[1152,128]{1,0:T(8,128)S(1)} %pad_maximum_fusion), channel_id=1, source_target_pairs={{0,2},{1,3},{4,6},{5,7},{8,10},{9,11},{12,14},{13,15},{18,16},{19,... | collective-permute-start | bytes 1769480 | tf_op jit(solution)/shard_map/ppermute | solution.py:681
  64.1 11.1 %factor_end.1 = (bf16[768,768]{1,0:T(8,128)(2,1)S(1)}, bf16[768,768]{1,0:T(8,128)(2,1)S(1)}) custom-call(s32[2]{0:T(128)S(1)} %pad_add_fusion.place, f32[512,512]{1,0:T(8,128)S(1)} %factor_start.1.side_in, f32[256,256]{1,0:T(8,128)S(1)} %get-tuple-element.56.b0, f32[256,256]{1,0:T(8,128)} %collective-permute-done.3.b1, ...), custom_call_target="tpu_custom_call" | custom-call | flops 10000000000 | bytes 10000000000 | tf_op jit(solution)/shard_map/factor_end/pallas_call | solution.py:182
  75.2 0.0 collective-permute-done.8.rest
  75.2 0.0 copy-done.1
  75.2 6.2 %own_rows.1 = (bf16[512,768]{1,0:T(8,128)(2,1)S(1)}, bf16[512,768]{1,0:T(8,128)(2,1)S(1)}, f32[512,512]{1,0:T(8,128)S(1)}, f32[512,768]{1,0:T(8,128)S(1)}) custom-call(s32[2]{0:T(128)S(1)} %pad_add_fusion.place, f32[1,1024,1024]{2,1,0:T(8,128)S(1)} %copy-done.1, bf16[768,768]{1,0:T(8,128)(2,1)S(1)} %get-tuple-element.66.high, ...), custom_call_target="tpu_custom_call" | custom-call | flops 500000000 | bytes 500000000 | tf_op jit(solution)/shard_map/own_rows/pallas_call | solution.py:182
  81.5 0.0 collective-permute-done.9.third
  81.5 1.4 %collective-permute-start.11 = (f32[768,128]{1,0:T(8,128)S(1)}, f32[768,128]{1,0:T(8,128)S(1)}, u32[]{:S(2)}, u32[]{:S(2)}) collective-permute-start(f32[768,128]{1,0:T(8,128)S(1)} %collective-permute-done.9.third), channel_id=1, source_target_pairs={{0,2},{1,3},{2,0},{3,1},{4,6},{5,7},{6,4},{7,5},{8,10},{9,11},{10,... | collective-permute-start | bytes 1179656 | tf_op jit(solution)/shard_map/ppermute | solution.py:681
  82.9 0.0 collective-permute-start.12
  82.9 0.0 collective-permute-done.10.c31
  82.9 6.9 %collective-permute-done.11.passed = f32[768,128]{1,0:T(8,128)S(1)} collective-permute-done((f32[768,128]{1,0:T(8,128)S(1)}, f32[768,128]{1,0:T(8,128)S(1)}, u32[]{:S(2)}, u32[]{:S(2)}) %collective-permute-start.11) | collective-permute-done | bytes 393248 | tf_op jit(solution)/shard_map/ppermute | solution.py:681
  89.8 2.7 %products.1 = (f32[1,1024,1024]{2,1,0:T(8,128)}, f32[512,512]{1,0:T(8,128)S(1)}) custom-call(s32[2]{0:T(128)S(1)} %pad_add_fusion.place, bf16[768,768]{1,0:T(8,128)(2,1)S(1)} %get-tuple-element.66.high, bf16[768,768]{1,0:T(8,128)(2,1)S(1)} %get-tuple-element.67.low, bf16[512,768]{1,0:T(8,128)(2,1)S(1)} %get-tuple-element.70.top, ...), custom_call_target="tpu_custom_call" | custom-call | flops 500000000 | bytes 500000000 | tf_op jit(solution)/shard_map/products/pallas_call | solution.py:182
  92.4 5.1 %collective-permute-done.12.last = f32[640,128]{1,0:T(8,128)S(1)} collective-permute-done((f32[640,128]{1,0:T(8,128)S(1)}, f32[640,128]{1,0:T(8,128)S(1)}, u32[]{:S(2)}, u32[]{:S(2)}) %collective-permute-start.12) | collective-permute-done | bytes 327712 | tf_op jit(solution)/shard_map/ppermute | solution.py:681
  97.5 4.5 %finish.1 = f32[1,1024,1024]{2,1,0:T(8,128)} custom-call(s32[2]{0:T(128)S(1)} %pad_add_fusion.place, f32[1,1024,1024]{2,1,0:T(8,128)} %get-tuple-element.77.before, bf16[768,768]{1,0:T(8,128)(2,1)S(1)} %get-tuple-element.66.high, bf16[768,768]{1,0:T(8,128)(2,1)S(1)} %get-tuple-element.67.low, ...), custom_call_target="tpu_custom_call", output_to_operand_aliasing={{}: (1, {})} | custom-call | flops 500000000 | bytes 500000000 | tf_op jit(solution)/shard_map/finish/pallas_call | solution.py:182
  (7 shorter events, 0.2 us)
Async XLA Ops:
  0.1 2.2 %copy-start = (f32[1,1024,1024]{2,1,0:T(8,128)S(1)}, f32[1,1024,1024]{2,1,0:T(8,128)}, u32[]{:S(2)}) copy-start(f32[1,1024,1024]{2,1,0:T(8,128)} %leaf.7) | copy-start | bytes 12582916
  3.5 7.3 %collective-permute-start = (f32[384,128]{1,0:T(8,128)S(1)}, f32[384,128]{1,0:T(8,128)S(1)}, u32[]{:S(2)}, u32[]{:S(2)}) collective-permute-start(f32[384,128]{1,0:T(8,128)S(1)} %cut_side.1.mine), channel_id=1, source_target_pairs={{0,2},{1,3},{2,0},{3,1},{4,6},{5,7},{6,4},{7,5},{8,10},{9,11},{10,... | collective-permute-start | bytes 589832 | tf_op jit(solution)/shard_map/ppermute | solution.py:681
  3.6 24.3 %collective-permute-start.1 = (f32[640,128]{1,0:T(8,128)S(1)}, f32[640,128]{1,0:T(8,128)S(1)}, u32[]{:S(2)}, u32[]{:S(2)}) collective-permute-start(f32[640,128]{1,0:T(8,128)S(1)} %cut_first.1.a0), channel_id=1, source_target_pairs={{0,16},{1,17},{2,18},{3,19},{4,20},{5,21},{6,22},{7,23},{8,24},{9,... | collective-permute-start | bytes 983048 | tf_op jit(solution)/shard_map/ppermute | solution.py:681
  7.7 20.3 %collective-permute-start.2 = (f32[1024,128]{1,0:T(8,128)S(1)}, f32[1024,128]{1,0:T(8,128)S(1)}, u32[]{:S(2)}, u32[]{:S(2)}) collective-permute-start(f32[1024,128]{1,0:T(8,128)S(1)} %get-tuple-element.49), channel_id=1, source_target_pairs={{0,2},{1,3},{2,0},{3,1},{4,6},{5,7},{6,4},{7,5},{8,10},{9,11},{10,... | collective-permute-start | bytes 1572872 | tf_op jit(solution)/shard_map/ppermute | solution.py:681
  17.8 14.7 %collective-permute-start.3 = (f32[256,256]{1,0:T(8,128)S(1)}, f32[256,256]{1,0:T(8,128)}, u32[]{:S(2)}, u32[]{:S(2)}) collective-permute-start(f32[256,256]{1,0:T(8,128)S(1)} %get-tuple-element.56.b0), channel_id=1, source_target_pairs={{0,16},{1,17},{2,18},{3,19},{4,20},{5,21},{6,22},{7,23},{8,24},{9,... | collective-permute-start | bytes 786440 | tf_op jit(solution)/shard_map/ppermute | solution.py:681
  27.9 6.5 %collective-permute-start.5 = (f32[256,256]{1,0:T(8,128)S(1)}, f32[256,256]{1,0:T(8,128)}, u32[]{:S(2)}, u32[]{:S(2)}) collective-permute-start(f32[256,256]{1,0:T(8,128)S(1)} %get-tuple-element.56.b0), channel_id=1, source_target_pairs={{0,2},{1,3},{2,0},{3,1},{4,6},{5,7},{6,4},{7,5},{8,10},{9,11},{10,... | collective-permute-start | bytes 786440 | tf_op jit(solution)/shard_map/ppermute | solution.py:681
  32.5 25.0 %collective-permute-start.4 = (f32[1024,128]{1,0:T(8,128)S(1)}, f32[1024,128]{1,0:T(8,128)S(1)}, u32[]{:S(2)}, u32[]{:S(2)}) collective-permute-start(f32[1024,128]{1,0:T(8,128)S(1)} %get-tuple-element.51.c01), channel_id=1, source_target_pairs={{0,16},{1,17},{2,18},{3,19},{4,20},{5,21},{6,22},{7,23},{8,24},{9,... | collective-permute-start | bytes 1572872 | tf_op jit(solution)/shard_map/ppermute | solution.py:681
  34.5 12.5 %collective-permute-start.6 = (f32[512,128]{1,0:T(8,128)S(1)}, f32[512,128]{1,0:T(8,128)S(1)}, u32[]{:S(2)}, u32[]{:S(2)}) collective-permute-start(f32[512,128]{1,0:T(8,128)S(1)} %slice.17), channel_id=1, source_target_pairs={{0,2},{1,3},{2,0},{3,1},{4,6},{5,7},{6,4},{7,5},{8,10},{9,11},{10,... | collective-permute-start | bytes 786440 | tf_op jit(solution)/shard_map/ppermute | solution.py:681
  36.2 9.3 %collective-permute-start.7 = (f32[256,256]{1,0:T(8,128)}, f32[256,256]{1,0:T(8,128)S(1)}, u32[]{:S(2)}, u32[]{:S(2)}) collective-permute-start(f32[256,256]{1,0:T(8,128)} %collective-permute-done.3.b1), channel_id=1, source_target_pairs={{0,2},{1,3},{2,0},{3,1},{4,6},{5,7},{6,4},{7,5},{8,10},{9,11},{10,... | collective-permute-start | bytes 786440 | tf_op jit(solution)/shard_map/ppermute | solution.py:681
  45.5 29.7 %collective-permute-start.8 = (f32[1408,128]{1,0:T(8,128)S(1)}, f32[1408,128]{1,0:T(8,128)S(1)}, u32[]{:S(2)}, u32[]{:S(2)}) collective-permute-start(f32[1408,128]{1,0:T(8,128)S(1)} %get-tuple-element.69), channel_id=1, source_target_pairs={{0,2},{1,3},{4,6},{5,7},{8,10},{9,11},{12,14},{13,15},{18,16},{19,... | collective-permute-start | bytes 2162696 | tf_op jit(solution)/shard_map/ppermute | solution.py:681
  57.5 24.0 %collective-permute-start.9 = (f32[768,128]{1,0:T(8,128)S(1)}, f32[768,128]{1,0:T(8,128)S(1)}, u32[]{:S(2)}, u32[]{:S(2)}) collective-permute-start(f32[768,128]{1,0:T(8,128)S(1)} %maximum_select_fusion), channel_id=1, source_target_pairs={{0,16},{1,17},{2,18},{3,19},{4,20},{5,21},{6,22},{7,23},{8,24},{9,... | collective-permute-start | bytes 1179656 | tf_op jit(solution)/shard_map/ppermute | solution.py:681
  62.3 12.9 %copy-start.1 = (f32[1,1024,1024]{2,1,0:T(8,128)S(1)}, f32[1,1024,1024]{2,1,0:T(8,128)}, u32[]{:S(2)}) copy-start(f32[1,1024,1024]{2,1,0:T(8,128)} %leaf.7) | copy-start | bytes 12582916
  62.3 20.6 %collective-permute-start.10 = (f32[1152,128]{1,0:T(8,128)S(1)}, f32[1152,128]{1,0:T(8,128)S(1)}, u32[]{:S(2)}, u32[]{:S(2)}) collective-permute-start(f32[1152,128]{1,0:T(8,128)S(1)} %pad_maximum_fusion), channel_id=1, source_target_pairs={{0,2},{1,3},{4,6},{5,7},{8,10},{9,11},{12,14},{13,15},{18,16},{19,... | collective-permute-start | bytes 1769480 | tf_op jit(solution)/shard_map/ppermute | solution.py:681
  81.5 8.3 %collective-permute-start.11 = (f32[768,128]{1,0:T(8,128)S(1)}, f32[768,128]{1,0:T(8,128)S(1)}, u32[]{:S(2)}, u32[]{:S(2)}) collective-permute-start(f32[768,128]{1,0:T(8,128)S(1)} %collective-permute-done.9.third), channel_id=1, source_target_pairs={{0,2},{1,3},{2,0},{3,1},{4,6},{5,7},{6,4},{7,5},{8,10},{9,11},{10,... | collective-permute-start | bytes 1179656 | tf_op jit(solution)/shard_map/ppermute | solution.py:681
  82.9 14.6 %collective-permute-start.12 = (f32[640,128]{1,0:T(8,128)S(1)}, f32[640,128]{1,0:T(8,128)S(1)}, u32[]{:S(2)}, u32[]{:S(2)}) collective-permute-start(f32[640,128]{1,0:T(8,128)S(1)} %slice_select_fusion), channel_id=1, source_target_pairs={{0,16},{1,17},{2,18},{3,19},{4,20},{5,21},{6,22},{7,23},{8,24},{9,... | collective-permute-start | bytes 983048 | tf_op jit(solution)/shard_map/ppermute | solution.py:681
